TPU v7x, 32 devices: a whole 2x2x4 slice. The times are simulated.
32 devices in a mesh: groups: 2 (over y), wide: 4 (over z), narrow: 2 (over x), sub: 2 (over core).
Axes of the slice: x: 2, y: 2, z: 4, core: 2. Of those that a mesh axis runs over, the one named last changes fastest.
Arguments:
- tokens: bfloat16 [96, 8192], P(('groups', 'wide'), ('narrow', 'sub')), parts along dimension 0, may hold values from -6 to 6
- gate_weight: bfloat16 [8192, 26624], P(('narrow', 'sub'), 'wide'), may hold values from -0.0625 to 0.0625
- up_weight: bfloat16 [8192, 26624], P(('narrow', 'sub'), 'wide'), may hold values from -0.0625 to 0.0625
- down_weight: bfloat16 [26624, 8192], P('wide', ('narrow', 'sub')), may hold values from -0.0390625 to 0.0390625
Outputs:
- mixed: bfloat16 [96, 8192], P(('groups', 'wide'), ('narrow', 'sub')), parts along dimension 0
There are 2 independent parts, one for each index of `groups`. A program takes and returns all parts, laid end to end along the dimension named above; an argument that names none is the same for every part. Nothing has to cross between parts.
All inputs are finite; a program needn't handle non-finite values.
Results may differ from a plain program's by a relative error of at most 0.0049.
Values may be sent and summed in bfloat16 or wider, within the bound.
No kernel may reach another device: no remote copies, remote signals or barrier semaphores. Data moves between devices by JAX's collectives and lax.ppermute only.
A program may use at most 192 MiB of HBM per device.

v0:
```python
import jax
import jax.numpy as jnp
from jax import lax
from jax.sharding import PartitionSpec as P


def activate(gate_sums, up_sums):
    return (jax.nn.silu(gate_sums) * up_sums).astype(jnp.bfloat16)


def per_device(tokens, gate_weight, up_weight, down_weight):
    hidden_units = gate_weight.shape[1]
    section = lax.all_gather(tokens, "wide", axis=0, tiled=True)
    gate_part = jnp.dot(section, gate_weight, preferred_element_type=jnp.float32)
    up_part = jnp.dot(section, up_weight, preferred_element_type=jnp.float32)
    projected = jnp.concatenate([gate_part, up_part], axis=1)
    summed = lax.psum(projected, ("narrow", "sub"))
    hidden = activate(summed[:, :hidden_units], summed[:, hidden_units:])
    mixed = lax.psum_scatter(
        jnp.dot(hidden, down_weight, preferred_element_type=jnp.float32),
        "wide",
        scatter_dimension=0,
        tiled=True,
    )
    return mixed.astype(jnp.bfloat16)


def solution(mesh):
    placed = (
        P(("groups", "wide"), ("narrow", "sub")),
        P(("narrow", "sub"), "wide"),
        P(("narrow", "sub"), "wide"),
        P("wide", ("narrow", "sub")),
    )
    return jax.shard_map(
        per_device,
        mesh=mesh,
        in_specs=placed,
        out_specs=P(("groups", "wide"), ("narrow", "sub")),
        check_vma=False,
    )
```

profile of v0, /device:TPU:0, one launch (start us, length us, event | category | flops | bytes accessed | tf_op | source)
XLA Modules:
  0.0 148.7 jit_solution(10305043913052936648)
XLA Ops:
  6.5 0.0 all-reduce.4.cloned.1.call-start
  6.5 15.8 %all-gather = bf16[4,12,2048]{2,1,0:T(8,128)(2,1)S(1)} all-gather(bf16[1,12,2048]{2,1,0:T(8,128)(2,1)} %bitcast.9), channel_id=1, replica_groups=mesh['groups'=2,'wide'=4,'narrow'=2,'sub'=2] {'wide'}, dimensions={0}, use_global_device_ids=true | all-gather | bytes 245760 | tf_op jit(solution)/shard_map/all_gather | solution.py:13
  22.4 11.2 %fusion.6 = f32[48,6656]{1,0:T(8,128)S(1)} fusion(bf16[48,2048]{1,0:T(8,128)(2,1)S(1)} %reshape.1, bf16[2048,6656]{1,0:T(8,128)(2,1)} %param.5), kind=kOutput, calls=%fused_computation.7 | convolution fusion | flops 1308622848 | bytes 28737536 | tf_op jit(solution)/shard_map/dot_general | solution.py:14
  33.6 11.2 %fusion.7 = f32[48,6656]{1,0:T(8,128)S(1)} fusion(bf16[48,2048]{1,0:T(8,128)(2,1)S(1)} %reshape.1, bf16[2048,6656]{1,0:T(8,128)(2,1)} %param.6), kind=kOutput, calls=%fused_computation.8 | convolution fusion | flops 1308622848 | bytes 28737536 | tf_op jit(solution)/shard_map/dot_general | solution.py:15
  44.8 1.7 %pad_maximum_fusion = f32[48,13312]{1,0:T(8,128)} fusion(f32[48,6656]{1,0:T(8,128)S(1)} %fusion.7, f32[48,6656]{1,0:T(8,128)S(1)} %fusion.6), kind=kLoop, calls=%fused_computation | loop fusion | flops 638976 | bytes 5111808 | tf_op jit(solution)/shard_map/concatenate | solution.py:16
  46.5 0.0 all-reduce.4.cloned.1.call-update
  46.5 0.0 copy-start
  46.5 60.5 %all-reduce.4.cloned.1.call-done = f32[48,13312]{1,0:T(8,128)} async-done(((f32[48,13312]{1,0:T(8,128)}), f32[48,13312]{1,0:T(8,128)}) %all-reduce.4.cloned.1.call-update) | async-done | bytes 2555920 | tf_op jit(solution)/shard_map/psum | solution.py:17
  107.0 11.9 %fusion.2 = f32[48,2048]{1,0:T(8,128)S(1)} fusion(bf16[6656,2048]{1,0:T(8,128)(2,1)} %param.7, f32[48,13312]{1,0:T(8,128)} %all-reduce.4.cloned.1.call-done), kind=kOutput, calls=%fused_computation.3 | convolution fusion | flops 1310539776 | bytes 30212096 | tf_op jit(solution)/shard_map/dot_general | solution.py:20
  119.0 18.4 %fusion = f32[16,2048]{1,0:T(8,128)S(1)} fusion(f32[48,2048]{1,0:T(8,128)S(1)} %fusion.2), kind=kCustom, calls=%all-reduce-scatter | all-reduce-scatter fusion | flops 131073 | bytes 524800
  137.4 1.7 %collective-permute-start = (bf16[12,2048]{1,0:T(8,128)(2,1)S(1)}, bf16[12,2048]{1,0:T(8,128)(2,1)S(1)}, u32[]{:S(2)}, u32[]{:S(2)}) collective-permute-start(bf16[12,2048]{1,0:T(8,128)(2,1)S(1)} %slice.10), channel_id=1, source_target_pairs={{0,4},{4,8},{8,12},{1,5},{5,9},{9,13},{2,6},{6,10},{10,14},{3,7},{... | collective-permute-start | bytes 147464
  139.1 0.0 copy-done
  139.1 0.6 dynamic-slice.4
  140.4 0.6 collective-permute-done
  141.0 0.2 concatenate.4
  141.2 0.7 dynamic-slice_convert_fusion
  (2 shorter events, 0.1 us)
Async XLA Ops:
  6.5 100.5 %all-reduce.4.cloned.1.call-start = ((), (), s32[]{:S(2)}) async-start(), calls=%async_computation | async-start | bytes 5111808 | tf_op jit(solution)/shard_map/psum | solution.py:17
  46.5 92.6 %copy-start = (u32[32]{0:T(128)S(1)}, u32[32]{0:T(128)}, u32[]{:S(2)}) copy-start(u32[32]{0:T(128)} %constant.6) | copy-start | bytes 388
  137.4 3.6 %collective-permute-start = (bf16[12,2048]{1,0:T(8,128)(2,1)S(1)}, bf16[12,2048]{1,0:T(8,128)(2,1)S(1)}, u32[]{:S(2)}, u32[]{:S(2)}) collective-permute-start(bf16[12,2048]{1,0:T(8,128)(2,1)S(1)} %slice.10), channel_id=1, source_target_pairs={{0,4},{4,8},{8,12},{1,5},{5,9},{9,13},{2,6},{6,10},{10,14},{3,7},{... | collective-permute-start | bytes 147464
Sparse Core Ops, SparseCore 0:
  46.6 60.3 all-reduce.3
where the time goes:
time: 149 us
  waiting for transfers between devices  61.2 us (41%)
  blocking collectives  34.3 us (23%)
  matrix products  34.3 us (23%)
  between operations  14.1 us (9%)
  starting transfers between devices  1.69 us (1%)
  other arithmetic  1.66 us (1%)
  local copies, waits for them, and re-layouts  1.51 us (1%)
    psum x1, waiting for transfers between devices, per_device(): summed = lax.psum(projected, ('narrow', 'sub'))  60.5 us
    unnamed x1, blocking collectives  18.4 us
    all_gather x1, blocking collectives, per_device(): section = lax.all_gather(tokens, 'wide', axis=0, tiled=True)  15.8 us
    dot_general x1, matrix products, per_device(): jnp.dot(hidden, down_weight, preferred_element_type=jnp.float32)  11.9 us
    dot_general x1, matrix products, per_device(): jnp.dot(section, gate_weight, preferred_element_type=jnp.float32)  11.2 us
    dot_general x1, matrix products, per_device(): up_part = jnp.dot(section, up_weight, preferred_element_type=jnp.float32)  11.2 us
  transfers between devices with their start and end apart: 2, of which 2 were waited for; matrix products, arithmetic and copies ran while one was open for 0% of the time, Pallas kernels for 0%

commit v1 on v0

v1 whole, which is shorter than its diff:
```python
import jax
import jax.numpy as jnp
from jax import lax
from jax.sharding import PartitionSpec as P

BF16 = jnp.bfloat16
F32 = jnp.float32


def activate(gate_sums, up_sums):
    return (jax.nn.silu(gate_sums) * up_sums).astype(BF16)


def general(tokens, gate_weight, up_weight, down_weight):
    section = lax.all_gather(tokens, "wide", axis=0, tiled=True)
    gate_part = jnp.dot(section, gate_weight, preferred_element_type=F32)
    up_part = jnp.dot(section, up_weight, preferred_element_type=F32)
    gate_sums = lax.psum(gate_part, ("narrow", "sub"))
    up_sums = lax.psum(up_part, ("narrow", "sub"))
    mixed = lax.psum_scatter(
        jnp.dot(activate(gate_sums, up_sums), down_weight, preferred_element_type=F32),
        "wide",
        scatter_dimension=0,
        tiled=True,
    )
    return mixed.astype(BF16)


def swap(x, axis):
    return lax.ppermute(x, axis, [(0, 1), (1, 0)])


def place(wide, narrow, sub):
    return (wide * 2 + narrow) * 2 + sub


def partner(position, wide, narrow, sub):
    return (wide + (position ^ (2 * sub + narrow))) % 4


def moves(position):
    return [
        (place(w, n, s), place(partner(position, w, n, s), n, s))
        for w in range(4)
        for n in range(2)
        for s in range(2)
    ]


AXES = ("wide", "narrow", "sub")


def shared(tokens, gate_weight, up_weight, down_weight):
    half = gate_weight.shape[1] // 2
    rows = tokens.shape[0]
    group = lax.axis_index("groups")
    pair = jnp.concatenate([tokens, swap(tokens, "groups")], axis=0)
    section = jnp.concatenate(
        [lax.ppermute(pair, AXES, [(owner, device) for device, owner in moves(p)]) for p in range(4)], axis=0
    )
    gate_half = lax.dynamic_slice_in_dim(gate_weight, group * half, half, axis=1)
    up_half = lax.dynamic_slice_in_dim(up_weight, group * half, half, axis=1)
    down_half = lax.dynamic_slice_in_dim(down_weight, group * half, half, axis=0)
    gate_part = jnp.dot(section, gate_half, preferred_element_type=F32)
    up_part = jnp.dot(section, up_half, preferred_element_type=F32)

    own = 4 * rows
    both = jnp.concatenate([gate_part, up_part], axis=1)
    both = both[:own] + swap(both[own:], "sub")
    own = 2 * rows
    sums = both[:own] + swap(both[own:].astype(BF16), "narrow").astype(F32)
    hidden = activate(sums[:, :half], sums[:, half:])
    hidden = jnp.concatenate([hidden, swap(hidden, "narrow")], axis=0)
    hidden = jnp.concatenate([hidden, swap(hidden, "sub")], axis=0)

    mixed = jnp.dot(hidden, down_half, preferred_element_type=F32).reshape(4, 2, rows, -1)
    mixed = mixed[:, 0] + swap(mixed[:, 1].astype(BF16), "groups").astype(F32)
    out = sum(lax.ppermute(mixed[p], AXES, moves(p)) for p in range(4))
    return out.astype(BF16)


def solution(mesh):
    placed = (
        P(("groups", "wide"), ("narrow", "sub")),
        P(("narrow", "sub"), "wide"),
        P(("narrow", "sub"), "wide"),
        P("wide", ("narrow", "sub")),
    )
    sizes = tuple(mesh.shape[axis] for axis in ("groups", "wide", "narrow", "sub"))
    return jax.shard_map(
        shared if sizes == (2, 4, 2, 2) else general,
        mesh=mesh,
        in_specs=placed,
        out_specs=P(("groups", "wide"), ("narrow", "sub")),
        check_vma=False,
    )
```

time: 149 us -> 91.9 us (0.62)
  blocking collectives: 34.3 us -> 0 us
  starting transfers between devices: 1.69 us -> 31.4 us
  waiting for transfers between devices: 61.2 us -> 36 us
  between operations: 14.1 us -> 0.21 us
  matrix products: 34.3 us -> 21.5 us
    psum x1 -> x0, waiting for transfers between devices: 60.5 us -> none  [per_device(): summed = lax.psum(projected, ('narrow', 'sub'))]
    ppermute x0 -> x14, waiting for transfers between devices: none -> 36 us  [the longest x6 25.4 us: swap(): return lax.ppermute(x, axis, [(0, 1), (1, 0)])]
    ppermute x0 -> x14, starting transfers between devices: none -> 31.4 us  [the longest x4 12.4 us: shared(): lax.ppermute(pair, AXES, [(owner, device) for device, owner in moves(p)])]
    unnamed x1 -> x0, blocking collectives: 18.4 us -> none
    all_gather x1 -> x0, blocking collectives: 15.8 us -> none  [per_device(): section = lax.all_gather(tokens, 'wide', axis=0, tiled=True)]
    dot_general x3, matrix products: 34.3 us -> 21.5 us  [the longest x1 7.2 us: shared(): jnp.dot(hidden, down_half, preferred_element_type=F32)]
    unnamed x1 -> x0, starting transfers between devices: 1.68 us -> none
  transfers between devices with their start and end apart: 2 -> 14, of which waited for: 2 -> 9; matrix products, arithmetic and copies ran while one was open for 0% -> 0% of each run, Pallas kernels for 0% -> 0%
where the time goes in v1:
time: 91.9 us; the launch traced here: 91.4 us
  waiting for transfers between devices  36 us (39%)
  starting transfers between devices  31.4 us (34%)
  matrix products  21.5 us (23%)
  other arithmetic  2.09 us (2%)
    ppermute x6, waiting for transfers between devices, swap(): return lax.ppermute(x, axis, [(0, 1), (1, 0)])  25.4 us
    ppermute x4, starting transfers between devices, shared(): lax.ppermute(pair, AXES, [(owner, device) for device, owner in moves(p)])  12.4 us
    ppermute x4, starting transfers between devices, shared(): out = sum((lax.ppermute(mixed[p], AXES, moves(p)) for p in range(4)))  10.2 us
    ppermute x6, starting transfers between devices, swap(): return lax.ppermute(x, axis, [(0, 1), (1, 0)])  8.74 us
    ppermute x4, waiting for transfers between devices, shared(): out = sum((lax.ppermute(mixed[p], AXES, moves(p)) for p in range(4)))  7.3 us
    dot_general x1, matrix products, shared(): jnp.dot(hidden, down_half, preferred_element_type=F32)  7.2 us
    dot_general x1, matrix products, shared(): up_part = jnp.dot(section, up_half, preferred_element_type=F32)  7.2 us
    dot_general x1, matrix products, shared(): gate_part = jnp.dot(section, gate_half, preferred_element_type=F32)  7.15 us
  transfers between devices with their start and end apart: 14, of which 9 were waited for; matrix products, arithmetic and copies ran while one was open for 0% of the time, Pallas kernels for 0%

profile of v1, /device:TPU:0, one launch (start us, length us, event | category | flops | bytes accessed | tf_op | source)
XLA Modules:
  0.0 91.4 jit_solution(3883628819199587111)
XLA Ops:
  0.0 3.0 %collective-permute-start = (bf16[12,2048]{1,0:T(8,128)(2,1)}, bf16[12,2048]{1,0:T(8,128)(2,1)S(1)}, u32[]{:S(2)}, u32[]{:S(2)}) collective-permute-start(bf16[12,2048]{1,0:T(8,128)(2,1)} %param.4), channel_id=1, source_target_pairs={{0,16},{16,0},{1,17},{17,1},{2,18},{18,2},{3,19},{19,3},{4,20},{20... | collective-permute-start | bytes 147464 | tf_op jit(solution)/shard_map/ppermute | solution.py:30
  3.0 2.5 %collective-permute-done = bf16[12,2048]{1,0:T(8,128)(2,1)S(1)} collective-permute-done((bf16[12,2048]{1,0:T(8,128)(2,1)}, bf16[12,2048]{1,0:T(8,128)(2,1)S(1)}, u32[]{:S(2)}, u32[]{:S(2)}) %collective-permute-start) | collective-permute-done | bytes 49184 | tf_op jit(solution)/shard_map/ppermute | solution.py:30
  5.4 0.9 pad_maximum_fusion.2
  7.0 4.0 %collective-permute-start.4 = (bf16[24,2048]{1,0:T(8,128)(2,1)S(1)}, bf16[24,2048]{1,0:T(8,128)(2,1)S(1)}, u32[]{:S(2)}, u32[]{:S(2)}) collective-permute-start(bf16[24,2048]{1,0:T(8,128)(2,1)S(1)} %pad_maximum_fusion.2), channel_id=1, source_target_pairs={{12,0},{5,1},{10,2},{3,3},{0,4},{9,5},{14,6},{7,7},{4,8},{13,9},{2... | collective-permute-start | bytes 294920 | tf_op jit(solution)/shard_map/ppermute | solution.py:59
  11.0 4.5 %collective-permute-start.3 = (bf16[24,2048]{1,0:T(8,128)(2,1)S(1)}, bf16[24,2048]{1,0:T(8,128)(2,1)S(1)}, u32[]{:S(2)}, u32[]{:S(2)}) collective-permute-start(bf16[24,2048]{1,0:T(8,128)(2,1)S(1)} %pad_maximum_fusion.2), channel_id=1, source_target_pairs={{8,0},{1,1},{14,2},{7,3},{12,4},{5,5},{2,6},{11,7},{0,8},{9,9},{6,... | collective-permute-start | bytes 294920 | tf_op jit(solution)/shard_map/ppermute | solution.py:59
  15.5 3.3 %collective-permute-start.2 = (bf16[24,2048]{1,0:T(8,128)(2,1)S(1)}, bf16[24,2048]{1,0:T(8,128)(2,1)S(1)}, u32[]{:S(2)}, u32[]{:S(2)}) collective-permute-start(bf16[24,2048]{1,0:T(8,128)(2,1)S(1)} %pad_maximum_fusion.2), channel_id=1, source_target_pairs={{4,0},{13,1},{2,2},{11,3},{8,4},{1,5},{6,6},{15,7},{12,8},{5,9},{1... | collective-permute-start | bytes 294920 | tf_op jit(solution)/shard_map/ppermute | solution.py:59
  18.8 3.2 %collective-permute-done.2 = bf16[24,2048]{1,0:T(8,128)(2,1)S(1)} collective-permute-done((bf16[24,2048]{1,0:T(8,128)(2,1)S(1)}, bf16[24,2048]{1,0:T(8,128)(2,1)S(1)}, u32[]{:S(2)}, u32[]{:S(2)}) %collective-permute-start.2) | collective-permute-done | bytes 98336 | tf_op jit(solution)/shard_map/ppermute | solution.py:59
  22.1 7.2 %fusion.2 = f32[96,3328]{1,0:T(8,128)S(1)} fusion(bf16[96,2048]{1,0:T(8,128)(2,1)S(1)} %constant_dynamic-update-slice_fusion, bf16[2048,6656]{1,0:T(8,128)(2,1)} %param.6, s32[]{:T(128)S(6)} %select_n.2), kind=kOutput, calls=%fused_computation.2 | convolution fusion | flops 1308622848 | bytes 15302660 | tf_op jit(solution)/shard_map/dot_general | solution.py:65
  29.2 7.1 %fusion.4 = f32[96,3328]{1,0:T(8,128)S(1)} fusion(bf16[96,2048]{1,0:T(8,128)(2,1)S(1)} %constant_dynamic-update-slice_fusion, bf16[2048,6656]{1,0:T(8,128)(2,1)} %param.5, s32[]{:T(128)S(6)} %select_n.2), kind=kOutput, calls=%fused_computation.4 | convolution fusion | flops 1308622848 | bytes 15302660 | tf_op jit(solution)/shard_map/dot_general | solution.py:64
  36.6 3.0 %collective-permute-done.5 = f32[48,6656]{1,0:T(8,128)S(1)} collective-permute-done((f32[48,6656]{1,0:T(8,128)S(1)}, f32[48,6656]{1,0:T(8,128)S(1)}, u32[]{:S(2)}, u32[]{:S(2)}) %collective-permute-start.5) | collective-permute-done | bytes 1277984 | tf_op jit(solution)/shard_map/ppermute | solution.py:30
  39.8 2.1 %collective-permute-start.6 = (bf16[24,6656]{1,0:T(8,128)(2,1)S(1)}, bf16[24,6656]{1,0:T(8,128)(2,1)S(1)}, u32[]{:S(2)}, u32[]{:S(2)}) collective-permute-start(bf16[24,6656]{1,0:T(8,128)(2,1)S(1)} %slice.86), channel_id=1, source_target_pairs={{0,2},{2,0},{1,3},{3,1},{4,6},{6,4},{5,7},{7,5},{8,10},{10,8},{9,1... | collective-permute-start | bytes 958472 | tf_op jit(solution)/shard_map/ppermute | solution.py:30
  41.9 7.8 %collective-permute-done.6 = bf16[24,6656]{1,0:T(8,128)(2,1)S(1)} collective-permute-done((bf16[24,6656]{1,0:T(8,128)(2,1)S(1)}, bf16[24,6656]{1,0:T(8,128)(2,1)S(1)}, u32[]{:S(2)}, u32[]{:S(2)}) %collective-permute-start.6) | collective-permute-done | bytes 319520 | tf_op jit(solution)/shard_map/ppermute | solution.py:30
  49.9 1.8 %collective-permute-start.7 = (bf16[24,3328]{1,0:T(8,128)(2,1)S(1)}, bf16[24,3328]{1,0:T(8,128)(2,1)S(1)}, u32[]{:S(2)}, u32[]{:S(2)}) collective-permute-start(bf16[24,3328]{1,0:T(8,128)(2,1)S(1)} %fusion.14), channel_id=1, source_target_pairs={{0,2},{2,0},{1,3},{3,1},{4,6},{6,4},{5,7},{7,5},{8,10},{10,8},{9,1... | collective-permute-start | bytes 479240 | tf_op jit(solution)/shard_map/ppermute | solution.py:30
  51.7 3.9 %collective-permute-done.7 = bf16[24,3328]{1,0:T(8,128)(2,1)S(1)} collective-permute-done((bf16[24,3328]{1,0:T(8,128)(2,1)S(1)}, bf16[24,3328]{1,0:T(8,128)(2,1)S(1)}, u32[]{:S(2)}, u32[]{:S(2)}) %collective-permute-start.7) | collective-permute-done | bytes 159776 | tf_op jit(solution)/shard_map/ppermute | solution.py:30
  55.7 1.6 %collective-permute-done.8 = bf16[48,3328]{1,0:T(8,128)(2,1)S(1)} collective-permute-done((bf16[48,3328]{1,0:T(8,128)(2,1)S(1)}, bf16[48,3328]{1,0:T(8,128)(2,1)S(1)}, u32[]{:S(2)}, u32[]{:S(2)}) %collective-permute-start.8) | collective-permute-done | bytes 319520 | tf_op jit(solution)/shard_map/ppermute | solution.py:30
  57.3 7.2 %fusion = f32[96,2048]{1,0:T(8,128)S(1)} fusion(bf16[6656,2048]{1,0:T(8,128)(2,1)} %param.7, s32[]{:T(128)S(6)} %select_n.2, bf16[48,3328]{1,0:T(8,128)(2,1)S(1)} %collective-permute-done.8, bf16[24,3328]{1,0:T(8,128)(2,1)S(1)} %collective-permute-done.7, bf16[24,3328]{1,0:T(8,128)(2,1)S(1)} %fusion.14), kind=kOutput, calls=%fused_computation | convolution fusion | flops 1310539776 | bytes 15056900 | tf_op jit(solution)/shard_map/dot_general | solution.py:76
  64.7 1.7 %collective-permute-start.9 = (bf16[4,12,2048]{2,1,0:T(8,128)(2,1)S(1)}, bf16[4,12,2048]{2,1,0:T(8,128)(2,1)S(1)}, u32[]{:S(2)}, u32[]{:S(2)}) collective-permute-start(bf16[4,12,2048]{2,1,0:T(8,128)(2,1)S(1)} %fusion.15), channel_id=1, source_target_pairs={{0,16},{16,0},{1,17},{17,1},{2,18},{18,2},{3,19},{19,3},{4,20},{20... | collective-permute-start | bytes 589832 | tf_op jit(solution)/shard_map/ppermute | solution.py:30
  66.4 6.7 %collective-permute-done.9 = bf16[4,12,2048]{2,1,0:T(8,128)(2,1)S(1)} collective-permute-done((bf16[4,12,2048]{2,1,0:T(8,128)(2,1)S(1)}, bf16[4,12,2048]{2,1,0:T(8,128)(2,1)S(1)}, u32[]{:S(2)}, u32[]{:S(2)}) %collective-permute-start.9) | collective-permute-done | bytes 196640 | tf_op jit(solution)/shard_map/ppermute | solution.py:30
  73.2 1.9 %collective-permute-start.11 = (f32[12,2048]{1,0:T(8,128)S(1)}, f32[12,2048]{1,0:T(8,128)S(1)}, u32[]{:S(2)}, u32[]{:S(2)}) collective-permute-start(f32[12,2048]{1,0:T(8,128)S(1)} %get-tuple-element.5), channel_id=1, source_target_pairs={{0,4},{1,13},{2,2},{3,11},{4,8},{5,1},{6,6},{7,15},{8,12},{9,5},{1... | collective-permute-start | bytes 294920 | tf_op jit(solution)/shard_map/ppermute | solution.py:78
  75.1 5.7 %collective-permute-start.13 = (f32[12,2048]{1,0:T(8,128)S(1)}, f32[12,2048]{1,0:T(8,128)S(1)}, u32[]{:S(2)}, u32[]{:S(2)}) collective-permute-start(f32[12,2048]{1,0:T(8,128)S(1)} %get-tuple-element.6), channel_id=1, source_target_pairs={{0,12},{1,5},{2,10},{3,3},{4,0},{5,9},{6,14},{7,7},{8,4},{9,13},{1... | collective-permute-start | bytes 294920 | tf_op jit(solution)/shard_map/ppermute | solution.py:78
  80.8 1.9 %collective-permute-start.12 = (f32[12,2048]{1,0:T(8,128)S(1)}, f32[12,2048]{1,0:T(8,128)S(1)}, u32[]{:S(2)}, u32[]{:S(2)}) collective-permute-start(f32[12,2048]{1,0:T(8,128)S(1)} %get-tuple-element.7), channel_id=1, source_target_pairs={{0,8},{1,1},{2,14},{3,7},{4,12},{5,5},{6,2},{7,11},{8,0},{9,9},{10... | collective-permute-start | bytes 294920 | tf_op jit(solution)/shard_map/ppermute | solution.py:78
  82.8 0.7 collective-permute-start.10
  83.5 1.1 %collective-permute-done.13 = f32[12,2048]{1,0:T(8,128)S(1)} collective-permute-done((f32[12,2048]{1,0:T(8,128)S(1)}, f32[12,2048]{1,0:T(8,128)S(1)}, u32[]{:S(2)}, u32[]{:S(2)}) %collective-permute-start.13) | collective-permute-done | bytes 98336 | tf_op jit(solution)/shard_map/ppermute | solution.py:78
  84.5 6.2 %collective-permute-done.12 = f32[12,2048]{1,0:T(8,128)S(1)} collective-permute-done((f32[12,2048]{1,0:T(8,128)S(1)}, f32[12,2048]{1,0:T(8,128)S(1)}, u32[]{:S(2)}, u32[]{:S(2)}) %collective-permute-start.12) | collective-permute-done | bytes 98336 | tf_op jit(solution)/shard_map/ppermute | solution.py:78
  (23 shorter events, 2.3 us)
Async XLA Ops:
  0.0 5.4 %collective-permute-start = (bf16[12,2048]{1,0:T(8,128)(2,1)}, bf16[12,2048]{1,0:T(8,128)(2,1)S(1)}, u32[]{:S(2)}, u32[]{:S(2)}) collective-permute-start(bf16[12,2048]{1,0:T(8,128)(2,1)} %param.4), channel_id=1, source_target_pairs={{0,16},{16,0},{1,17},{17,1},{2,18},{18,2},{3,19},{19,3},{4,20},{20... | collective-permute-start | bytes 147464 | tf_op jit(solution)/shard_map/ppermute | solution.py:30
  6.3 12.4 %collective-permute-start.1 = (bf16[24,2048]{1,0:T(8,128)(2,1)S(1)}, bf16[24,2048]{1,0:T(8,128)(2,1)S(1)}, u32[]{:S(2)}, u32[]{:S(2)}) collective-permute-start(bf16[24,2048]{1,0:T(8,128)(2,1)S(1)} %pad_maximum_fusion.2), channel_id=1, source_target_pairs={{0,0},{9,1},{6,2},{15,3},{4,4},{13,5},{10,6},{3,7},{8,8},{1,9},{14... | collective-permute-start | bytes 294920 | tf_op jit(solution)/shard_map/ppermute | solution.py:59
  7.0 15.1 %collective-permute-start.4 = (bf16[24,2048]{1,0:T(8,128)(2,1)S(1)}, bf16[24,2048]{1,0:T(8,128)(2,1)S(1)}, u32[]{:S(2)}, u32[]{:S(2)}) collective-permute-start(bf16[24,2048]{1,0:T(8,128)(2,1)S(1)} %pad_maximum_fusion.2), channel_id=1, source_target_pairs={{12,0},{5,1},{10,2},{3,3},{0,4},{9,5},{14,6},{7,7},{4,8},{13,9},{2... | collective-permute-start | bytes 294920 | tf_op jit(solution)/shard_map/ppermute | solution.py:59
  11.0 11.0 %collective-permute-start.3 = (bf16[24,2048]{1,0:T(8,128)(2,1)S(1)}, bf16[24,2048]{1,0:T(8,128)(2,1)S(1)}, u32[]{:S(2)}, u32[]{:S(2)}) collective-permute-start(bf16[24,2048]{1,0:T(8,128)(2,1)S(1)} %pad_maximum_fusion.2), channel_id=1, source_target_pairs={{8,0},{1,1},{14,2},{7,3},{12,4},{5,5},{2,6},{11,7},{0,8},{9,9},{6,... | collective-permute-start | bytes 294920 | tf_op jit(solution)/shard_map/ppermute | solution.py:59
  15.5 6.5 %collective-permute-start.2 = (bf16[24,2048]{1,0:T(8,128)(2,1)S(1)}, bf16[24,2048]{1,0:T(8,128)(2,1)S(1)}, u32[]{:S(2)}, u32[]{:S(2)}) collective-permute-start(bf16[24,2048]{1,0:T(8,128)(2,1)S(1)} %pad_maximum_fusion.2), channel_id=1, source_target_pairs={{4,0},{13,1},{2,2},{11,3},{8,4},{1,5},{6,6},{15,7},{12,8},{5,9},{1... | collective-permute-start | bytes 294920 | tf_op jit(solution)/shard_map/ppermute | solution.py:59
  36.5 3.1 %collective-permute-start.5 = (f32[48,6656]{1,0:T(8,128)S(1)}, f32[48,6656]{1,0:T(8,128)S(1)}, u32[]{:S(2)}, u32[]{:S(2)}) collective-permute-start(f32[48,6656]{1,0:T(8,128)S(1)} %pad_maximum_fusion), channel_id=1, source_target_pairs={{0,1},{1,0},{2,3},{3,2},{4,5},{5,4},{6,7},{7,6},{8,9},{9,8},{10,11... | collective-permute-start | bytes 3833864 | tf_op jit(solution)/shard_map/ppermute | solution.py:30
  39.8 9.9 %collective-permute-start.6 = (bf16[24,6656]{1,0:T(8,128)(2,1)S(1)}, bf16[24,6656]{1,0:T(8,128)(2,1)S(1)}, u32[]{:S(2)}, u32[]{:S(2)}) collective-permute-start(bf16[24,6656]{1,0:T(8,128)(2,1)S(1)} %slice.86), channel_id=1, source_target_pairs={{0,2},{2,0},{1,3},{3,1},{4,6},{6,4},{5,7},{7,5},{8,10},{10,8},{9,1... | collective-permute-start | bytes 958472 | tf_op jit(solution)/shard_map/ppermute | solution.py:30
  49.9 5.7 %collective-permute-start.7 = (bf16[24,3328]{1,0:T(8,128)(2,1)S(1)}, bf16[24,3328]{1,0:T(8,128)(2,1)S(1)}, u32[]{:S(2)}, u32[]{:S(2)}) collective-permute-start(bf16[24,3328]{1,0:T(8,128)(2,1)S(1)} %fusion.14), channel_id=1, source_target_pairs={{0,2},{2,0},{1,3},{3,1},{4,6},{6,4},{5,7},{7,5},{8,10},{10,8},{9,1... | collective-permute-start | bytes 479240 | tf_op jit(solution)/shard_map/ppermute | solution.py:30
  55.7 1.7 %collective-permute-start.8 = (bf16[48,3328]{1,0:T(8,128)(2,1)S(1)}, bf16[48,3328]{1,0:T(8,128)(2,1)S(1)}, u32[]{:S(2)}, u32[]{:S(2)}) collective-permute-start(bf16[48,3328]{1,0:T(8,128)(2,1)S(1)} %pad_maximum_fusion.1), channel_id=1, source_target_pairs={{0,1},{1,0},{2,3},{3,2},{4,5},{5,4},{6,7},{7,6},{8,9},{9,8},{10,11... | collective-permute-start | bytes 958472 | tf_op jit(solution)/shard_map/ppermute | solution.py:30
  64.7 8.4 %collective-permute-start.9 = (bf16[4,12,2048]{2,1,0:T(8,128)(2,1)S(1)}, bf16[4,12,2048]{2,1,0:T(8,128)(2,1)S(1)}, u32[]{:S(2)}, u32[]{:S(2)}) collective-permute-start(bf16[4,12,2048]{2,1,0:T(8,128)(2,1)S(1)} %fusion.15), channel_id=1, source_target_pairs={{0,16},{16,0},{1,17},{17,1},{2,18},{18,2},{3,19},{19,3},{4,20},{20... | collective-permute-start | bytes 589832 | tf_op jit(solution)/shard_map/ppermute | solution.py:30
  73.2 10.3 %collective-permute-start.11 = (f32[12,2048]{1,0:T(8,128)S(1)}, f32[12,2048]{1,0:T(8,128)S(1)}, u32[]{:S(2)}, u32[]{:S(2)}) collective-permute-start(f32[12,2048]{1,0:T(8,128)S(1)} %get-tuple-element.5), channel_id=1, source_target_pairs={{0,4},{1,13},{2,2},{3,11},{4,8},{5,1},{6,6},{7,15},{8,12},{9,5},{1... | collective-permute-start | bytes 294920 | tf_op jit(solution)/shard_map/ppermute | solution.py:78
  75.1 9.4 %collective-permute-start.13 = (f32[12,2048]{1,0:T(8,128)S(1)}, f32[12,2048]{1,0:T(8,128)S(1)}, u32[]{:S(2)}, u32[]{:S(2)}) collective-permute-start(f32[12,2048]{1,0:T(8,128)S(1)} %get-tuple-element.6), channel_id=1, source_target_pairs={{0,12},{1,5},{2,10},{3,3},{4,0},{5,9},{6,14},{7,7},{8,4},{9,13},{1... | collective-permute-start | bytes 294920 | tf_op jit(solution)/shard_map/ppermute | solution.py:78
  80.8 9.9 %collective-permute-start.12 = (f32[12,2048]{1,0:T(8,128)S(1)}, f32[12,2048]{1,0:T(8,128)S(1)}, u32[]{:S(2)}, u32[]{:S(2)}) collective-permute-start(f32[12,2048]{1,0:T(8,128)S(1)} %get-tuple-element.7), channel_id=1, source_target_pairs={{0,8},{1,1},{2,14},{3,7},{4,12},{5,5},{6,2},{7,11},{8,0},{9,9},{10... | collective-permute-start | bytes 294920 | tf_op jit(solution)/shard_map/ppermute | solution.py:78
  82.8 8.0 %collective-permute-start.10 = (f32[12,2048]{1,0:T(8,128)S(1)}, f32[12,2048]{1,0:T(8,128)S(1)}, u32[]{:S(2)}, u32[]{:S(2)}) collective-permute-start(f32[12,2048]{1,0:T(8,128)S(1)} %get-tuple-element.8), channel_id=1, source_target_pairs={{0,0},{1,9},{2,6},{3,15},{4,4},{5,13},{6,10},{7,3},{8,8},{9,1},{10... | collective-permute-start | bytes 294920 | tf_op jit(solution)/shard_map/ppermute | solution.py:78

commit v2 on v1

--- a/solution.py
+++ b/solution.py
@@ -30,34 +30,23 @@
     return lax.ppermute(x, axis, [(0, 1), (1, 0)])
 
 
-def place(wide, narrow, sub):
-    return (wide * 2 + narrow) * 2 + sub
+PARTS = ("groups", "wide")
 
 
-def partner(position, wide, narrow, sub):
-    return (wide + (position ^ (2 * sub + narrow))) % 4
-
-
-def moves(position):
-    return [
-        (place(w, n, s), place(partner(position, w, n, s), n, s))
-        for w in range(4)
-        for n in range(2)
-        for s in range(2)
-    ]
-
-
-AXES = ("wide", "narrow", "sub")
+def quarters(x, core, chip):
+    x = x.reshape(2, 2, -1, x.shape[-1])
+    x = jnp.where(core == 0, x, x[::-1])
+    x = jnp.where(chip == 0, x, x[:, ::-1])
+    return x.reshape(-1, x.shape[-1])
 
 
 def shared(tokens, gate_weight, up_weight, down_weight):
     half = gate_weight.shape[1] // 2
-    rows = tokens.shape[0]
-    group = lax.axis_index("groups")
-    pair = jnp.concatenate([tokens, swap(tokens, "groups")], axis=0)
-    section = jnp.concatenate(
-        [lax.ppermute(pair, AXES, [(owner, device) for device, owner in moves(p)]) for p in range(4)], axis=0
-    )
+    rows, features = tokens.shape
+    group, chip, core = (lax.axis_index(axis) for axis in ("groups", "narrow", "sub"))
+    lined = jnp.broadcast_to(tokens.reshape(1, -1, 128), (8, rows * features // 128, 128))
+    section = lax.all_to_all(lined, PARTS, 0, 0, tiled=True).reshape(8 * rows, features)
+    section = quarters(section, core, chip)
     gate_half = lax.dynamic_slice_in_dim(gate_weight, group * half, half, axis=1)
     up_half = lax.dynamic_slice_in_dim(up_weight, group * half, half, axis=1)
     down_half = lax.dynamic_slice_in_dim(down_weight, group * half, half, axis=0)
@@ -73,10 +62,10 @@
     hidden = jnp.concatenate([hidden, swap(hidden, "narrow")], axis=0)
     hidden = jnp.concatenate([hidden, swap(hidden, "sub")], axis=0)
 
-    mixed = jnp.dot(hidden, down_half, preferred_element_type=F32).reshape(4, 2, rows, -1)
-    mixed = mixed[:, 0] + swap(mixed[:, 1].astype(BF16), "groups").astype(F32)
-    out = sum(lax.ppermute(mixed[p], AXES, moves(p)) for p in range(4))
-    return out.astype(BF16)
+    mixed = jnp.dot(hidden, down_half, preferred_element_type=F32)
+    mixed = quarters(mixed.astype(BF16), core, chip).reshape(8, -1, 128)
+    mixed = lax.all_to_all(mixed, PARTS, 0, 0, tiled=True).astype(F32)
+    return jnp.sum(mixed, axis=0).astype(BF16).reshape(rows, features)
 
 
 def solution(mesh):

time: 91.9 us -> 80.8 us (0.88)
  starting transfers between devices: 31.4 us -> 10.5 us
  blocking collectives: 0 us -> 15.6 us
  waiting for transfers between devices: 36 us -> 29.1 us
  local copies, waits for them, and re-layouts: 0.22 us -> 2.76 us
  other arithmetic: 2.09 us -> 0.84 us
    ppermute x8 -> x0, starting transfers between devices: 22.6 us -> none  [the longest x4 12.4 us: shared(): lax.ppermute(pair, AXES, [(owner, device) for device, owner in moves(p)])]
    all_to_all x0 -> x1, blocking collectives: none -> 15.6 us  [shared(): mixed = lax.all_to_all(mixed, PARTS, 0, 0, tiled=True).astype(F32)]
    all_to_all x0 -> x1, waiting for transfers between devices: none -> 12.6 us  [shared(): lax.all_to_all(lined, PARTS, 0, 0, tiled=True).reshape(8 * rows, features)]
    ppermute x8 -> x0, waiting for transfers between devices: 10.5 us -> none  [the longest x4 7.3 us: shared(): out = sum((lax.ppermute(mixed[p], AXES, moves(p)) for p in range(4)))]
    ppermute x6 -> x4, waiting for transfers between devices: 25.4 us -> 16.5 us  [swap(): return lax.ppermute(x, axis, [(0, 1), (1, 0)])]
    all_to_all x0 -> x1, starting transfers between devices: none -> 7.28 us  [shared(): lax.all_to_all(lined, PARTS, 0, 0, tiled=True).reshape(8 * rows, features)]
    ppermute x6 -> x4, starting transfers between devices: 8.74 us -> 3.23 us  [swap(): return lax.ppermute(x, axis, [(0, 1), (1, 0)])]
    broadcast_in_dim x0 -> x2, local copies, waits for them, and re-layouts: none -> 1.69 us  [shared(): jnp.broadcast_to(tokens.reshape(1, -1, 128), (8, rows * features // 128,...]
  transfers between devices with their start and end apart: 14 -> 5, of which waited for: 9 -> 5; matrix products, arithmetic and copies ran while one was open for 0% -> 0% of each run, Pallas kernels for 0% -> 0%
where the time goes in v2:
time: 80.8 us; the launch traced here: 80.4 us
  waiting for transfers between devices  29.1 us (36%)
  matrix products  21.5 us (27%)
  blocking collectives  15.6 us (19%)
  starting transfers between devices  10.5 us (13%)
  local copies, waits for them, and re-layouts  2.76 us (3%)
  other arithmetic  0.84 us (1%)
    ppermute x4, waiting for transfers between devices, swap(): return lax.ppermute(x, axis, [(0, 1), (1, 0)])  16.5 us
    all_to_all x1, blocking collectives, shared(): mixed = lax.all_to_all(mixed, PARTS, 0, 0, tiled=True).astype(F32)  15.6 us
    all_to_all x1, waiting for transfers between devices, shared(): lax.all_to_all(lined, PARTS, 0, 0, tiled=True).reshape(8 * rows, features)  12.6 us
    all_to_all x1, starting transfers between devices, shared(): lax.all_to_all(lined, PARTS, 0, 0, tiled=True).reshape(8 * rows, features)  7.28 us
    dot_general x1, matrix products, shared(): up_part = jnp.dot(section, up_half, preferred_element_type=F32)  7.2 us
    dot_general x1, matrix products, shared(): mixed = jnp.dot(hidden, down_half, preferred_element_type=F32)  7.19 us
    dot_general x1, matrix products, shared(): gate_part = jnp.dot(section, gate_half, preferred_element_type=F32)  7.15 us
    ppermute x4, starting transfers between devices, swap(): return lax.ppermute(x, axis, [(0, 1), (1, 0)])  3.23 us
  transfers between devices with their start and end apart: 5, of which 5 were waited for; matrix products, arithmetic and copies ran while one was open for 0% of the time, Pallas kernels for 0%

profile of v2, /device:TPU:0, one launch (start us, length us, event | category | flops | bytes accessed | tf_op | source)
XLA Modules:
  0.0 80.4 jit_solution(4186635135514933711)
XLA Ops:
  0.0 0.9 %broadcast_in_dim.7 = bf16[192,128]{1,0:T(8,128)(2,1)S(1)} reshape(bf16[12,2048]{1,0:T(8,128)(2,1)} %param.4) | data formatting | bytes 98304 | tf_op jit(solution)/shard_map/broadcast_in_dim | solution.py:47
  0.9 0.8 %broadcast_in_dim.8 = bf16[8,192,128]{2,1,0:T(8,128)(2,1)} broadcast(bf16[192,128]{1,0:T(8,128)(2,1)S(1)} %broadcast_in_dim.7), dimensions={1,2} | broadcast | bytes 442368 | tf_op jit(solution)/shard_map/broadcast_in_dim | solution.py:47
  1.7 7.3 %all-to-all-start = ((bf16[8,192,128]{2,1,0:T(8,128)(2,1)}), bf16[8,192,128]{2,1,0:T(8,128)(2,1)S(1)}, u32[]{:S(2)}, u32[]{:S(2)}) async-start(bf16[8,192,128]{2,1,0:T(8,128)(2,1)} %broadcast_in_dim.8), calls=%async_computation | async-start | bytes 786432 | tf_op jit(solution)/shard_map/all_to_all | solution.py:48
  9.0 12.6 %all-to-all-done = bf16[8,192,128]{2,1,0:T(8,128)(2,1)S(1)} async-done(((bf16[8,192,128]{2,1,0:T(8,128)(2,1)}), bf16[8,192,128]{2,1,0:T(8,128)(2,1)S(1)}, u32[]{:S(2)}, u32[]{:S(2)}) %all-to-all-start) | async-done | bytes 393248 | tf_op jit(solution)/shard_map/all_to_all | solution.py:48
  21.6 0.2 reshape_reshape.6
  21.9 7.2 %fusion.2 = f32[96,3328]{1,0:T(8,128)S(1)} fusion(bf16[96,2048]{1,0:T(8,128)(2,1)S(1)} %bitcast.6, bf16[2048,6656]{1,0:T(8,128)(2,1)} %param.6, s32[]{:T(128)S(6)} %select_n.31), kind=kOutput, calls=%fused_computation.2 | convolution fusion | flops 1308622848 | bytes 15302660 | tf_op jit(solution)/shard_map/dot_general | solution.py:54
  29.1 7.1 %fusion.4 = f32[96,3328]{1,0:T(8,128)S(1)} fusion(bf16[96,2048]{1,0:T(8,128)(2,1)S(1)} %bitcast.7, bf16[2048,6656]{1,0:T(8,128)(2,1)} %param.5, s32[]{:T(128)S(6)} %select_n.31), kind=kOutput, calls=%fused_computation.4 | convolution fusion | flops 1308622848 | bytes 15302660 | tf_op jit(solution)/shard_map/dot_general | solution.py:53
  36.2 0.1 pad_maximum_fusion
  36.3 0.1 collective-permute-start
  36.4 3.0 %collective-permute-done = f32[48,6656]{1,0:T(8,128)S(1)} collective-permute-done((f32[48,6656]{1,0:T(8,128)S(1)}, f32[48,6656]{1,0:T(8,128)S(1)}, u32[]{:S(2)}, u32[]{:S(2)}) %collective-permute-start) | collective-permute-done | bytes 1277984 | tf_op jit(solution)/shard_map/ppermute | solution.py:30
  39.4 0.2 fusion.10
  39.6 1.5 %collective-permute-start.1 = (bf16[24,6656]{1,0:T(8,128)(2,1)S(1)}, bf16[24,6656]{1,0:T(8,128)(2,1)S(1)}, u32[]{:S(2)}, u32[]{:S(2)}) collective-permute-start(bf16[24,6656]{1,0:T(8,128)(2,1)S(1)} %slice.45), channel_id=1, source_target_pairs={{0,2},{2,0},{1,3},{3,1},{4,6},{6,4},{5,7},{7,5},{8,10},{10,8},{9,1... | collective-permute-start | bytes 958472 | tf_op jit(solution)/shard_map/ppermute | solution.py:30
  41.2 8.1 %collective-permute-done.1 = bf16[24,6656]{1,0:T(8,128)(2,1)S(1)} collective-permute-done((bf16[24,6656]{1,0:T(8,128)(2,1)S(1)}, bf16[24,6656]{1,0:T(8,128)(2,1)S(1)}, u32[]{:S(2)}, u32[]{:S(2)}) %collective-permute-start.1) | collective-permute-done | bytes 319520 | tf_op jit(solution)/shard_map/ppermute | solution.py:30
  49.3 0.1 slice_add_fusion
  49.4 0.1 fusion.16
  49.5 1.5 %collective-permute-start.2 = (bf16[24,3328]{1,0:T(8,128)(2,1)S(1)}, bf16[24,3328]{1,0:T(8,128)(2,1)S(1)}, u32[]{:S(2)}, u32[]{:S(2)}) collective-permute-start(bf16[24,3328]{1,0:T(8,128)(2,1)S(1)} %fusion.16), channel_id=1, source_target_pairs={{0,2},{2,0},{1,3},{3,1},{4,6},{6,4},{5,7},{7,5},{8,10},{10,8},{9,1... | collective-permute-start | bytes 479240 | tf_op jit(solution)/shard_map/ppermute | solution.py:30
  51.0 3.8 %collective-permute-done.2 = bf16[24,3328]{1,0:T(8,128)(2,1)S(1)} collective-permute-done((bf16[24,3328]{1,0:T(8,128)(2,1)S(1)}, bf16[24,3328]{1,0:T(8,128)(2,1)S(1)}, u32[]{:S(2)}, u32[]{:S(2)}) %collective-permute-start.2) | collective-permute-done | bytes 159776 | tf_op jit(solution)/shard_map/ppermute | solution.py:30
  54.9 0.1 collective-permute-start.3
  55.0 1.6 %collective-permute-done.3 = bf16[48,3328]{1,0:T(8,128)(2,1)S(1)} collective-permute-done((bf16[48,3328]{1,0:T(8,128)(2,1)S(1)}, bf16[48,3328]{1,0:T(8,128)(2,1)S(1)}, u32[]{:S(2)}, u32[]{:S(2)}) %collective-permute-start.3) | collective-permute-done | bytes 319520 | tf_op jit(solution)/shard_map/ppermute | solution.py:30
  56.6 7.2 %fusion.6 = bf16[96,2048]{1,0:T(8,128)(2,1)S(1)} fusion(bf16[6656,2048]{1,0:T(8,128)(2,1)} %param.7, s32[]{:T(128)S(6)} %select_n.31, bf16[48,3328]{1,0:T(8,128)(2,1)S(1)} %collective-permute-done.3, bf16[24,3328]{1,0:T(8,128)(2,1)S(1)} %collective-permute-done.2, bf16[24,3328]{1,0:T(8,128)(2,1)S(1)} %fusion.16), kind=kOutput, calls=%fused_computation.8 | convolution fusion | flops 1310736384 | bytes 14663684 | tf_op jit(solution)/shard_map/dot_general | solution.py:65
  63.8 0.1 reverse_select_fusion.1
  63.9 0.2 reshape_reshape.7
  64.1 15.6 %all_to_all.10 = bf16[8,192,128]{2,1,0:T(8,128)(2,1)S(1)} all-to-all(bf16[8,192,128]{2,1,0:T(8,128)(2,1)S(1)} %reshape_reshape.7), channel_id=1, replica_groups=mesh['groups'=2,'wide'=4,'narrow'=2,'sub'=2] {'groups','wide'}, dimensions={0} | all-to-all | bytes 786432 | tf_op jit(solution)/shard_map/all_to_all | solution.py:67
  79.7 0.7 reshape.13
  (6 shorter events, 0.3 us)
Async XLA Ops:
  1.7 19.9 %all-to-all-start = ((bf16[8,192,128]{2,1,0:T(8,128)(2,1)}), bf16[8,192,128]{2,1,0:T(8,128)(2,1)S(1)}, u32[]{:S(2)}, u32[]{:S(2)}) async-start(bf16[8,192,128]{2,1,0:T(8,128)(2,1)} %broadcast_in_dim.8), calls=%async_computation | async-start | bytes 786432 | tf_op jit(solution)/shard_map/all_to_all | solution.py:48
  36.3 3.1 %collective-permute-start = (f32[48,6656]{1,0:T(8,128)S(1)}, f32[48,6656]{1,0:T(8,128)S(1)}, u32[]{:S(2)}, u32[]{:S(2)}) collective-permute-start(f32[48,6656]{1,0:T(8,128)S(1)} %pad_maximum_fusion), channel_id=1, source_target_pairs={{0,1},{1,0},{2,3},{3,2},{4,5},{5,4},{6,7},{7,6},{8,9},{9,8},{10,11... | collective-permute-start | bytes 3833864 | tf_op jit(solution)/shard_map/ppermute | solution.py:30
  39.6 9.6 %collective-permute-start.1 = (bf16[24,6656]{1,0:T(8,128)(2,1)S(1)}, bf16[24,6656]{1,0:T(8,128)(2,1)S(1)}, u32[]{:S(2)}, u32[]{:S(2)}) collective-permute-start(bf16[24,6656]{1,0:T(8,128)(2,1)S(1)} %slice.45), channel_id=1, source_target_pairs={{0,2},{2,0},{1,3},{3,1},{4,6},{6,4},{5,7},{7,5},{8,10},{10,8},{9,1... | collective-permute-start | bytes 958472 | tf_op jit(solution)/shard_map/ppermute | solution.py:30
  49.5 5.4 %collective-permute-start.2 = (bf16[24,3328]{1,0:T(8,128)(2,1)S(1)}, bf16[24,3328]{1,0:T(8,128)(2,1)S(1)}, u32[]{:S(2)}, u32[]{:S(2)}) collective-permute-start(bf16[24,3328]{1,0:T(8,128)(2,1)S(1)} %fusion.16), channel_id=1, source_target_pairs={{0,2},{2,0},{1,3},{3,1},{4,6},{6,4},{5,7},{7,5},{8,10},{10,8},{9,1... | collective-permute-start | bytes 479240 | tf_op jit(solution)/shard_map/ppermute | solution.py:30
  54.9 1.7 %collective-permute-start.3 = (bf16[48,3328]{1,0:T(8,128)(2,1)S(1)}, bf16[48,3328]{1,0:T(8,128)(2,1)S(1)}, u32[]{:S(2)}, u32[]{:S(2)}) collective-permute-start(bf16[48,3328]{1,0:T(8,128)(2,1)S(1)} %pad_maximum_fusion.1), channel_id=1, source_target_pairs={{0,1},{1,0},{2,3},{3,2},{4,5},{5,4},{6,7},{7,6},{8,9},{9,8},{10,11... | collective-permute-start | bytes 958472 | tf_op jit(solution)/shard_map/ppermute | solution.py:30

commit v3 on v0

v3 whole, which is shorter than its diff:
```python
import functools

import jax
import jax.numpy as jnp
from jax import lax
from jax.experimental import pallas as pl
from jax.experimental.pallas import tpu as pltpu
from jax.sharding import PartitionSpec as P

BF16 = jnp.bfloat16
F32 = jnp.float32


def activate(gate_sums, up_sums):
    return (jax.nn.silu(gate_sums) * up_sums).astype(BF16)


def general(tokens, gate_weight, up_weight, down_weight):
    section = lax.all_gather(tokens, "wide", axis=0, tiled=True)
    gate_part = jnp.dot(section, gate_weight, preferred_element_type=F32)
    up_part = jnp.dot(section, up_weight, preferred_element_type=F32)
    gate_sums = lax.psum(gate_part, ("narrow", "sub"))
    up_sums = lax.psum(up_part, ("narrow", "sub"))
    mixed = lax.psum_scatter(
        jnp.dot(activate(gate_sums, up_sums), down_weight, preferred_element_type=F32),
        "wide",
        scatter_dimension=0,
        tiled=True,
    )
    return mixed.astype(BF16)


def swap(x, axis):
    return lax.ppermute(x, axis, [(0, 1), (1, 0)])


BLOCK = 256
SLOTS = 4
VMEM = pl.BlockSpec(memory_space=pltpu.VMEM)
ANY = pl.BlockSpec(memory_space=pl.ANY)
GRANT = pltpu.CompilerParams(vmem_limit_bytes=32 * 2**20)


def sums_kernel(first, width, tokens, gate, up, send, keep, held, sems):
    core = lax.axis_index("sub")
    half = width // 2
    blocks = half // BLOCK

    def copies(step):
        at_keep = step // blocks
        side = jnp.where(at_keep == 1, core, 1 - core)
        column = first + side * half + (step - at_keep * blocks) * BLOCK
        columns = pl.ds(pl.multiple_of(column, 128), BLOCK)
        slot = lax.rem(step, SLOTS)
        return [
            pltpu.make_async_copy(weight.at[:, columns], held.at[slot, i], sems.at[slot, i])
            for i, weight in enumerate((gate, up))
        ]

    def start(step):
        for copy in copies(step):
            copy.start()

    for step in range(min(SLOTS, 2 * blocks)):
        start(jnp.int32(step))

    for side, out in enumerate((send, keep)):

        @pl.loop(0, blocks)
        def _(block):
            step = side * blocks + block
            slot = lax.rem(step, SLOTS)
            for i, copy in enumerate(copies(step)):
                copy.wait()
                column = pl.multiple_of(i * half + block * BLOCK, 128)
                out[:, pl.ds(column, BLOCK)] = jnp.dot(
                    tokens[...], held[slot, i], preferred_element_type=F32
                ).astype(out.dtype)

            @pl.when(step + SLOTS < 2 * blocks)
            def _():
                start(step + SLOTS)


def sums(tokens, gate, up, first, width):
    rows, depth = tokens.shape
    return pl.pallas_call(
        functools.partial(sums_kernel, first, width),
        out_shape=(jax.ShapeDtypeStruct((rows, width), BF16), jax.ShapeDtypeStruct((rows, width), F32)),
        in_specs=[VMEM, ANY, ANY],
        out_specs=(VMEM, VMEM),
        scratch_shapes=[
            pltpu.VMEM((SLOTS, 2, depth, BLOCK), BF16),
            pltpu.SemaphoreType.DMA((SLOTS, 2)),
        ],
        compiler_params=GRANT,
        cost_estimate=pl.CostEstimate(
            flops=4 * rows * depth * width, bytes_accessed=4 * depth * width, transcendentals=0
        ),
        name="gate_and_up",
    )(tokens, gate, up)


def down_kernel(first, width, mine, other, weight, total, out, held, sems):
    core = lax.axis_index("sub")
    half = width // 2
    blocks = half // BLOCK

    def copy(step):
        at_other = step // blocks
        side = jnp.where(at_other == 1, 1 - core, core)
        row = first + side * half + (step - at_other * blocks) * BLOCK
        slot = lax.rem(step, SLOTS)
        return pltpu.make_async_copy(
            weight.at[pl.ds(pl.multiple_of(row, 128), BLOCK), :], held.at[slot], sems.at[slot]
        )

    for step in range(min(SLOTS, 2 * blocks)):
        copy(jnp.int32(step)).start()
    out[...] = total[...]

    for side, hidden in enumerate((mine, other)):

        @pl.loop(0, blocks)
        def _(block):
            step = side * blocks + block
            copy(step).wait()
            units = pl.ds(pl.multiple_of(block * BLOCK, 128), BLOCK)
            out[...] += jnp.dot(
                hidden[:, units], held[lax.rem(step, SLOTS)], preferred_element_type=F32
            )

            @pl.when(step + SLOTS < 2 * blocks)
            def _():
                copy(step + SLOTS).start()


def down(mine, other, weight, total, first, width):
    rows, features = total.shape
    return pl.pallas_call(
        functools.partial(down_kernel, first, width),
        out_shape=jax.ShapeDtypeStruct(total.shape, F32),
        in_specs=[VMEM, VMEM, ANY, VMEM],
        out_specs=VMEM,
        scratch_shapes=[pltpu.VMEM((SLOTS, BLOCK, features), BF16), pltpu.SemaphoreType.DMA((SLOTS,))],
        compiler_params=GRANT,
        cost_estimate=pl.CostEstimate(
            flops=2 * rows * features * width, bytes_accessed=2 * features * width, transcendentals=0
        ),
        name="down",
    )(mine, other, weight, total)


def halves(x, chip):
    gate, up = jnp.split(x, 2, axis=1)
    quarter = gate.shape[1] // 2

    def of(place):
        return jnp.concatenate(
            [lax.dynamic_slice_in_dim(part, place * quarter, quarter, axis=1) for part in (gate, up)], axis=1
        )

    return of(chip), of(1 - chip)


def split(units):
    lumps = units // 512
    more = (lumps + 1) // 2 * 512
    return ((0, more), (more, units - more))


def chunked(tokens, gate_weight, up_weight, down_weight):
    rows, features = tokens.shape
    chip = lax.axis_index("narrow")
    lined = jnp.broadcast_to(tokens.reshape(1, -1, 128), (4, rows * features // 128, 128))
    section = lax.all_to_all(lined, "wide", 0, 0, tiled=True).reshape(4 * rows, features)
    mixed = jnp.zeros((4 * rows, down_weight.shape[1]), F32)
    for first, width in split(gate_weight.shape[1]):
        send, keep = sums(section, gate_weight, up_weight, first, width)
        own, away = halves(keep + swap(send, "sub").astype(F32), chip)
        gate_up = own + swap(away.astype(BF16), "narrow").astype(F32)
        hidden = activate(*jnp.split(gate_up, 2, axis=1))
        theirs = swap(hidden, "narrow")
        mine = jnp.where(
            chip == 0,
            jnp.concatenate([hidden, theirs], axis=1),
            jnp.concatenate([theirs, hidden], axis=1),
        )
        mixed = down(mine, swap(mine, "sub"), down_weight, mixed, first, width)
    mixed = mixed.astype(BF16).reshape(4, -1, 128)
    mixed = lax.all_to_all(mixed, "wide", 0, 0, tiled=True).astype(F32)
    return jnp.sum(mixed, axis=0).astype(BF16).reshape(rows, features)


def solution(mesh):
    placed = (
        P(("groups", "wide"), ("narrow", "sub")),
        P(("narrow", "sub"), "wide"),
        P(("narrow", "sub"), "wide"),
        P("wide", ("narrow", "sub")),
    )
    sizes = tuple(mesh.shape[axis] for axis in ("groups", "wide", "narrow", "sub"))
    return jax.shard_map(
        chunked if sizes == (2, 4, 2, 2) else general,
        mesh=mesh,
        in_specs=placed,
        out_specs=P(("groups", "wide"), ("narrow", "sub")),
        check_vma=False,
    )
```

time: 149 us -> 78.6 us (0.53)
  waiting for transfers between devices: 61.2 us -> 10.6 us
  Pallas kernels: 0 us -> 35.4 us
  matrix products: 34.3 us -> 0 us
  between operations: 14.1 us -> 0.22 us
  blocking collectives: 34.3 us -> 24.1 us
  starting transfers between devices: 1.69 us -> 5.55 us
    psum x1 -> x0, waiting for transfers between devices: 60.5 us -> none  [per_device(): summed = lax.psum(projected, ('narrow', 'sub'))]
    pallas_call x0 -> x4, Pallas kernels: none -> 35.4 us  [the longest x2 23.2 us: sums(): pl.pallas_call(functools.partial(sums_kernel, first, width), out_shape=(j...]
    dot_general x3 -> x0, matrix products: 34.3 us -> none  [the longest x1 11.9 us: per_device(): jnp.dot(hidden, down_weight, preferred_element_type=jnp.float32)]
    all_to_all x0 -> x2, blocking collectives: none -> 24.1 us  [the longest x1 13.6 us: chunked(): lax.all_to_all(lined, 'wide', 0, 0, tiled=True).reshape(4 * rows, features)]
    unnamed x1 -> x0, blocking collectives: 18.4 us -> none
    all_gather x1 -> x0, blocking collectives: 15.8 us -> none  [per_device(): section = lax.all_gather(tokens, 'wide', axis=0, tiled=True)]
    ppermute x0 -> x8, waiting for transfers between devices: none -> 10.6 us  [swap(): return lax.ppermute(x, axis, [(0, 1), (1, 0)])]
    ppermute x0 -> x8, starting transfers between devices: none -> 5.55 us  [swap(): return lax.ppermute(x, axis, [(0, 1), (1, 0)])]
  transfers between devices with their start and end apart: 2 -> 8, of which waited for: 2 -> 5; matrix products, arithmetic and copies ran while one was open for 0% -> 1% of each run, Pallas kernels for 0% -> 24%
where the time goes in v3:
time: 78.6 us; the launch traced here: 78.3 us
  Pallas kernels  35.4 us (45%)
  blocking collectives  24.1 us (31%)
  waiting for transfers between devices  10.6 us (13%)
  starting transfers between devices  5.55 us (7%)
  local copies, waits for them, and re-layouts  1.99 us (3%)
    pallas_call x2, Pallas kernels, sums(): pl.pallas_call(functools.partial(sums_kernel, first, width), out_shape=(j...  23.2 us
    all_to_all x1, blocking collectives, chunked(): lax.all_to_all(lined, 'wide', 0, 0, tiled=True).reshape(4 * rows, features)  13.6 us
    pallas_call x2, Pallas kernels, down(): pl.pallas_call(functools.partial(down_kernel, first, width), out_shape=ja...  12.2 us
    ppermute x8, waiting for transfers between devices, swap(): return lax.ppermute(x, axis, [(0, 1), (1, 0)])  10.6 us
    all_to_all x1, blocking collectives, chunked(): mixed = lax.all_to_all(mixed, 'wide', 0, 0, tiled=True).astype(F32)  10.5 us
    ppermute x8, starting transfers between devices, swap(): return lax.ppermute(x, axis, [(0, 1), (1, 0)])  5.55 us
  transfers between devices with their start and end apart: 8, of which 5 were waited for; matrix products, arithmetic and copies ran while one was open for 1% of the time, Pallas kernels for 24%

profile of v3, /device:TPU:0, one launch (start us, length us, event | category | flops | bytes accessed | tf_op | source)
XLA Modules:
  0.0 78.3 jit_solution(693735404839254986)
XLA Ops:
  0.0 0.9 %broadcast_in_dim.10 = bf16[192,128]{1,0:T(8,128)(2,1)S(1)} reshape(bf16[12,2048]{1,0:T(8,128)(2,1)} %param.4) | data formatting | bytes 98304 | tf_op jit(solution)/shard_map/broadcast_in_dim | solution.py:175
  0.9 13.6 %all_to_all.10 = bf16[4,192,128]{2,1,0:T(8,128)(2,1)S(1)} all-to-all(bf16[4,192,128]{2,1,0:T(8,128)(2,1)S(1)} %broadcast_in_dim.11), channel_id=1, replica_groups=mesh['groups'=2,'wide'=4,'narrow'=2,'sub'=2] {'wide'}, dimensions={0} | all-to-all | bytes 393216 | tf_op jit(solution)/shard_map/all_to_all | solution.py:176
  14.5 0.1 reshape.11.tokens
  14.6 10.8 %gate_and_up.2 = (bf16[48,3072]{1,0:T(8,128)(2,1)S(1)}, f32[48,3072]{1,0:T(8,128)S(1)}) custom-call(bf16[48,2048]{1,0:T(8,128)(2,1)S(1)} %reshape.11.tokens, bf16[2048,6656]{1,0:T(8,128)(2,1)} %gate.3, bf16[2048,6656]{1,0:T(8,128)(2,1)} %up.3), custom_call_target="tpu_custom_call" | custom-call | flops 1207959552 | bytes 25165824 | tf_op jit(solution)/shard_map/gate_and_up/pallas_call | solution.py:87
  25.4 0.1 collective-permute-start
  25.5 12.4 %gate_and_up.3 = (bf16[48,3584]{1,0:T(8,128)(2,1)S(1)}, f32[48,3584]{1,0:T(8,128)S(1)}) custom-call(bf16[48,2048]{1,0:T(8,128)(2,1)S(1)} %reshape.11.tokens, bf16[2048,6656]{1,0:T(8,128)(2,1)} %gate.3, bf16[2048,6656]{1,0:T(8,128)(2,1)} %up.3), custom_call_target="tpu_custom_call" | custom-call | flops 1409286144 | bytes 29360128 | tf_op jit(solution)/shard_map/gate_and_up/pallas_call | solution.py:87
  37.9 0.5 collective-permute-start.4
  38.6 1.6 %collective-permute-start.1 = (bf16[48,1536]{1,0:T(8,128)(2,1)S(1)}, bf16[48,1536]{1,0:T(8,128)(2,1)S(1)}, u32[]{:S(2)}, u32[]{:S(2)}) collective-permute-start(bf16[48,1536]{1,0:T(8,128)(2,1)S(1)} %pad_maximum_fusion.1), channel_id=1, source_target_pairs={{0,2},{2,0},{1,3},{3,1},{4,6},{6,4},{5,7},{7,5},{8,10},{10,8},{9,1... | collective-permute-start | bytes 442376 | tf_op jit(solution)/shard_map/ppermute | solution.py:34
  40.2 0.1 convert_add_fusion
  40.4 1.1 %collective-permute-start.5 = (bf16[48,1792]{1,0:T(8,128)(2,1)S(1)}, bf16[48,1792]{1,0:T(8,128)(2,1)S(1)}, u32[]{:S(2)}, u32[]{:S(2)}) collective-permute-start(bf16[48,1792]{1,0:T(8,128)(2,1)S(1)} %pad_maximum_fusion), channel_id=1, source_target_pairs={{0,2},{2,0},{1,3},{3,1},{4,6},{6,4},{5,7},{7,5},{8,10},{10,8},{9,1... | collective-permute-start | bytes 516104 | tf_op jit(solution)/shard_map/ppermute | solution.py:34
  41.5 3.9 %collective-permute-done.1 = bf16[48,1536]{1,0:T(8,128)(2,1)S(1)} collective-permute-done((bf16[48,1536]{1,0:T(8,128)(2,1)S(1)}, bf16[48,1536]{1,0:T(8,128)(2,1)S(1)}, u32[]{:S(2)}, u32[]{:S(2)}) %collective-permute-start.1) | collective-permute-done | bytes 147488 | tf_op jit(solution)/shard_map/ppermute | solution.py:34
  45.4 2.7 %collective-permute-done.5 = bf16[48,1792]{1,0:T(8,128)(2,1)S(1)} collective-permute-done((bf16[48,1792]{1,0:T(8,128)(2,1)S(1)}, bf16[48,1792]{1,0:T(8,128)(2,1)S(1)}, u32[]{:S(2)}, u32[]{:S(2)}) %collective-permute-start.5) | collective-permute-done | bytes 172064 | tf_op jit(solution)/shard_map/ppermute | solution.py:34
  48.2 1.6 %collective-permute-start.6 = (bf16[48,896]{1,0:T(8,128)(2,1)S(1)}, bf16[48,896]{1,0:T(8,128)(2,1)S(1)}, u32[]{:S(2)}, u32[]{:S(2)}) collective-permute-start(bf16[48,896]{1,0:T(8,128)(2,1)S(1)} %fusion), channel_id=1, source_target_pairs={{0,2},{2,0},{1,3},{3,1},{4,6},{6,4},{5,7},{7,5},{8,10},{10,8},{9,1... | collective-permute-start | bytes 258056 | tf_op jit(solution)/shard_map/ppermute | solution.py:34
  49.8 0.6 collective-permute-start.2
  50.4 2.7 %collective-permute-done.6 = bf16[48,896]{1,0:T(8,128)(2,1)S(1)} collective-permute-done((bf16[48,896]{1,0:T(8,128)(2,1)S(1)}, bf16[48,896]{1,0:T(8,128)(2,1)S(1)}, u32[]{:S(2)}, u32[]{:S(2)}) %collective-permute-start.6) | collective-permute-done | bytes 86048 | tf_op jit(solution)/shard_map/ppermute | solution.py:34
  53.2 0.1 collective-permute-start.7
  53.3 1.0 %collective-permute-done.2 = bf16[48,768]{1,0:T(8,128)(2,1)S(1)} collective-permute-done((bf16[48,768]{1,0:T(8,128)(2,1)S(1)}, bf16[48,768]{1,0:T(8,128)(2,1)S(1)}, u32[]{:S(2)}, u32[]{:S(2)}) %collective-permute-start.2) | collective-permute-done | bytes 73760 | tf_op jit(solution)/shard_map/ppermute | solution.py:34
  54.3 0.1 collective-permute-start.3
  54.4 0.3 collective-permute-done.7.other
  54.7 6.6 %down.2.total = f32[48,2048]{1,0:T(8,128)S(1)} custom-call(bf16[48,1792]{1,0:T(8,128)(2,1)S(1)} %maximum_select_fusion.mine, bf16[48,1792]{1,0:T(8,128)(2,1)S(1)} %collective-permute-done.7.other, bf16[6656,2048]{1,0:T(8,128)(2,1)} %weight.3, f32[48,2048]{1,0:T(8,128)S(1)} %broadcast_in_dim.12.total), custom_call_target="tpu_custom_call" | custom-call | flops 704643072 | bytes 14680064 | tf_op jit(solution)/shard_map/down/pallas_call | solution.py:140
  61.3 5.7 %down.3 = f32[48,2048]{1,0:T(8,128)S(1)} custom-call(bf16[48,1536]{1,0:T(8,128)(2,1)S(1)} %maximum_select_fusion.1.mine, bf16[48,1536]{1,0:T(8,128)(2,1)S(1)} %collective-permute-done.3.other, bf16[6656,2048]{1,0:T(8,128)(2,1)} %weight.3, f32[48,2048]{1,0:T(8,128)S(1)} %down.2.total), custom_call_target="tpu_custom_call" | custom-call | flops 603979776 | bytes 12582912 | tf_op jit(solution)/shard_map/down/pallas_call | solution.py:140
  67.0 0.1 reshape.12
  67.1 10.5 %all_to_all.11 = bf16[4,192,128]{2,1,0:T(8,128)(2,1)S(1)} all-to-all(bf16[4,192,128]{2,1,0:T(8,128)(2,1)S(1)} %reshape.12), channel_id=1, replica_groups=mesh['groups'=2,'wide'=4,'narrow'=2,'sub'=2] {'wide'}, dimensions={0} | all-to-all | bytes 393216 | tf_op jit(solution)/shard_map/all_to_all | solution.py:191
  77.6 0.7 reshape.13
  (22 shorter events, 0.6 us)
Async XLA Ops:
  25.4 13.0 %collective-permute-start = (bf16[48,3072]{1,0:T(8,128)(2,1)S(1)}, bf16[48,3072]{1,0:T(8,128)(2,1)S(1)}, u32[]{:S(2)}, u32[]{:S(2)}) collective-permute-start(bf16[48,3072]{1,0:T(8,128)(2,1)S(1)} %get-tuple-element.10), channel_id=1, source_target_pairs={{0,1},{1,0},{2,3},{3,2},{4,5},{5,4},{6,7},{7,6},{8,9},{9,8},{10,11... | collective-permute-start | bytes 884744 | tf_op jit(solution)/shard_map/ppermute | solution.py:34
  37.9 2.3 %collective-permute-start.4 = (bf16[48,3584]{1,0:T(8,128)(2,1)S(1)}, bf16[48,3584]{1,0:T(8,128)(2,1)S(1)}, u32[]{:S(2)}, u32[]{:S(2)}) collective-permute-start(bf16[48,3584]{1,0:T(8,128)(2,1)S(1)} %get-tuple-element.12), channel_id=1, source_target_pairs={{0,1},{1,0},{2,3},{3,2},{4,5},{5,4},{6,7},{7,6},{8,9},{9,8},{10,11... | collective-permute-start | bytes 1032200 | tf_op jit(solution)/shard_map/ppermute | solution.py:34
  38.6 6.8 %collective-permute-start.1 = (bf16[48,1536]{1,0:T(8,128)(2,1)S(1)}, bf16[48,1536]{1,0:T(8,128)(2,1)S(1)}, u32[]{:S(2)}, u32[]{:S(2)}) collective-permute-start(bf16[48,1536]{1,0:T(8,128)(2,1)S(1)} %pad_maximum_fusion.1), channel_id=1, source_target_pairs={{0,2},{2,0},{1,3},{3,1},{4,6},{6,4},{5,7},{7,5},{8,10},{10,8},{9,1... | collective-permute-start | bytes 442376 | tf_op jit(solution)/shard_map/ppermute | solution.py:34
  40.4 7.8 %collective-permute-start.5 = (bf16[48,1792]{1,0:T(8,128)(2,1)S(1)}, bf16[48,1792]{1,0:T(8,128)(2,1)S(1)}, u32[]{:S(2)}, u32[]{:S(2)}) collective-permute-start(bf16[48,1792]{1,0:T(8,128)(2,1)S(1)} %pad_maximum_fusion), channel_id=1, source_target_pairs={{0,2},{2,0},{1,3},{3,1},{4,6},{6,4},{5,7},{7,5},{8,10},{10,8},{9,1... | collective-permute-start | bytes 516104 | tf_op jit(solution)/shard_map/ppermute | solution.py:34
  48.2 4.9 %collective-permute-start.6 = (bf16[48,896]{1,0:T(8,128)(2,1)S(1)}, bf16[48,896]{1,0:T(8,128)(2,1)S(1)}, u32[]{:S(2)}, u32[]{:S(2)}) collective-permute-start(bf16[48,896]{1,0:T(8,128)(2,1)S(1)} %fusion), channel_id=1, source_target_pairs={{0,2},{2,0},{1,3},{3,1},{4,6},{6,4},{5,7},{7,5},{8,10},{10,8},{9,1... | collective-permute-start | bytes 258056 | tf_op jit(solution)/shard_map/ppermute | solution.py:34
  49.8 4.4 %collective-permute-start.2 = (bf16[48,768]{1,0:T(8,128)(2,1)S(1)}, bf16[48,768]{1,0:T(8,128)(2,1)S(1)}, u32[]{:S(2)}, u32[]{:S(2)}) collective-permute-start(bf16[48,768]{1,0:T(8,128)(2,1)S(1)} %fusion.1), channel_id=1, source_target_pairs={{0,2},{2,0},{1,3},{3,1},{4,6},{6,4},{5,7},{7,5},{8,10},{10,8},{9,1... | collective-permute-start | bytes 221192 | tf_op jit(solution)/shard_map/ppermute | solution.py:34
  53.2 1.5 %collective-permute-start.7 = (bf16[48,1792]{1,0:T(8,128)(2,1)S(1)}, bf16[48,1792]{1,0:T(8,128)(2,1)S(1)}, u32[]{:S(2)}, u32[]{:S(2)}) collective-permute-start(bf16[48,1792]{1,0:T(8,128)(2,1)S(1)} %maximum_select_fusion.mine), channel_id=1, source_target_pairs={{0,1},{1,0},{2,3},{3,2},{4,5},{5,4},{6,7},{7,6},{8,9},{9,8},{10,11... | collective-permute-start | bytes 516104 | tf_op jit(solution)/shard_map/ppermute | solution.py:34
  54.3 7.0 %collective-permute-start.3 = (bf16[48,1536]{1,0:T(8,128)(2,1)S(1)}, bf16[48,1536]{1,0:T(8,128)(2,1)S(1)}, u32[]{:S(2)}, u32[]{:S(2)}) collective-permute-start(bf16[48,1536]{1,0:T(8,128)(2,1)S(1)} %maximum_select_fusion.1.mine), channel_id=1, source_target_pairs={{0,1},{1,0},{2,3},{3,2},{4,5},{5,4},{6,7},{7,6},{8,9},{9,8},{10,11... | collective-permute-start | bytes 442376 | tf_op jit(solution)/shard_map/ppermute | solution.py:34

commit v4 on v3

--- a/solution.py
+++ b/solution.py
@@ -35,13 +35,98 @@
 
 
 BLOCK = 256
-SLOTS = 4
 VMEM = pl.BlockSpec(memory_space=pltpu.VMEM)
 ANY = pl.BlockSpec(memory_space=pl.ANY)
-GRANT = pltpu.CompilerParams(vmem_limit_bytes=32 * 2**20)
-
-
-def sums_kernel(first, width, tokens, gate, up, send, keep, held, sems):
+HBM = pl.BlockSpec(memory_space=pltpu.HBM)
+GRANT = pltpu.CompilerParams(vmem_limit_bytes=6 * 2**20)
+STREAM = pltpu.CompilerParams(vmem_limit_bytes=14 * 2**20)
+SLOTS = 4
+
+
+def held_in(x):
+    return pltpu.with_memory_space_constraint(x, pltpu.VMEM)
+
+
+def left_in_hbm(x):
+    return pltpu.with_memory_space_constraint(x, pltpu.HBM)
+
+
+def unit_blocks(first, width, core_first):
+    half = width // 2
+    core = lax.axis_index("sub")
+    for side in (core, 1 - core) if core_first else (1 - core, core):
+        for block in range(half // BLOCK):
+            yield pl.multiple_of(first + side * half + block * BLOCK, BLOCK)
+
+
+def sums_fetch(first, width, gate, up, held, sems):
+    for step, unit in enumerate(unit_blocks(first, width, False)):
+        for i, weight in enumerate((gate, up)):
+            yield pltpu.make_async_copy(weight.at[:, pl.ds(unit, BLOCK)], held.at[step, i], sems.at[step, i])
+
+
+def sums_held(depth, width):
+    return (width // BLOCK, 2, depth, BLOCK)
+
+
+def sums_body(tokens, held, send, keep):
+    blocks = held.shape[0] // 2
+    for side, out in enumerate((send, keep)):
+
+        @pl.loop(0, blocks)
+        def _(block):
+            for i in range(2):
+                column = pl.multiple_of((i * blocks + block) * BLOCK, BLOCK)
+                out[:, pl.ds(column, BLOCK)] = jnp.dot(
+                    tokens[...], held[side * blocks + block, i], preferred_element_type=F32
+                ).astype(out.dtype)
+
+
+def load_kernel(first, width, gate, up, held, sems):
+    copies = list(sums_fetch(first, width, gate, up, held, sems))
+    for copy in copies:
+        copy.start()
+    for copy in copies:
+        copy.wait()
+
+
+def load(gate, up, first, width):
+    shape = sums_held(gate.shape[0], width)
+    return pl.pallas_call(
+        functools.partial(load_kernel, first, width),
+        out_shape=pltpu.VMEM(shape, BF16),
+        in_specs=[HBM, HBM],
+        out_specs=VMEM,
+        scratch_shapes=[pltpu.SemaphoreType.DMA(shape[:2])],
+        compiler_params=GRANT,
+        cost_estimate=pl.CostEstimate(
+            flops=0, bytes_accessed=4 * gate.shape[0] * width, transcendentals=0
+        ),
+        name="load",
+    )(left_in_hbm(gate), left_in_hbm(up))
+
+
+def first_sums_kernel(tokens, held, send, keep):
+    sums_body(tokens, held, send, keep)
+
+
+def first_sums(tokens, held):
+    rows, depth = tokens.shape
+    units = held.shape[0] * BLOCK
+    return pl.pallas_call(
+        first_sums_kernel,
+        out_shape=(jax.ShapeDtypeStruct((rows, units), BF16), jax.ShapeDtypeStruct((rows, units), F32)),
+        in_specs=[VMEM, VMEM],
+        out_specs=(VMEM, VMEM),
+        compiler_params=GRANT,
+        cost_estimate=pl.CostEstimate(
+            flops=4 * rows * depth * units, bytes_accessed=4 * depth * units, transcendentals=0
+        ),
+        name="first_sums",
+    )(tokens, held_in(held))
+
+
+def sums_kernel(first, width, tokens, gate, up, after, send, keep, held, sems):
     core = lax.axis_index("sub")
     half = width // 2
     blocks = half // BLOCK
@@ -82,23 +167,23 @@
                 start(step + SLOTS)
 
 
-def sums(tokens, gate, up, first, width):
+def sums(tokens, gate, up, after, first, width):
     rows, depth = tokens.shape
     return pl.pallas_call(
         functools.partial(sums_kernel, first, width),
         out_shape=(jax.ShapeDtypeStruct((rows, width), BF16), jax.ShapeDtypeStruct((rows, width), F32)),
-        in_specs=[VMEM, ANY, ANY],
+        in_specs=[VMEM, HBM, HBM, ANY],
         out_specs=(VMEM, VMEM),
         scratch_shapes=[
             pltpu.VMEM((SLOTS, 2, depth, BLOCK), BF16),
             pltpu.SemaphoreType.DMA((SLOTS, 2)),
         ],
-        compiler_params=GRANT,
+        compiler_params=STREAM,
         cost_estimate=pl.CostEstimate(
             flops=4 * rows * depth * width, bytes_accessed=4 * depth * width, transcendentals=0
         ),
         name="gate_and_up",
-    )(tokens, gate, up)
+    )(tokens, left_in_hbm(gate), left_in_hbm(up), after)
 
 
 def down_kernel(first, width, mine, other, weight, total, out, held, sems):
@@ -140,15 +225,15 @@
     return pl.pallas_call(
         functools.partial(down_kernel, first, width),
         out_shape=jax.ShapeDtypeStruct(total.shape, F32),
-        in_specs=[VMEM, VMEM, ANY, VMEM],
+        in_specs=[VMEM, VMEM, HBM, VMEM],
         out_specs=VMEM,
         scratch_shapes=[pltpu.VMEM((SLOTS, BLOCK, features), BF16), pltpu.SemaphoreType.DMA((SLOTS,))],
-        compiler_params=GRANT,
+        compiler_params=STREAM,
         cost_estimate=pl.CostEstimate(
             flops=2 * rows * features * width, bytes_accessed=2 * features * width, transcendentals=0
         ),
         name="down",
-    )(mine, other, weight, total)
+    )(mine, other, left_in_hbm(weight), total)
 
 
 def halves(x, chip):
@@ -164,32 +249,49 @@
 
 
 def split(units):
-    lumps = units // 512
-    more = (lumps + 1) // 2 * 512
-    return ((0, more), (more, units - more))
+    more = (units // 512 + 1) // 2 * 512
+    return ((0, units - more), (units - more, more))
+
+
+def across(x, apart):
+    return lax.ppermute(x, "wide", [(i, i ^ apart) for i in range(4)])
 
 
 def chunked(tokens, gate_weight, up_weight, down_weight):
-    rows, features = tokens.shape
+    rows = tokens.shape[0]
     chip = lax.axis_index("narrow")
-    lined = jnp.broadcast_to(tokens.reshape(1, -1, 128), (4, rows * features // 128, 128))
-    section = lax.all_to_all(lined, "wide", 0, 0, tiled=True).reshape(4 * rows, features)
-    mixed = jnp.zeros((4 * rows, down_weight.shape[1]), F32)
-    for first, width in split(gate_weight.shape[1]):
-        send, keep = sums(section, gate_weight, up_weight, first, width)
+    chunks = split(gate_weight.shape[1])
+    section = jnp.concatenate([tokens] + [across(tokens, apart) for apart in (1, 2, 3)], axis=0)
+    held = load(gate_weight, up_weight, *chunks[0])
+
+    def quarters(send, keep):
         own, away = halves(keep + swap(send, "sub").astype(F32), chip)
-        gate_up = own + swap(away.astype(BF16), "narrow").astype(F32)
+        return own, away.astype(BF16)
+
+    def hidden_half(own, away):
+        gate_up = own + swap(away, "narrow").astype(F32)
         hidden = activate(*jnp.split(gate_up, 2, axis=1))
         theirs = swap(hidden, "narrow")
-        mine = jnp.where(
+        return jnp.where(
             chip == 0,
             jnp.concatenate([hidden, theirs], axis=1),
             jnp.concatenate([theirs, hidden], axis=1),
         )
-        mixed = down(mine, swap(mine, "sub"), down_weight, mixed, first, width)
-    mixed = mixed.astype(BF16).reshape(4, -1, 128)
-    mixed = lax.all_to_all(mixed, "wide", 0, 0, tiled=True).astype(F32)
-    return jnp.sum(mixed, axis=0).astype(BF16).reshape(rows, features)
+
+    send, keep = first_sums(section, held)
+    own, away = quarters(send, keep)
+    send, keep = sums(section, gate_weight, up_weight, away, *chunks[1])
+    mixed = jnp.zeros((4 * rows, down_weight.shape[1]), F32)
+    for index, chunk in enumerate(chunks):
+        if index > 0:
+            own, away = quarters(send, keep)
+        mine = hidden_half(own, away)
+        mixed = down(mine, swap(mine, "sub"), down_weight, mixed, *chunk)
+    blocks = mixed.reshape(4, rows, -1)
+    out = blocks[0]
+    for apart in (1, 2, 3):
+        out = out + across(blocks[apart].astype(BF16), apart).astype(F32)
+    return out.astype(BF16)
 
 
 def solution(mesh):

time: 78.6 us -> 72.3 us (0.920)
  blocking collectives: 24.1 us -> 0 us
  starting transfers between devices: 5.55 us -> 13.7 us
  waiting for transfers between devices: 10.6 us -> 17.6 us
  Pallas kernels: 35.4 us -> 39.1 us
  local copies, waits for them, and re-layouts: 1.99 us -> 0.29 us
    all_to_all x2 -> x0, blocking collectives: 24.1 us -> none  [the longest x1 13.6 us: chunked(): lax.all_to_all(lined, 'wide', 0, 0, tiled=True).reshape(4 * rows, features)]
    pallas_call x0 -> x2, Pallas kernels: none -> 14.5 us  [the longest x1 8.77 us: load(): pl.pallas_call(functools.partial(load_kernel, first, width), out_shape=pl...]
    pallas_call x2 -> x1, Pallas kernels: 23.2 us -> 12.4 us  [sums(): pl.pallas_call(functools.partial(sums_kernel, first, width), out_shape=(j...]
    ppermute x0 -> x6, starting transfers between devices: none -> 10.1 us  [across(): return lax.ppermute(x, 'wide', [(i, i ^ apart) for i in range(4)])]
    ppermute x0 -> x6, waiting for transfers between devices: none -> 5.02 us  [across(): return lax.ppermute(x, 'wide', [(i, i ^ apart) for i in range(4)])]
    ppermute x8, waiting for transfers between devices: 10.6 us -> 12.6 us  [swap(): return lax.ppermute(x, axis, [(0, 1), (1, 0)])]
    ppermute x8, starting transfers between devices: 5.55 us -> 3.6 us  [swap(): return lax.ppermute(x, axis, [(0, 1), (1, 0)])]
    broadcast_in_dim x2 -> x0, local copies, waits for them, and re-layouts: 0.92 us -> none  [chunked(): jnp.broadcast_to(tokens.reshape(1, -1, 128), (4, rows * features // 128,...]
  transfers between devices with their start and end apart: 8 -> 14, of which waited for: 5 -> 6; matrix products, arithmetic and copies ran while one was open for 1% -> 1% of each run, Pallas kernels for 24% -> 37%
where the time goes in v4:
time: 72.3 us; the launch traced here: 72.1 us
  Pallas kernels  39.1 us (54%)
  waiting for transfers between devices  17.6 us (24%)
  starting transfers between devices  13.7 us (19%)
  other arithmetic  1.14 us (2%)
    ppermute x8, waiting for transfers between devices, swap(): return lax.ppermute(x, axis, [(0, 1), (1, 0)])  12.6 us
    pallas_call x1, Pallas kernels, sums(): pl.pallas_call(functools.partial(sums_kernel, first, width), out_shape=(j...  12.4 us
    pallas_call x2, Pallas kernels, down(): pl.pallas_call(functools.partial(down_kernel, first, width), out_shape=ja...  12.2 us
    ppermute x6, starting transfers between devices, across(): return lax.ppermute(x, 'wide', [(i, i ^ apart) for i in range(4)])  10.1 us
    pallas_call x1, Pallas kernels, load(): pl.pallas_call(functools.partial(load_kernel, first, width), out_shape=pl...  8.77 us
    pallas_call x1, Pallas kernels, first_sums(): pl.pallas_call(first_sums_kernel, out_shape=(jax.ShapeDtypeStruct((rows,...  5.72 us
    ppermute x6, waiting for transfers between devices, across(): return lax.ppermute(x, 'wide', [(i, i ^ apart) for i in range(4)])  5.02 us
    ppermute x8, starting transfers between devices, swap(): return lax.ppermute(x, axis, [(0, 1), (1, 0)])  3.6 us
  transfers between devices with their start and end apart: 14, of which 6 were waited for; matrix products, arithmetic and copies ran while one was open for 1% of the time, Pallas kernels for 37%

profile of v4, /device:TPU:0, one launch (start us, length us, event | category | flops | bytes accessed | tf_op | source)
XLA Modules:
  0.0 72.1 jit_solution(10241835673633930008)
XLA Ops:
  0.0 5.0 %collective-permute-start.2 = (bf16[12,2048]{1,0:T(8,128)(2,1)}, bf16[12,2048]{1,0:T(8,128)(2,1)S(1)}, u32[]{:S(2)}, u32[]{:S(2)}) collective-permute-start(bf16[12,2048]{1,0:T(8,128)(2,1)} %param.4), channel_id=1, source_target_pairs={{0,12},{4,8},{8,4},{12,0},{1,13},{5,9},{9,5},{13,1},{2,14},{6,10},... | collective-permute-start | bytes 147464 | tf_op jit(solution)/shard_map/ppermute | solution.py:257
  5.1 0.6 collective-permute-start
  5.7 8.8 %load.1.held = bf16[12,2,2048,256]{3,2,1,0:T(8,128)(2,1)S(1)} custom-call(bf16[2048,6656]{1,0:T(8,128)(2,1)} %gate.3, bf16[2048,6656]{1,0:T(8,128)(2,1)} %up.3), custom_call_target="tpu_custom_call" | custom-call | bytes 25165824 | tf_op jit(solution)/shard_map/load/pallas_call | solution.py:95
  14.6 5.7 %first_sums.1 = (bf16[48,3072]{1,0:T(8,128)(2,1)S(1)}, f32[48,3072]{1,0:T(8,128)S(1)}) custom-call(bf16[48,2048]{1,0:T(8,128)(2,1)S(1)} %pad_maximum_fusion.tokens, bf16[12,2,2048,256]{3,2,1,0:T(8,128)(2,1)S(1)} %load.1.held), custom_call_target="tpu_custom_call" | custom-call | flops 1207959552 | bytes 25165824 | tf_op jit(solution)/shard_map/first_sums/pallas_call | solution.py:116
  20.3 0.1 collective-permute-start.3
  20.4 1.6 %collective-permute-done.3 = bf16[48,3072]{1,0:T(8,128)(2,1)S(1)} collective-permute-done((bf16[48,3072]{1,0:T(8,128)(2,1)S(1)}, bf16[48,3072]{1,0:T(8,128)(2,1)S(1)}, u32[]{:S(2)}, u32[]{:S(2)}) %collective-permute-start.3) | collective-permute-done | bytes 294944 | tf_op jit(solution)/shard_map/ppermute | solution.py:34
  22.1 1.7 %collective-permute-start.8 = (bf16[48,1536]{1,0:T(8,128)(2,1)S(1)}, bf16[48,1536]{1,0:T(8,128)(2,1)S(1)}, u32[]{:S(2)}, u32[]{:S(2)}) collective-permute-start(bf16[48,1536]{1,0:T(8,128)(2,1)S(1)} %pad_maximum_fusion.2.after), channel_id=1, source_target_pairs={{0,2},{2,0},{1,3},{3,1},{4,6},{6,4},{5,7},{7,5},{8,10},{10,8},{9,1... | collective-permute-start | bytes 442376 | tf_op jit(solution)/shard_map/ppermute | solution.py:34
  23.8 12.4 %gate_and_up.1 = (bf16[48,3584]{1,0:T(8,128)(2,1)S(1)}, f32[48,3584]{1,0:T(8,128)S(1)}) custom-call(bf16[48,2048]{1,0:T(8,128)(2,1)S(1)} %pad_maximum_fusion.tokens, bf16[2048,6656]{1,0:T(8,128)(2,1)} %gate.3, bf16[2048,6656]{1,0:T(8,128)(2,1)} %up.3, bf16[48,1536]{1,0:T(8,128)(2,1)S(1)} %pad_maximum_fusion.2.after), custom_call_target="tpu_custom_call" | custom-call | flops 1409286144 | bytes 29360128 | tf_op jit(solution)/shard_map/gate_and_up/pallas_call | solution.py:172
  36.2 0.1 collective-permute-start.4
  36.4 0.4 collective-permute-start.9
  36.9 1.1 %collective-permute-done.4 = bf16[48,3584]{1,0:T(8,128)(2,1)S(1)} collective-permute-done((bf16[48,3584]{1,0:T(8,128)(2,1)S(1)}, bf16[48,3584]{1,0:T(8,128)(2,1)S(1)}, u32[]{:S(2)}, u32[]{:S(2)}) %collective-permute-start.4) | collective-permute-done | bytes 344096 | tf_op jit(solution)/shard_map/ppermute | solution.py:34
  38.1 0.7 collective-permute-start.5
  38.8 6.0 %collective-permute-done.5 = bf16[48,1792]{1,0:T(8,128)(2,1)S(1)} collective-permute-done((bf16[48,1792]{1,0:T(8,128)(2,1)S(1)}, bf16[48,1792]{1,0:T(8,128)(2,1)S(1)}, u32[]{:S(2)}, u32[]{:S(2)}) %collective-permute-start.5) | collective-permute-done | bytes 172064 | tf_op jit(solution)/shard_map/ppermute | solution.py:34
  44.9 0.5 collective-permute-start.6
  45.5 0.1 collective-permute-start.10
  45.5 3.9 %collective-permute-done.6 = bf16[48,896]{1,0:T(8,128)(2,1)S(1)} collective-permute-done((bf16[48,896]{1,0:T(8,128)(2,1)S(1)}, bf16[48,896]{1,0:T(8,128)(2,1)S(1)}, u32[]{:S(2)}, u32[]{:S(2)}) %collective-permute-start.6) | collective-permute-done | bytes 86048 | tf_op jit(solution)/shard_map/ppermute | solution.py:34
  49.5 0.1 collective-permute-start.7
  49.6 5.7 %down.2.total = f32[48,2048]{1,0:T(8,128)S(1)} custom-call(bf16[48,1536]{1,0:T(8,128)(2,1)S(1)} %maximum_select_fusion.1.mine, bf16[48,1536]{1,0:T(8,128)(2,1)S(1)} %collective-permute-done.10.other, bf16[6656,2048]{1,0:T(8,128)(2,1)} %weight.3, f32[48,2048]{1,0:T(8,128)S(1)} %broadcast_in_dim.3.total), custom_call_target="tpu_custom_call" | custom-call | flops 603979776 | bytes 12582912 | tf_op jit(solution)/shard_map/down/pallas_call | solution.py:225
  55.3 6.6 %down.3 = f32[48,2048]{1,0:T(8,128)S(1)} custom-call(bf16[48,1792]{1,0:T(8,128)(2,1)S(1)} %maximum_select_fusion.mine, bf16[48,1792]{1,0:T(8,128)(2,1)S(1)} %collective-permute-done.7.other, bf16[6656,2048]{1,0:T(8,128)(2,1)} %weight.3, f32[48,2048]{1,0:T(8,128)S(1)} %down.2.total), custom_call_target="tpu_custom_call" | custom-call | flops 704643072 | bytes 14680064 | tf_op jit(solution)/shard_map/down/pallas_call | solution.py:225
  62.0 3.7 %collective-permute-start.13 = (bf16[12,2048]{1,0:T(8,128)(2,1)S(1)}, bf16[12,2048]{1,0:T(8,128)(2,1)S(1)}, u32[]{:S(2)}, u32[]{:S(2)}) collective-permute-start(bf16[12,2048]{1,0:T(8,128)(2,1)S(1)} %get-tuple-element.18), channel_id=1, source_target_pairs={{0,12},{4,8},{8,4},{12,0},{1,13},{5,9},{9,5},{13,1},{2,14},{6,10},... | collective-permute-start | bytes 147464 | tf_op jit(solution)/shard_map/ppermute | solution.py:257
  65.7 0.8 %collective-permute-start.11 = (bf16[12,2048]{1,0:T(8,128)(2,1)S(1)}, bf16[12,2048]{1,0:T(8,128)(2,1)S(1)}, u32[]{:S(2)}, u32[]{:S(2)}) collective-permute-start(bf16[12,2048]{1,0:T(8,128)(2,1)S(1)} %get-tuple-element.17), channel_id=1, source_target_pairs={{0,4},{4,0},{8,12},{12,8},{1,5},{5,1},{9,13},{13,9},{2,6},{6,2},{1... | collective-permute-start | bytes 147464 | tf_op jit(solution)/shard_map/ppermute | solution.py:257
  66.4 2.4 %collective-permute-done.13 = bf16[12,2048]{1,0:T(8,128)(2,1)S(1)} collective-permute-done((bf16[12,2048]{1,0:T(8,128)(2,1)S(1)}, bf16[12,2048]{1,0:T(8,128)(2,1)S(1)}, u32[]{:S(2)}, u32[]{:S(2)}) %collective-permute-start.13) | collective-permute-done | bytes 49184 | tf_op jit(solution)/shard_map/ppermute | solution.py:257
  68.8 2.6 %collective-permute-done.12 = bf16[12,2048]{1,0:T(8,128)(2,1)S(1)} collective-permute-done((bf16[12,2048]{1,0:T(8,128)(2,1)S(1)}, bf16[12,2048]{1,0:T(8,128)(2,1)S(1)}, u32[]{:S(2)}, u32[]{:S(2)}) %collective-permute-start.12) | collective-permute-done | bytes 49184 | tf_op jit(solution)/shard_map/ppermute | solution.py:257
  71.5 0.7 fusion.4
  (34 shorter events, 0.8 us)
Async XLA Ops:
  0.0 14.5 %copy-start = (bf16[12,2048]{1,0:T(8,128)(2,1)S(1)}, bf16[12,2048]{1,0:T(8,128)(2,1)}, u32[]{:S(2)}) copy-start(bf16[12,2048]{1,0:T(8,128)(2,1)} %param.4) | copy-start | bytes 147460
  0.0 14.5 %collective-permute-start.2 = (bf16[12,2048]{1,0:T(8,128)(2,1)}, bf16[12,2048]{1,0:T(8,128)(2,1)S(1)}, u32[]{:S(2)}, u32[]{:S(2)}) collective-permute-start(bf16[12,2048]{1,0:T(8,128)(2,1)} %param.4), channel_id=1, source_target_pairs={{0,12},{4,8},{8,4},{12,0},{1,13},{5,9},{9,5},{13,1},{2,14},{6,10},... | collective-permute-start | bytes 147464 | tf_op jit(solution)/shard_map/ppermute | solution.py:257
  5.1 9.4 %collective-permute-start.1 = (bf16[12,2048]{1,0:T(8,128)(2,1)}, bf16[12,2048]{1,0:T(8,128)(2,1)S(1)}, u32[]{:S(2)}, u32[]{:S(2)}) collective-permute-start(bf16[12,2048]{1,0:T(8,128)(2,1)} %param.4), channel_id=1, source_target_pairs={{0,8},{4,12},{8,0},{12,4},{1,9},{5,13},{9,1},{13,5},{2,10},{6,14},... | collective-permute-start | bytes 147464 | tf_op jit(solution)/shard_map/ppermute | solution.py:257
  5.1 9.4 %collective-permute-start = (bf16[12,2048]{1,0:T(8,128)(2,1)}, bf16[12,2048]{1,0:T(8,128)(2,1)S(1)}, u32[]{:S(2)}, u32[]{:S(2)}) collective-permute-start(bf16[12,2048]{1,0:T(8,128)(2,1)} %param.4), channel_id=1, source_target_pairs={{0,4},{4,0},{8,12},{12,8},{1,5},{5,1},{9,13},{13,9},{2,6},{6,2},{1... | collective-permute-start | bytes 147464 | tf_op jit(solution)/shard_map/ppermute | solution.py:257
  20.3 1.6 %collective-permute-start.3 = (bf16[48,3072]{1,0:T(8,128)(2,1)S(1)}, bf16[48,3072]{1,0:T(8,128)(2,1)S(1)}, u32[]{:S(2)}, u32[]{:S(2)}) collective-permute-start(bf16[48,3072]{1,0:T(8,128)(2,1)S(1)} %get-tuple-element.10), channel_id=1, source_target_pairs={{0,1},{1,0},{2,3},{3,2},{4,5},{5,4},{6,7},{7,6},{8,9},{9,8},{10,11... | collective-permute-start | bytes 884744 | tf_op jit(solution)/shard_map/ppermute | solution.py:34
  22.1 14.2 %collective-permute-start.8 = (bf16[48,1536]{1,0:T(8,128)(2,1)S(1)}, bf16[48,1536]{1,0:T(8,128)(2,1)S(1)}, u32[]{:S(2)}, u32[]{:S(2)}) collective-permute-start(bf16[48,1536]{1,0:T(8,128)(2,1)S(1)} %pad_maximum_fusion.2.after), channel_id=1, source_target_pairs={{0,2},{2,0},{1,3},{3,1},{4,6},{6,4},{5,7},{7,5},{8,10},{10,8},{9,1... | collective-permute-start | bytes 442376 | tf_op jit(solution)/shard_map/ppermute | solution.py:34
  36.2 1.7 %collective-permute-start.4 = (bf16[48,3584]{1,0:T(8,128)(2,1)S(1)}, bf16[48,3584]{1,0:T(8,128)(2,1)S(1)}, u32[]{:S(2)}, u32[]{:S(2)}) collective-permute-start(bf16[48,3584]{1,0:T(8,128)(2,1)S(1)} %get-tuple-element.12), channel_id=1, source_target_pairs={{0,1},{1,0},{2,3},{3,2},{4,5},{5,4},{6,7},{7,6},{8,9},{9,8},{10,11... | collective-permute-start | bytes 1032200 | tf_op jit(solution)/shard_map/ppermute | solution.py:34
  36.4 9.0 %collective-permute-start.9 = (bf16[48,768]{1,0:T(8,128)(2,1)S(1)}, bf16[48,768]{1,0:T(8,128)(2,1)S(1)}, u32[]{:S(2)}, u32[]{:S(2)}) collective-permute-start(bf16[48,768]{1,0:T(8,128)(2,1)S(1)} %fusion.1), channel_id=1, source_target_pairs={{0,2},{2,0},{1,3},{3,1},{4,6},{6,4},{5,7},{7,5},{8,10},{10,8},{9,1... | collective-permute-start | bytes 221192 | tf_op jit(solution)/shard_map/ppermute | solution.py:34
  38.1 6.7 %collective-permute-start.5 = (bf16[48,1792]{1,0:T(8,128)(2,1)S(1)}, bf16[48,1792]{1,0:T(8,128)(2,1)S(1)}, u32[]{:S(2)}, u32[]{:S(2)}) collective-permute-start(bf16[48,1792]{1,0:T(8,128)(2,1)S(1)} %pad_maximum_fusion.1), channel_id=1, source_target_pairs={{0,2},{2,0},{1,3},{3,1},{4,6},{6,4},{5,7},{7,5},{8,10},{10,8},{9,1... | collective-permute-start | bytes 516104 | tf_op jit(solution)/shard_map/ppermute | solution.py:34
  44.9 4.6 %collective-permute-start.6 = (bf16[48,896]{1,0:T(8,128)(2,1)S(1)}, bf16[48,896]{1,0:T(8,128)(2,1)S(1)}, u32[]{:S(2)}, u32[]{:S(2)}) collective-permute-start(bf16[48,896]{1,0:T(8,128)(2,1)S(1)} %fusion), channel_id=1, source_target_pairs={{0,2},{2,0},{1,3},{3,1},{4,6},{6,4},{5,7},{7,5},{8,10},{10,8},{9,1... | collective-permute-start | bytes 258056 | tf_op jit(solution)/shard_map/ppermute | solution.py:34
  45.5 4.1 %collective-permute-start.10 = (bf16[48,1536]{1,0:T(8,128)(2,1)S(1)}, bf16[48,1536]{1,0:T(8,128)(2,1)S(1)}, u32[]{:S(2)}, u32[]{:S(2)}) collective-permute-start(bf16[48,1536]{1,0:T(8,128)(2,1)S(1)} %maximum_select_fusion.1.mine), channel_id=1, source_target_pairs={{0,1},{1,0},{2,3},{3,2},{4,5},{5,4},{6,7},{7,6},{8,9},{9,8},{10,11... | collective-permute-start | bytes 442376 | tf_op jit(solution)/shard_map/ppermute | solution.py:34
  49.5 5.8 %collective-permute-start.7 = (bf16[48,1792]{1,0:T(8,128)(2,1)S(1)}, bf16[48,1792]{1,0:T(8,128)(2,1)S(1)}, u32[]{:S(2)}, u32[]{:S(2)}) collective-permute-start(bf16[48,1792]{1,0:T(8,128)(2,1)S(1)} %maximum_select_fusion.mine), channel_id=1, source_target_pairs={{0,1},{1,0},{2,3},{3,2},{4,5},{5,4},{6,7},{7,6},{8,9},{9,8},{10,11... | collective-permute-start | bytes 516104 | tf_op jit(solution)/shard_map/ppermute | solution.py:34
  62.0 6.8 %collective-permute-start.13 = (bf16[12,2048]{1,0:T(8,128)(2,1)S(1)}, bf16[12,2048]{1,0:T(8,128)(2,1)S(1)}, u32[]{:S(2)}, u32[]{:S(2)}) collective-permute-start(bf16[12,2048]{1,0:T(8,128)(2,1)S(1)} %get-tuple-element.18), channel_id=1, source_target_pairs={{0,12},{4,8},{8,4},{12,0},{1,13},{5,9},{9,5},{13,1},{2,14},{6,10},... | collective-permute-start | bytes 147464 | tf_op jit(solution)/shard_map/ppermute | solution.py:257
  65.7 5.8 %collective-permute-start.12 = (bf16[12,2048]{1,0:T(8,128)(2,1)S(1)}, bf16[12,2048]{1,0:T(8,128)(2,1)S(1)}, u32[]{:S(2)}, u32[]{:S(2)}) collective-permute-start(bf16[12,2048]{1,0:T(8,128)(2,1)S(1)} %get-tuple-element.19), channel_id=1, source_target_pairs={{0,8},{4,12},{8,0},{12,4},{1,9},{5,13},{9,1},{13,5},{2,10},{6,14},... | collective-permute-start | bytes 147464 | tf_op jit(solution)/shard_map/ppermute | solution.py:257
  65.7 5.8 %collective-permute-start.11 = (bf16[12,2048]{1,0:T(8,128)(2,1)S(1)}, bf16[12,2048]{1,0:T(8,128)(2,1)S(1)}, u32[]{:S(2)}, u32[]{:S(2)}) collective-permute-start(bf16[12,2048]{1,0:T(8,128)(2,1)S(1)} %get-tuple-element.17), channel_id=1, source_target_pairs={{0,4},{4,0},{8,12},{12,8},{1,5},{5,1},{9,13},{13,9},{2,6},{6,2},{1... | collective-permute-start | bytes 147464 | tf_op jit(solution)/shard_map/ppermute | solution.py:257

commit v5 on v4

v5 whole, which is shorter than its diff:
```python
import functools

import jax
import jax.numpy as jnp
from jax import lax
from jax.experimental import pallas as pl
from jax.experimental.pallas import tpu as pltpu
from jax.sharding import PartitionSpec as P

BF16 = jnp.bfloat16
F32 = jnp.float32


def activate(gate_sums, up_sums):
    return (jax.nn.silu(gate_sums) * up_sums).astype(BF16)


def general(tokens, gate_weight, up_weight, down_weight):
    section = lax.all_gather(tokens, "wide", axis=0, tiled=True)
    gate_part = jnp.dot(section, gate_weight, preferred_element_type=F32)
    up_part = jnp.dot(section, up_weight, preferred_element_type=F32)
    gate_sums = lax.psum(gate_part, ("narrow", "sub"))
    up_sums = lax.psum(up_part, ("narrow", "sub"))
    mixed = lax.psum_scatter(
        jnp.dot(activate(gate_sums, up_sums), down_weight, preferred_element_type=F32),
        "wide",
        scatter_dimension=0,
        tiled=True,
    )
    return mixed.astype(BF16)


def swap(x, axis):
    return lax.ppermute(x, axis, [(0, 1), (1, 0)])


BLOCK = 256
VMEM = pl.BlockSpec(memory_space=pltpu.VMEM)
ANY = pl.BlockSpec(memory_space=pl.ANY)
HBM = pl.BlockSpec(memory_space=pltpu.HBM)
GRANT = pltpu.CompilerParams(vmem_limit_bytes=6 * 2**20)


def held_in(x):
    return pltpu.with_memory_space_constraint(x, pltpu.VMEM)


def left_in_hbm(x):
    return pltpu.with_memory_space_constraint(x, pltpu.HBM)


def unit_blocks(first, width, core_first):
    half = width // 2
    core = lax.axis_index("sub")
    for side in (core, 1 - core) if core_first else (1 - core, core):
        for block in range(half // BLOCK):
            yield pl.multiple_of(first + side * half + block * BLOCK, BLOCK)


def sums_fetch(first, width, gate, up, held, sems):
    for step, unit in enumerate(unit_blocks(first, width, False)):
        for i, weight in enumerate((gate, up)):
            yield pltpu.make_async_copy(weight.at[:, pl.ds(unit, BLOCK)], held.at[step, i], sems.at[step, i])


def sums_held(depth, width):
    return (width // BLOCK, 2, depth, BLOCK)


def sums_body(tokens, held, send, keep, copies=()):
    blocks = held.shape[0] // 2

    def block_sums(out, side, block):
        for i in range(2):
            column = i * blocks + block
            if not isinstance(block, int):
                column = pl.multiple_of(column * BLOCK, BLOCK)
            else:
                column = column * BLOCK
            out[:, pl.ds(column, BLOCK)] = jnp.dot(
                tokens[...], held[side * blocks + block, i], preferred_element_type=F32
            ).astype(out.dtype)

    for side, out in enumerate((send, keep)):
        if copies:
            for block in range(blocks):
                step = side * blocks + block
                for copy in copies[2 * step : 2 * step + 2]:
                    copy.wait()
                block_sums(out, side, block)
        else:
            pl.loop(0, blocks)(functools.partial(block_sums, out, side))


def load_kernel(first, width, gate, up, held, sems):
    copies = list(sums_fetch(first, width, gate, up, held, sems))
    for copy in copies:
        copy.start()
    for copy in copies:
        copy.wait()


def load(gate, up, first, width):
    shape = sums_held(gate.shape[0], width)
    return pl.pallas_call(
        functools.partial(load_kernel, first, width),
        out_shape=pltpu.VMEM(shape, BF16),
        in_specs=[HBM, HBM],
        out_specs=VMEM,
        scratch_shapes=[pltpu.SemaphoreType.DMA(shape[:2])],
        compiler_params=GRANT,
        cost_estimate=pl.CostEstimate(
            flops=0, bytes_accessed=4 * gate.shape[0] * width, transcendentals=0
        ),
        name="load",
    )(left_in_hbm(gate), left_in_hbm(up))


def first_sums_kernel(tokens, held, send, keep):
    sums_body(tokens, held, send, keep)


def first_sums(tokens, held):
    rows, depth = tokens.shape
    units = held.shape[0] * BLOCK
    return pl.pallas_call(
        first_sums_kernel,
        out_shape=(jax.ShapeDtypeStruct((rows, units), BF16), jax.ShapeDtypeStruct((rows, units), F32)),
        in_specs=[VMEM, VMEM],
        out_specs=(VMEM, VMEM),
        compiler_params=GRANT,
        cost_estimate=pl.CostEstimate(
            flops=4 * rows * depth * units, bytes_accessed=4 * depth * units, transcendentals=0
        ),
        name="first_sums",
    )(tokens, held_in(held))


def sums_kernel(first, width, tokens, gate, up, after, send, keep, held, sems):
    copies = list(sums_fetch(first, width, gate, up, held, sems))
    for copy in copies:
        copy.start()
    sums_body(tokens, held, send, keep, copies)


def sums(tokens, gate, up, after, first, width):
    rows, depth = tokens.shape
    shape = sums_held(depth, width)
    return pl.pallas_call(
        functools.partial(sums_kernel, first, width),
        out_shape=(jax.ShapeDtypeStruct((rows, width), BF16), jax.ShapeDtypeStruct((rows, width), F32)),
        in_specs=[VMEM, HBM, HBM, ANY],
        out_specs=(VMEM, VMEM),
        scratch_shapes=[pltpu.VMEM(shape, BF16), pltpu.SemaphoreType.DMA(shape[:2])],
        compiler_params=pltpu.CompilerParams(vmem_limit_bytes=4 * depth * width + 4 * 2**20),
        cost_estimate=pl.CostEstimate(
            flops=4 * rows * depth * width, bytes_accessed=4 * depth * width, transcendentals=0
        ),
        name="sums",
    )(tokens, left_in_hbm(gate), left_in_hbm(up), after)


def down_kernel(first, width, mine, other, weight, total, out):
    core = lax.axis_index("sub")
    half = width // 2
    out[...] = total[...]
    for side, hidden in ((core, mine), (1 - core, other)):

        @pl.loop(0, half // BLOCK)
        def _(block):
            units = pl.ds(pl.multiple_of(block * BLOCK, BLOCK), BLOCK)
            rows = pl.ds(pl.multiple_of(first + side * half + block * BLOCK, BLOCK), BLOCK)
            out[...] += jnp.dot(hidden[:, units], weight[rows, :], preferred_element_type=F32)


def down(mine, other, weight, total, first, width):
    rows, features = total.shape
    return pl.pallas_call(
        functools.partial(down_kernel, first, width),
        out_shape=jax.ShapeDtypeStruct(total.shape, F32),
        in_specs=[VMEM] * 4,
        out_specs=VMEM,
        compiler_params=GRANT,
        cost_estimate=pl.CostEstimate(
            flops=2 * rows * features * width, bytes_accessed=2 * features * width, transcendentals=0
        ),
        name="down",
    )(mine, other, held_in(weight), total)


def split(units):
    lumps = units // 512
    ends = [lumps * part // 13 * 512 for part in (0, 6, 10, 13)]
    return [(start, end - start) for start, end in zip(ends, ends[1:])]


def across(x, apart):
    return lax.ppermute(x, "wide", [(i, i ^ apart) for i in range(4)])


def chunked(tokens, gate_weight, up_weight, down_weight):
    rows = tokens.shape[0]
    chunks = split(gate_weight.shape[1])
    section = jnp.concatenate([tokens] + [across(tokens, apart) for apart in (1, 2, 3)], axis=0)
    held = load(gate_weight, up_weight, *chunks[0])

    def core_sums(send, keep):
        total = keep + swap(send, "sub").astype(F32)
        return total, total.astype(BF16)

    def hidden_half(total, sent):
        return activate(*jnp.split(total + swap(sent, "narrow").astype(F32), 2, axis=1))

    parts = [core_sums(*first_sums(section, held))]
    for chunk in chunks[1:]:
        parts.append(core_sums(*sums(section, gate_weight, up_weight, parts[-1][1], *chunk)))
    mixed = jnp.zeros((4 * rows, down_weight.shape[1]), F32)
    for chunk, part in zip(chunks, parts):
        mine = hidden_half(*part)
        mixed = down(mine, swap(mine, "sub"), down_weight, mixed, *chunk)
    blocks = mixed.reshape(4, rows, -1)
    out = blocks[0]
    for apart in (1, 2, 3):
        out = out + across(blocks[apart].astype(BF16), apart).astype(F32)
    return out.astype(BF16)


def solution(mesh):
    placed = (
        P(("groups", "wide"), ("narrow", "sub")),
        P(("narrow", "sub"), "wide"),
        P(("narrow", "sub"), "wide"),
        P("wide", ("narrow", "sub")),
    )
    sizes = tuple(mesh.shape[axis] for axis in ("groups", "wide", "narrow", "sub"))
    return jax.shard_map(
        chunked if sizes == (2, 4, 2, 2) else general,
        mesh=mesh,
        in_specs=placed,
        out_specs=P(("groups", "wide"), ("narrow", "sub")),
        check_vma=False,
    )
```

time: 72.3 us -> 65.1 us (0.900)
  waiting for transfers between devices: 17.6 us -> 13.3 us
  Pallas kernels: 39.1 us -> 35 us
  starting transfers between devices: 13.7 us -> 14.9 us
    ppermute x8 -> x9, waiting for transfers between devices: 12.6 us -> 7.21 us  [swap(): return lax.ppermute(x, axis, [(0, 1), (1, 0)])]
    pallas_call x2 -> x3, Pallas kernels: 12.2 us -> 7.81 us  [down(): pl.pallas_call(functools.partial(down_kernel, first, width), out_shape=ja...]
    ppermute x8 -> x9, starting transfers between devices: 3.6 us -> 4.87 us  [swap(): return lax.ppermute(x, axis, [(0, 1), (1, 0)])]
    ppermute x6, waiting for transfers between devices: 5.02 us -> 6.13 us  [across(): return lax.ppermute(x, 'wide', [(i, i ^ apart) for i in range(4)])]
    pallas_call x1 -> x2, Pallas kernels: 12.4 us -> 12.7 us  [sums(): pl.pallas_call(functools.partial(sums_kernel, first, width), out_shape=(j...]
  transfers between devices with their start and end apart: 14 -> 15, of which waited for: 6 -> 8; matrix products, arithmetic and copies ran while one was open for 1% -> 1% of each run, Pallas kernels for 37% -> 32%
where the time goes in v5:
time: 65.1 us; the launch traced here: 65 us
  Pallas kernels  35 us (54%)
  starting transfers between devices  14.9 us (23%)
  waiting for transfers between devices  13.3 us (20%)
  other arithmetic  1.25 us (2%)
    pallas_call x2, Pallas kernels, sums(): pl.pallas_call(functools.partial(sums_kernel, first, width), out_shape=(j...  12.7 us
    ppermute x6, starting transfers between devices, across(): return lax.ppermute(x, 'wide', [(i, i ^ apart) for i in range(4)])  10.1 us
    pallas_call x1, Pallas kernels, load(): pl.pallas_call(functools.partial(load_kernel, first, width), out_shape=pl...  8.77 us
    pallas_call x3, Pallas kernels, down(): pl.pallas_call(functools.partial(down_kernel, first, width), out_shape=ja...  7.81 us
    ppermute x9, waiting for transfers between devices, swap(): return lax.ppermute(x, axis, [(0, 1), (1, 0)])  7.21 us
    ppermute x6, waiting for transfers between devices, across(): return lax.ppermute(x, 'wide', [(i, i ^ apart) for i in range(4)])  6.13 us
    pallas_call x1, Pallas kernels, first_sums(): pl.pallas_call(first_sums_kernel, out_shape=(jax.ShapeDtypeStruct((rows,...  5.72 us
    ppermute x9, starting transfers between devices, swap(): return lax.ppermute(x, axis, [(0, 1), (1, 0)])  4.87 us
  transfers between devices with their start and end apart: 15, of which 8 were waited for; matrix products, arithmetic and copies ran while one was open for 1% of the time, Pallas kernels for 32%

profile of v5, /device:TPU:0, one launch (start us, length us, event | category | flops | bytes accessed | tf_op | source)
XLA Modules:
  0.0 65.0 jit_solution(4981196307896826124)
XLA Ops:
  0.0 3.0 %collective-permute-start = (bf16[12,2048]{1,0:T(8,128)(2,1)}, bf16[12,2048]{1,0:T(8,128)(2,1)S(1)}, u32[]{:S(2)}, u32[]{:S(2)}) collective-permute-start(bf16[12,2048]{1,0:T(8,128)(2,1)} %param.4), channel_id=1, source_target_pairs={{0,4},{4,0},{8,12},{12,8},{1,5},{5,1},{9,13},{13,9},{2,6},{6,2},{1... | collective-permute-start | bytes 147464 | tf_op jit(solution)/shard_map/ppermute | solution.py:198
  3.0 2.6 %collective-permute-start.1 = (bf16[12,2048]{1,0:T(8,128)(2,1)}, bf16[12,2048]{1,0:T(8,128)(2,1)S(1)}, u32[]{:S(2)}, u32[]{:S(2)}) collective-permute-start(bf16[12,2048]{1,0:T(8,128)(2,1)} %param.4), channel_id=1, source_target_pairs={{0,8},{4,12},{8,0},{12,4},{1,9},{5,13},{9,1},{13,5},{2,10},{6,14},... | collective-permute-start | bytes 147464 | tf_op jit(solution)/shard_map/ppermute | solution.py:198
  5.6 8.8 %load.1.held = bf16[12,2,2048,256]{3,2,1,0:T(8,128)(2,1)S(1)} custom-call(bf16[2048,6656]{1,0:T(8,128)(2,1)} %gate.5, bf16[2048,6656]{1,0:T(8,128)(2,1)} %up.5), custom_call_target="tpu_custom_call" | custom-call | bytes 25165824 | tf_op jit(solution)/shard_map/load/pallas_call | solution.py:105
  14.5 5.7 %first_sums.1 = (bf16[48,3072]{1,0:T(8,128)(2,1)S(1)}, f32[48,3072]{1,0:T(8,128)S(1)}) custom-call(bf16[48,2048]{1,0:T(8,128)(2,1)S(1)} %pad_maximum_fusion.tokens, bf16[12,2,2048,256]{3,2,1,0:T(8,128)(2,1)S(1)} %load.1.held), custom_call_target="tpu_custom_call" | custom-call | flops 1207959552 | bytes 25165824 | tf_op jit(solution)/shard_map/first_sums/pallas_call | solution.py:126
  20.3 1.6 %collective-permute-done.3 = bf16[48,3072]{1,0:T(8,128)(2,1)S(1)} collective-permute-done((bf16[48,3072]{1,0:T(8,128)(2,1)S(1)}, bf16[48,3072]{1,0:T(8,128)(2,1)S(1)}, u32[]{:S(2)}, u32[]{:S(2)}) %collective-permute-start.3) | collective-permute-done | bytes 294944 | tf_op jit(solution)/shard_map/ppermute | solution.py:34
  21.9 6.7 %sums.2 = (bf16[48,2048]{1,0:T(8,128)(2,1)S(1)}, f32[48,2048]{1,0:T(8,128)S(1)}) custom-call(bf16[48,2048]{1,0:T(8,128)(2,1)S(1)} %pad_maximum_fusion.tokens, bf16[2048,6656]{1,0:T(8,128)(2,1)} %gate.5, bf16[2048,6656]{1,0:T(8,128)(2,1)} %up.5, bf16[48,3072]{1,0:T(8,128)(2,1)S(1)} %fusion.after), custom_call_target="tpu_custom_call" | custom-call | flops 805306368 | bytes 16777216 | tf_op jit(solution)/shard_map/sums/pallas_call | solution.py:149
  28.6 0.2 collective-permute-start.4
  28.8 1.7 %collective-permute-start.10 = (bf16[48,3072]{1,0:T(8,128)(2,1)S(1)}, bf16[48,3072]{1,0:T(8,128)(2,1)S(1)}, u32[]{:S(2)}, u32[]{:S(2)}) collective-permute-start(bf16[48,3072]{1,0:T(8,128)(2,1)S(1)} %fusion.after), channel_id=1, source_target_pairs={{0,2},{2,0},{1,3},{3,1},{4,6},{6,4},{5,7},{7,5},{8,10},{10,8},{9,1... | collective-permute-start | bytes 884744 | tf_op jit(solution)/shard_map/ppermute | solution.py:34
  30.7 1.4 %collective-permute-start.8 = (bf16[48,2048]{1,0:T(8,128)(2,1)S(1)}, bf16[48,2048]{1,0:T(8,128)(2,1)S(1)}, u32[]{:S(2)}, u32[]{:S(2)}) collective-permute-start(bf16[48,2048]{1,0:T(8,128)(2,1)S(1)} %fusion.2.after), channel_id=1, source_target_pairs={{0,2},{2,0},{1,3},{3,1},{4,6},{6,4},{5,7},{7,5},{8,10},{10,8},{9,1... | collective-permute-start | bytes 589832 | tf_op jit(solution)/shard_map/ppermute | solution.py:34
  32.0 6.0 %sums.3 = (bf16[48,1536]{1,0:T(8,128)(2,1)S(1)}, f32[48,1536]{1,0:T(8,128)S(1)}) custom-call(bf16[48,2048]{1,0:T(8,128)(2,1)S(1)} %pad_maximum_fusion.tokens, bf16[2048,6656]{1,0:T(8,128)(2,1)} %gate.5, bf16[2048,6656]{1,0:T(8,128)(2,1)} %up.5, bf16[48,2048]{1,0:T(8,128)(2,1)S(1)} %fusion.2.after), custom_call_target="tpu_custom_call" | custom-call | flops 603979776 | bytes 12582912 | tf_op jit(solution)/shard_map/sums/pallas_call | solution.py:149
  38.1 0.5 collective-permute-done.10
  38.9 0.5 collective-permute-done.5
  39.5 1.2 %collective-permute-start.6 = (bf16[48,1536]{1,0:T(8,128)(2,1)S(1)}, bf16[48,1536]{1,0:T(8,128)(2,1)S(1)}, u32[]{:S(2)}, u32[]{:S(2)}) collective-permute-start(bf16[48,1536]{1,0:T(8,128)(2,1)S(1)} %fusion.3), channel_id=1, source_target_pairs={{0,2},{2,0},{1,3},{3,1},{4,6},{6,4},{5,7},{7,5},{8,10},{10,8},{9,1... | collective-permute-start | bytes 442376 | tf_op jit(solution)/shard_map/ppermute | solution.py:34
  40.7 1.6 %collective-permute-done.8 = bf16[48,2048]{1,0:T(8,128)(2,1)S(1)} collective-permute-done((bf16[48,2048]{1,0:T(8,128)(2,1)S(1)}, bf16[48,2048]{1,0:T(8,128)(2,1)S(1)}, u32[]{:S(2)}, u32[]{:S(2)}) %collective-permute-start.8) | collective-permute-done | bytes 196640 | tf_op jit(solution)/shard_map/ppermute | solution.py:34
  42.5 2.9 %collective-permute-done.6 = bf16[48,1536]{1,0:T(8,128)(2,1)S(1)} collective-permute-done((bf16[48,1536]{1,0:T(8,128)(2,1)S(1)}, bf16[48,1536]{1,0:T(8,128)(2,1)S(1)}, u32[]{:S(2)}, u32[]{:S(2)}) %collective-permute-start.6) | collective-permute-done | bytes 147488 | tf_op jit(solution)/shard_map/ppermute | solution.py:34
  45.8 3.6 %down.3.total = f32[48,2048]{1,0:T(8,128)S(1)} custom-call(bf16[48,1536]{1,0:T(8,128)(2,1)S(1)} %fusion.1.mine, bf16[48,1536]{1,0:T(8,128)(2,1)S(1)} %collective-permute-done.11.other, bf16[6656,2048]{1,0:T(8,128)(2,1)S(1)} %bitcast.1, f32[48,2048]{1,0:T(8,128)S(1)} %broadcast_in_dim.3.total), custom_call_target="tpu_custom_call" | custom-call | flops 603979776 | bytes 12582912 | tf_op jit(solution)/shard_map/down/pallas_call | solution.py:178
  49.4 2.4 %down.4.total = f32[48,2048]{1,0:T(8,128)S(1)} custom-call(bf16[48,1024]{1,0:T(8,128)(2,1)S(1)} %fusion.4.mine, bf16[48,1024]{1,0:T(8,128)(2,1)S(1)} %collective-permute-done.9.other, bf16[6656,2048]{1,0:T(8,128)(2,1)S(1)} %bitcast.1, f32[48,2048]{1,0:T(8,128)S(1)} %down.3.total), custom_call_target="tpu_custom_call" | custom-call | flops 402653184 | bytes 8388608 | tf_op jit(solution)/shard_map/down/pallas_call | solution.py:178
  51.8 1.8 %down.5 = f32[48,2048]{1,0:T(8,128)S(1)} custom-call(bf16[48,768]{1,0:T(8,128)(2,1)S(1)} %fusion.5.mine, bf16[48,768]{1,0:T(8,128)(2,1)S(1)} %collective-permute-done.7.other, bf16[6656,2048]{1,0:T(8,128)(2,1)S(1)} %bitcast.1, f32[48,2048]{1,0:T(8,128)S(1)} %down.4.total), custom_call_target="tpu_custom_call" | custom-call | flops 301989888 | bytes 6291456 | tf_op jit(solution)/shard_map/down/pallas_call | solution.py:178
  53.7 1.0 %collective-permute-start.12 = (bf16[12,2048]{1,0:T(8,128)(2,1)S(1)}, bf16[12,2048]{1,0:T(8,128)(2,1)S(1)}, u32[]{:S(2)}, u32[]{:S(2)}) collective-permute-start(bf16[12,2048]{1,0:T(8,128)(2,1)S(1)} %get-tuple-element.17), channel_id=1, source_target_pairs={{0,4},{4,0},{8,12},{12,8},{1,5},{5,1},{9,13},{13,9},{2,6},{6,2},{1... | collective-permute-start | bytes 147464 | tf_op jit(solution)/shard_map/ppermute | solution.py:198
  54.7 3.5 %collective-permute-start.13 = (bf16[12,2048]{1,0:T(8,128)(2,1)S(1)}, bf16[12,2048]{1,0:T(8,128)(2,1)S(1)}, u32[]{:S(2)}, u32[]{:S(2)}) collective-permute-start(bf16[12,2048]{1,0:T(8,128)(2,1)S(1)} %get-tuple-element.19), channel_id=1, source_target_pairs={{0,8},{4,12},{8,0},{12,4},{1,9},{5,13},{9,1},{13,5},{2,10},{6,14},... | collective-permute-start | bytes 147464 | tf_op jit(solution)/shard_map/ppermute | solution.py:198
  58.2 0.1 collective-permute-done.12
  58.3 4.1 %collective-permute-done.13 = bf16[12,2048]{1,0:T(8,128)(2,1)S(1)} collective-permute-done((bf16[12,2048]{1,0:T(8,128)(2,1)S(1)}, bf16[12,2048]{1,0:T(8,128)(2,1)S(1)}, u32[]{:S(2)}, u32[]{:S(2)}) %collective-permute-start.13) | collective-permute-done | bytes 49184 | tf_op jit(solution)/shard_map/ppermute | solution.py:198
  62.4 1.9 %collective-permute-done.14 = bf16[12,2048]{1,0:T(8,128)(2,1)S(1)} collective-permute-done((bf16[12,2048]{1,0:T(8,128)(2,1)S(1)}, bf16[12,2048]{1,0:T(8,128)(2,1)S(1)}, u32[]{:S(2)}, u32[]{:S(2)}) %collective-permute-start.14) | collective-permute-done | bytes 49184 | tf_op jit(solution)/shard_map/ppermute | solution.py:198
  64.3 0.7 %fusion.8 = bf16[12,2048]{1,0:T(8,128)(2,1)} fusion(f32[48,2048]{1,0:T(8,128)S(1)} %down.5, bf16[12,2048]{1,0:T(8,128)(2,1)S(1)} %collective-permute-done.14, bf16[12,2048]{1,0:T(8,128)(2,1)S(1)} %collective-permute-done.13, bf16[12,2048]{1,0:T(8,128)(2,1)S(1)} %collective-permute-done.12), kind=kLoop, calls=%fused_computation.19 | loop fusion | flops 172032 | bytes 294912 | tf_op jit(solution)/shard_map/convert_element_type | solution.py:225
  (44 shorter events, 1.1 us)
Async XLA Ops:
  0.0 14.4 %copy-start = (bf16[12,2048]{1,0:T(8,128)(2,1)S(1)}, bf16[12,2048]{1,0:T(8,128)(2,1)}, u32[]{:S(2)}) copy-start(bf16[12,2048]{1,0:T(8,128)(2,1)} %param.4) | copy-start | bytes 147460
  0.0 14.4 %collective-permute-start = (bf16[12,2048]{1,0:T(8,128)(2,1)}, bf16[12,2048]{1,0:T(8,128)(2,1)S(1)}, u32[]{:S(2)}, u32[]{:S(2)}) collective-permute-start(bf16[12,2048]{1,0:T(8,128)(2,1)} %param.4), channel_id=1, source_target_pairs={{0,4},{4,0},{8,12},{12,8},{1,5},{5,1},{9,13},{13,9},{2,6},{6,2},{1... | collective-permute-start | bytes 147464 | tf_op jit(solution)/shard_map/ppermute | solution.py:198
  3.0 11.4 %collective-permute-start.1 = (bf16[12,2048]{1,0:T(8,128)(2,1)}, bf16[12,2048]{1,0:T(8,128)(2,1)S(1)}, u32[]{:S(2)}, u32[]{:S(2)}) collective-permute-start(bf16[12,2048]{1,0:T(8,128)(2,1)} %param.4), channel_id=1, source_target_pairs={{0,8},{4,12},{8,0},{12,4},{1,9},{5,13},{9,1},{13,5},{2,10},{6,14},... | collective-permute-start | bytes 147464 | tf_op jit(solution)/shard_map/ppermute | solution.py:198
  5.6 8.8 %collective-permute-start.2 = (bf16[12,2048]{1,0:T(8,128)(2,1)}, bf16[12,2048]{1,0:T(8,128)(2,1)S(1)}, u32[]{:S(2)}, u32[]{:S(2)}) collective-permute-start(bf16[12,2048]{1,0:T(8,128)(2,1)} %param.4), channel_id=1, source_target_pairs={{0,12},{4,8},{8,4},{12,0},{1,13},{5,9},{9,5},{13,1},{2,14},{6,10},... | collective-permute-start | bytes 147464 | tf_op jit(solution)/shard_map/ppermute | solution.py:198
  20.2 1.6 %collective-permute-start.3 = (bf16[48,3072]{1,0:T(8,128)(2,1)S(1)}, bf16[48,3072]{1,0:T(8,128)(2,1)S(1)}, u32[]{:S(2)}, u32[]{:S(2)}) collective-permute-start(bf16[48,3072]{1,0:T(8,128)(2,1)S(1)} %get-tuple-element.12), channel_id=1, source_target_pairs={{0,1},{1,0},{2,3},{3,2},{4,5},{5,4},{6,7},{7,6},{8,9},{9,8},{10,11... | collective-permute-start | bytes 884744 | tf_op jit(solution)/shard_map/ppermute | solution.py:34
  28.6 1.9 %collective-permute-start.4 = (bf16[48,2048]{1,0:T(8,128)(2,1)S(1)}, bf16[48,2048]{1,0:T(8,128)(2,1)S(1)}, u32[]{:S(2)}, u32[]{:S(2)}) collective-permute-start(bf16[48,2048]{1,0:T(8,128)(2,1)S(1)} %get-tuple-element.14), channel_id=1, source_target_pairs={{0,1},{1,0},{2,3},{3,2},{4,5},{5,4},{6,7},{7,6},{8,9},{9,8},{10,11... | collective-permute-start | bytes 589832 | tf_op jit(solution)/shard_map/ppermute | solution.py:34
  28.8 9.8 %collective-permute-start.10 = (bf16[48,3072]{1,0:T(8,128)(2,1)S(1)}, bf16[48,3072]{1,0:T(8,128)(2,1)S(1)}, u32[]{:S(2)}, u32[]{:S(2)}) collective-permute-start(bf16[48,3072]{1,0:T(8,128)(2,1)S(1)} %fusion.after), channel_id=1, source_target_pairs={{0,2},{2,0},{1,3},{3,1},{4,6},{6,4},{5,7},{7,5},{8,10},{10,8},{9,1... | collective-permute-start | bytes 884744 | tf_op jit(solution)/shard_map/ppermute | solution.py:34
  30.5 15.2 %slice-start = ((s8[27262976]{0:T(1024)(128)(4,1)}), s8[4194304]{0:T(1024)(128)(4,1)S(1)}, s32[]{:S(2)}) async-start(s8[27262976]{0:T(1024)(128)(4,1)} %bitcast), calls=%async_computation | async-start | bytes 8388608
  30.6 15.1 %slice-start.1 = ((s8[27262976]{0:T(1024)(128)(4,1)}), s8[4194304]{0:T(1024)(128)(4,1)S(1)}, s32[]{:S(2)}) async-start(s8[27262976]{0:T(1024)(128)(4,1)} %bitcast), calls=%async_computation.1 | async-start | bytes 8388608
  30.6 15.1 %slice-start.2 = ((s8[27262976]{0:T(1024)(128)(4,1)}), s8[4194304]{0:T(1024)(128)(4,1)S(1)}, s32[]{:S(2)}) async-start(s8[27262976]{0:T(1024)(128)(4,1)} %bitcast), calls=%async_computation.2 | async-start | bytes 8388608
  30.6 15.1 %slice-start.3 = ((s8[27262976]{0:T(1024)(128)(4,1)}), s8[4194304]{0:T(1024)(128)(4,1)S(1)}, s32[]{:S(2)}) async-start(s8[27262976]{0:T(1024)(128)(4,1)} %bitcast), calls=%async_computation.3 | async-start | bytes 8388608
  30.6 15.1 %slice-start.4 = ((s8[27262976]{0:T(1024)(128)(4,1)}), s8[4194304]{0:T(1024)(128)(4,1)S(1)}, s32[]{:S(2)}) async-start(s8[27262976]{0:T(1024)(128)(4,1)} %bitcast), calls=%async_computation.4 | async-start | bytes 8388608
  30.6 15.1 %slice-start.5 = ((s8[27262976]{0:T(1024)(128)(4,1)}), s8[4194304]{0:T(1024)(128)(4,1)S(1)}, s32[]{:S(2)}) async-start(s8[27262976]{0:T(1024)(128)(4,1)} %bitcast), calls=%async_computation.5 | async-start | bytes 8388608
  30.6 15.1 %slice-start.6 = ((s8[27262976]{0:T(1024)(128)(4,1)}), s8[2097152]{0:T(1024)(128)(4,1)S(1)}, s32[]{:S(2)}) async-start(s8[27262976]{0:T(1024)(128)(4,1)} %bitcast), calls=%async_computation.6 | async-start | bytes 4194304
  30.7 11.7 %collective-permute-start.8 = (bf16[48,2048]{1,0:T(8,128)(2,1)S(1)}, bf16[48,2048]{1,0:T(8,128)(2,1)S(1)}, u32[]{:S(2)}, u32[]{:S(2)}) collective-permute-start(bf16[48,2048]{1,0:T(8,128)(2,1)S(1)} %fusion.2.after), channel_id=1, source_target_pairs={{0,2},{2,0},{1,3},{3,1},{4,6},{6,4},{5,7},{7,5},{8,10},{10,8},{9,1... | collective-permute-start | bytes 589832 | tf_op jit(solution)/shard_map/ppermute | solution.py:34
  38.0 1.4 %collective-permute-start.5 = (bf16[48,1536]{1,0:T(8,128)(2,1)S(1)}, bf16[48,1536]{1,0:T(8,128)(2,1)S(1)}, u32[]{:S(2)}, u32[]{:S(2)}) collective-permute-start(bf16[48,1536]{1,0:T(8,128)(2,1)S(1)} %get-tuple-element.16), channel_id=1, source_target_pairs={{0,1},{1,0},{2,3},{3,2},{4,5},{5,4},{6,7},{7,6},{8,9},{9,8},{10,11... | collective-permute-start | bytes 442376 | tf_op jit(solution)/shard_map/ppermute | solution.py:34
  38.8 6.8 %collective-permute-start.11 = (bf16[48,1536]{1,0:T(8,128)(2,1)S(1)}, bf16[48,1536]{1,0:T(8,128)(2,1)S(1)}, u32[]{:S(2)}, u32[]{:S(2)}) collective-permute-start(bf16[48,1536]{1,0:T(8,128)(2,1)S(1)} %fusion.1.mine), channel_id=1, source_target_pairs={{0,1},{1,0},{2,3},{3,2},{4,5},{5,4},{6,7},{7,6},{8,9},{9,8},{10,11... | collective-permute-start | bytes 442376 | tf_op jit(solution)/shard_map/ppermute | solution.py:34
  39.5 6.0 %collective-permute-start.6 = (bf16[48,1536]{1,0:T(8,128)(2,1)S(1)}, bf16[48,1536]{1,0:T(8,128)(2,1)S(1)}, u32[]{:S(2)}, u32[]{:S(2)}) collective-permute-start(bf16[48,1536]{1,0:T(8,128)(2,1)S(1)} %fusion.3), channel_id=1, source_target_pairs={{0,2},{2,0},{1,3},{3,1},{4,6},{6,4},{5,7},{7,5},{8,10},{10,8},{9,1... | collective-permute-start | bytes 442376 | tf_op jit(solution)/shard_map/ppermute | solution.py:34
  42.4 6.9 %collective-permute-start.9 = (bf16[48,1024]{1,0:T(8,128)(2,1)S(1)}, bf16[48,1024]{1,0:T(8,128)(2,1)S(1)}, u32[]{:S(2)}, u32[]{:S(2)}) collective-permute-start(bf16[48,1024]{1,0:T(8,128)(2,1)S(1)} %fusion.4.mine), channel_id=1, source_target_pairs={{0,1},{1,0},{2,3},{3,2},{4,5},{5,4},{6,7},{7,6},{8,9},{9,8},{10,11... | collective-permute-start | bytes 294920 | tf_op jit(solution)/shard_map/ppermute | solution.py:34
  45.6 6.2 %collective-permute-start.7 = (bf16[48,768]{1,0:T(8,128)(2,1)S(1)}, bf16[48,768]{1,0:T(8,128)(2,1)S(1)}, u32[]{:S(2)}, u32[]{:S(2)}) collective-permute-start(bf16[48,768]{1,0:T(8,128)(2,1)S(1)} %fusion.5.mine), channel_id=1, source_target_pairs={{0,1},{1,0},{2,3},{3,2},{4,5},{5,4},{6,7},{7,6},{8,9},{9,8},{10,11... | collective-permute-start | bytes 221192 | tf_op jit(solution)/shard_map/ppermute | solution.py:34
  53.7 4.5 %collective-permute-start.12 = (bf16[12,2048]{1,0:T(8,128)(2,1)S(1)}, bf16[12,2048]{1,0:T(8,128)(2,1)S(1)}, u32[]{:S(2)}, u32[]{:S(2)}) collective-permute-start(bf16[12,2048]{1,0:T(8,128)(2,1)S(1)} %get-tuple-element.17), channel_id=1, source_target_pairs={{0,4},{4,0},{8,12},{12,8},{1,5},{5,1},{9,13},{13,9},{2,6},{6,2},{1... | collective-permute-start | bytes 147464 | tf_op jit(solution)/shard_map/ppermute | solution.py:198
  54.7 7.7 %collective-permute-start.13 = (bf16[12,2048]{1,0:T(8,128)(2,1)S(1)}, bf16[12,2048]{1,0:T(8,128)(2,1)S(1)}, u32[]{:S(2)}, u32[]{:S(2)}) collective-permute-start(bf16[12,2048]{1,0:T(8,128)(2,1)S(1)} %get-tuple-element.19), channel_id=1, source_target_pairs={{0,8},{4,12},{8,0},{12,4},{1,9},{5,13},{9,1},{13,5},{2,10},{6,14},... | collective-permute-start | bytes 147464 | tf_op jit(solution)/shard_map/ppermute | solution.py:198
  58.2 6.1 %collective-permute-start.14 = (bf16[12,2048]{1,0:T(8,128)(2,1)S(1)}, bf16[12,2048]{1,0:T(8,128)(2,1)S(1)}, u32[]{:S(2)}, u32[]{:S(2)}) collective-permute-start(bf16[12,2048]{1,0:T(8,128)(2,1)S(1)} %get-tuple-element.18), channel_id=1, source_target_pairs={{0,12},{4,8},{8,4},{12,0},{1,13},{5,9},{9,5},{13,1},{2,14},{6,10},... | collective-permute-start | bytes 147464 | tf_op jit(solution)/shard_map/ppermute | solution.py:198

commit v6 on v5

--- a/solution.py
+++ b/solution.py
@@ -163,14 +163,15 @@
 def down_kernel(first, width, mine, other, weight, total, out):
     core = lax.axis_index("sub")
     half = width // 2
-    out[...] = total[...]
-    for side, hidden in ((core, mine), (1 - core, other)):
-
-        @pl.loop(0, half // BLOCK)
-        def _(block):
-            units = pl.ds(pl.multiple_of(block * BLOCK, BLOCK), BLOCK)
-            rows = pl.ds(pl.multiple_of(first + side * half + block * BLOCK, BLOCK), BLOCK)
-            out[...] += jnp.dot(hidden[:, units], weight[rows, :], preferred_element_type=F32)
+    starts = [pl.multiple_of(first + side * half, BLOCK) for side in (core, 1 - core)]
+
+    @pl.loop(0, out.shape[1] // BLOCK)
+    def _(block):
+        columns = pl.ds(pl.multiple_of(block * BLOCK, BLOCK), BLOCK)
+        part = total[:, columns]
+        for start, hidden in zip(starts, (mine, other)):
+            part += jnp.dot(hidden[...], weight[pl.ds(start, half), columns], preferred_element_type=F32)
+        out[:, columns] = part
 
 
 def down(mine, other, weight, total, first, width):
@@ -208,21 +209,31 @@
         total = keep + swap(send, "sub").astype(F32)
         return total, total.astype(BF16)
 
-    def hidden_half(total, sent):
-        return activate(*jnp.split(total + swap(sent, "narrow").astype(F32), 2, axis=1))
-
-    parts = [core_sums(*first_sums(section, held))]
-    for chunk in chunks[1:]:
-        parts.append(core_sums(*sums(section, gate_weight, up_weight, parts[-1][1], *chunk)))
+    def hidden_half(total, received):
+        return activate(*jnp.split(total + received.astype(F32), 2, axis=1))
+
+    def add(mixed, mine, chunk):
+        return down(mine, swap(mine, "sub"), down_weight, mixed, *chunk)
+
     mixed = jnp.zeros((4 * rows, down_weight.shape[1]), F32)
-    for chunk, part in zip(chunks, parts):
-        mine = hidden_half(*part)
-        mixed = down(mine, swap(mine, "sub"), down_weight, mixed, *chunk)
-    blocks = mixed.reshape(4, rows, -1)
+    total, sent = core_sums(*first_sums(section, held))
+    send, keep = sums(section, gate_weight, up_weight, sent, *chunks[1])
+    received, send = lax.optimization_barrier((swap(sent, "narrow"), send))
+    mine = hidden_half(total, received)
+    total, sent = core_sums(send, keep)
+    send, keep = sums(section, gate_weight, up_weight, sent, *chunks[2])
+    mixed = add(mixed, mine, chunks[0])
+    received, send = lax.optimization_barrier((swap(sent, "narrow"), send))
+    mine = hidden_half(total, received)
+    total, sent = core_sums(send, keep)
+    mixed = add(mixed, mine, chunks[1])
+    received, mixed = lax.optimization_barrier((swap(sent, "narrow"), mixed))
+    mixed = add(mixed, hidden_half(total, received), chunks[2])
+    blocks = mixed.reshape(4, rows, 2, -1).swapaxes(1, 2).reshape(4, 2 * rows, -1)
     out = blocks[0]
-    for apart in (1, 2, 3):
-        out = out + across(blocks[apart].astype(BF16), apart).astype(F32)
-    return out.astype(BF16)
+    for received in [across(blocks[apart].astype(BF16), apart) for apart in (3, 2, 1)]:
+        out = out + received.astype(F32)
+    return out.astype(BF16).reshape(2, rows, -1).swapaxes(0, 1).reshape(rows, -1)
 
 
 def solution(mesh):

time: 65.1 us -> 66.6 us (1.023)
  local copies, waits for them, and re-layouts: 0.1 us -> 5.57 us
  waiting for transfers between devices: 13.3 us -> 9.78 us
  starting transfers between devices: 14.9 us -> 15.6 us
    unnamed x16 -> x18, local copies, waits for them, and re-layouts: 0.04 us -> 4.82 us
    ppermute x6, waiting for transfers between devices: 6.13 us -> 3.96 us  [across(): return lax.ppermute(x, 'wide', [(i, i ^ apart) for i in range(4)])]
    ppermute x9, waiting for transfers between devices: 7.21 us -> 5.82 us  [swap(): return lax.ppermute(x, axis, [(0, 1), (1, 0)])]
  transfers between devices with their start and end apart: 15 -> 15, of which waited for: 8 -> 7; matrix products, arithmetic and copies ran while one was open for 1% -> 1% of each run, Pallas kernels for 32% -> 40%
where the time goes in v6:
time: 66.6 us; the launch traced here: 66.5 us
  Pallas kernels  34.5 us (52%)
  starting transfers between devices  15.6 us (23%)
  waiting for transfers between devices  9.78 us (15%)
  local copies, waits for them, and re-layouts  5.57 us (8%)
    pallas_call x2, Pallas kernels, sums(): pl.pallas_call(functools.partial(sums_kernel, first, width), out_shape=(j...  12.2 us
    ppermute x6, starting transfers between devices, across(): return lax.ppermute(x, 'wide', [(i, i ^ apart) for i in range(4)])  10.2 us
    pallas_call x1, Pallas kernels, load(): pl.pallas_call(functools.partial(load_kernel, first, width), out_shape=pl...  8.77 us
    pallas_call x3, Pallas kernels, down(): pl.pallas_call(functools.partial(down_kernel, first, width), out_shape=ja...  7.86 us
    ppermute x9, waiting for transfers between devices, swap(): return lax.ppermute(x, axis, [(0, 1), (1, 0)])  5.82 us
    pallas_call x1, Pallas kernels, first_sums(): pl.pallas_call(first_sums_kernel, out_shape=(jax.ShapeDtypeStruct((rows,...  5.72 us
    ppermute x9, starting transfers between devices, swap(): return lax.ppermute(x, axis, [(0, 1), (1, 0)])  5.44 us
    unnamed x18, local copies, waits for them, and re-layouts  4.82 us
  transfers between devices with their start and end apart: 15, of which 7 were waited for; matrix products, arithmetic and copies ran while one was open for 1% of the time, Pallas kernels for 40%

profile of v6, /device:TPU:0, one launch (start us, length us, event | category | flops | bytes accessed | tf_op | source)
XLA Modules:
  0.0 66.5 jit_solution(6373305159718321450)
XLA Ops:
  0.0 3.0 %collective-permute-start = (bf16[12,2048]{1,0:T(8,128)(2,1)}, bf16[12,2048]{1,0:T(8,128)(2,1)S(1)}, u32[]{:S(2)}, u32[]{:S(2)}) collective-permute-start(bf16[12,2048]{1,0:T(8,128)(2,1)} %param.4), channel_id=1, source_target_pairs={{0,4},{4,0},{8,12},{12,8},{1,5},{5,1},{9,13},{13,9},{2,6},{6,2},{1... | collective-permute-start | bytes 147464 | tf_op jit(solution)/shard_map/ppermute | solution.py:199
  3.0 2.6 %collective-permute-start.1 = (bf16[12,2048]{1,0:T(8,128)(2,1)}, bf16[12,2048]{1,0:T(8,128)(2,1)S(1)}, u32[]{:S(2)}, u32[]{:S(2)}) collective-permute-start(bf16[12,2048]{1,0:T(8,128)(2,1)} %param.4), channel_id=1, source_target_pairs={{0,8},{4,12},{8,0},{12,4},{1,9},{5,13},{9,1},{13,5},{2,10},{6,14},... | collective-permute-start | bytes 147464 | tf_op jit(solution)/shard_map/ppermute | solution.py:199
  5.6 8.8 %load.1.held = bf16[12,2,2048,256]{3,2,1,0:T(8,128)(2,1)S(1)} custom-call(bf16[2048,6656]{1,0:T(8,128)(2,1)} %gate.5, bf16[2048,6656]{1,0:T(8,128)(2,1)} %up.5), custom_call_target="tpu_custom_call" | custom-call | bytes 25165824 | tf_op jit(solution)/shard_map/load/pallas_call | solution.py:105
  14.5 5.7 %first_sums.1 = (bf16[48,3072]{1,0:T(8,128)(2,1)S(1)}, f32[48,3072]{1,0:T(8,128)S(1)}) custom-call(bf16[48,2048]{1,0:T(8,128)(2,1)S(1)} %pad_maximum_fusion.tokens, bf16[12,2,2048,256]{3,2,1,0:T(8,128)(2,1)S(1)} %load.1.held), custom_call_target="tpu_custom_call" | custom-call | flops 1207959552 | bytes 25165824 | tf_op jit(solution)/shard_map/first_sums/pallas_call | solution.py:126
  20.3 1.6 %collective-permute-done.3 = bf16[48,3072]{1,0:T(8,128)(2,1)S(1)} collective-permute-done((bf16[48,3072]{1,0:T(8,128)(2,1)S(1)}, bf16[48,3072]{1,0:T(8,128)(2,1)S(1)}, u32[]{:S(2)}, u32[]{:S(2)}) %collective-permute-start.3) | collective-permute-done | bytes 294944 | tf_op jit(solution)/shard_map/ppermute | solution.py:34
  21.9 1.8 %collective-permute-start.4 = (bf16[48,3072]{1,0:T(8,128)(2,1)S(1)}, bf16[48,3072]{1,0:T(8,128)(2,1)S(1)}, u32[]{:S(2)}, u32[]{:S(2)}) collective-permute-start(bf16[48,3072]{1,0:T(8,128)(2,1)S(1)} %fusion.after), channel_id=1, source_target_pairs={{0,2},{2,0},{1,3},{3,1},{4,6},{6,4},{5,7},{7,5},{8,10},{10,8},{9,1... | collective-permute-start | bytes 884744 | tf_op jit(solution)/shard_map/ppermute | solution.py:34
  23.7 6.6 %sums.2 = (bf16[48,2048]{1,0:T(8,128)(2,1)S(1)}, f32[48,2048]{1,0:T(8,128)S(1)}) custom-call(bf16[48,2048]{1,0:T(8,128)(2,1)S(1)} %pad_maximum_fusion.tokens, bf16[2048,6656]{1,0:T(8,128)(2,1)} %gate.5, bf16[2048,6656]{1,0:T(8,128)(2,1)} %up.5, bf16[48,3072]{1,0:T(8,128)(2,1)S(1)} %fusion.after), custom_call_target="tpu_custom_call" | custom-call | flops 805306368 | bytes 16777216 | tf_op jit(solution)/shard_map/sums/pallas_call | solution.py:149
  31.1 1.4 %collective-permute-done.5 = bf16[48,2048]{1,0:T(8,128)(2,1)S(1)} collective-permute-done((bf16[48,2048]{1,0:T(8,128)(2,1)S(1)}, bf16[48,2048]{1,0:T(8,128)(2,1)S(1)}, u32[]{:S(2)}, u32[]{:S(2)}) %collective-permute-start.5) | collective-permute-done | bytes 196640 | tf_op jit(solution)/shard_map/ppermute | solution.py:34
  32.5 1.8 %collective-permute-start.6 = (bf16[48,2048]{1,0:T(8,128)(2,1)S(1)}, bf16[48,2048]{1,0:T(8,128)(2,1)S(1)}, u32[]{:S(2)}, u32[]{:S(2)}) collective-permute-start(bf16[48,2048]{1,0:T(8,128)(2,1)S(1)} %fusion.2.after), channel_id=1, source_target_pairs={{0,2},{2,0},{1,3},{3,1},{4,6},{6,4},{5,7},{7,5},{8,10},{10,8},{9,1... | collective-permute-start | bytes 589832 | tf_op jit(solution)/shard_map/ppermute | solution.py:34
  34.6 5.5 %sums.3 = (bf16[48,1536]{1,0:T(8,128)(2,1)S(1)}, f32[48,1536]{1,0:T(8,128)S(1)}) custom-call(bf16[48,2048]{1,0:T(8,128)(2,1)S(1)} %pad_maximum_fusion.tokens, bf16[2048,6656]{1,0:T(8,128)(2,1)} %gate.5, bf16[2048,6656]{1,0:T(8,128)(2,1)} %up.5, bf16[48,2048]{1,0:T(8,128)(2,1)S(1)} %fusion.2.after), custom_call_target="tpu_custom_call" | custom-call | flops 603979776 | bytes 12582912 | tf_op jit(solution)/shard_map/sums/pallas_call | solution.py:149
  40.1 0.8 %collective-permute-start.7 = (bf16[48,1536]{1,0:T(8,128)(2,1)S(1)}, bf16[48,1536]{1,0:T(8,128)(2,1)S(1)}, u32[]{:S(2)}, u32[]{:S(2)}) collective-permute-start(bf16[48,1536]{1,0:T(8,128)(2,1)S(1)} %get-tuple-element.24), channel_id=1, source_target_pairs={{0,1},{1,0},{2,3},{3,2},{4,5},{5,4},{6,7},{7,6},{8,9},{9,8},{10,11... | collective-permute-start | bytes 442376 | tf_op jit(solution)/shard_map/ppermute | solution.py:34
  41.0 0.9 %collective-permute-done.7 = bf16[48,1536]{1,0:T(8,128)(2,1)S(1)} collective-permute-done((bf16[48,1536]{1,0:T(8,128)(2,1)S(1)}, bf16[48,1536]{1,0:T(8,128)(2,1)S(1)}, u32[]{:S(2)}, u32[]{:S(2)}) %collective-permute-start.7) | collective-permute-done | bytes 147488 | tf_op jit(solution)/shard_map/ppermute | solution.py:34
  41.9 0.8 %collective-permute-start.8 = (bf16[48,1536]{1,0:T(8,128)(2,1)S(1)}, bf16[48,1536]{1,0:T(8,128)(2,1)S(1)}, u32[]{:S(2)}, u32[]{:S(2)}) collective-permute-start(bf16[48,1536]{1,0:T(8,128)(2,1)S(1)} %fusion.3), channel_id=1, source_target_pairs={{0,2},{2,0},{1,3},{3,1},{4,6},{6,4},{5,7},{7,5},{8,10},{10,8},{9,1... | collective-permute-start | bytes 442376 | tf_op jit(solution)/shard_map/ppermute | solution.py:34
  42.9 1.1 %slice-done.3 = s8[4194304]{0:T(1024)(128)(4,1)S(1)} async-done(((s8[27262976]{0:T(1024)(128)(4,1)}), s8[4194304]{0:T(1024)(128)(4,1)S(1)}, s32[]{:S(2)}) %slice-start.3) | async-done | bytes 4194328
  44.1 1.2 %slice-done.4 = s8[4194304]{0:T(1024)(128)(4,1)S(1)} async-done(((s8[27262976]{0:T(1024)(128)(4,1)}), s8[4194304]{0:T(1024)(128)(4,1)S(1)}, s32[]{:S(2)}) %slice-start.4) | async-done | bytes 4194328
  45.3 1.2 %slice-done.5 = s8[4194304]{0:T(1024)(128)(4,1)S(1)} async-done(((s8[27262976]{0:T(1024)(128)(4,1)}), s8[4194304]{0:T(1024)(128)(4,1)S(1)}, s32[]{:S(2)}) %slice-start.5) | async-done | bytes 4194328
  47.1 3.3 %down.3.total = f32[48,2048]{1,0:T(8,128)S(1)} custom-call(bf16[48,1536]{1,0:T(8,128)(2,1)S(1)} %fusion.1.mine, bf16[48,1536]{1,0:T(8,128)(2,1)S(1)} %collective-permute-done.10.other, bf16[6656,2048]{1,0:T(8,128)(2,1)S(1)} %bitcast.11, f32[48,2048]{1,0:T(8,128)S(1)} %broadcast_in_dim.3.total), custom_call_target="tpu_custom_call" | custom-call | flops 603979776 | bytes 12582912 | tf_op jit(solution)/shard_map/down/pallas_call | solution.py:179
  50.3 2.5 %down.4.total = f32[48,2048]{1,0:T(8,128)S(1)} custom-call(bf16[48,1024]{1,0:T(8,128)(2,1)S(1)} %fusion.4.mine, bf16[48,1024]{1,0:T(8,128)(2,1)S(1)} %collective-permute-done.9.other, bf16[6656,2048]{1,0:T(8,128)(2,1)S(1)} %bitcast.11, f32[48,2048]{1,0:T(8,128)S(1)} %down.3.total), custom_call_target="tpu_custom_call" | custom-call | flops 402653184 | bytes 8388608 | tf_op jit(solution)/shard_map/down/pallas_call | solution.py:179
  53.0 1.3 %collective-permute-done.11.other = bf16[48,768]{1,0:T(8,128)(2,1)S(1)} collective-permute-done((bf16[48,768]{1,0:T(8,128)(2,1)S(1)}, bf16[48,768]{1,0:T(8,128)(2,1)S(1)}, u32[]{:S(2)}, u32[]{:S(2)}) %collective-permute-start.11) | collective-permute-done | bytes 73760 | tf_op jit(solution)/shard_map/ppermute | solution.py:34
  54.3 2.1 %down.5 = f32[48,2048]{1,0:T(8,128)S(1)} custom-call(bf16[48,768]{1,0:T(8,128)(2,1)S(1)} %fusion.5.mine, bf16[48,768]{1,0:T(8,128)(2,1)S(1)} %collective-permute-done.11.other, bf16[6656,2048]{1,0:T(8,128)(2,1)S(1)} %bitcast.11, f32[48,2048]{1,0:T(8,128)S(1)} %down.4.total), custom_call_target="tpu_custom_call" | custom-call | flops 301989888 | bytes 6291456 | tf_op jit(solution)/shard_map/down/pallas_call | solution.py:179
  56.9 3.7 %collective-permute-start.12 = (bf16[24,1024]{1,0:T(8,128)(2,1)S(1)}, bf16[24,1024]{1,0:T(8,128)(2,1)S(1)}, u32[]{:S(2)}, u32[]{:S(2)}) collective-permute-start(bf16[24,1024]{1,0:T(8,128)(2,1)S(1)} %convert_element_type.72), channel_id=1, source_target_pairs={{0,12},{4,8},{8,4},{12,0},{1,13},{5,9},{9,5},{13,1},{2,14},{6,10},... | collective-permute-start | bytes 147464 | tf_op jit(solution)/shard_map/ppermute | solution.py:199
  60.7 0.8 %collective-permute-start.14 = (bf16[24,1024]{1,0:T(8,128)(2,1)S(1)}, bf16[24,1024]{1,0:T(8,128)(2,1)S(1)}, u32[]{:S(2)}, u32[]{:S(2)}) collective-permute-start(bf16[24,1024]{1,0:T(8,128)(2,1)S(1)} %convert_element_type.76), channel_id=1, source_target_pairs={{0,4},{4,0},{8,12},{12,8},{1,5},{5,1},{9,13},{13,9},{2,6},{6,2},{1... | collective-permute-start | bytes 147464 | tf_op jit(solution)/shard_map/ppermute | solution.py:199
  61.7 1.5 %collective-permute-done.12 = bf16[24,1024]{1,0:T(8,128)(2,1)S(1)} collective-permute-done((bf16[24,1024]{1,0:T(8,128)(2,1)S(1)}, bf16[24,1024]{1,0:T(8,128)(2,1)S(1)}, u32[]{:S(2)}, u32[]{:S(2)}) %collective-permute-start.12) | collective-permute-done | bytes 49184 | tf_op jit(solution)/shard_map/ppermute | solution.py:199
  63.2 2.5 %collective-permute-done.13 = bf16[24,1024]{1,0:T(8,128)(2,1)S(1)} collective-permute-done((bf16[24,1024]{1,0:T(8,128)(2,1)S(1)}, bf16[24,1024]{1,0:T(8,128)(2,1)S(1)}, u32[]{:S(2)}, u32[]{:S(2)}) %collective-permute-start.13) | collective-permute-done | bytes 49184 | tf_op jit(solution)/shard_map/ppermute | solution.py:199
  (55 shorter events, 3.7 us)
Async XLA Ops:
  0.0 14.4 %copy-start = (bf16[12,2048]{1,0:T(8,128)(2,1)S(1)}, bf16[12,2048]{1,0:T(8,128)(2,1)}, u32[]{:S(2)}) copy-start(bf16[12,2048]{1,0:T(8,128)(2,1)} %param.4) | copy-start | bytes 147460
  0.0 14.4 %collective-permute-start = (bf16[12,2048]{1,0:T(8,128)(2,1)}, bf16[12,2048]{1,0:T(8,128)(2,1)S(1)}, u32[]{:S(2)}, u32[]{:S(2)}) collective-permute-start(bf16[12,2048]{1,0:T(8,128)(2,1)} %param.4), channel_id=1, source_target_pairs={{0,4},{4,0},{8,12},{12,8},{1,5},{5,1},{9,13},{13,9},{2,6},{6,2},{1... | collective-permute-start | bytes 147464 | tf_op jit(solution)/shard_map/ppermute | solution.py:199
  3.0 11.4 %collective-permute-start.1 = (bf16[12,2048]{1,0:T(8,128)(2,1)}, bf16[12,2048]{1,0:T(8,128)(2,1)S(1)}, u32[]{:S(2)}, u32[]{:S(2)}) collective-permute-start(bf16[12,2048]{1,0:T(8,128)(2,1)} %param.4), channel_id=1, source_target_pairs={{0,8},{4,12},{8,0},{12,4},{1,9},{5,13},{9,1},{13,5},{2,10},{6,14},... | collective-permute-start | bytes 147464 | tf_op jit(solution)/shard_map/ppermute | solution.py:199
  5.6 8.8 %collective-permute-start.2 = (bf16[12,2048]{1,0:T(8,128)(2,1)}, bf16[12,2048]{1,0:T(8,128)(2,1)S(1)}, u32[]{:S(2)}, u32[]{:S(2)}) collective-permute-start(bf16[12,2048]{1,0:T(8,128)(2,1)} %param.4), channel_id=1, source_target_pairs={{0,12},{4,8},{8,4},{12,0},{1,13},{5,9},{9,5},{13,1},{2,14},{6,10},... | collective-permute-start | bytes 147464 | tf_op jit(solution)/shard_map/ppermute | solution.py:199
  20.2 1.6 %collective-permute-start.3 = (bf16[48,3072]{1,0:T(8,128)(2,1)S(1)}, bf16[48,3072]{1,0:T(8,128)(2,1)S(1)}, u32[]{:S(2)}, u32[]{:S(2)}) collective-permute-start(bf16[48,3072]{1,0:T(8,128)(2,1)S(1)} %get-tuple-element.18), channel_id=1, source_target_pairs={{0,1},{1,0},{2,3},{3,2},{4,5},{5,4},{6,7},{7,6},{8,9},{9,8},{10,11... | collective-permute-start | bytes 884744 | tf_op jit(solution)/shard_map/ppermute | solution.py:34
  21.9 9.1 %collective-permute-start.4 = (bf16[48,3072]{1,0:T(8,128)(2,1)S(1)}, bf16[48,3072]{1,0:T(8,128)(2,1)S(1)}, u32[]{:S(2)}, u32[]{:S(2)}) collective-permute-start(bf16[48,3072]{1,0:T(8,128)(2,1)S(1)} %fusion.after), channel_id=1, source_target_pairs={{0,2},{2,0},{1,3},{3,1},{4,6},{6,4},{5,7},{7,5},{8,10},{10,8},{9,1... | collective-permute-start | bytes 884744 | tf_op jit(solution)/shard_map/ppermute | solution.py:34
  31.1 1.4 %collective-permute-start.5 = (bf16[48,2048]{1,0:T(8,128)(2,1)S(1)}, bf16[48,2048]{1,0:T(8,128)(2,1)S(1)}, u32[]{:S(2)}, u32[]{:S(2)}) collective-permute-start(bf16[48,2048]{1,0:T(8,128)(2,1)S(1)} %get-tuple-element.21), channel_id=1, source_target_pairs={{0,1},{1,0},{2,3},{3,2},{4,5},{5,4},{6,7},{7,6},{8,9},{9,8},{10,11... | collective-permute-start | bytes 589832 | tf_op jit(solution)/shard_map/ppermute | solution.py:34
  32.5 7.5 %collective-permute-start.6 = (bf16[48,2048]{1,0:T(8,128)(2,1)S(1)}, bf16[48,2048]{1,0:T(8,128)(2,1)S(1)}, u32[]{:S(2)}, u32[]{:S(2)}) collective-permute-start(bf16[48,2048]{1,0:T(8,128)(2,1)S(1)} %fusion.2.after), channel_id=1, source_target_pairs={{0,2},{2,0},{1,3},{3,1},{4,6},{6,4},{5,7},{7,5},{8,10},{10,8},{9,1... | collective-permute-start | bytes 589832 | tf_op jit(solution)/shard_map/ppermute | solution.py:34
  34.3 8.6 %slice-start = ((s8[27262976]{0:T(1024)(128)(4,1)}), s8[4194304]{0:T(1024)(128)(4,1)S(1)}, s32[]{:S(2)}) async-start(s8[27262976]{0:T(1024)(128)(4,1)} %bitcast.10), calls=%async_computation | async-start | bytes 8388608
  34.4 8.5 %slice-start.1 = ((s8[27262976]{0:T(1024)(128)(4,1)}), s8[4194304]{0:T(1024)(128)(4,1)S(1)}, s32[]{:S(2)}) async-start(s8[27262976]{0:T(1024)(128)(4,1)} %bitcast.10), calls=%async_computation.1 | async-start | bytes 8388608
  34.4 8.5 %slice-start.2 = ((s8[27262976]{0:T(1024)(128)(4,1)}), s8[4194304]{0:T(1024)(128)(4,1)S(1)}, s32[]{:S(2)}) async-start(s8[27262976]{0:T(1024)(128)(4,1)} %bitcast.10), calls=%async_computation.2 | async-start | bytes 8388608
  34.4 9.6 %slice-start.3 = ((s8[27262976]{0:T(1024)(128)(4,1)}), s8[4194304]{0:T(1024)(128)(4,1)S(1)}, s32[]{:S(2)}) async-start(s8[27262976]{0:T(1024)(128)(4,1)} %bitcast.10), calls=%async_computation.3 | async-start | bytes 8388608
  34.4 10.8 %slice-start.4 = ((s8[27262976]{0:T(1024)(128)(4,1)}), s8[4194304]{0:T(1024)(128)(4,1)S(1)}, s32[]{:S(2)}) async-start(s8[27262976]{0:T(1024)(128)(4,1)} %bitcast.10), calls=%async_computation.4 | async-start | bytes 8388608
  34.5 12.0 %slice-start.5 = ((s8[27262976]{0:T(1024)(128)(4,1)}), s8[4194304]{0:T(1024)(128)(4,1)S(1)}, s32[]{:S(2)}) async-start(s8[27262976]{0:T(1024)(128)(4,1)} %bitcast.10), calls=%async_computation.5 | async-start | bytes 8388608
  34.5 12.6 %slice-start.6 = ((s8[27262976]{0:T(1024)(128)(4,1)}), s8[2097152]{0:T(1024)(128)(4,1)S(1)}, s32[]{:S(2)}) async-start(s8[27262976]{0:T(1024)(128)(4,1)} %bitcast.10), calls=%async_computation.6 | async-start | bytes 4194304
  34.5 8.4 %collective-permute-start.10 = (bf16[48,1536]{1,0:T(8,128)(2,1)S(1)}, bf16[48,1536]{1,0:T(8,128)(2,1)S(1)}, u32[]{:S(2)}, u32[]{:S(2)}) collective-permute-start(bf16[48,1536]{1,0:T(8,128)(2,1)S(1)} %fusion.1.mine), channel_id=1, source_target_pairs={{0,1},{1,0},{2,3},{3,2},{4,5},{5,4},{6,7},{7,6},{8,9},{9,8},{10,11... | collective-permute-start | bytes 442376 | tf_op jit(solution)/shard_map/ppermute | solution.py:34
  40.1 1.8 %collective-permute-start.7 = (bf16[48,1536]{1,0:T(8,128)(2,1)S(1)}, bf16[48,1536]{1,0:T(8,128)(2,1)S(1)}, u32[]{:S(2)}, u32[]{:S(2)}) collective-permute-start(bf16[48,1536]{1,0:T(8,128)(2,1)S(1)} %get-tuple-element.24), channel_id=1, source_target_pairs={{0,1},{1,0},{2,3},{3,2},{4,5},{5,4},{6,7},{7,6},{8,9},{9,8},{10,11... | collective-permute-start | bytes 442376 | tf_op jit(solution)/shard_map/ppermute | solution.py:34
  41.9 10.9 %collective-permute-start.8 = (bf16[48,1536]{1,0:T(8,128)(2,1)S(1)}, bf16[48,1536]{1,0:T(8,128)(2,1)S(1)}, u32[]{:S(2)}, u32[]{:S(2)}) collective-permute-start(bf16[48,1536]{1,0:T(8,128)(2,1)S(1)} %fusion.3), channel_id=1, source_target_pairs={{0,2},{2,0},{1,3},{3,1},{4,6},{6,4},{5,7},{7,5},{8,10},{10,8},{9,1... | collective-permute-start | bytes 442376 | tf_op jit(solution)/shard_map/ppermute | solution.py:34
  42.8 7.5 %collective-permute-start.9 = (bf16[48,1024]{1,0:T(8,128)(2,1)S(1)}, bf16[48,1024]{1,0:T(8,128)(2,1)S(1)}, u32[]{:S(2)}, u32[]{:S(2)}) collective-permute-start(bf16[48,1024]{1,0:T(8,128)(2,1)S(1)} %fusion.4.mine), channel_id=1, source_target_pairs={{0,1},{1,0},{2,3},{3,2},{4,5},{5,4},{6,7},{7,6},{8,9},{9,8},{10,11... | collective-permute-start | bytes 294920 | tf_op jit(solution)/shard_map/ppermute | solution.py:34
  52.9 1.3 %collective-permute-start.11 = (bf16[48,768]{1,0:T(8,128)(2,1)S(1)}, bf16[48,768]{1,0:T(8,128)(2,1)S(1)}, u32[]{:S(2)}, u32[]{:S(2)}) collective-permute-start(bf16[48,768]{1,0:T(8,128)(2,1)S(1)} %fusion.5.mine), channel_id=1, source_target_pairs={{0,1},{1,0},{2,3},{3,2},{4,5},{5,4},{6,7},{7,6},{8,9},{9,8},{10,11... | collective-permute-start | bytes 221192 | tf_op jit(solution)/shard_map/ppermute | solution.py:34
  56.9 6.3 %collective-permute-start.12 = (bf16[24,1024]{1,0:T(8,128)(2,1)S(1)}, bf16[24,1024]{1,0:T(8,128)(2,1)S(1)}, u32[]{:S(2)}, u32[]{:S(2)}) collective-permute-start(bf16[24,1024]{1,0:T(8,128)(2,1)S(1)} %convert_element_type.72), channel_id=1, source_target_pairs={{0,12},{4,8},{8,4},{12,0},{1,13},{5,9},{9,5},{13,1},{2,14},{6,10},... | collective-permute-start | bytes 147464 | tf_op jit(solution)/shard_map/ppermute | solution.py:199
  60.6 5.1 %collective-permute-start.13 = (bf16[24,1024]{1,0:T(8,128)(2,1)S(1)}, bf16[24,1024]{1,0:T(8,128)(2,1)S(1)}, u32[]{:S(2)}, u32[]{:S(2)}) collective-permute-start(bf16[24,1024]{1,0:T(8,128)(2,1)S(1)} %convert_element_type.74), channel_id=1, source_target_pairs={{0,8},{4,12},{8,0},{12,4},{1,9},{5,13},{9,1},{13,5},{2,10},{6,14},... | collective-permute-start | bytes 147464 | tf_op jit(solution)/shard_map/ppermute | solution.py:199
  60.7 5.0 %collective-permute-start.14 = (bf16[24,1024]{1,0:T(8,128)(2,1)S(1)}, bf16[24,1024]{1,0:T(8,128)(2,1)S(1)}, u32[]{:S(2)}, u32[]{:S(2)}) collective-permute-start(bf16[24,1024]{1,0:T(8,128)(2,1)S(1)} %convert_element_type.76), channel_id=1, source_target_pairs={{0,4},{4,0},{8,12},{12,8},{1,5},{5,1},{9,13},{13,9},{2,6},{6,2},{1... | collective-permute-start | bytes 147464 | tf_op jit(solution)/shard_map/ppermute | solution.py:199

commit v7 on v6

v7 whole, which is shorter than its diff:
```python
import functools

import jax
import jax.numpy as jnp
from jax import lax
from jax.experimental import pallas as pl
from jax.experimental.pallas import tpu as pltpu
from jax.sharding import PartitionSpec as P

BF16 = jnp.bfloat16
F32 = jnp.float32


def activate(gate_sums, up_sums):
    return (jax.nn.silu(gate_sums) * up_sums).astype(BF16)


def general(tokens, gate_weight, up_weight, down_weight):
    section = lax.all_gather(tokens, "wide", axis=0, tiled=True)
    gate_part = jnp.dot(section, gate_weight, preferred_element_type=F32)
    up_part = jnp.dot(section, up_weight, preferred_element_type=F32)
    gate_sums = lax.psum(gate_part, ("narrow", "sub"))
    up_sums = lax.psum(up_part, ("narrow", "sub"))
    mixed = lax.psum_scatter(
        jnp.dot(activate(gate_sums, up_sums), down_weight, preferred_element_type=F32),
        "wide",
        scatter_dimension=0,
        tiled=True,
    )
    return mixed.astype(BF16)


def swap(x, axis):
    return lax.ppermute(x, axis, [(0, 1), (1, 0)])


BLOCK = 256
VMEM = pl.BlockSpec(memory_space=pltpu.VMEM)
ANY = pl.BlockSpec(memory_space=pl.ANY)
HBM = pl.BlockSpec(memory_space=pltpu.HBM)
GRANT = pltpu.CompilerParams(vmem_limit_bytes=6 * 2**20)


def held_in(x):
    return pltpu.with_memory_space_constraint(x, pltpu.VMEM)


def left_in_hbm(x):
    return pltpu.with_memory_space_constraint(x, pltpu.HBM)


def block_copies(first, half, step, gate, up, dst, sem):
    core = lax.axis_index("sub")
    mine = jnp.int32(step >= half // BLOCK)
    side = jnp.where(mine == 1, core, 1 - core)
    unit = first + side * half + (step - mine * (half // BLOCK)) * BLOCK
    columns = pl.ds(pl.multiple_of(unit, BLOCK), BLOCK)
    return [
        pltpu.make_async_copy(weight.at[:, columns], dst.at[i], sem.at[i]) for i, weight in enumerate((gate, up))
    ]


def load_kernel(first, half, gate, up, held, sems):
    copies = [
        copy
        for step in range(held.shape[0])
        for copy in block_copies(first, half, step, gate, up, held.at[step], sems.at[step])
    ]
    for copy in copies:
        copy.start()
    for copy in copies:
        copy.wait()


def load(gate, up, chunk, steps):
    depth = gate.shape[0]
    return pl.pallas_call(
        functools.partial(load_kernel, chunk[0], chunk[1] // 2),
        out_shape=pltpu.VMEM((steps, 2, depth, BLOCK), BF16),
        in_specs=[HBM, HBM],
        out_specs=VMEM,
        scratch_shapes=[pltpu.SemaphoreType.DMA((steps, 2))],
        compiler_params=GRANT,
        cost_estimate=pl.CostEstimate(
            flops=0, bytes_accessed=4 * steps * depth * BLOCK, transcendentals=0
        ),
        name="load",
    )(left_in_hbm(gate), left_in_hbm(up))


def sums_kernel(first, steps, tokens, gate, up, *refs):
    send, keep, streamed, sems = refs[-4:]
    held = refs[0] if steps else None
    half = send.shape[1] // 2
    blocks = half // BLOCK

    def copies(step):
        at = step - steps
        return block_copies(first, half, step, gate, up, streamed.at[at], sems.at[at])

    for step in range(steps, 2 * blocks):
        for copy in copies(step):
            copy.start()

    def add(out, start, source, block):
        for i in range(2):
            column = pl.multiple_of((i * blocks + block - start) * BLOCK, BLOCK)
            out[:, pl.ds(column, BLOCK)] = jnp.dot(tokens[...], source[i], preferred_element_type=F32).astype(
                out.dtype
            )

    for side, out in enumerate((send, keep)):
        start, end = side * blocks, (side + 1) * blocks

        middle = min(max(steps, start), end)
        if start < middle:

            @pl.loop(start, middle)
            def _(step):
                add(out, start, held.at[step], step)

        if middle < end:

            @pl.loop(middle, end)
            def _(step):
                for copy in copies(step):
                    copy.wait()
                add(out, start, streamed.at[step - steps], step)


def sums(tokens, gate, up, chunk, held=None):
    rows, depth = tokens.shape
    first, width = chunk
    steps = 0 if held is None else held.shape[0]
    shape = (width // BLOCK - steps, 2, depth, BLOCK)
    return pl.pallas_call(
        functools.partial(sums_kernel, first, steps),
        out_shape=(jax.ShapeDtypeStruct((rows, width), BF16), jax.ShapeDtypeStruct((rows, width), F32)),
        in_specs=[VMEM, HBM, HBM] + [VMEM] * (steps > 0),
        out_specs=(VMEM, VMEM),
        scratch_shapes=[pltpu.VMEM(shape, BF16), pltpu.SemaphoreType.DMA(shape[:2])],
        compiler_params=pltpu.CompilerParams(vmem_limit_bytes=4 * shape[0] * depth * BLOCK + 4 * 2**20),
        cost_estimate=pl.CostEstimate(
            flops=4 * rows * depth * width, bytes_accessed=4 * depth * width, transcendentals=0
        ),
        name="sums",
    )(tokens, left_in_hbm(gate), left_in_hbm(up), *([held_in(held)] if steps else []))


def down_kernel(first, width, mine, other, weight, total, out):
    core = lax.axis_index("sub")
    half = width // 2
    starts = [pl.multiple_of(first + side * half, BLOCK) for side in (core, 1 - core)]

    @pl.loop(0, out.shape[1] // BLOCK)
    def _(block):
        columns = pl.ds(pl.multiple_of(block * BLOCK, BLOCK), BLOCK)
        part = total[:, columns]
        for start, hidden in zip(starts, (mine, other)):
            part += jnp.dot(hidden[...], weight[pl.ds(start, half), columns], preferred_element_type=F32)
        out[:, columns] = part


def down(mine, other, weight, total, first, width):
    rows, features = total.shape
    return pl.pallas_call(
        functools.partial(down_kernel, first, width),
        out_shape=jax.ShapeDtypeStruct(total.shape, F32),
        in_specs=[VMEM] * 4,
        out_specs=VMEM,
        compiler_params=GRANT,
        cost_estimate=pl.CostEstimate(
            flops=2 * rows * features * width, bytes_accessed=2 * features * width, transcendentals=0
        ),
        name="down",
    )(mine, other, held_in(weight), total)


def split(units):
    more = units // 512 * 9 // 13 * 512
    return (0, more), (more, units - more)


def across(x, apart):
    return lax.ppermute(x, "wide", [(i, i ^ apart) for i in range(4)])


def chunked(tokens, gate_weight, up_weight, down_weight):
    rows = tokens.shape[0]
    chunks = split(gate_weight.shape[1])
    section = jnp.concatenate([tokens] + [across(tokens, apart) for apart in (1, 2, 3)], axis=0)
    held = load(gate_weight, up_weight, chunks[0], 8)

    def core_sums(send, keep):
        total = keep + swap(send, "sub").astype(F32)
        return total, total.astype(BF16)

    def hidden_half(total, received):
        return activate(*jnp.split(total + received.astype(F32), 2, axis=1))

    def add(mixed, mine, chunk):
        return down(mine, swap(mine, "sub"), down_weight, mixed, *chunk)

    mixed = jnp.zeros((4 * rows, down_weight.shape[1]), F32)
    send, keep = sums(section, gate_weight, up_weight, chunks[0], held)
    total, sent = core_sums(send, keep)
    later, _ = lax.optimization_barrier((section, sent))
    send, keep = sums(later, gate_weight, up_weight, chunks[1])
    received, send = lax.optimization_barrier((swap(sent, "narrow"), send))
    mine = hidden_half(total, received)
    total, sent = core_sums(send, keep)
    mixed = add(mixed, mine, chunks[0])
    received, mixed = lax.optimization_barrier((swap(sent, "narrow"), mixed))
    mixed = add(mixed, hidden_half(total, received), chunks[1])
    blocks = mixed.reshape(4, rows, 2, -1).swapaxes(1, 2).reshape(4, 2 * rows, -1)
    out = blocks[0]
    for received in [across(blocks[apart].astype(BF16), apart) for apart in (3, 2, 1)]:
        out = out + received.astype(F32)
    return out.astype(BF16).reshape(2, rows, -1).swapaxes(0, 1).reshape(rows, -1)


def solution(mesh):
    placed = (
        P(("groups", "wide"), ("narrow", "sub")),
        P(("narrow", "sub"), "wide"),
        P(("narrow", "sub"), "wide"),
        P("wide", ("narrow", "sub")),
    )
    sizes = tuple(mesh.shape[axis] for axis in ("groups", "wide", "narrow", "sub"))
    return jax.shard_map(
        chunked if sizes == (2, 4, 2, 2) else general,
        mesh=mesh,
        in_specs=placed,
        out_specs=P(("groups", "wide"), ("narrow", "sub")),
        check_vma=False,
    )
```

time: 66.6 us -> 59.5 us (0.89)
  Pallas kernels: 34.5 us -> 29.4 us
  local copies, waits for them, and re-layouts: 5.57 us -> 1.48 us
  waiting for transfers between devices: 9.78 us -> 13.3 us
  starting transfers between devices: 15.6 us -> 14.3 us
    pallas_call x4 -> x3, Pallas kernels: 26.7 us -> 22.4 us  [the longest x2 16.2 us: sums(): pl.pallas_call(functools.partial(sums_kernel, first, steps), out_shape=(j...]
    unnamed x18, local copies, waits for them, and re-layouts: 4.82 us -> 0.73 us
    ppermute x6, waiting for transfers between devices: 3.96 us -> 5.74 us  [across(): return lax.ppermute(x, 'wide', [(i, i ^ apart) for i in range(4)])]
    ppermute x9 -> x6, waiting for transfers between devices: 5.82 us -> 7.56 us  [swap(): return lax.ppermute(x, axis, [(0, 1), (1, 0)])]
    ppermute x9 -> x6, starting transfers between devices: 5.44 us -> 4.12 us  [swap(): return lax.ppermute(x, axis, [(0, 1), (1, 0)])]
    pallas_call x3 -> x2, Pallas kernels: 7.86 us -> 6.94 us  [down(): pl.pallas_call(functools.partial(down_kernel, first, width), out_shape=ja...]
  transfers between devices with their start and end apart: 15 -> 12, of which waited for: 7 -> 9; matrix products, arithmetic and copies ran while one was open for 1% -> 1% of each run, Pallas kernels for 40% -> 30%
where the time goes in v7:
time: 59.5 us; the launch traced here: 59.3 us
  Pallas kernels  29.4 us (49%)
  starting transfers between devices  14.3 us (24%)
  waiting for transfers between devices  13.3 us (22%)
  local copies, waits for them, and re-layouts  1.48 us (2%)
    pallas_call x2, Pallas kernels, sums(): pl.pallas_call(functools.partial(sums_kernel, first, steps), out_shape=(j...  16.2 us
    ppermute x6, starting transfers between devices, across(): return lax.ppermute(x, 'wide', [(i, i ^ apart) for i in range(4)])  10.2 us
    ppermute x6, waiting for transfers between devices, swap(): return lax.ppermute(x, axis, [(0, 1), (1, 0)])  7.56 us
    pallas_call x2, Pallas kernels, down(): pl.pallas_call(functools.partial(down_kernel, first, width), out_shape=ja...  6.94 us
    pallas_call x1, Pallas kernels, load(): pl.pallas_call(functools.partial(load_kernel, chunk[0], chunk[1] // 2), o...  6.18 us
    ppermute x6, waiting for transfers between devices, across(): return lax.ppermute(x, 'wide', [(i, i ^ apart) for i in range(4)])  5.74 us
    ppermute x6, starting transfers between devices, swap(): return lax.ppermute(x, axis, [(0, 1), (1, 0)])  4.12 us
  transfers between devices with their start and end apart: 12, of which 9 were waited for; matrix products, arithmetic and copies ran while one was open for 1% of the time, Pallas kernels for 30%

profile of v7, /device:TPU:0, one launch (start us, length us, event | category | flops | bytes accessed | tf_op | source)
XLA Modules:
  0.0 59.3 jit_solution(1213344612268141220)
XLA Ops:
  0.0 3.0 %collective-permute-start = (bf16[12,2048]{1,0:T(8,128)(2,1)}, bf16[12,2048]{1,0:T(8,128)(2,1)S(1)}, u32[]{:S(2)}, u32[]{:S(2)}) collective-permute-start(bf16[12,2048]{1,0:T(8,128)(2,1)} %param.4), channel_id=1, source_target_pairs={{0,4},{4,0},{8,12},{12,8},{1,5},{5,1},{9,13},{13,9},{2,6},{6,2},{1... | collective-permute-start | bytes 147464 | tf_op jit(solution)/shard_map/ppermute | solution.py:185
  3.0 2.6 %collective-permute-start.1 = (bf16[12,2048]{1,0:T(8,128)(2,1)}, bf16[12,2048]{1,0:T(8,128)(2,1)S(1)}, u32[]{:S(2)}, u32[]{:S(2)}) collective-permute-start(bf16[12,2048]{1,0:T(8,128)(2,1)} %param.4), channel_id=1, source_target_pairs={{0,8},{4,12},{8,0},{12,4},{1,9},{5,13},{9,1},{13,5},{2,10},{6,14},... | collective-permute-start | bytes 147464 | tf_op jit(solution)/shard_map/ppermute | solution.py:185
  5.6 6.2 %load.1.refs_0_ = bf16[8,2,2048,256]{3,2,1,0:T(8,128)(2,1)S(1)} custom-call(bf16[2048,6656]{1,0:T(8,128)(2,1)} %gate.5, bf16[2048,6656]{1,0:T(8,128)(2,1)} %up.5), custom_call_target="tpu_custom_call" | custom-call | bytes 16777216 | tf_op jit(solution)/shard_map/load/pallas_call | solution.py:77
  12.0 8.8 %sums.2 = (bf16[48,4608]{1,0:T(8,128)(2,1)S(1)}, f32[48,4608]{1,0:T(8,128)S(1)}) custom-call(bf16[48,2048]{1,0:T(8,128)(2,1)S(1)} %pad_maximum_fusion.tokens, bf16[2048,6656]{1,0:T(8,128)(2,1)} %gate.5, bf16[2048,6656]{1,0:T(8,128)(2,1)} %up.5, bf16[8,2,2048,256]{3,2,1,0:T(8,128)(2,1)S(1)} %load.1.refs_0_), custom_call_target="tpu_custom_call" | custom-call | flops 1811939328 | bytes 37748736 | tf_op jit(solution)/shard_map/sums/pallas_call | solution.py:136
  20.9 1.8 %collective-permute-done.3 = bf16[48,4608]{1,0:T(8,128)(2,1)S(1)} collective-permute-done((bf16[48,4608]{1,0:T(8,128)(2,1)S(1)}, bf16[48,4608]{1,0:T(8,128)(2,1)S(1)}, u32[]{:S(2)}, u32[]{:S(2)}) %collective-permute-start.3) | collective-permute-done | bytes 442400 | tf_op jit(solution)/shard_map/ppermute | solution.py:34
  22.8 1.7 %collective-permute-start.4 = (bf16[48,4608]{1,0:T(8,128)(2,1)S(1)}, bf16[48,4608]{1,0:T(8,128)(2,1)S(1)}, u32[]{:S(2)}, u32[]{:S(2)}) collective-permute-start(bf16[48,4608]{1,0:T(8,128)(2,1)S(1)} %fusion), channel_id=1, source_target_pairs={{0,2},{2,0},{1,3},{3,1},{4,6},{6,4},{5,7},{7,5},{8,10},{10,8},{9,1... | collective-permute-start | bytes 1327112 | tf_op jit(solution)/shard_map/ppermute | solution.py:34
  24.5 7.4 %sums.3 = (bf16[48,2048]{1,0:T(8,128)(2,1)S(1)}, f32[48,2048]{1,0:T(8,128)S(1)}) custom-call(bf16[48,2048]{1,0:T(8,128)(2,1)S(1)} %pad_maximum_fusion.tokens, bf16[2048,6656]{1,0:T(8,128)(2,1)} %gate.5, bf16[2048,6656]{1,0:T(8,128)(2,1)} %up.5), custom_call_target="tpu_custom_call" | custom-call | flops 805306368 | bytes 16777216 | tf_op jit(solution)/shard_map/sums/pallas_call | solution.py:136
  31.9 3.1 %collective-permute-done.4 = bf16[48,4608]{1,0:T(8,128)(2,1)S(1)} collective-permute-done((bf16[48,4608]{1,0:T(8,128)(2,1)S(1)}, bf16[48,4608]{1,0:T(8,128)(2,1)S(1)}, u32[]{:S(2)}, u32[]{:S(2)}) %collective-permute-start.4) | collective-permute-done | bytes 442400 | tf_op jit(solution)/shard_map/ppermute | solution.py:34
  35.2 0.1 fusion.1.mine
  35.4 0.6 collective-permute-start.7
  35.9 0.6 %collective-permute-done.5 = bf16[48,2048]{1,0:T(8,128)(2,1)S(1)} collective-permute-done((bf16[48,2048]{1,0:T(8,128)(2,1)S(1)}, bf16[48,2048]{1,0:T(8,128)(2,1)S(1)}, u32[]{:S(2)}, u32[]{:S(2)}) %collective-permute-start.5) | collective-permute-done | bytes 196640 | tf_op jit(solution)/shard_map/ppermute | solution.py:34
  36.6 1.7 %collective-permute-start.6 = (bf16[48,2048]{1,0:T(8,128)(2,1)S(1)}, bf16[48,2048]{1,0:T(8,128)(2,1)S(1)}, u32[]{:S(2)}, u32[]{:S(2)}) collective-permute-start(bf16[48,2048]{1,0:T(8,128)(2,1)S(1)} %fusion.2), channel_id=1, source_target_pairs={{0,2},{2,0},{1,3},{3,1},{4,6},{6,4},{5,7},{7,5},{8,10},{10,8},{9,1... | collective-permute-start | bytes 589832 | tf_op jit(solution)/shard_map/ppermute | solution.py:34
  38.4 4.5 %down.2.total = f32[48,2048]{1,0:T(8,128)S(1)} custom-call(bf16[48,2304]{1,0:T(8,128)(2,1)S(1)} %fusion.1.mine, bf16[48,2304]{1,0:T(8,128)(2,1)S(1)} %collective-permute-done.7.other, bf16[6656,2048]{1,0:T(8,128)(2,1)S(1)} %bitcast.11, f32[48,2048]{1,0:T(8,128)S(1)} %broadcast_in_dim.3.total), custom_call_target="tpu_custom_call" | custom-call | flops 905969664 | bytes 18874368 | tf_op jit(solution)/shard_map/down/pallas_call | solution.py:166
  42.9 0.7 %collective-permute-done.6 = bf16[48,2048]{1,0:T(8,128)(2,1)S(1)} collective-permute-done((bf16[48,2048]{1,0:T(8,128)(2,1)S(1)}, bf16[48,2048]{1,0:T(8,128)(2,1)S(1)}, u32[]{:S(2)}, u32[]{:S(2)}) %collective-permute-start.6) | collective-permute-done | bytes 196640 | tf_op jit(solution)/shard_map/ppermute | solution.py:34
  43.8 1.3 %collective-permute-done.8.other = bf16[48,1024]{1,0:T(8,128)(2,1)S(1)} collective-permute-done((bf16[48,1024]{1,0:T(8,128)(2,1)S(1)}, bf16[48,1024]{1,0:T(8,128)(2,1)S(1)}, u32[]{:S(2)}, u32[]{:S(2)}) %collective-permute-start.8) | collective-permute-done | bytes 98336 | tf_op jit(solution)/shard_map/ppermute | solution.py:34
  45.1 2.5 %down.3 = f32[48,2048]{1,0:T(8,128)S(1)} custom-call(bf16[48,1024]{1,0:T(8,128)(2,1)S(1)} %fusion.3.mine, bf16[48,1024]{1,0:T(8,128)(2,1)S(1)} %collective-permute-done.8.other, bf16[6656,2048]{1,0:T(8,128)(2,1)S(1)} %bitcast.11, f32[48,2048]{1,0:T(8,128)S(1)} %down.2.total), custom_call_target="tpu_custom_call" | custom-call | flops 402653184 | bytes 8388608 | tf_op jit(solution)/shard_map/down/pallas_call | solution.py:166
  47.6 0.3 reshape.21
  48.1 1.9 %collective-permute-start.10 = (bf16[24,1024]{1,0:T(8,128)(2,1)S(1)}, bf16[24,1024]{1,0:T(8,128)(2,1)S(1)}, u32[]{:S(2)}, u32[]{:S(2)}) collective-permute-start(bf16[24,1024]{1,0:T(8,128)(2,1)S(1)} %convert_element_type.58), channel_id=1, source_target_pairs={{0,8},{4,12},{8,0},{12,4},{1,9},{5,13},{9,1},{13,5},{2,10},{6,14},... | collective-permute-start | bytes 147464 | tf_op jit(solution)/shard_map/ppermute | solution.py:185
  50.0 2.5 %collective-permute-start.11 = (bf16[24,1024]{1,0:T(8,128)(2,1)S(1)}, bf16[24,1024]{1,0:T(8,128)(2,1)S(1)}, u32[]{:S(2)}, u32[]{:S(2)}) collective-permute-start(bf16[24,1024]{1,0:T(8,128)(2,1)S(1)} %convert_element_type.60), channel_id=1, source_target_pairs={{0,4},{4,0},{8,12},{12,8},{1,5},{5,1},{9,13},{13,9},{2,6},{6,2},{1... | collective-permute-start | bytes 147464 | tf_op jit(solution)/shard_map/ppermute | solution.py:185
  52.6 0.1 collective-permute-start.9
  52.9 1.1 %collective-permute-done.10 = bf16[24,1024]{1,0:T(8,128)(2,1)S(1)} collective-permute-done((bf16[24,1024]{1,0:T(8,128)(2,1)S(1)}, bf16[24,1024]{1,0:T(8,128)(2,1)S(1)}, u32[]{:S(2)}, u32[]{:S(2)}) %collective-permute-start.10) | collective-permute-done | bytes 49184 | tf_op jit(solution)/shard_map/ppermute | solution.py:185
  54.0 0.7 %collective-permute-done.11 = bf16[24,1024]{1,0:T(8,128)(2,1)S(1)} collective-permute-done((bf16[24,1024]{1,0:T(8,128)(2,1)S(1)}, bf16[24,1024]{1,0:T(8,128)(2,1)S(1)}, u32[]{:S(2)}, u32[]{:S(2)}) %collective-permute-start.11) | collective-permute-done | bytes 49184 | tf_op jit(solution)/shard_map/ppermute | solution.py:185
  54.6 3.9 %collective-permute-done.9 = bf16[24,1024]{1,0:T(8,128)(2,1)S(1)} collective-permute-done((bf16[24,1024]{1,0:T(8,128)(2,1)S(1)}, bf16[24,1024]{1,0:T(8,128)(2,1)S(1)}, u32[]{:S(2)}, u32[]{:S(2)}) %collective-permute-start.9) | collective-permute-done | bytes 49184 | tf_op jit(solution)/shard_map/ppermute | solution.py:185
  58.7 0.6 %copy.8 = bf16[2,8,2,1024]{3,1,2,0:T(8,128)(2,1)} copy(bf16[2,8,2,1024]{3,2,1,0:T(2,128)(2,1)S(1)} %bitcast.15) | data formatting | bytes 131072
  (44 shorter events, 1.2 us)
Async XLA Ops:
  0.0 11.9 %copy-start = (bf16[12,2048]{1,0:T(8,128)(2,1)S(1)}, bf16[12,2048]{1,0:T(8,128)(2,1)}, u32[]{:S(2)}) copy-start(bf16[12,2048]{1,0:T(8,128)(2,1)} %param.4) | copy-start | bytes 147460
  0.0 11.8 %collective-permute-start = (bf16[12,2048]{1,0:T(8,128)(2,1)}, bf16[12,2048]{1,0:T(8,128)(2,1)S(1)}, u32[]{:S(2)}, u32[]{:S(2)}) collective-permute-start(bf16[12,2048]{1,0:T(8,128)(2,1)} %param.4), channel_id=1, source_target_pairs={{0,4},{4,0},{8,12},{12,8},{1,5},{5,1},{9,13},{13,9},{2,6},{6,2},{1... | collective-permute-start | bytes 147464 | tf_op jit(solution)/shard_map/ppermute | solution.py:185
  3.0 8.8 %collective-permute-start.1 = (bf16[12,2048]{1,0:T(8,128)(2,1)}, bf16[12,2048]{1,0:T(8,128)(2,1)S(1)}, u32[]{:S(2)}, u32[]{:S(2)}) collective-permute-start(bf16[12,2048]{1,0:T(8,128)(2,1)} %param.4), channel_id=1, source_target_pairs={{0,8},{4,12},{8,0},{12,4},{1,9},{5,13},{9,1},{13,5},{2,10},{6,14},... | collective-permute-start | bytes 147464 | tf_op jit(solution)/shard_map/ppermute | solution.py:185
  5.6 6.3 %collective-permute-start.2 = (bf16[12,2048]{1,0:T(8,128)(2,1)}, bf16[12,2048]{1,0:T(8,128)(2,1)S(1)}, u32[]{:S(2)}, u32[]{:S(2)}) collective-permute-start(bf16[12,2048]{1,0:T(8,128)(2,1)} %param.4), channel_id=1, source_target_pairs={{0,12},{4,8},{8,4},{12,0},{1,13},{5,9},{9,5},{13,1},{2,14},{6,10},... | collective-permute-start | bytes 147464 | tf_op jit(solution)/shard_map/ppermute | solution.py:185
  20.8 1.9 %collective-permute-start.3 = (bf16[48,4608]{1,0:T(8,128)(2,1)S(1)}, bf16[48,4608]{1,0:T(8,128)(2,1)S(1)}, u32[]{:S(2)}, u32[]{:S(2)}) collective-permute-start(bf16[48,4608]{1,0:T(8,128)(2,1)S(1)} %get-tuple-element.15), channel_id=1, source_target_pairs={{0,1},{1,0},{2,3},{3,2},{4,5},{5,4},{6,7},{7,6},{8,9},{9,8},{10,11... | collective-permute-start | bytes 1327112 | tf_op jit(solution)/shard_map/ppermute | solution.py:34
  22.7 15.6 %slice-start = ((s8[27262976]{0:T(1024)(128)(4,1)}), s8[4194304]{0:T(1024)(128)(4,1)S(1)}, s32[]{:S(2)}) async-start(s8[27262976]{0:T(1024)(128)(4,1)} %bitcast.10), calls=%async_computation | async-start | bytes 8388608
  22.8 15.6 %slice-start.1 = ((s8[27262976]{0:T(1024)(128)(4,1)}), s8[4194304]{0:T(1024)(128)(4,1)S(1)}, s32[]{:S(2)}) async-start(s8[27262976]{0:T(1024)(128)(4,1)} %bitcast.10), calls=%async_computation.1 | async-start | bytes 8388608
  22.8 15.6 %slice-start.2 = ((s8[27262976]{0:T(1024)(128)(4,1)}), s8[4194304]{0:T(1024)(128)(4,1)S(1)}, s32[]{:S(2)}) async-start(s8[27262976]{0:T(1024)(128)(4,1)} %bitcast.10), calls=%async_computation.2 | async-start | bytes 8388608
  22.8 15.6 %slice-start.3 = ((s8[27262976]{0:T(1024)(128)(4,1)}), s8[4194304]{0:T(1024)(128)(4,1)S(1)}, s32[]{:S(2)}) async-start(s8[27262976]{0:T(1024)(128)(4,1)} %bitcast.10), calls=%async_computation.3 | async-start | bytes 8388608
  22.8 15.6 %slice-start.4 = ((s8[27262976]{0:T(1024)(128)(4,1)}), s8[4194304]{0:T(1024)(128)(4,1)S(1)}, s32[]{:S(2)}) async-start(s8[27262976]{0:T(1024)(128)(4,1)} %bitcast.10), calls=%async_computation.4 | async-start | bytes 8388608
  22.8 15.6 %slice-start.5 = ((s8[27262976]{0:T(1024)(128)(4,1)}), s8[4194304]{0:T(1024)(128)(4,1)S(1)}, s32[]{:S(2)}) async-start(s8[27262976]{0:T(1024)(128)(4,1)} %bitcast.10), calls=%async_computation.5 | async-start | bytes 8388608
  22.8 15.6 %slice-start.6 = ((s8[27262976]{0:T(1024)(128)(4,1)}), s8[2097152]{0:T(1024)(128)(4,1)S(1)}, s32[]{:S(2)}) async-start(s8[27262976]{0:T(1024)(128)(4,1)} %bitcast.10), calls=%async_computation.6 | async-start | bytes 4194304
  22.8 12.3 %collective-permute-start.4 = (bf16[48,4608]{1,0:T(8,128)(2,1)S(1)}, bf16[48,4608]{1,0:T(8,128)(2,1)S(1)}, u32[]{:S(2)}, u32[]{:S(2)}) collective-permute-start(bf16[48,4608]{1,0:T(8,128)(2,1)S(1)} %fusion), channel_id=1, source_target_pairs={{0,2},{2,0},{1,3},{3,1},{4,6},{6,4},{5,7},{7,5},{8,10},{10,8},{9,1... | collective-permute-start | bytes 1327112 | tf_op jit(solution)/shard_map/ppermute | solution.py:34
  35.1 1.4 %collective-permute-start.5 = (bf16[48,2048]{1,0:T(8,128)(2,1)S(1)}, bf16[48,2048]{1,0:T(8,128)(2,1)S(1)}, u32[]{:S(2)}, u32[]{:S(2)}) collective-permute-start(bf16[48,2048]{1,0:T(8,128)(2,1)S(1)} %get-tuple-element.19), channel_id=1, source_target_pairs={{0,1},{1,0},{2,3},{3,2},{4,5},{5,4},{6,7},{7,6},{8,9},{9,8},{10,11... | collective-permute-start | bytes 589832 | tf_op jit(solution)/shard_map/ppermute | solution.py:34
  35.4 2.9 %collective-permute-start.7 = (bf16[48,2304]{1,0:T(8,128)(2,1)S(1)}, bf16[48,2304]{1,0:T(8,128)(2,1)S(1)}, u32[]{:S(2)}, u32[]{:S(2)}) collective-permute-start(bf16[48,2304]{1,0:T(8,128)(2,1)S(1)} %fusion.1.mine), channel_id=1, source_target_pairs={{0,1},{1,0},{2,3},{3,2},{4,5},{5,4},{6,7},{7,6},{8,9},{9,8},{10,11... | collective-permute-start | bytes 663560 | tf_op jit(solution)/shard_map/ppermute | solution.py:34
  36.6 7.0 %collective-permute-start.6 = (bf16[48,2048]{1,0:T(8,128)(2,1)S(1)}, bf16[48,2048]{1,0:T(8,128)(2,1)S(1)}, u32[]{:S(2)}, u32[]{:S(2)}) collective-permute-start(bf16[48,2048]{1,0:T(8,128)(2,1)S(1)} %fusion.2), channel_id=1, source_target_pairs={{0,2},{2,0},{1,3},{3,1},{4,6},{6,4},{5,7},{7,5},{8,10},{10,8},{9,1... | collective-permute-start | bytes 589832 | tf_op jit(solution)/shard_map/ppermute | solution.py:34
  43.7 1.4 %collective-permute-start.8 = (bf16[48,1024]{1,0:T(8,128)(2,1)S(1)}, bf16[48,1024]{1,0:T(8,128)(2,1)S(1)}, u32[]{:S(2)}, u32[]{:S(2)}) collective-permute-start(bf16[48,1024]{1,0:T(8,128)(2,1)S(1)} %fusion.3.mine), channel_id=1, source_target_pairs={{0,1},{1,0},{2,3},{3,2},{4,5},{5,4},{6,7},{7,6},{8,9},{9,8},{10,11... | collective-permute-start | bytes 294920 | tf_op jit(solution)/shard_map/ppermute | solution.py:34
  48.1 5.9 %collective-permute-start.10 = (bf16[24,1024]{1,0:T(8,128)(2,1)S(1)}, bf16[24,1024]{1,0:T(8,128)(2,1)S(1)}, u32[]{:S(2)}, u32[]{:S(2)}) collective-permute-start(bf16[24,1024]{1,0:T(8,128)(2,1)S(1)} %convert_element_type.58), channel_id=1, source_target_pairs={{0,8},{4,12},{8,0},{12,4},{1,9},{5,13},{9,1},{13,5},{2,10},{6,14},... | collective-permute-start | bytes 147464 | tf_op jit(solution)/shard_map/ppermute | solution.py:185
  50.0 4.6 %collective-permute-start.11 = (bf16[24,1024]{1,0:T(8,128)(2,1)S(1)}, bf16[24,1024]{1,0:T(8,128)(2,1)S(1)}, u32[]{:S(2)}, u32[]{:S(2)}) collective-permute-start(bf16[24,1024]{1,0:T(8,128)(2,1)S(1)} %convert_element_type.60), channel_id=1, source_target_pairs={{0,4},{4,0},{8,12},{12,8},{1,5},{5,1},{9,13},{13,9},{2,6},{6,2},{1... | collective-permute-start | bytes 147464 | tf_op jit(solution)/shard_map/ppermute | solution.py:185
  52.6 6.0 %collective-permute-start.9 = (bf16[24,1024]{1,0:T(8,128)(2,1)S(1)}, bf16[24,1024]{1,0:T(8,128)(2,1)S(1)}, u32[]{:S(2)}, u32[]{:S(2)}) collective-permute-start(bf16[24,1024]{1,0:T(8,128)(2,1)S(1)} %convert_element_type.56), channel_id=1, source_target_pairs={{0,12},{4,8},{8,4},{12,0},{1,13},{5,9},{9,5},{13,1},{2,14},{6,10},... | collective-permute-start | bytes 147464 | tf_op jit(solution)/shard_map/ppermute | solution.py:185

commit v8 on v7

--- a/solution.py
+++ b/solution.py
@@ -177,7 +177,7 @@
 
 
 def split(units):
-    more = units // 512 * 9 // 13 * 512
+    more = units // 512 * 8 // 13 * 512
     return (0, more), (more, units - more)
 
 
@@ -188,7 +188,9 @@
 def chunked(tokens, gate_weight, up_weight, down_weight):
     rows = tokens.shape[0]
     chunks = split(gate_weight.shape[1])
-    section = jnp.concatenate([tokens] + [across(tokens, apart) for apart in (1, 2, 3)], axis=0)
+    section = tokens
+    for apart in (3, 2, 1):
+        section = lax.optimization_barrier(jnp.concatenate([section, across(tokens, apart)], axis=0))
     held = load(gate_weight, up_weight, chunks[0], 8)
 
     def core_sums(send, keep):
@@ -206,7 +208,7 @@
     total, sent = core_sums(send, keep)
     later, _ = lax.optimization_barrier((section, sent))
     send, keep = sums(later, gate_weight, up_weight, chunks[1])
-    received, send = lax.optimization_barrier((swap(sent, "narrow"), send))
+    received, keep = lax.optimization_barrier((swap(sent, "narrow"), keep))
     mine = hidden_half(total, received)
     total, sent = core_sums(send, keep)
     mixed = add(mixed, mine, chunks[0])
@@ -214,8 +216,9 @@
     mixed = add(mixed, hidden_half(total, received), chunks[1])
     blocks = mixed.reshape(4, rows, 2, -1).swapaxes(1, 2).reshape(4, 2 * rows, -1)
     out = blocks[0]
-    for received in [across(blocks[apart].astype(BF16), apart) for apart in (3, 2, 1)]:
-        out = out + received.astype(F32)
+    for place, apart in enumerate((3, 2, 1), 1):
+        received = across(blocks[place].astype(BF16), apart)
+        out = lax.optimization_barrier(out + received.astype(F32))
     return out.astype(BF16).reshape(2, rows, -1).swapaxes(0, 1).reshape(rows, -1)
 
 

time: 59.5 us -> 56.9 us (0.956)
  waiting for transfers between devices: 13.3 us -> 9.46 us
  local copies, waits for them, and re-layouts: 1.48 us -> 3.19 us
  starting transfers between devices: 14.3 us -> 13.5 us
    ppermute x6, waiting for transfers between devices: 7.56 us -> 5.2 us  [swap(): return lax.ppermute(x, axis, [(0, 1), (1, 0)])]
    unnamed x18, local copies, waits for them, and re-layouts: 0.73 us -> 2.43 us
    ppermute x6, waiting for transfers between devices: 5.74 us -> 4.26 us  [across(): return lax.ppermute(x, 'wide', [(i, i ^ apart) for i in range(4)])]
    ppermute x6, starting transfers between devices: 4.12 us -> 3.25 us  [swap(): return lax.ppermute(x, axis, [(0, 1), (1, 0)])]
  transfers between devices with their start and end apart: 12 -> 12, of which waited for: 9 -> 7; matrix products, arithmetic and copies ran while one was open for 1% -> 1% of each run, Pallas kernels for 30% -> 33%
where the time goes in v8:
time: 56.9 us; the launch traced here: 56.7 us
  Pallas kernels  29.6 us (52%)
  starting transfers between devices  13.5 us (24%)
  waiting for transfers between devices  9.46 us (17%)
  local copies, waits for them, and re-layouts  3.19 us (6%)
  other arithmetic  0.59 us (1%)
    pallas_call x2, Pallas kernels, sums(): pl.pallas_call(functools.partial(sums_kernel, first, steps), out_shape=(j...  16.5 us
    ppermute x6, starting transfers between devices, across(): return lax.ppermute(x, 'wide', [(i, i ^ apart) for i in range(4)])  10.2 us
    pallas_call x2, Pallas kernels, down(): pl.pallas_call(functools.partial(down_kernel, first, width), out_shape=ja...  6.91 us
    pallas_call x1, Pallas kernels, load(): pl.pallas_call(functools.partial(load_kernel, chunk[0], chunk[1] // 2), o...  6.18 us
    ppermute x6, waiting for transfers between devices, swap(): return lax.ppermute(x, axis, [(0, 1), (1, 0)])  5.2 us
    ppermute x6, waiting for transfers between devices, across(): return lax.ppermute(x, 'wide', [(i, i ^ apart) for i in range(4)])  4.26 us
    ppermute x6, starting transfers between devices, swap(): return lax.ppermute(x, axis, [(0, 1), (1, 0)])  3.25 us
    unnamed x18, local copies, waits for them, and re-layouts  2.43 us
  transfers between devices with their start and end apart: 12, of which 7 were waited for; matrix products, arithmetic and copies ran while one was open for 1% of the time, Pallas kernels for 33%

profile of v8, /device:TPU:0, one launch (start us, length us, event | category | flops | bytes accessed | tf_op | source)
XLA Modules:
  0.0 56.7 jit_solution(17319058165244387593)
XLA Ops:
  0.0 5.0 %collective-permute-start = (bf16[12,2048]{1,0:T(8,128)(2,1)}, bf16[12,2048]{1,0:T(8,128)(2,1)S(1)}, u32[]{:S(2)}, u32[]{:S(2)}) collective-permute-start(bf16[12,2048]{1,0:T(8,128)(2,1)} %param.4), channel_id=1, source_target_pairs={{0,12},{4,8},{8,4},{12,0},{1,13},{5,9},{9,5},{13,1},{2,14},{6,10},... | collective-permute-start | bytes 147464 | tf_op jit(solution)/shard_map/ppermute | solution.py:185
  5.1 0.6 %collective-permute-start.2 = (bf16[12,2048]{1,0:T(8,128)(2,1)}, bf16[12,2048]{1,0:T(8,128)(2,1)S(1)}, u32[]{:S(2)}, u32[]{:S(2)}) collective-permute-start(bf16[12,2048]{1,0:T(8,128)(2,1)} %param.4), channel_id=1, source_target_pairs={{0,4},{4,0},{8,12},{12,8},{1,5},{5,1},{9,13},{13,9},{2,6},{6,2},{1... | collective-permute-start | bytes 147464 | tf_op jit(solution)/shard_map/ppermute | solution.py:185
  5.7 6.2 %load.1.refs_0_ = bf16[8,2,2048,256]{3,2,1,0:T(8,128)(2,1)S(1)} custom-call(bf16[2048,6656]{1,0:T(8,128)(2,1)} %gate.5, bf16[2048,6656]{1,0:T(8,128)(2,1)} %up.5), custom_call_target="tpu_custom_call" | custom-call | bytes 16777216 | tf_op jit(solution)/shard_map/load/pallas_call | solution.py:77
  12.0 7.8 %sums.2 = (bf16[48,4096]{1,0:T(8,128)(2,1)S(1)}, f32[48,4096]{1,0:T(8,128)S(1)}) custom-call(bf16[48,2048]{1,0:T(8,128)(2,1)S(1)} %pad_maximum_fusion.tokens, bf16[2048,6656]{1,0:T(8,128)(2,1)} %gate.5, bf16[2048,6656]{1,0:T(8,128)(2,1)} %up.5, bf16[8,2,2048,256]{3,2,1,0:T(8,128)(2,1)S(1)} %load.1.refs_0_), custom_call_target="tpu_custom_call" | custom-call | flops 1610612736 | bytes 33554432 | tf_op jit(solution)/shard_map/sums/pallas_call | solution.py:136
  19.9 1.7 %collective-permute-done.3 = bf16[48,4096]{1,0:T(8,128)(2,1)S(1)} collective-permute-done((bf16[48,4096]{1,0:T(8,128)(2,1)S(1)}, bf16[48,4096]{1,0:T(8,128)(2,1)S(1)}, u32[]{:S(2)}, u32[]{:S(2)}) %collective-permute-start.3) | collective-permute-done | bytes 393248 | tf_op jit(solution)/shard_map/ppermute | solution.py:34
  21.8 1.7 %collective-permute-start.4 = (bf16[48,4096]{1,0:T(8,128)(2,1)S(1)}, bf16[48,4096]{1,0:T(8,128)(2,1)S(1)}, u32[]{:S(2)}, u32[]{:S(2)}) collective-permute-start(bf16[48,4096]{1,0:T(8,128)(2,1)S(1)} %fusion), channel_id=1, source_target_pairs={{0,2},{2,0},{1,3},{3,1},{4,6},{6,4},{5,7},{7,5},{8,10},{10,8},{9,1... | collective-permute-start | bytes 1179656 | tf_op jit(solution)/shard_map/ppermute | solution.py:34
  23.5 8.7 %sums.3 = (bf16[48,2560]{1,0:T(8,128)(2,1)S(1)}, f32[48,2560]{1,0:T(8,128)S(1)}) custom-call(bf16[48,2048]{1,0:T(8,128)(2,1)S(1)} %pad_maximum_fusion.tokens, bf16[2048,6656]{1,0:T(8,128)(2,1)} %gate.5, bf16[2048,6656]{1,0:T(8,128)(2,1)} %up.5), custom_call_target="tpu_custom_call" | custom-call | flops 1006632960 | bytes 20971520 | tf_op jit(solution)/shard_map/sums/pallas_call | solution.py:136
  32.3 0.7 %collective-permute-done.4 = bf16[48,4096]{1,0:T(8,128)(2,1)S(1)} collective-permute-done((bf16[48,4096]{1,0:T(8,128)(2,1)S(1)}, bf16[48,4096]{1,0:T(8,128)(2,1)S(1)}, u32[]{:S(2)}, u32[]{:S(2)}) %collective-permute-start.4) | collective-permute-done | bytes 393248 | tf_op jit(solution)/shard_map/ppermute | solution.py:34
  33.1 0.1 fusion.1.mine
  33.3 0.5 collective-permute-done.5
  33.8 1.3 %collective-permute-start.6 = (bf16[48,2560]{1,0:T(8,128)(2,1)S(1)}, bf16[48,2560]{1,0:T(8,128)(2,1)S(1)}, u32[]{:S(2)}, u32[]{:S(2)}) collective-permute-start(bf16[48,2560]{1,0:T(8,128)(2,1)S(1)} %fusion.2), channel_id=1, source_target_pairs={{0,2},{2,0},{1,3},{3,1},{4,6},{6,4},{5,7},{7,5},{8,10},{10,8},{9,1... | collective-permute-start | bytes 737288 | tf_op jit(solution)/shard_map/ppermute | solution.py:34
  35.2 1.1 %slice-done.5 = s8[4194304]{0:T(1024)(128)(4,1)S(1)} async-done(((s8[27262976]{0:T(1024)(128)(4,1)}), s8[4194304]{0:T(1024)(128)(4,1)S(1)}, s32[]{:S(2)}) %slice-start.5) | async-done | bytes 4194328
  36.3 0.6 %slice-done.6 = s8[2097152]{0:T(1024)(128)(4,1)S(1)} async-done(((s8[27262976]{0:T(1024)(128)(4,1)}), s8[2097152]{0:T(1024)(128)(4,1)S(1)}, s32[]{:S(2)}) %slice-start.6) | async-done | bytes 2097176
  36.9 4.0 %down.2.total = f32[48,2048]{1,0:T(8,128)S(1)} custom-call(bf16[48,2048]{1,0:T(8,128)(2,1)S(1)} %fusion.1.mine, bf16[48,2048]{1,0:T(8,128)(2,1)S(1)} %collective-permute-done.7.other, bf16[6656,2048]{1,0:T(8,128)(2,1)S(1)} %bitcast.11, f32[48,2048]{1,0:T(8,128)S(1)} %broadcast_in_dim.3.total), custom_call_target="tpu_custom_call" | custom-call | flops 805306368 | bytes 16777216 | tf_op jit(solution)/shard_map/down/pallas_call | solution.py:166
  40.9 1.0 %collective-permute-done.6 = bf16[48,2560]{1,0:T(8,128)(2,1)S(1)} collective-permute-done((bf16[48,2560]{1,0:T(8,128)(2,1)S(1)}, bf16[48,2560]{1,0:T(8,128)(2,1)S(1)}, u32[]{:S(2)}, u32[]{:S(2)}) %collective-permute-start.6) | collective-permute-done | bytes 245792 | tf_op jit(solution)/shard_map/ppermute | solution.py:34
  42.1 1.3 %collective-permute-done.8.other = bf16[48,1280]{1,0:T(8,128)(2,1)S(1)} collective-permute-done((bf16[48,1280]{1,0:T(8,128)(2,1)S(1)}, bf16[48,1280]{1,0:T(8,128)(2,1)S(1)}, u32[]{:S(2)}, u32[]{:S(2)}) %collective-permute-start.8) | collective-permute-done | bytes 122912 | tf_op jit(solution)/shard_map/ppermute | solution.py:34
  43.4 2.9 %down.3 = f32[48,2048]{1,0:T(8,128)S(1)} custom-call(bf16[48,1280]{1,0:T(8,128)(2,1)S(1)} %fusion.3.mine, bf16[48,1280]{1,0:T(8,128)(2,1)S(1)} %collective-permute-done.8.other, bf16[6656,2048]{1,0:T(8,128)(2,1)S(1)} %bitcast.11, f32[48,2048]{1,0:T(8,128)S(1)} %down.2.total), custom_call_target="tpu_custom_call" | custom-call | flops 503316480 | bytes 10485760 | tf_op jit(solution)/shard_map/down/pallas_call | solution.py:166
  46.3 0.3 reshape.21
  46.8 3.7 %collective-permute-start.9 = (bf16[24,1024]{1,0:T(8,128)(2,1)S(1)}, bf16[24,1024]{1,0:T(8,128)(2,1)S(1)}, u32[]{:S(2)}, u32[]{:S(2)}) collective-permute-start(bf16[24,1024]{1,0:T(8,128)(2,1)S(1)} %convert_element_type.56), channel_id=1, source_target_pairs={{0,12},{4,8},{8,4},{12,0},{1,13},{5,9},{9,5},{13,1},{2,14},{6,10},... | collective-permute-start | bytes 147464 | tf_op jit(solution)/shard_map/ppermute | solution.py:185
  50.5 0.1 copy.12
  50.8 0.8 %collective-permute-start.11 = (bf16[24,1024]{1,0:T(8,128)(2,1)S(1)}, bf16[24,1024]{1,0:T(8,128)(2,1)S(1)}, u32[]{:S(2)}, u32[]{:S(2)}) collective-permute-start(bf16[24,1024]{1,0:T(8,128)(2,1)S(1)} %convert_element_type.60), channel_id=1, source_target_pairs={{0,4},{4,0},{8,12},{12,8},{1,5},{5,1},{9,13},{13,9},{2,6},{6,2},{1... | collective-permute-start | bytes 147464 | tf_op jit(solution)/shard_map/ppermute | solution.py:185
  51.6 1.3 %collective-permute-done.9 = bf16[24,1024]{1,0:T(8,128)(2,1)S(1)} collective-permute-done((bf16[24,1024]{1,0:T(8,128)(2,1)S(1)}, bf16[24,1024]{1,0:T(8,128)(2,1)S(1)}, u32[]{:S(2)}, u32[]{:S(2)}) %collective-permute-start.9) | collective-permute-done | bytes 49184 | tf_op jit(solution)/shard_map/ppermute | solution.py:185
  52.9 2.9 %collective-permute-done.10 = bf16[24,1024]{1,0:T(8,128)(2,1)S(1)} collective-permute-done((bf16[24,1024]{1,0:T(8,128)(2,1)S(1)}, bf16[24,1024]{1,0:T(8,128)(2,1)S(1)}, u32[]{:S(2)}, u32[]{:S(2)}) %collective-permute-start.10) | collective-permute-done | bytes 49184 | tf_op jit(solution)/shard_map/ppermute | solution.py:185
  56.1 0.6 %copy.8 = bf16[2,8,2,1024]{3,1,2,0:T(8,128)(2,1)} copy(bf16[2,8,2,1024]{3,2,1,0:T(2,128)(2,1)S(1)} %bitcast.15) | data formatting | bytes 131072
  (48 shorter events, 1.3 us)
Async XLA Ops:
  0.0 11.9 %copy-start = (bf16[12,2048]{1,0:T(8,128)(2,1)S(1)}, bf16[12,2048]{1,0:T(8,128)(2,1)}, u32[]{:S(2)}) copy-start(bf16[12,2048]{1,0:T(8,128)(2,1)} %param.4) | copy-start | bytes 147460
  0.0 11.9 %collective-permute-start = (bf16[12,2048]{1,0:T(8,128)(2,1)}, bf16[12,2048]{1,0:T(8,128)(2,1)S(1)}, u32[]{:S(2)}, u32[]{:S(2)}) collective-permute-start(bf16[12,2048]{1,0:T(8,128)(2,1)} %param.4), channel_id=1, source_target_pairs={{0,12},{4,8},{8,4},{12,0},{1,13},{5,9},{9,5},{13,1},{2,14},{6,10},... | collective-permute-start | bytes 147464 | tf_op jit(solution)/shard_map/ppermute | solution.py:185
  5.1 6.9 %collective-permute-start.1 = (bf16[12,2048]{1,0:T(8,128)(2,1)}, bf16[12,2048]{1,0:T(8,128)(2,1)S(1)}, u32[]{:S(2)}, u32[]{:S(2)}) collective-permute-start(bf16[12,2048]{1,0:T(8,128)(2,1)} %param.4), channel_id=1, source_target_pairs={{0,8},{4,12},{8,0},{12,4},{1,9},{5,13},{9,1},{13,5},{2,10},{6,14},... | collective-permute-start | bytes 147464 | tf_op jit(solution)/shard_map/ppermute | solution.py:185
  5.1 6.9 %collective-permute-start.2 = (bf16[12,2048]{1,0:T(8,128)(2,1)}, bf16[12,2048]{1,0:T(8,128)(2,1)S(1)}, u32[]{:S(2)}, u32[]{:S(2)}) collective-permute-start(bf16[12,2048]{1,0:T(8,128)(2,1)} %param.4), channel_id=1, source_target_pairs={{0,4},{4,0},{8,12},{12,8},{1,5},{5,1},{9,13},{13,9},{2,6},{6,2},{1... | collective-permute-start | bytes 147464 | tf_op jit(solution)/shard_map/ppermute | solution.py:185
  19.8 1.8 %collective-permute-start.3 = (bf16[48,4096]{1,0:T(8,128)(2,1)S(1)}, bf16[48,4096]{1,0:T(8,128)(2,1)S(1)}, u32[]{:S(2)}, u32[]{:S(2)}) collective-permute-start(bf16[48,4096]{1,0:T(8,128)(2,1)S(1)} %get-tuple-element.15), channel_id=1, source_target_pairs={{0,1},{1,0},{2,3},{3,2},{4,5},{5,4},{6,7},{7,6},{8,9},{9,8},{10,11... | collective-permute-start | bytes 1179656 | tf_op jit(solution)/shard_map/ppermute | solution.py:34
  21.6 13.5 %slice-start = ((s8[27262976]{0:T(1024)(128)(4,1)}), s8[4194304]{0:T(1024)(128)(4,1)S(1)}, s32[]{:S(2)}) async-start(s8[27262976]{0:T(1024)(128)(4,1)} %bitcast.10), calls=%async_computation | async-start | bytes 8388608
  21.7 13.4 %slice-start.1 = ((s8[27262976]{0:T(1024)(128)(4,1)}), s8[4194304]{0:T(1024)(128)(4,1)S(1)}, s32[]{:S(2)}) async-start(s8[27262976]{0:T(1024)(128)(4,1)} %bitcast.10), calls=%async_computation.1 | async-start | bytes 8388608
  21.7 13.4 %slice-start.2 = ((s8[27262976]{0:T(1024)(128)(4,1)}), s8[4194304]{0:T(1024)(128)(4,1)S(1)}, s32[]{:S(2)}) async-start(s8[27262976]{0:T(1024)(128)(4,1)} %bitcast.10), calls=%async_computation.2 | async-start | bytes 8388608
  21.7 13.4 %slice-start.3 = ((s8[27262976]{0:T(1024)(128)(4,1)}), s8[4194304]{0:T(1024)(128)(4,1)S(1)}, s32[]{:S(2)}) async-start(s8[27262976]{0:T(1024)(128)(4,1)} %bitcast.10), calls=%async_computation.3 | async-start | bytes 8388608
  21.7 13.4 %slice-start.4 = ((s8[27262976]{0:T(1024)(128)(4,1)}), s8[4194304]{0:T(1024)(128)(4,1)S(1)}, s32[]{:S(2)}) async-start(s8[27262976]{0:T(1024)(128)(4,1)} %bitcast.10), calls=%async_computation.4 | async-start | bytes 8388608
  21.7 14.5 %slice-start.5 = ((s8[27262976]{0:T(1024)(128)(4,1)}), s8[4194304]{0:T(1024)(128)(4,1)S(1)}, s32[]{:S(2)}) async-start(s8[27262976]{0:T(1024)(128)(4,1)} %bitcast.10), calls=%async_computation.5 | async-start | bytes 8388608
  21.7 15.1 %slice-start.6 = ((s8[27262976]{0:T(1024)(128)(4,1)}), s8[2097152]{0:T(1024)(128)(4,1)S(1)}, s32[]{:S(2)}) async-start(s8[27262976]{0:T(1024)(128)(4,1)} %bitcast.10), calls=%async_computation.6 | async-start | bytes 4194304
  21.8 11.2 %collective-permute-start.4 = (bf16[48,4096]{1,0:T(8,128)(2,1)S(1)}, bf16[48,4096]{1,0:T(8,128)(2,1)S(1)}, u32[]{:S(2)}, u32[]{:S(2)}) collective-permute-start(bf16[48,4096]{1,0:T(8,128)(2,1)S(1)} %fusion), channel_id=1, source_target_pairs={{0,2},{2,0},{1,3},{3,1},{4,6},{6,4},{5,7},{7,5},{8,10},{10,8},{9,1... | collective-permute-start | bytes 1179656 | tf_op jit(solution)/shard_map/ppermute | solution.py:34
  32.2 1.6 %collective-permute-start.5 = (bf16[48,2560]{1,0:T(8,128)(2,1)S(1)}, bf16[48,2560]{1,0:T(8,128)(2,1)S(1)}, u32[]{:S(2)}, u32[]{:S(2)}) collective-permute-start(bf16[48,2560]{1,0:T(8,128)(2,1)S(1)} %get-tuple-element.19), channel_id=1, source_target_pairs={{0,1},{1,0},{2,3},{3,2},{4,5},{5,4},{6,7},{7,6},{8,9},{9,8},{10,11... | collective-permute-start | bytes 737288 | tf_op jit(solution)/shard_map/ppermute | solution.py:34
  33.2 1.9 %collective-permute-start.7 = (bf16[48,2048]{1,0:T(8,128)(2,1)S(1)}, bf16[48,2048]{1,0:T(8,128)(2,1)S(1)}, u32[]{:S(2)}, u32[]{:S(2)}) collective-permute-start(bf16[48,2048]{1,0:T(8,128)(2,1)S(1)} %fusion.1.mine), channel_id=1, source_target_pairs={{0,1},{1,0},{2,3},{3,2},{4,5},{5,4},{6,7},{7,6},{8,9},{9,8},{10,11... | collective-permute-start | bytes 589832 | tf_op jit(solution)/shard_map/ppermute | solution.py:34
  33.8 8.1 %collective-permute-start.6 = (bf16[48,2560]{1,0:T(8,128)(2,1)S(1)}, bf16[48,2560]{1,0:T(8,128)(2,1)S(1)}, u32[]{:S(2)}, u32[]{:S(2)}) collective-permute-start(bf16[48,2560]{1,0:T(8,128)(2,1)S(1)} %fusion.2), channel_id=1, source_target_pairs={{0,2},{2,0},{1,3},{3,1},{4,6},{6,4},{5,7},{7,5},{8,10},{10,8},{9,1... | collective-permute-start | bytes 737288 | tf_op jit(solution)/shard_map/ppermute | solution.py:34
  42.0 1.4 %collective-permute-start.8 = (bf16[48,1280]{1,0:T(8,128)(2,1)S(1)}, bf16[48,1280]{1,0:T(8,128)(2,1)S(1)}, u32[]{:S(2)}, u32[]{:S(2)}) collective-permute-start(bf16[48,1280]{1,0:T(8,128)(2,1)S(1)} %fusion.3.mine), channel_id=1, source_target_pairs={{0,1},{1,0},{2,3},{3,2},{4,5},{5,4},{6,7},{7,6},{8,9},{9,8},{10,11... | collective-permute-start | bytes 368648 | tf_op jit(solution)/shard_map/ppermute | solution.py:34
  46.8 6.1 %collective-permute-start.9 = (bf16[24,1024]{1,0:T(8,128)(2,1)S(1)}, bf16[24,1024]{1,0:T(8,128)(2,1)S(1)}, u32[]{:S(2)}, u32[]{:S(2)}) collective-permute-start(bf16[24,1024]{1,0:T(8,128)(2,1)S(1)} %convert_element_type.56), channel_id=1, source_target_pairs={{0,12},{4,8},{8,4},{12,0},{1,13},{5,9},{9,5},{13,1},{2,14},{6,10},... | collective-permute-start | bytes 147464 | tf_op jit(solution)/shard_map/ppermute | solution.py:185
  50.7 5.1 %collective-permute-start.10 = (bf16[24,1024]{1,0:T(8,128)(2,1)S(1)}, bf16[24,1024]{1,0:T(8,128)(2,1)S(1)}, u32[]{:S(2)}, u32[]{:S(2)}) collective-permute-start(bf16[24,1024]{1,0:T(8,128)(2,1)S(1)} %convert_element_type.58), channel_id=1, source_target_pairs={{0,8},{4,12},{8,0},{12,4},{1,9},{5,13},{9,1},{13,5},{2,10},{6,14},... | collective-permute-start | bytes 147464 | tf_op jit(solution)/shard_map/ppermute | solution.py:185
  50.8 5.1 %collective-permute-start.11 = (bf16[24,1024]{1,0:T(8,128)(2,1)S(1)}, bf16[24,1024]{1,0:T(8,128)(2,1)S(1)}, u32[]{:S(2)}, u32[]{:S(2)}) collective-permute-start(bf16[24,1024]{1,0:T(8,128)(2,1)S(1)} %convert_element_type.60), channel_id=1, source_target_pairs={{0,4},{4,0},{8,12},{12,8},{1,5},{5,1},{9,13},{13,9},{2,6},{6,2},{1... | collective-permute-start | bytes 147464 | tf_op jit(solution)/shard_map/ppermute | solution.py:185

commit v9 on v8

--- a/solution.py
+++ b/solution.py
@@ -56,15 +56,20 @@
     unit = first + side * half + (step - mine * (half // BLOCK)) * BLOCK
     columns = pl.ds(pl.multiple_of(unit, BLOCK), BLOCK)
     return [
-        pltpu.make_async_copy(weight.at[:, columns], dst.at[i], sem.at[i]) for i, weight in enumerate((gate, up))
+        pltpu.make_async_copy(weight.at[:, columns], dst.at[:, pl.ds(i * BLOCK, BLOCK)], sem.at[i])
+        for i, weight in enumerate((gate, up))
     ]
+
+
+def pair(ref, at):
+    return ref.at[:, pl.ds(pl.multiple_of(at * 2 * BLOCK, 2 * BLOCK), 2 * BLOCK)]
 
 
 def load_kernel(first, half, gate, up, held, sems):
     copies = [
         copy
-        for step in range(held.shape[0])
-        for copy in block_copies(first, half, step, gate, up, held.at[step], sems.at[step])
+        for step in range(sems.shape[0])
+        for copy in block_copies(first, half, step, gate, up, pair(held, step), sems.at[step])
     ]
     for copy in copies:
         copy.start()
@@ -76,7 +81,7 @@
     depth = gate.shape[0]
     return pl.pallas_call(
         functools.partial(load_kernel, chunk[0], chunk[1] // 2),
-        out_shape=pltpu.VMEM((steps, 2, depth, BLOCK), BF16),
+        out_shape=pltpu.VMEM((depth, steps * 2 * BLOCK), BF16),
         in_specs=[HBM, HBM],
         out_specs=VMEM,
         scratch_shapes=[pltpu.SemaphoreType.DMA((steps, 2))],
@@ -96,18 +101,17 @@
 
     def copies(step):
         at = step - steps
-        return block_copies(first, half, step, gate, up, streamed.at[at], sems.at[at])
+        return block_copies(first, half, step, gate, up, pair(streamed, at), sems.at[at])
 
     for step in range(steps, 2 * blocks):
         for copy in copies(step):
             copy.start()
 
     def add(out, start, source, block):
+        both = jnp.dot(tokens[...], source[...], preferred_element_type=F32).astype(out.dtype)
         for i in range(2):
             column = pl.multiple_of((i * blocks + block - start) * BLOCK, BLOCK)
-            out[:, pl.ds(column, BLOCK)] = jnp.dot(tokens[...], source[i], preferred_element_type=F32).astype(
-                out.dtype
-            )
+            out[:, pl.ds(column, BLOCK)] = both[:, i * BLOCK : (i + 1) * BLOCK]
 
     for side, out in enumerate((send, keep)):
         start, end = side * blocks, (side + 1) * blocks
@@ -117,7 +121,7 @@
 
             @pl.loop(start, middle)
             def _(step):
-                add(out, start, held.at[step], step)
+                add(out, start, pair(held, step), step)
 
         if middle < end:
 
@@ -125,21 +129,24 @@
             def _(step):
                 for copy in copies(step):
                     copy.wait()
-                add(out, start, streamed.at[step - steps], step)
+                add(out, start, pair(streamed, step - steps), step)
 
 
 def sums(tokens, gate, up, chunk, held=None):
     rows, depth = tokens.shape
     first, width = chunk
-    steps = 0 if held is None else held.shape[0]
-    shape = (width // BLOCK - steps, 2, depth, BLOCK)
+    steps = 0 if held is None else held.shape[1] // (2 * BLOCK)
+    streamed = width // BLOCK - steps
     return pl.pallas_call(
         functools.partial(sums_kernel, first, steps),
         out_shape=(jax.ShapeDtypeStruct((rows, width), BF16), jax.ShapeDtypeStruct((rows, width), F32)),
         in_specs=[VMEM, HBM, HBM] + [VMEM] * (steps > 0),
         out_specs=(VMEM, VMEM),
-        scratch_shapes=[pltpu.VMEM(shape, BF16), pltpu.SemaphoreType.DMA(shape[:2])],
-        compiler_params=pltpu.CompilerParams(vmem_limit_bytes=4 * shape[0] * depth * BLOCK + 4 * 2**20),
+        scratch_shapes=[
+            pltpu.VMEM((depth, streamed * 2 * BLOCK), BF16),
+            pltpu.SemaphoreType.DMA((streamed, 2)),
+        ],
+        compiler_params=pltpu.CompilerParams(vmem_limit_bytes=4 * streamed * depth * BLOCK + 4 * 2**20),
         cost_estimate=pl.CostEstimate(
             flops=4 * rows * depth * width, bytes_accessed=4 * depth * width, transcendentals=0
         ),
@@ -147,33 +154,67 @@
     )(tokens, left_in_hbm(gate), left_in_hbm(up), *([held_in(held)] if steps else []))
 
 
-def down_kernel(first, width, mine, other, weight, total, out):
+def partial_sums(first, half, sides, hiddens, weight, columns):
     core = lax.axis_index("sub")
-    half = width // 2
-    starts = [pl.multiple_of(first + side * half, BLOCK) for side in (core, 1 - core)]
-
-    @pl.loop(0, out.shape[1] // BLOCK)
+    part = 0.0
+    for side, hidden in zip(sides, hiddens):
+        start = pl.multiple_of(first + jnp.where(core == side, 0, half), BLOCK)
+        part += jnp.dot(hidden[...], weight[pl.ds(start, half), columns], preferred_element_type=F32)
+    return part
+
+
+def down_kernel(first, half, sides, weight, *refs):
+    hiddens, out = refs[: len(sides)], refs[-1]
+    totals = refs[len(sides) : -1]
+    wide = 2 * BLOCK
+
+    @pl.loop(0, out.shape[1] // wide)
     def _(block):
-        columns = pl.ds(pl.multiple_of(block * BLOCK, BLOCK), BLOCK)
-        part = total[:, columns]
-        for start, hidden in zip(starts, (mine, other)):
-            part += jnp.dot(hidden[...], weight[pl.ds(start, half), columns], preferred_element_type=F32)
+        columns = pl.ds(pl.multiple_of(block * wide, wide), wide)
+        part = partial_sums(first, half, sides, hiddens, weight, columns)
+        for total in totals:
+            part += total[:, columns]
         out[:, columns] = part
 
 
-def down(mine, other, weight, total, first, width):
-    rows, features = total.shape
+def last_down_kernel(first, half, sides, weight, hidden, total, own, *sends):
+    rows, columns = own.shape[0] // 2, own.shape[1]
+    wide = 2 * BLOCK
+    for block in range(columns // wide):
+        at = block * wide
+        parts = []
+        for start in (at, columns + at):
+            part = partial_sums(first, half, sides, [hidden], weight, pl.ds(start, wide))
+            parts.append(part + total[:, pl.ds(start, wide)])
+        for place, out in enumerate((own, *sends)):
+            pieces = [part[place * rows : (place + 1) * rows] for part in parts]
+            out[:, pl.ds(at, wide)] = jnp.concatenate(pieces, axis=0).astype(out.dtype)
+
+
+def down(weight, chunk, sides, hiddens, total=None, last=False):
+    rows, half = hiddens[0].shape
+    features = weight.shape[1]
+    if last:
+        packed = (rows // 2, features // 2)
+        out_shape = (jax.ShapeDtypeStruct(packed, F32),) + (jax.ShapeDtypeStruct(packed, BF16),) * 3
+        kernel = last_down_kernel
+    else:
+        out_shape = jax.ShapeDtypeStruct((rows, features), F32)
+        kernel = down_kernel
+    operands = [held_in(weight), *hiddens] + ([] if total is None else [total])
     return pl.pallas_call(
-        functools.partial(down_kernel, first, width),
-        out_shape=jax.ShapeDtypeStruct(total.shape, F32),
-        in_specs=[VMEM] * 4,
-        out_specs=VMEM,
+        functools.partial(kernel, chunk[0], half, sides),
+        out_shape=out_shape,
+        in_specs=[VMEM] * len(operands),
+        out_specs=(VMEM,) * 4 if last else VMEM,
         compiler_params=GRANT,
         cost_estimate=pl.CostEstimate(
-            flops=2 * rows * features * width, bytes_accessed=2 * features * width, transcendentals=0
+            flops=2 * rows * features * half * len(sides),
+            bytes_accessed=2 * features * half * len(sides),
+            transcendentals=0,
         ),
         name="down",
-    )(mine, other, held_in(weight), total)
+    )(*operands)
 
 
 def split(units):
@@ -191,7 +232,7 @@
     section = tokens
     for apart in (3, 2, 1):
         section = lax.optimization_barrier(jnp.concatenate([section, across(tokens, apart)], axis=0))
-    held = load(gate_weight, up_weight, chunks[0], 8)
+    held = load(gate_weight, up_weight, chunks[0], 5)
 
     def core_sums(send, keep):
         total = keep + swap(send, "sub").astype(F32)
@@ -200,10 +241,6 @@
     def hidden_half(total, received):
         return activate(*jnp.split(total + received.astype(F32), 2, axis=1))
 
-    def add(mixed, mine, chunk):
-        return down(mine, swap(mine, "sub"), down_weight, mixed, *chunk)
-
-    mixed = jnp.zeros((4 * rows, down_weight.shape[1]), F32)
     send, keep = sums(section, gate_weight, up_weight, chunks[0], held)
     total, sent = core_sums(send, keep)
     later, _ = lax.optimization_barrier((section, sent))
@@ -211,14 +248,13 @@
     received, keep = lax.optimization_barrier((swap(sent, "narrow"), keep))
     mine = hidden_half(total, received)
     total, sent = core_sums(send, keep)
-    mixed = add(mixed, mine, chunks[0])
+    mixed = down(down_weight, chunks[0], (0, 1), (mine, swap(mine, "sub")))
     received, mixed = lax.optimization_barrier((swap(sent, "narrow"), mixed))
-    mixed = add(mixed, hidden_half(total, received), chunks[1])
-    blocks = mixed.reshape(4, rows, 2, -1).swapaxes(1, 2).reshape(4, 2 * rows, -1)
-    out = blocks[0]
-    for place, apart in enumerate((3, 2, 1), 1):
-        received = across(blocks[place].astype(BF16), apart)
-        out = lax.optimization_barrier(out + received.astype(F32))
+    mine = hidden_half(total, received)
+    mixed = down(down_weight, chunks[1], (0,), (mine,), mixed)
+    out, *blocks = down(down_weight, chunks[1], (1,), (swap(mine, "sub"),), mixed, last=True)
+    for block, apart in zip(blocks, (3, 2, 1)):
+        out = lax.optimization_barrier(out + across(block, apart).astype(F32))
     return out.astype(BF16).reshape(2, rows, -1).swapaxes(0, 1).reshape(rows, -1)
 
 

time: 56.9 us -> 53.6 us (0.942)
  Pallas kernels: 29.6 us -> 27.3 us
    pallas_call x1, Pallas kernels: 6.18 us -> 4.23 us  [load(): pl.pallas_call(functools.partial(load_kernel, chunk[0], chunk[1] // 2), o...]
    pallas_call x2 -> x3, Pallas kernels: 6.91 us -> 5.77 us  [down(): pl.pallas_call(functools.partial(kernel, chunk[0], half, sides), out_shap...]
    pallas_call x2, Pallas kernels: 16.5 us -> 17.3 us  [sums(): pl.pallas_call(functools.partial(sums_kernel, first, steps), out_shape=(j...]
    ppermute x6, waiting for transfers between devices: 5.2 us -> 4.46 us  [swap(): return lax.ppermute(x, axis, [(0, 1), (1, 0)])]
    reshape x3 -> x0, local copies, waits for them, and re-layouts: 0.57 us -> none  [chunked(): mixed.reshape(4, rows, 2, -1).swapaxes(1, 2).reshape(4, 2 * rows, -1)]
where the time goes in v9:
time: 53.6 us; the launch traced here: 53.4 us
  Pallas kernels  27.3 us (51%)
  starting transfers between devices  13.2 us (25%)
  waiting for transfers between devices  9.27 us (17%)
  local copies, waits for them, and re-layouts  2.66 us (5%)
  other arithmetic  0.64 us (1%)
    pallas_call x2, Pallas kernels, sums(): pl.pallas_call(functools.partial(sums_kernel, first, steps), out_shape=(j...  17.3 us
    ppermute x6, starting transfers between devices, across(): return lax.ppermute(x, 'wide', [(i, i ^ apart) for i in range(4)])  10.1 us
    pallas_call x3, Pallas kernels, down(): pl.pallas_call(functools.partial(kernel, chunk[0], half, sides), out_shap...  5.77 us
    ppermute x6, waiting for transfers between devices, across(): return lax.ppermute(x, 'wide', [(i, i ^ apart) for i in range(4)])  4.81 us
    ppermute x6, waiting for transfers between devices, swap(): return lax.ppermute(x, axis, [(0, 1), (1, 0)])  4.46 us
    pallas_call x1, Pallas kernels, load(): pl.pallas_call(functools.partial(load_kernel, chunk[0], chunk[1] // 2), o...  4.23 us
    ppermute x6, starting transfers between devices, swap(): return lax.ppermute(x, axis, [(0, 1), (1, 0)])  3.12 us
    unnamed x18, local copies, waits for them, and re-layouts  2.59 us
  transfers between devices with their start and end apart: 12, of which 7 were waited for; matrix products, arithmetic and copies ran while one was open for 1% of the time, Pallas kernels for 33%

profile of v9, /device:TPU:0, one launch (start us, length us, event | category | flops | bytes accessed | tf_op | source)
XLA Modules:
  0.0 53.4 jit_solution(13857989312817782782)
XLA Ops:
  0.0 5.0 %collective-permute-start = (bf16[12,2048]{1,0:T(8,128)(2,1)}, bf16[12,2048]{1,0:T(8,128)(2,1)S(1)}, u32[]{:S(2)}, u32[]{:S(2)}) collective-permute-start(bf16[12,2048]{1,0:T(8,128)(2,1)} %param.4), channel_id=1, source_target_pairs={{0,12},{4,8},{8,4},{12,0},{1,13},{5,9},{9,5},{13,1},{2,14},{6,10},... | collective-permute-start | bytes 147464 | tf_op jit(solution)/shard_map/ppermute | solution.py:226
  5.1 0.6 %collective-permute-start.1 = (bf16[12,2048]{1,0:T(8,128)(2,1)}, bf16[12,2048]{1,0:T(8,128)(2,1)S(1)}, u32[]{:S(2)}, u32[]{:S(2)}) collective-permute-start(bf16[12,2048]{1,0:T(8,128)(2,1)} %param.4), channel_id=1, source_target_pairs={{0,8},{4,12},{8,0},{12,4},{1,9},{5,13},{9,1},{13,5},{2,10},{6,14},... | collective-permute-start | bytes 147464 | tf_op jit(solution)/shard_map/ppermute | solution.py:226
  5.7 4.2 %load.1.refs_0_ = bf16[2048,2560]{1,0:T(8,128)(2,1)S(1)} custom-call(bf16[2048,6656]{1,0:T(8,128)(2,1)} %gate.5, bf16[2048,6656]{1,0:T(8,128)(2,1)} %up.5), custom_call_target="tpu_custom_call" | custom-call | bytes 10485760 | tf_op jit(solution)/shard_map/load/pallas_call | solution.py:82
  10.0 0.9 %collective-permute-done.1 = bf16[12,2048]{1,0:T(8,128)(2,1)S(1)} collective-permute-done((bf16[12,2048]{1,0:T(8,128)(2,1)}, bf16[12,2048]{1,0:T(8,128)(2,1)S(1)}, u32[]{:S(2)}, u32[]{:S(2)}) %collective-permute-start.1) | collective-permute-done | bytes 49184 | tf_op jit(solution)/shard_map/ppermute | solution.py:226
  11.0 8.6 %sums.2 = (bf16[48,4096]{1,0:T(8,128)(2,1)S(1)}, f32[48,4096]{1,0:T(8,128)S(1)}) custom-call(bf16[48,2048]{1,0:T(8,128)(2,1)S(1)} %pad_maximum_fusion.tokens, bf16[2048,6656]{1,0:T(8,128)(2,1)} %gate.5, bf16[2048,6656]{1,0:T(8,128)(2,1)} %up.5, bf16[2048,2560]{1,0:T(8,128)(2,1)S(1)} %load.1.refs_0_), custom_call_target="tpu_custom_call" | custom-call | flops 1610612736 | bytes 33554432 | tf_op jit(solution)/shard_map/sums/pallas_call | solution.py:140
  19.7 1.7 %collective-permute-done.3 = bf16[48,4096]{1,0:T(8,128)(2,1)S(1)} collective-permute-done((bf16[48,4096]{1,0:T(8,128)(2,1)S(1)}, bf16[48,4096]{1,0:T(8,128)(2,1)S(1)}, u32[]{:S(2)}, u32[]{:S(2)}) %collective-permute-start.3) | collective-permute-done | bytes 393248 | tf_op jit(solution)/shard_map/ppermute | solution.py:34
  21.5 1.6 %collective-permute-start.4 = (bf16[48,4096]{1,0:T(8,128)(2,1)S(1)}, bf16[48,4096]{1,0:T(8,128)(2,1)S(1)}, u32[]{:S(2)}, u32[]{:S(2)}) collective-permute-start(bf16[48,4096]{1,0:T(8,128)(2,1)S(1)} %fusion), channel_id=1, source_target_pairs={{0,2},{2,0},{1,3},{3,1},{4,6},{6,4},{5,7},{7,5},{8,10},{10,8},{9,1... | collective-permute-start | bytes 1179656 | tf_op jit(solution)/shard_map/ppermute | solution.py:34
  23.1 8.7 %sums.3 = (bf16[48,2560]{1,0:T(8,128)(2,1)S(1)}, f32[48,2560]{1,0:T(8,128)S(1)}) custom-call(bf16[48,2048]{1,0:T(8,128)(2,1)S(1)} %pad_maximum_fusion.tokens, bf16[2048,6656]{1,0:T(8,128)(2,1)} %gate.5, bf16[2048,6656]{1,0:T(8,128)(2,1)} %up.5), custom_call_target="tpu_custom_call" | custom-call | flops 1006632960 | bytes 20971520 | tf_op jit(solution)/shard_map/sums/pallas_call | solution.py:140
  31.9 0.9 %collective-permute-done.4 = bf16[48,4096]{1,0:T(8,128)(2,1)S(1)} collective-permute-done((bf16[48,4096]{1,0:T(8,128)(2,1)S(1)}, bf16[48,4096]{1,0:T(8,128)(2,1)S(1)}, u32[]{:S(2)}, u32[]{:S(2)}) %collective-permute-start.4) | collective-permute-done | bytes 393248 | tf_op jit(solution)/shard_map/ppermute | solution.py:34
  32.8 0.1 convert_add_fusion
  33.1 0.3 collective-permute-done.5
  33.4 1.3 %collective-permute-start.6 = (bf16[48,2560]{1,0:T(8,128)(2,1)S(1)}, bf16[48,2560]{1,0:T(8,128)(2,1)S(1)}, u32[]{:S(2)}, u32[]{:S(2)}) collective-permute-start(bf16[48,2560]{1,0:T(8,128)(2,1)S(1)} %fusion.2), channel_id=1, source_target_pairs={{0,2},{2,0},{1,3},{3,1},{4,6},{6,4},{5,7},{7,5},{8,10},{10,8},{9,1... | collective-permute-start | bytes 737288 | tf_op jit(solution)/shard_map/ppermute | solution.py:34
  34.8 1.2 %slice-done.5 = s8[4194304]{0:T(1024)(128)(4,1)S(1)} async-done(((s8[27262976]{0:T(1024)(128)(4,1)}), s8[4194304]{0:T(1024)(128)(4,1)S(1)}, s32[]{:S(2)}) %slice-start.5) | async-done | bytes 4194328
  36.0 0.6 %slice-done.6 = s8[2097152]{0:T(1024)(128)(4,1)S(1)} async-done(((s8[27262976]{0:T(1024)(128)(4,1)}), s8[2097152]{0:T(1024)(128)(4,1)S(1)}, s32[]{:S(2)}) %slice-start.6) | async-done | bytes 2097176
  36.6 3.4 %down.3.refs_1_ = f32[48,2048]{1,0:T(8,128)S(1)} custom-call(bf16[6656,2048]{1,0:T(8,128)(2,1)S(1)} %bitcast.5, bf16[48,2048]{1,0:T(8,128)(2,1)S(1)} %fusion.1.refs_0_, bf16[48,2048]{1,0:T(8,128)(2,1)S(1)} %collective-permute-done.7.refs_1_), custom_call_target="tpu_custom_call" | custom-call | flops 805306368 | bytes 16777216 | tf_op jit(solution)/shard_map/down/pallas_call | solution.py:205
  40.0 1.6 %collective-permute-done.6 = bf16[48,2560]{1,0:T(8,128)(2,1)S(1)} collective-permute-done((bf16[48,2560]{1,0:T(8,128)(2,1)S(1)}, bf16[48,2560]{1,0:T(8,128)(2,1)S(1)}, u32[]{:S(2)}, u32[]{:S(2)}) %collective-permute-start.6) | collective-permute-done | bytes 245792 | tf_op jit(solution)/shard_map/ppermute | solution.py:34
  41.8 1.4 %down.4.total = f32[48,2048]{1,0:T(8,128)S(1)} custom-call(bf16[6656,2048]{1,0:T(8,128)(2,1)S(1)} %bitcast.5, bf16[48,1280]{1,0:T(8,128)(2,1)S(1)} %fusion.3.refs_0_, f32[48,2048]{1,0:T(8,128)S(1)} %down.3.refs_1_), custom_call_target="tpu_custom_call" | custom-call | flops 251658240 | bytes 5242880 | tf_op jit(solution)/shard_map/down/pallas_call | solution.py:205
  43.2 1.0 %down.5 = (f32[24,1024]{1,0:T(8,128)S(1)}, bf16[24,1024]{1,0:T(8,128)(2,1)S(1)}, bf16[24,1024]{1,0:T(8,128)(2,1)S(1)}, bf16[24,1024]{1,0:T(8,128)(2,1)S(1)}) custom-call(bf16[6656,2048]{1,0:T(8,128)(2,1)S(1)} %bitcast.5, bf16[48,1280]{1,0:T(8,128)(2,1)S(1)} %collective-permute-done.8.hidden, f32[48,2048]{1,0:T(8,128)S(1)} %down.4.total), custom_call_target="tpu_custom_call" | custom-call | flops 251658240 | bytes 5242880 | tf_op jit(solution)/shard_map/down/pallas_call | solution.py:205
  44.2 2.9 %collective-permute-start.9 = (bf16[24,1024]{1,0:T(8,128)(2,1)S(1)}, bf16[24,1024]{1,0:T(8,128)(2,1)S(1)}, u32[]{:S(2)}, u32[]{:S(2)}) collective-permute-start(bf16[24,1024]{1,0:T(8,128)(2,1)S(1)} %get-tuple-element.28), channel_id=1, source_target_pairs={{0,12},{4,8},{8,4},{12,0},{1,13},{5,9},{9,5},{13,1},{2,14},{6,10},... | collective-permute-start | bytes 147464 | tf_op jit(solution)/shard_map/ppermute | solution.py:226
  47.2 0.2 collective-permute-start.10
  47.3 1.4 %collective-permute-start.11 = (bf16[24,1024]{1,0:T(8,128)(2,1)S(1)}, bf16[24,1024]{1,0:T(8,128)(2,1)S(1)}, u32[]{:S(2)}, u32[]{:S(2)}) collective-permute-start(bf16[24,1024]{1,0:T(8,128)(2,1)S(1)} %get-tuple-element.30), channel_id=1, source_target_pairs={{0,4},{4,0},{8,12},{12,8},{1,5},{5,1},{9,13},{13,9},{2,6},{6,2},{1... | collective-permute-start | bytes 147464 | tf_op jit(solution)/shard_map/ppermute | solution.py:226
  48.7 1.9 %collective-permute-done.9 = bf16[24,1024]{1,0:T(8,128)(2,1)S(1)} collective-permute-done((bf16[24,1024]{1,0:T(8,128)(2,1)S(1)}, bf16[24,1024]{1,0:T(8,128)(2,1)S(1)}, u32[]{:S(2)}, u32[]{:S(2)}) %collective-permute-start.9) | collective-permute-done | bytes 49184 | tf_op jit(solution)/shard_map/ppermute | solution.py:226
  50.6 2.0 %collective-permute-done.10 = bf16[24,1024]{1,0:T(8,128)(2,1)S(1)} collective-permute-done((bf16[24,1024]{1,0:T(8,128)(2,1)S(1)}, bf16[24,1024]{1,0:T(8,128)(2,1)S(1)}, u32[]{:S(2)}, u32[]{:S(2)}) %collective-permute-start.10) | collective-permute-done | bytes 49184 | tf_op jit(solution)/shard_map/ppermute | solution.py:226
  52.8 0.6 %copy.7 = bf16[2,8,2,1024]{3,1,2,0:T(8,128)(2,1)} copy(bf16[2,8,2,1024]{3,2,1,0:T(2,128)(2,1)S(1)} %bitcast.7) | data formatting | bytes 131072
  (39 shorter events, 1.0 us)
Async XLA Ops:
  0.0 9.9 %copy-start = (bf16[12,2048]{1,0:T(8,128)(2,1)S(1)}, bf16[12,2048]{1,0:T(8,128)(2,1)}, u32[]{:S(2)}) copy-start(bf16[12,2048]{1,0:T(8,128)(2,1)} %param.4) | copy-start | bytes 147460
  0.0 9.9 %collective-permute-start = (bf16[12,2048]{1,0:T(8,128)(2,1)}, bf16[12,2048]{1,0:T(8,128)(2,1)S(1)}, u32[]{:S(2)}, u32[]{:S(2)}) collective-permute-start(bf16[12,2048]{1,0:T(8,128)(2,1)} %param.4), channel_id=1, source_target_pairs={{0,12},{4,8},{8,4},{12,0},{1,13},{5,9},{9,5},{13,1},{2,14},{6,10},... | collective-permute-start | bytes 147464 | tf_op jit(solution)/shard_map/ppermute | solution.py:226
  5.1 5.9 %collective-permute-start.2 = (bf16[12,2048]{1,0:T(8,128)(2,1)}, bf16[12,2048]{1,0:T(8,128)(2,1)S(1)}, u32[]{:S(2)}, u32[]{:S(2)}) collective-permute-start(bf16[12,2048]{1,0:T(8,128)(2,1)} %param.4), channel_id=1, source_target_pairs={{0,4},{4,0},{8,12},{12,8},{1,5},{5,1},{9,13},{13,9},{2,6},{6,2},{1... | collective-permute-start | bytes 147464 | tf_op jit(solution)/shard_map/ppermute | solution.py:226
  5.1 5.8 %collective-permute-start.1 = (bf16[12,2048]{1,0:T(8,128)(2,1)}, bf16[12,2048]{1,0:T(8,128)(2,1)S(1)}, u32[]{:S(2)}, u32[]{:S(2)}) collective-permute-start(bf16[12,2048]{1,0:T(8,128)(2,1)} %param.4), channel_id=1, source_target_pairs={{0,8},{4,12},{8,0},{12,4},{1,9},{5,13},{9,1},{13,5},{2,10},{6,14},... | collective-permute-start | bytes 147464 | tf_op jit(solution)/shard_map/ppermute | solution.py:226
  19.6 1.8 %collective-permute-start.3 = (bf16[48,4096]{1,0:T(8,128)(2,1)S(1)}, bf16[48,4096]{1,0:T(8,128)(2,1)S(1)}, u32[]{:S(2)}, u32[]{:S(2)}) collective-permute-start(bf16[48,4096]{1,0:T(8,128)(2,1)S(1)} %get-tuple-element.19), channel_id=1, source_target_pairs={{0,1},{1,0},{2,3},{3,2},{4,5},{5,4},{6,7},{7,6},{8,9},{9,8},{10,11... | collective-permute-start | bytes 1179656 | tf_op jit(solution)/shard_map/ppermute | solution.py:34
  21.4 13.4 %slice-start = ((s8[27262976]{0:T(1024)(128)(4,1)}), s8[4194304]{0:T(1024)(128)(4,1)S(1)}, s32[]{:S(2)}) async-start(s8[27262976]{0:T(1024)(128)(4,1)} %bitcast.4), calls=%async_computation | async-start | bytes 8388608
  21.5 13.3 %slice-start.1 = ((s8[27262976]{0:T(1024)(128)(4,1)}), s8[4194304]{0:T(1024)(128)(4,1)S(1)}, s32[]{:S(2)}) async-start(s8[27262976]{0:T(1024)(128)(4,1)} %bitcast.4), calls=%async_computation.1 | async-start | bytes 8388608
  21.5 13.3 %slice-start.2 = ((s8[27262976]{0:T(1024)(128)(4,1)}), s8[4194304]{0:T(1024)(128)(4,1)S(1)}, s32[]{:S(2)}) async-start(s8[27262976]{0:T(1024)(128)(4,1)} %bitcast.4), calls=%async_computation.2 | async-start | bytes 8388608
  21.5 13.2 %slice-start.3 = ((s8[27262976]{0:T(1024)(128)(4,1)}), s8[4194304]{0:T(1024)(128)(4,1)S(1)}, s32[]{:S(2)}) async-start(s8[27262976]{0:T(1024)(128)(4,1)} %bitcast.4), calls=%async_computation.3 | async-start | bytes 8388608
  21.5 13.3 %slice-start.4 = ((s8[27262976]{0:T(1024)(128)(4,1)}), s8[4194304]{0:T(1024)(128)(4,1)S(1)}, s32[]{:S(2)}) async-start(s8[27262976]{0:T(1024)(128)(4,1)} %bitcast.4), calls=%async_computation.4 | async-start | bytes 8388608
  21.5 14.5 %slice-start.5 = ((s8[27262976]{0:T(1024)(128)(4,1)}), s8[4194304]{0:T(1024)(128)(4,1)S(1)}, s32[]{:S(2)}) async-start(s8[27262976]{0:T(1024)(128)(4,1)} %bitcast.4), calls=%async_computation.5 | async-start | bytes 8388608
  21.5 15.1 %slice-start.6 = ((s8[27262976]{0:T(1024)(128)(4,1)}), s8[2097152]{0:T(1024)(128)(4,1)S(1)}, s32[]{:S(2)}) async-start(s8[27262976]{0:T(1024)(128)(4,1)} %bitcast.4), calls=%async_computation.6 | async-start | bytes 4194304
  21.5 11.2 %collective-permute-start.4 = (bf16[48,4096]{1,0:T(8,128)(2,1)S(1)}, bf16[48,4096]{1,0:T(8,128)(2,1)S(1)}, u32[]{:S(2)}, u32[]{:S(2)}) collective-permute-start(bf16[48,4096]{1,0:T(8,128)(2,1)S(1)} %fusion), channel_id=1, source_target_pairs={{0,2},{2,0},{1,3},{3,1},{4,6},{6,4},{5,7},{7,5},{8,10},{10,8},{9,1... | collective-permute-start | bytes 1179656 | tf_op jit(solution)/shard_map/ppermute | solution.py:34
  31.8 1.6 %collective-permute-start.5 = (bf16[48,2560]{1,0:T(8,128)(2,1)S(1)}, bf16[48,2560]{1,0:T(8,128)(2,1)S(1)}, u32[]{:S(2)}, u32[]{:S(2)}) collective-permute-start(bf16[48,2560]{1,0:T(8,128)(2,1)S(1)} %get-tuple-element.23), channel_id=1, source_target_pairs={{0,1},{1,0},{2,3},{3,2},{4,5},{5,4},{6,7},{7,6},{8,9},{9,8},{10,11... | collective-permute-start | bytes 737288 | tf_op jit(solution)/shard_map/ppermute | solution.py:34
  33.0 1.7 %collective-permute-start.7 = (bf16[48,2048]{1,0:T(8,128)(2,1)S(1)}, bf16[48,2048]{1,0:T(8,128)(2,1)S(1)}, u32[]{:S(2)}, u32[]{:S(2)}) collective-permute-start(bf16[48,2048]{1,0:T(8,128)(2,1)S(1)} %fusion.1.refs_0_), channel_id=1, source_target_pairs={{0,1},{1,0},{2,3},{3,2},{4,5},{5,4},{6,7},{7,6},{8,9},{9,8},{10,11... | collective-permute-start | bytes 589832 | tf_op jit(solution)/shard_map/ppermute | solution.py:34
  33.4 8.1 %collective-permute-start.6 = (bf16[48,2560]{1,0:T(8,128)(2,1)S(1)}, bf16[48,2560]{1,0:T(8,128)(2,1)S(1)}, u32[]{:S(2)}, u32[]{:S(2)}) collective-permute-start(bf16[48,2560]{1,0:T(8,128)(2,1)S(1)} %fusion.2), channel_id=1, source_target_pairs={{0,2},{2,0},{1,3},{3,1},{4,6},{6,4},{5,7},{7,5},{8,10},{10,8},{9,1... | collective-permute-start | bytes 737288 | tf_op jit(solution)/shard_map/ppermute | solution.py:34
  41.7 1.5 %collective-permute-start.8 = (bf16[48,1280]{1,0:T(8,128)(2,1)S(1)}, bf16[48,1280]{1,0:T(8,128)(2,1)S(1)}, u32[]{:S(2)}, u32[]{:S(2)}) collective-permute-start(bf16[48,1280]{1,0:T(8,128)(2,1)S(1)} %fusion.3.refs_0_), channel_id=1, source_target_pairs={{0,1},{1,0},{2,3},{3,2},{4,5},{5,4},{6,7},{7,6},{8,9},{9,8},{10,11... | collective-permute-start | bytes 368648 | tf_op jit(solution)/shard_map/ppermute | solution.py:34
  44.2 6.4 %collective-permute-start.9 = (bf16[24,1024]{1,0:T(8,128)(2,1)S(1)}, bf16[24,1024]{1,0:T(8,128)(2,1)S(1)}, u32[]{:S(2)}, u32[]{:S(2)}) collective-permute-start(bf16[24,1024]{1,0:T(8,128)(2,1)S(1)} %get-tuple-element.28), channel_id=1, source_target_pairs={{0,12},{4,8},{8,4},{12,0},{1,13},{5,9},{9,5},{13,1},{2,14},{6,10},... | collective-permute-start | bytes 147464 | tf_op jit(solution)/shard_map/ppermute | solution.py:226
  47.2 5.4 %collective-permute-start.10 = (bf16[24,1024]{1,0:T(8,128)(2,1)S(1)}, bf16[24,1024]{1,0:T(8,128)(2,1)S(1)}, u32[]{:S(2)}, u32[]{:S(2)}) collective-permute-start(bf16[24,1024]{1,0:T(8,128)(2,1)S(1)} %get-tuple-element.29), channel_id=1, source_target_pairs={{0,8},{4,12},{8,0},{12,4},{1,9},{5,13},{9,1},{13,5},{2,10},{6,14},... | collective-permute-start | bytes 147464 | tf_op jit(solution)/shard_map/ppermute | solution.py:226
  47.3 5.3 %collective-permute-start.11 = (bf16[24,1024]{1,0:T(8,128)(2,1)S(1)}, bf16[24,1024]{1,0:T(8,128)(2,1)S(1)}, u32[]{:S(2)}, u32[]{:S(2)}) collective-permute-start(bf16[24,1024]{1,0:T(8,128)(2,1)S(1)} %get-tuple-element.30), channel_id=1, source_target_pairs={{0,4},{4,0},{8,12},{12,8},{1,5},{5,1},{9,13},{13,9},{2,6},{6,2},{1... | collective-permute-start | bytes 147464 | tf_op jit(solution)/shard_map/ppermute | solution.py:226

commit v10 on v9

--- a/solution.py
+++ b/solution.py
@@ -232,7 +232,7 @@
     section = tokens
     for apart in (3, 2, 1):
         section = lax.optimization_barrier(jnp.concatenate([section, across(tokens, apart)], axis=0))
-    held = load(gate_weight, up_weight, chunks[0], 5)
+    held = load(gate_weight, up_weight, chunks[0], 7)
 
     def core_sums(send, keep):
         total = keep + swap(send, "sub").astype(F32)

time: 53.6 us -> 53.7 us (level)
    pallas_call x1, Pallas kernels: 4.23 us -> 5.53 us  [load(): pl.pallas_call(functools.partial(load_kernel, chunk[0], chunk[1] // 2), o...]
    pallas_call x2, Pallas kernels: 17.3 us -> 16.5 us  [sums(): pl.pallas_call(functools.partial(sums_kernel, first, steps), out_shape=(j...]
  transfers between devices with their start and end apart: 12 -> 12, of which waited for: 7 -> 7; matrix products, arithmetic and copies ran while one was open for 1% -> 1% of each run, Pallas kernels for 33% -> 35%
where the time goes in v10:
time: 53.7 us; the launch traced here: 53.6 us
  Pallas kernels  27.8 us (52%)
  starting transfers between devices  13.4 us (25%)
  waiting for transfers between devices  8.96 us (17%)
  local copies, waits for them, and re-layouts  2.5 us (5%)
  other arithmetic  0.64 us (1%)
    pallas_call x2, Pallas kernels, sums(): pl.pallas_call(functools.partial(sums_kernel, first, steps), out_shape=(j...  16.5 us
    ppermute x6, starting transfers between devices, across(): return lax.ppermute(x, 'wide', [(i, i ^ apart) for i in range(4)])  10.1 us
    pallas_call x3, Pallas kernels, down(): pl.pallas_call(functools.partial(kernel, chunk[0], half, sides), out_shap...  5.77 us
    pallas_call x1, Pallas kernels, load(): pl.pallas_call(functools.partial(load_kernel, chunk[0], chunk[1] // 2), o...  5.53 us
    ppermute x6, waiting for transfers between devices, swap(): return lax.ppermute(x, axis, [(0, 1), (1, 0)])  4.55 us
    ppermute x6, waiting for transfers between devices, across(): return lax.ppermute(x, 'wide', [(i, i ^ apart) for i in range(4)])  4.41 us
    ppermute x6, starting transfers between devices, swap(): return lax.ppermute(x, axis, [(0, 1), (1, 0)])  3.28 us
    unnamed x18, local copies, waits for them, and re-layouts  2.43 us
  transfers between devices with their start and end apart: 12, of which 7 were waited for; matrix products, arithmetic and copies ran while one was open for 1% of the time, Pallas kernels for 35%

profile of v10, /device:TPU:0, one launch (start us, length us, event | category | flops | bytes accessed | tf_op | source)
XLA Modules:
  0.0 53.6 jit_solution(16200015181671990690)
XLA Ops:
  0.0 5.0 %collective-permute-start = (bf16[12,2048]{1,0:T(8,128)(2,1)}, bf16[12,2048]{1,0:T(8,128)(2,1)S(1)}, u32[]{:S(2)}, u32[]{:S(2)}) collective-permute-start(bf16[12,2048]{1,0:T(8,128)(2,1)} %param.4), channel_id=1, source_target_pairs={{0,12},{4,8},{8,4},{12,0},{1,13},{5,9},{9,5},{13,1},{2,14},{6,10},... | collective-permute-start | bytes 147464 | tf_op jit(solution)/shard_map/ppermute | solution.py:226
  5.1 0.6 %collective-permute-start.1 = (bf16[12,2048]{1,0:T(8,128)(2,1)}, bf16[12,2048]{1,0:T(8,128)(2,1)S(1)}, u32[]{:S(2)}, u32[]{:S(2)}) collective-permute-start(bf16[12,2048]{1,0:T(8,128)(2,1)} %param.4), channel_id=1, source_target_pairs={{0,8},{4,12},{8,0},{12,4},{1,9},{5,13},{9,1},{13,5},{2,10},{6,14},... | collective-permute-start | bytes 147464 | tf_op jit(solution)/shard_map/ppermute | solution.py:226
  5.7 5.5 %load.1.refs_0_ = bf16[2048,3584]{1,0:T(8,128)(2,1)S(1)} custom-call(bf16[2048,6656]{1,0:T(8,128)(2,1)} %gate.5, bf16[2048,6656]{1,0:T(8,128)(2,1)} %up.5), custom_call_target="tpu_custom_call" | custom-call | bytes 14680064 | tf_op jit(solution)/shard_map/load/pallas_call | solution.py:82
  11.4 7.8 %sums.2 = (bf16[48,4096]{1,0:T(8,128)(2,1)S(1)}, f32[48,4096]{1,0:T(8,128)S(1)}) custom-call(bf16[48,2048]{1,0:T(8,128)(2,1)S(1)} %pad_maximum_fusion.tokens, bf16[2048,6656]{1,0:T(8,128)(2,1)} %gate.5, bf16[2048,6656]{1,0:T(8,128)(2,1)} %up.5, bf16[2048,3584]{1,0:T(8,128)(2,1)S(1)} %load.1.refs_0_), custom_call_target="tpu_custom_call" | custom-call | flops 1610612736 | bytes 33554432 | tf_op jit(solution)/shard_map/sums/pallas_call | solution.py:140
  19.2 1.7 %collective-permute-done.3 = bf16[48,4096]{1,0:T(8,128)(2,1)S(1)} collective-permute-done((bf16[48,4096]{1,0:T(8,128)(2,1)S(1)}, bf16[48,4096]{1,0:T(8,128)(2,1)S(1)}, u32[]{:S(2)}, u32[]{:S(2)}) %collective-permute-start.3) | collective-permute-done | bytes 393248 | tf_op jit(solution)/shard_map/ppermute | solution.py:34
  20.9 0.1 fusion
  21.1 1.7 %collective-permute-start.4 = (bf16[48,4096]{1,0:T(8,128)(2,1)S(1)}, bf16[48,4096]{1,0:T(8,128)(2,1)S(1)}, u32[]{:S(2)}, u32[]{:S(2)}) collective-permute-start(bf16[48,4096]{1,0:T(8,128)(2,1)S(1)} %fusion), channel_id=1, source_target_pairs={{0,2},{2,0},{1,3},{3,1},{4,6},{6,4},{5,7},{7,5},{8,10},{10,8},{9,1... | collective-permute-start | bytes 1179656 | tf_op jit(solution)/shard_map/ppermute | solution.py:34
  22.8 8.7 %sums.3 = (bf16[48,2560]{1,0:T(8,128)(2,1)S(1)}, f32[48,2560]{1,0:T(8,128)S(1)}) custom-call(bf16[48,2048]{1,0:T(8,128)(2,1)S(1)} %pad_maximum_fusion.tokens, bf16[2048,6656]{1,0:T(8,128)(2,1)} %gate.5, bf16[2048,6656]{1,0:T(8,128)(2,1)} %up.5), custom_call_target="tpu_custom_call" | custom-call | flops 1006632960 | bytes 20971520 | tf_op jit(solution)/shard_map/sums/pallas_call | solution.py:140
  31.6 0.7 %collective-permute-done.4 = bf16[48,4096]{1,0:T(8,128)(2,1)S(1)} collective-permute-done((bf16[48,4096]{1,0:T(8,128)(2,1)S(1)}, bf16[48,4096]{1,0:T(8,128)(2,1)S(1)}, u32[]{:S(2)}, u32[]{:S(2)}) %collective-permute-start.4) | collective-permute-done | bytes 393248 | tf_op jit(solution)/shard_map/ppermute | solution.py:34
  32.3 0.1 convert_add_fusion
  32.5 0.1 fusion.1.refs_0_
  32.7 0.5 collective-permute-done.5
  33.2 1.3 %collective-permute-start.6 = (bf16[48,2560]{1,0:T(8,128)(2,1)S(1)}, bf16[48,2560]{1,0:T(8,128)(2,1)S(1)}, u32[]{:S(2)}, u32[]{:S(2)}) collective-permute-start(bf16[48,2560]{1,0:T(8,128)(2,1)S(1)} %fusion.2), channel_id=1, source_target_pairs={{0,2},{2,0},{1,3},{3,1},{4,6},{6,4},{5,7},{7,5},{8,10},{10,8},{9,1... | collective-permute-start | bytes 737288 | tf_op jit(solution)/shard_map/ppermute | solution.py:34
  34.5 1.1 %slice-done.5 = s8[4194304]{0:T(1024)(128)(4,1)S(1)} async-done(((s8[27262976]{0:T(1024)(128)(4,1)}), s8[4194304]{0:T(1024)(128)(4,1)S(1)}, s32[]{:S(2)}) %slice-start.5) | async-done | bytes 4194328
  35.6 0.6 %slice-done.6 = s8[2097152]{0:T(1024)(128)(4,1)S(1)} async-done(((s8[27262976]{0:T(1024)(128)(4,1)}), s8[2097152]{0:T(1024)(128)(4,1)S(1)}, s32[]{:S(2)}) %slice-start.6) | async-done | bytes 2097176
  36.2 3.4 %down.3.refs_1_ = f32[48,2048]{1,0:T(8,128)S(1)} custom-call(bf16[6656,2048]{1,0:T(8,128)(2,1)S(1)} %bitcast.5, bf16[48,2048]{1,0:T(8,128)(2,1)S(1)} %fusion.1.refs_0_, bf16[48,2048]{1,0:T(8,128)(2,1)S(1)} %collective-permute-done.7.refs_1_), custom_call_target="tpu_custom_call" | custom-call | flops 805306368 | bytes 16777216 | tf_op jit(solution)/shard_map/down/pallas_call | solution.py:205
  39.6 1.7 %collective-permute-done.6 = bf16[48,2560]{1,0:T(8,128)(2,1)S(1)} collective-permute-done((bf16[48,2560]{1,0:T(8,128)(2,1)S(1)}, bf16[48,2560]{1,0:T(8,128)(2,1)S(1)}, u32[]{:S(2)}, u32[]{:S(2)}) %collective-permute-start.6) | collective-permute-done | bytes 245792 | tf_op jit(solution)/shard_map/ppermute | solution.py:34
  41.5 1.4 %down.4.total = f32[48,2048]{1,0:T(8,128)S(1)} custom-call(bf16[6656,2048]{1,0:T(8,128)(2,1)S(1)} %bitcast.5, bf16[48,1280]{1,0:T(8,128)(2,1)S(1)} %fusion.3.refs_0_, f32[48,2048]{1,0:T(8,128)S(1)} %down.3.refs_1_), custom_call_target="tpu_custom_call" | custom-call | flops 251658240 | bytes 5242880 | tf_op jit(solution)/shard_map/down/pallas_call | solution.py:205
  42.9 1.0 %down.5 = (f32[24,1024]{1,0:T(8,128)S(1)}, bf16[24,1024]{1,0:T(8,128)(2,1)S(1)}, bf16[24,1024]{1,0:T(8,128)(2,1)S(1)}, bf16[24,1024]{1,0:T(8,128)(2,1)S(1)}) custom-call(bf16[6656,2048]{1,0:T(8,128)(2,1)S(1)} %bitcast.5, bf16[48,1280]{1,0:T(8,128)(2,1)S(1)} %collective-permute-done.8.hidden, f32[48,2048]{1,0:T(8,128)S(1)} %down.4.total), custom_call_target="tpu_custom_call" | custom-call | flops 251658240 | bytes 5242880 | tf_op jit(solution)/shard_map/down/pallas_call | solution.py:205
  43.9 3.7 %collective-permute-start.9 = (bf16[24,1024]{1,0:T(8,128)(2,1)S(1)}, bf16[24,1024]{1,0:T(8,128)(2,1)S(1)}, u32[]{:S(2)}, u32[]{:S(2)}) collective-permute-start(bf16[24,1024]{1,0:T(8,128)(2,1)S(1)} %get-tuple-element.28), channel_id=1, source_target_pairs={{0,12},{4,8},{8,4},{12,0},{1,13},{5,9},{9,5},{13,1},{2,14},{6,10},... | collective-permute-start | bytes 147464 | tf_op jit(solution)/shard_map/ppermute | solution.py:226
  47.6 0.7 %collective-permute-start.11 = (bf16[24,1024]{1,0:T(8,128)(2,1)S(1)}, bf16[24,1024]{1,0:T(8,128)(2,1)S(1)}, u32[]{:S(2)}, u32[]{:S(2)}) collective-permute-start(bf16[24,1024]{1,0:T(8,128)(2,1)S(1)} %get-tuple-element.30), channel_id=1, source_target_pairs={{0,4},{4,0},{8,12},{12,8},{1,5},{5,1},{9,13},{13,9},{2,6},{6,2},{1... | collective-permute-start | bytes 147464 | tf_op jit(solution)/shard_map/ppermute | solution.py:226
  48.4 1.9 %collective-permute-done.9 = bf16[24,1024]{1,0:T(8,128)(2,1)S(1)} collective-permute-done((bf16[24,1024]{1,0:T(8,128)(2,1)S(1)}, bf16[24,1024]{1,0:T(8,128)(2,1)S(1)}, u32[]{:S(2)}, u32[]{:S(2)}) %collective-permute-start.9) | collective-permute-done | bytes 49184 | tf_op jit(solution)/shard_map/ppermute | solution.py:226
  50.3 2.4 %collective-permute-done.10 = bf16[24,1024]{1,0:T(8,128)(2,1)S(1)} collective-permute-done((bf16[24,1024]{1,0:T(8,128)(2,1)S(1)}, bf16[24,1024]{1,0:T(8,128)(2,1)S(1)}, u32[]{:S(2)}, u32[]{:S(2)}) %collective-permute-start.10) | collective-permute-done | bytes 49184 | tf_op jit(solution)/shard_map/ppermute | solution.py:226
  52.9 0.6 %copy.7 = bf16[2,8,2,1024]{3,1,2,0:T(8,128)(2,1)} copy(bf16[2,8,2,1024]{3,2,1,0:T(2,128)(2,1)S(1)} %bitcast.7) | data formatting | bytes 131072
  (39 shorter events, 0.8 us)
Async XLA Ops:
  0.0 11.2 %copy-start = (bf16[12,2048]{1,0:T(8,128)(2,1)S(1)}, bf16[12,2048]{1,0:T(8,128)(2,1)}, u32[]{:S(2)}) copy-start(bf16[12,2048]{1,0:T(8,128)(2,1)} %param.4) | copy-start | bytes 147460
  0.0 11.2 %collective-permute-start = (bf16[12,2048]{1,0:T(8,128)(2,1)}, bf16[12,2048]{1,0:T(8,128)(2,1)S(1)}, u32[]{:S(2)}, u32[]{:S(2)}) collective-permute-start(bf16[12,2048]{1,0:T(8,128)(2,1)} %param.4), channel_id=1, source_target_pairs={{0,12},{4,8},{8,4},{12,0},{1,13},{5,9},{9,5},{13,1},{2,14},{6,10},... | collective-permute-start | bytes 147464 | tf_op jit(solution)/shard_map/ppermute | solution.py:226
  5.1 6.3 %collective-permute-start.2 = (bf16[12,2048]{1,0:T(8,128)(2,1)}, bf16[12,2048]{1,0:T(8,128)(2,1)S(1)}, u32[]{:S(2)}, u32[]{:S(2)}) collective-permute-start(bf16[12,2048]{1,0:T(8,128)(2,1)} %param.4), channel_id=1, source_target_pairs={{0,4},{4,0},{8,12},{12,8},{1,5},{5,1},{9,13},{13,9},{2,6},{6,2},{1... | collective-permute-start | bytes 147464 | tf_op jit(solution)/shard_map/ppermute | solution.py:226
  5.1 6.2 %collective-permute-start.1 = (bf16[12,2048]{1,0:T(8,128)(2,1)}, bf16[12,2048]{1,0:T(8,128)(2,1)S(1)}, u32[]{:S(2)}, u32[]{:S(2)}) collective-permute-start(bf16[12,2048]{1,0:T(8,128)(2,1)} %param.4), channel_id=1, source_target_pairs={{0,8},{4,12},{8,0},{12,4},{1,9},{5,13},{9,1},{13,5},{2,10},{6,14},... | collective-permute-start | bytes 147464 | tf_op jit(solution)/shard_map/ppermute | solution.py:226
  19.2 1.8 %collective-permute-start.3 = (bf16[48,4096]{1,0:T(8,128)(2,1)S(1)}, bf16[48,4096]{1,0:T(8,128)(2,1)S(1)}, u32[]{:S(2)}, u32[]{:S(2)}) collective-permute-start(bf16[48,4096]{1,0:T(8,128)(2,1)S(1)} %get-tuple-element.19), channel_id=1, source_target_pairs={{0,1},{1,0},{2,3},{3,2},{4,5},{5,4},{6,7},{7,6},{8,9},{9,8},{10,11... | collective-permute-start | bytes 1179656 | tf_op jit(solution)/shard_map/ppermute | solution.py:34
  20.9 13.5 %slice-start = ((s8[27262976]{0:T(1024)(128)(4,1)}), s8[4194304]{0:T(1024)(128)(4,1)S(1)}, s32[]{:S(2)}) async-start(s8[27262976]{0:T(1024)(128)(4,1)} %bitcast.4), calls=%async_computation | async-start | bytes 8388608
  21.0 13.4 %slice-start.1 = ((s8[27262976]{0:T(1024)(128)(4,1)}), s8[4194304]{0:T(1024)(128)(4,1)S(1)}, s32[]{:S(2)}) async-start(s8[27262976]{0:T(1024)(128)(4,1)} %bitcast.4), calls=%async_computation.1 | async-start | bytes 8388608
  21.1 13.4 %slice-start.2 = ((s8[27262976]{0:T(1024)(128)(4,1)}), s8[4194304]{0:T(1024)(128)(4,1)S(1)}, s32[]{:S(2)}) async-start(s8[27262976]{0:T(1024)(128)(4,1)} %bitcast.4), calls=%async_computation.2 | async-start | bytes 8388608
  21.1 13.4 %slice-start.3 = ((s8[27262976]{0:T(1024)(128)(4,1)}), s8[4194304]{0:T(1024)(128)(4,1)S(1)}, s32[]{:S(2)}) async-start(s8[27262976]{0:T(1024)(128)(4,1)} %bitcast.4), calls=%async_computation.3 | async-start | bytes 8388608
  21.1 13.4 %slice-start.4 = ((s8[27262976]{0:T(1024)(128)(4,1)}), s8[4194304]{0:T(1024)(128)(4,1)S(1)}, s32[]{:S(2)}) async-start(s8[27262976]{0:T(1024)(128)(4,1)} %bitcast.4), calls=%async_computation.4 | async-start | bytes 8388608
  21.1 14.5 %slice-start.5 = ((s8[27262976]{0:T(1024)(128)(4,1)}), s8[4194304]{0:T(1024)(128)(4,1)S(1)}, s32[]{:S(2)}) async-start(s8[27262976]{0:T(1024)(128)(4,1)} %bitcast.4), calls=%async_computation.5 | async-start | bytes 8388608
  21.1 15.1 %slice-start.6 = ((s8[27262976]{0:T(1024)(128)(4,1)}), s8[2097152]{0:T(1024)(128)(4,1)S(1)}, s32[]{:S(2)}) async-start(s8[27262976]{0:T(1024)(128)(4,1)} %bitcast.4), calls=%async_computation.6 | async-start | bytes 4194304
  21.1 11.2 %collective-permute-start.4 = (bf16[48,4096]{1,0:T(8,128)(2,1)S(1)}, bf16[48,4096]{1,0:T(8,128)(2,1)S(1)}, u32[]{:S(2)}, u32[]{:S(2)}) collective-permute-start(bf16[48,4096]{1,0:T(8,128)(2,1)S(1)} %fusion), channel_id=1, source_target_pairs={{0,2},{2,0},{1,3},{3,1},{4,6},{6,4},{5,7},{7,5},{8,10},{10,8},{9,1... | collective-permute-start | bytes 1179656 | tf_op jit(solution)/shard_map/ppermute | solution.py:34
  31.5 1.6 %collective-permute-start.5 = (bf16[48,2560]{1,0:T(8,128)(2,1)S(1)}, bf16[48,2560]{1,0:T(8,128)(2,1)S(1)}, u32[]{:S(2)}, u32[]{:S(2)}) collective-permute-start(bf16[48,2560]{1,0:T(8,128)(2,1)S(1)} %get-tuple-element.23), channel_id=1, source_target_pairs={{0,1},{1,0},{2,3},{3,2},{4,5},{5,4},{6,7},{7,6},{8,9},{9,8},{10,11... | collective-permute-start | bytes 737288 | tf_op jit(solution)/shard_map/ppermute | solution.py:34
  32.6 1.9 %collective-permute-start.7 = (bf16[48,2048]{1,0:T(8,128)(2,1)S(1)}, bf16[48,2048]{1,0:T(8,128)(2,1)S(1)}, u32[]{:S(2)}, u32[]{:S(2)}) collective-permute-start(bf16[48,2048]{1,0:T(8,128)(2,1)S(1)} %fusion.1.refs_0_), channel_id=1, source_target_pairs={{0,1},{1,0},{2,3},{3,2},{4,5},{5,4},{6,7},{7,6},{8,9},{9,8},{10,11... | collective-permute-start | bytes 589832 | tf_op jit(solution)/shard_map/ppermute | solution.py:34
  33.2 8.1 %collective-permute-start.6 = (bf16[48,2560]{1,0:T(8,128)(2,1)S(1)}, bf16[48,2560]{1,0:T(8,128)(2,1)S(1)}, u32[]{:S(2)}, u32[]{:S(2)}) collective-permute-start(bf16[48,2560]{1,0:T(8,128)(2,1)S(1)} %fusion.2), channel_id=1, source_target_pairs={{0,2},{2,0},{1,3},{3,1},{4,6},{6,4},{5,7},{7,5},{8,10},{10,8},{9,1... | collective-permute-start | bytes 737288 | tf_op jit(solution)/shard_map/ppermute | solution.py:34
  41.4 1.5 %collective-permute-start.8 = (bf16[48,1280]{1,0:T(8,128)(2,1)S(1)}, bf16[48,1280]{1,0:T(8,128)(2,1)S(1)}, u32[]{:S(2)}, u32[]{:S(2)}) collective-permute-start(bf16[48,1280]{1,0:T(8,128)(2,1)S(1)} %fusion.3.refs_0_), channel_id=1, source_target_pairs={{0,1},{1,0},{2,3},{3,2},{4,5},{5,4},{6,7},{7,6},{8,9},{9,8},{10,11... | collective-permute-start | bytes 368648 | tf_op jit(solution)/shard_map/ppermute | solution.py:34
  43.9 6.3 %collective-permute-start.9 = (bf16[24,1024]{1,0:T(8,128)(2,1)S(1)}, bf16[24,1024]{1,0:T(8,128)(2,1)S(1)}, u32[]{:S(2)}, u32[]{:S(2)}) collective-permute-start(bf16[24,1024]{1,0:T(8,128)(2,1)S(1)} %get-tuple-element.28), channel_id=1, source_target_pairs={{0,12},{4,8},{8,4},{12,0},{1,13},{5,9},{9,5},{13,1},{2,14},{6,10},... | collective-permute-start | bytes 147464 | tf_op jit(solution)/shard_map/ppermute | solution.py:226
  47.6 5.0 %collective-permute-start.10 = (bf16[24,1024]{1,0:T(8,128)(2,1)S(1)}, bf16[24,1024]{1,0:T(8,128)(2,1)S(1)}, u32[]{:S(2)}, u32[]{:S(2)}) collective-permute-start(bf16[24,1024]{1,0:T(8,128)(2,1)S(1)} %get-tuple-element.29), channel_id=1, source_target_pairs={{0,8},{4,12},{8,0},{12,4},{1,9},{5,13},{9,1},{13,5},{2,10},{6,14},... | collective-permute-start | bytes 147464 | tf_op jit(solution)/shard_map/ppermute | solution.py:226
  47.6 5.1 %collective-permute-start.11 = (bf16[24,1024]{1,0:T(8,128)(2,1)S(1)}, bf16[24,1024]{1,0:T(8,128)(2,1)S(1)}, u32[]{:S(2)}, u32[]{:S(2)}) collective-permute-start(bf16[24,1024]{1,0:T(8,128)(2,1)S(1)} %get-tuple-element.30), channel_id=1, source_target_pairs={{0,4},{4,0},{8,12},{12,8},{1,5},{5,1},{9,13},{13,9},{2,6},{6,2},{1... | collective-permute-start | bytes 147464 | tf_op jit(solution)/shard_map/ppermute | solution.py:226

commit v11 on v10

--- a/solution.py
+++ b/solution.py
@@ -49,6 +49,83 @@
     return pltpu.with_memory_space_constraint(x, pltpu.HBM)
 
 
+SLOTS = 6
+
+
+def beside_kernel(*refs):
+    refs[-1][...] = jnp.zeros_like(refs[-1])
+
+
+def beside(weight, *operands):
+    operands = [left_in_hbm(weight), *operands]
+    return pl.pallas_call(
+        beside_kernel,
+        out_shape=jax.ShapeDtypeStruct((8, 128), F32),
+        in_specs=[HBM] + [ANY] * (len(operands) - 1),
+        out_specs=VMEM,
+        compiler_params=GRANT,
+        cost_estimate=pl.CostEstimate(flops=0, bytes_accessed=2 * weight.size, transcendentals=0),
+        name="beside",
+    )(*operands)
+
+
+def sums_kernel(first, tokens, gate, up, after, send, keep, slots, sems):
+    half = send.shape[1] // 2
+    blocks = half // BLOCK
+    core = lax.axis_index("sub")
+
+    def columns(step):
+        mine = jnp.int32(step >= blocks)
+        side = jnp.where(mine == 1, core, 1 - core)
+        unit = first + side * half + (step - mine * blocks) * BLOCK
+        return pl.ds(pl.multiple_of(unit, BLOCK), BLOCK)
+
+    def slot(step):
+        at = lax.rem(step, SLOTS)
+        return slots.at[:, pl.ds(pl.multiple_of(at * BLOCK, BLOCK), BLOCK)], sems.at[at]
+
+    def copy(step):
+        return pltpu.make_async_copy(up.at[:, columns(step)], *slot(step))
+
+    for step in range(min(SLOTS, 2 * blocks)):
+        copy(jnp.int32(step)).start()
+
+    for side, out in enumerate((send, keep)):
+
+        @pl.loop(0, blocks)
+        def _(block):
+            step = side * blocks + block
+            at = pl.multiple_of(block * BLOCK, BLOCK)
+            out[:, pl.ds(at, BLOCK)] = jnp.dot(
+                tokens[...], gate[:, columns(step)], preferred_element_type=F32
+            ).astype(out.dtype)
+            copy(step).wait()
+            out[:, pl.ds(pl.multiple_of(half + at, BLOCK), BLOCK)] = jnp.dot(
+                tokens[...], slot(step)[0][...], preferred_element_type=F32
+            ).astype(out.dtype)
+
+            @pl.when(step + SLOTS < 2 * blocks)
+            def _():
+                copy(step + SLOTS).start()
+
+
+def sums(tokens, gate, up, chunk, after):
+    rows, depth = tokens.shape
+    first, width = chunk
+    return pl.pallas_call(
+        functools.partial(sums_kernel, first),
+        out_shape=(jax.ShapeDtypeStruct((rows, width), BF16), jax.ShapeDtypeStruct((rows, width), F32)),
+        in_specs=[VMEM, VMEM, HBM, ANY],
+        out_specs=(VMEM, VMEM),
+        scratch_shapes=[pltpu.VMEM((depth, SLOTS * BLOCK), BF16), pltpu.SemaphoreType.DMA((SLOTS,))],
+        compiler_params=pltpu.CompilerParams(vmem_limit_bytes=2 * SLOTS * depth * BLOCK + 2 * 2**20),
+        cost_estimate=pl.CostEstimate(
+            flops=4 * rows * depth * width, bytes_accessed=4 * depth * width, transcendentals=0
+        ),
+        name="sums",
+    )(tokens, held_in(gate), left_in_hbm(up), after)
+
+
 def block_copies(first, half, step, gate, up, dst, sem):
     core = lax.axis_index("sub")
     mine = jnp.int32(step >= half // BLOCK)
@@ -65,35 +142,7 @@
     return ref.at[:, pl.ds(pl.multiple_of(at * 2 * BLOCK, 2 * BLOCK), 2 * BLOCK)]
 
 
-def load_kernel(first, half, gate, up, held, sems):
-    copies = [
-        copy
-        for step in range(sems.shape[0])
-        for copy in block_copies(first, half, step, gate, up, pair(held, step), sems.at[step])
-    ]
-    for copy in copies:
-        copy.start()
-    for copy in copies:
-        copy.wait()
-
-
-def load(gate, up, chunk, steps):
-    depth = gate.shape[0]
-    return pl.pallas_call(
-        functools.partial(load_kernel, chunk[0], chunk[1] // 2),
-        out_shape=pltpu.VMEM((depth, steps * 2 * BLOCK), BF16),
-        in_specs=[HBM, HBM],
-        out_specs=VMEM,
-        scratch_shapes=[pltpu.SemaphoreType.DMA((steps, 2))],
-        compiler_params=GRANT,
-        cost_estimate=pl.CostEstimate(
-            flops=0, bytes_accessed=4 * steps * depth * BLOCK, transcendentals=0
-        ),
-        name="load",
-    )(left_in_hbm(gate), left_in_hbm(up))
-
-
-def sums_kernel(first, steps, tokens, gate, up, *refs):
+def stream_kernel(first, steps, tokens, gate, up, *refs):
     send, keep, streamed, sems = refs[-4:]
     held = refs[0] if steps else None
     half = send.shape[1] // 2
@@ -132,13 +181,13 @@
                 add(out, start, pair(streamed, step - steps), step)
 
 
-def sums(tokens, gate, up, chunk, held=None):
+def stream_sums(tokens, gate, up, chunk, held=None):
     rows, depth = tokens.shape
     first, width = chunk
     steps = 0 if held is None else held.shape[1] // (2 * BLOCK)
     streamed = width // BLOCK - steps
     return pl.pallas_call(
-        functools.partial(sums_kernel, first, steps),
+        functools.partial(stream_kernel, first, steps),
         out_shape=(jax.ShapeDtypeStruct((rows, width), BF16), jax.ShapeDtypeStruct((rows, width), F32)),
         in_specs=[VMEM, HBM, HBM] + [VMEM] * (steps > 0),
         out_specs=(VMEM, VMEM),
@@ -150,7 +199,7 @@
         cost_estimate=pl.CostEstimate(
             flops=4 * rows * depth * width, bytes_accessed=4 * depth * width, transcendentals=0
         ),
-        name="sums",
+        name="stream_sums",
     )(tokens, left_in_hbm(gate), left_in_hbm(up), *([held_in(held)] if steps else []))
 
 
@@ -232,8 +281,6 @@
     section = tokens
     for apart in (3, 2, 1):
         section = lax.optimization_barrier(jnp.concatenate([section, across(tokens, apart)], axis=0))
-    held = load(gate_weight, up_weight, chunks[0], 7)
-
     def core_sums(send, keep):
         total = keep + swap(send, "sub").astype(F32)
         return total, total.astype(BF16)
@@ -241,10 +288,11 @@
     def hidden_half(total, received):
         return activate(*jnp.split(total + received.astype(F32), 2, axis=1))
 
-    send, keep = sums(section, gate_weight, up_weight, chunks[0], held)
+    ready = beside(gate_weight)
+    send, keep = sums(section, gate_weight, up_weight, chunks[0], ready)
     total, sent = core_sums(send, keep)
     later, _ = lax.optimization_barrier((section, sent))
-    send, keep = sums(later, gate_weight, up_weight, chunks[1])
+    send, keep = stream_sums(later, gate_weight, up_weight, chunks[1])
     received, keep = lax.optimization_barrier((swap(sent, "narrow"), keep))
     mine = hidden_half(total, received)
     total, sent = core_sums(send, keep)

time: 53.7 us -> 58.5 us (1.089)
  waiting for transfers between devices: 8.96 us -> 13.5 us
    ppermute x6, waiting for transfers between devices: 4.41 us -> 9.06 us  [across(): return lax.ppermute(x, 'wide', [(i, i ^ apart) for i in range(4)])]
    unnamed x18 -> x20, local copies, waits for them, and re-layouts: 2.43 us -> 2.65 us
  transfers between devices with their start and end apart: 12 -> 12, of which waited for: 7 -> 8; matrix products, arithmetic and copies ran while one was open for 1% -> 1% of each run, Pallas kernels for 35% -> 23%
where the time goes in v11:
time: 58.5 us; the launch traced here: 58.4 us
  Pallas kernels  28.1 us (48%)
  waiting for transfers between devices  13.5 us (23%)
  starting transfers between devices  13.2 us (23%)
  local copies, waits for them, and re-layouts  2.72 us (5%)
  other arithmetic  0.59 us (1%)
    pallas_call x1, Pallas kernels, sums(): pl.pallas_call(functools.partial(sums_kernel, first), out_shape=(jax.Shap...  13.6 us
    ppermute x6, starting transfers between devices, across(): return lax.ppermute(x, 'wide', [(i, i ^ apart) for i in range(4)])  10.1 us
    ppermute x6, waiting for transfers between devices, across(): return lax.ppermute(x, 'wide', [(i, i ^ apart) for i in range(4)])  9.06 us
    pallas_call x1, Pallas kernels, stream_sums(): pl.pallas_call(functools.partial(stream_kernel, first, steps), out_shape=...  8.71 us
    pallas_call x3, Pallas kernels, down(): pl.pallas_call(functools.partial(kernel, chunk[0], half, sides), out_shap...  5.77 us
    ppermute x6, waiting for transfers between devices, swap(): return lax.ppermute(x, axis, [(0, 1), (1, 0)])  4.44 us
    ppermute x6, starting transfers between devices, swap(): return lax.ppermute(x, axis, [(0, 1), (1, 0)])  3.1 us
    unnamed x20, local copies, waits for them, and re-layouts  2.65 us
  transfers between devices with their start and end apart: 12, of which 8 were waited for; matrix products, arithmetic and copies ran while one was open for 1% of the time, Pallas kernels for 23%

profile of v11, /device:TPU:0, one launch (start us, length us, event | category | flops | bytes accessed | tf_op | source)
XLA Modules:
  0.0 58.4 jit_solution(14508368999906493091)
XLA Ops:
  0.0 5.0 %collective-permute-start = (bf16[12,2048]{1,0:T(8,128)(2,1)}, bf16[12,2048]{1,0:T(8,128)(2,1)S(1)}, u32[]{:S(2)}, u32[]{:S(2)}) collective-permute-start(bf16[12,2048]{1,0:T(8,128)(2,1)} %param.4), channel_id=1, source_target_pairs={{0,12},{4,8},{8,4},{12,0},{1,13},{5,9},{9,5},{13,1},{2,14},{6,10},... | collective-permute-start | bytes 147464 | tf_op jit(solution)/shard_map/ppermute | solution.py:275
  5.1 0.6 %collective-permute-start.1 = (bf16[12,2048]{1,0:T(8,128)(2,1)}, bf16[12,2048]{1,0:T(8,128)(2,1)S(1)}, u32[]{:S(2)}, u32[]{:S(2)}) collective-permute-start(bf16[12,2048]{1,0:T(8,128)(2,1)} %param.4), channel_id=1, source_target_pairs={{0,8},{4,12},{8,0},{12,4},{1,9},{5,13},{9,1},{13,5},{2,10},{6,14},... | collective-permute-start | bytes 147464 | tf_op jit(solution)/shard_map/ppermute | solution.py:275
  5.7 2.5 %collective-permute-done = bf16[12,2048]{1,0:T(8,128)(2,1)S(1)} collective-permute-done((bf16[12,2048]{1,0:T(8,128)(2,1)}, bf16[12,2048]{1,0:T(8,128)(2,1)S(1)}, u32[]{:S(2)}, u32[]{:S(2)}) %collective-permute-start) | collective-permute-done | bytes 49184 | tf_op jit(solution)/shard_map/ppermute | solution.py:275
  8.3 2.6 %collective-permute-done.1 = bf16[12,2048]{1,0:T(8,128)(2,1)S(1)} collective-permute-done((bf16[12,2048]{1,0:T(8,128)(2,1)}, bf16[12,2048]{1,0:T(8,128)(2,1)S(1)}, u32[]{:S(2)}, u32[]{:S(2)}) %collective-permute-start.1) | collective-permute-done | bytes 49184 | tf_op jit(solution)/shard_map/ppermute | solution.py:275
  11.0 13.6 %sums.1 = (bf16[48,4096]{1,0:T(8,128)(2,1)S(1)}, f32[48,4096]{1,0:T(8,128)S(1)}) custom-call(bf16[48,2048]{1,0:T(8,128)(2,1)S(1)} %pad_maximum_fusion.tokens, bf16[2048,6656]{1,0:T(8,128)(2,1)S(1)} %copy-done, bf16[2048,6656]{1,0:T(8,128)(2,1)} %up.3, f32[8,128]{1,0:T(8,128)S(1)} %beside.1.after), custom_call_target="tpu_custom_call" | custom-call | flops 1610612736 | bytes 33554432 | tf_op jit(solution)/shard_map/sums/pallas_call | solution.py:115
  24.7 1.7 %collective-permute-done.3 = bf16[48,4096]{1,0:T(8,128)(2,1)S(1)} collective-permute-done((bf16[48,4096]{1,0:T(8,128)(2,1)S(1)}, bf16[48,4096]{1,0:T(8,128)(2,1)S(1)}, u32[]{:S(2)}, u32[]{:S(2)}) %collective-permute-start.3) | collective-permute-done | bytes 393248 | tf_op jit(solution)/shard_map/ppermute | solution.py:34
  26.5 1.6 %collective-permute-start.4 = (bf16[48,4096]{1,0:T(8,128)(2,1)S(1)}, bf16[48,4096]{1,0:T(8,128)(2,1)S(1)}, u32[]{:S(2)}, u32[]{:S(2)}) collective-permute-start(bf16[48,4096]{1,0:T(8,128)(2,1)S(1)} %fusion), channel_id=1, source_target_pairs={{0,2},{2,0},{1,3},{3,1},{4,6},{6,4},{5,7},{7,5},{8,10},{10,8},{9,1... | collective-permute-start | bytes 1179656 | tf_op jit(solution)/shard_map/ppermute | solution.py:34
  28.1 8.7 %stream_sums.1 = (bf16[48,2560]{1,0:T(8,128)(2,1)S(1)}, f32[48,2560]{1,0:T(8,128)S(1)}) custom-call(bf16[48,2048]{1,0:T(8,128)(2,1)S(1)} %pad_maximum_fusion.tokens, bf16[2048,6656]{1,0:T(8,128)(2,1)} %gate.3, bf16[2048,6656]{1,0:T(8,128)(2,1)} %up.3), custom_call_target="tpu_custom_call" | custom-call | flops 1006632960 | bytes 20971520 | tf_op jit(solution)/shard_map/stream_sums/pallas_call | solution.py:189
  36.9 0.9 %collective-permute-done.4 = bf16[48,4096]{1,0:T(8,128)(2,1)S(1)} collective-permute-done((bf16[48,4096]{1,0:T(8,128)(2,1)S(1)}, bf16[48,4096]{1,0:T(8,128)(2,1)S(1)}, u32[]{:S(2)}, u32[]{:S(2)}) %collective-permute-start.4) | collective-permute-done | bytes 393248 | tf_op jit(solution)/shard_map/ppermute | solution.py:34
  38.0 0.3 collective-permute-done.5
  38.4 1.3 %collective-permute-start.6 = (bf16[48,2560]{1,0:T(8,128)(2,1)S(1)}, bf16[48,2560]{1,0:T(8,128)(2,1)S(1)}, u32[]{:S(2)}, u32[]{:S(2)}) collective-permute-start(bf16[48,2560]{1,0:T(8,128)(2,1)S(1)} %fusion.2), channel_id=1, source_target_pairs={{0,2},{2,0},{1,3},{3,1},{4,6},{6,4},{5,7},{7,5},{8,10},{10,8},{9,1... | collective-permute-start | bytes 737288 | tf_op jit(solution)/shard_map/ppermute | solution.py:34
  39.7 0.1 slice-done.4
  39.8 1.2 %slice-done.5 = s8[4194304]{0:T(1024)(128)(4,1)S(1)} async-done(((s8[27262976]{0:T(1024)(128)(4,1)}), s8[4194304]{0:T(1024)(128)(4,1)S(1)}, s32[]{:S(2)}) %slice-start.5) | async-done | bytes 4194328
  41.0 0.6 %slice-done.6 = s8[2097152]{0:T(1024)(128)(4,1)S(1)} async-done(((s8[27262976]{0:T(1024)(128)(4,1)}), s8[2097152]{0:T(1024)(128)(4,1)S(1)}, s32[]{:S(2)}) %slice-start.6) | async-done | bytes 2097176
  41.6 3.4 %down.3.refs_1_ = f32[48,2048]{1,0:T(8,128)S(1)} custom-call(bf16[6656,2048]{1,0:T(8,128)(2,1)S(1)} %bitcast.5, bf16[48,2048]{1,0:T(8,128)(2,1)S(1)} %fusion.1.refs_0_, bf16[48,2048]{1,0:T(8,128)(2,1)S(1)} %collective-permute-done.7.refs_1_), custom_call_target="tpu_custom_call" | custom-call | flops 805306368 | bytes 16777216 | tf_op jit(solution)/shard_map/down/pallas_call | solution.py:254
  45.0 1.5 %collective-permute-done.6 = bf16[48,2560]{1,0:T(8,128)(2,1)S(1)} collective-permute-done((bf16[48,2560]{1,0:T(8,128)(2,1)S(1)}, bf16[48,2560]{1,0:T(8,128)(2,1)S(1)}, u32[]{:S(2)}, u32[]{:S(2)}) %collective-permute-start.6) | collective-permute-done | bytes 245792 | tf_op jit(solution)/shard_map/ppermute | solution.py:34
  46.8 1.4 %down.4.total = f32[48,2048]{1,0:T(8,128)S(1)} custom-call(bf16[6656,2048]{1,0:T(8,128)(2,1)S(1)} %bitcast.5, bf16[48,1280]{1,0:T(8,128)(2,1)S(1)} %fusion.3.refs_0_, f32[48,2048]{1,0:T(8,128)S(1)} %down.3.refs_1_), custom_call_target="tpu_custom_call" | custom-call | flops 251658240 | bytes 5242880 | tf_op jit(solution)/shard_map/down/pallas_call | solution.py:254
  48.2 1.0 %down.5 = (f32[24,1024]{1,0:T(8,128)S(1)}, bf16[24,1024]{1,0:T(8,128)(2,1)S(1)}, bf16[24,1024]{1,0:T(8,128)(2,1)S(1)}, bf16[24,1024]{1,0:T(8,128)(2,1)S(1)}) custom-call(bf16[6656,2048]{1,0:T(8,128)(2,1)S(1)} %bitcast.5, bf16[48,1280]{1,0:T(8,128)(2,1)S(1)} %collective-permute-done.8.hidden, f32[48,2048]{1,0:T(8,128)S(1)} %down.4.total), custom_call_target="tpu_custom_call" | custom-call | flops 251658240 | bytes 5242880 | tf_op jit(solution)/shard_map/down/pallas_call | solution.py:254
  49.2 2.9 %collective-permute-start.9 = (bf16[24,1024]{1,0:T(8,128)(2,1)S(1)}, bf16[24,1024]{1,0:T(8,128)(2,1)S(1)}, u32[]{:S(2)}, u32[]{:S(2)}) collective-permute-start(bf16[24,1024]{1,0:T(8,128)(2,1)S(1)} %get-tuple-element.28), channel_id=1, source_target_pairs={{0,12},{4,8},{8,4},{12,0},{1,13},{5,9},{9,5},{13,1},{2,14},{6,10},... | collective-permute-start | bytes 147464 | tf_op jit(solution)/shard_map/ppermute | solution.py:275
  52.1 0.2 collective-permute-start.10
  52.3 1.4 %collective-permute-start.11 = (bf16[24,1024]{1,0:T(8,128)(2,1)S(1)}, bf16[24,1024]{1,0:T(8,128)(2,1)S(1)}, u32[]{:S(2)}, u32[]{:S(2)}) collective-permute-start(bf16[24,1024]{1,0:T(8,128)(2,1)S(1)} %get-tuple-element.30), channel_id=1, source_target_pairs={{0,4},{4,0},{8,12},{12,8},{1,5},{5,1},{9,13},{13,9},{2,6},{6,2},{1... | collective-permute-start | bytes 147464 | tf_op jit(solution)/shard_map/ppermute | solution.py:275
  53.6 1.9 %collective-permute-done.9 = bf16[24,1024]{1,0:T(8,128)(2,1)S(1)} collective-permute-done((bf16[24,1024]{1,0:T(8,128)(2,1)S(1)}, bf16[24,1024]{1,0:T(8,128)(2,1)S(1)}, u32[]{:S(2)}, u32[]{:S(2)}) %collective-permute-start.9) | collective-permute-done | bytes 49184 | tf_op jit(solution)/shard_map/ppermute | solution.py:275
  55.6 2.0 %collective-permute-done.10 = bf16[24,1024]{1,0:T(8,128)(2,1)S(1)} collective-permute-done((bf16[24,1024]{1,0:T(8,128)(2,1)S(1)}, bf16[24,1024]{1,0:T(8,128)(2,1)S(1)}, u32[]{:S(2)}, u32[]{:S(2)}) %collective-permute-start.10) | collective-permute-done | bytes 49184 | tf_op jit(solution)/shard_map/ppermute | solution.py:275
  57.7 0.6 %copy.7 = bf16[2,8,2,1024]{3,1,2,0:T(8,128)(2,1)} copy(bf16[2,8,2,1024]{3,2,1,0:T(2,128)(2,1)S(1)} %bitcast.7) | data formatting | bytes 131072
  (41 shorter events, 1.0 us)
Async XLA Ops:
  0.0 8.2 %copy-start.1 = (bf16[12,2048]{1,0:T(8,128)(2,1)S(1)}, bf16[12,2048]{1,0:T(8,128)(2,1)}, u32[]{:S(2)}) copy-start(bf16[12,2048]{1,0:T(8,128)(2,1)} %param.4) | copy-start | bytes 147460
  0.0 11.0 %copy-start = (bf16[2048,6656]{1,0:T(8,128)(2,1)S(1)}, bf16[2048,6656]{1,0:T(8,128)(2,1)}, u32[]{:S(2)}) copy-start(bf16[2048,6656]{1,0:T(8,128)(2,1)} %gate.3) | copy-start | bytes 81788928
  0.0 8.2 %collective-permute-start = (bf16[12,2048]{1,0:T(8,128)(2,1)}, bf16[12,2048]{1,0:T(8,128)(2,1)S(1)}, u32[]{:S(2)}, u32[]{:S(2)}) collective-permute-start(bf16[12,2048]{1,0:T(8,128)(2,1)} %param.4), channel_id=1, source_target_pairs={{0,12},{4,8},{8,4},{12,0},{1,13},{5,9},{9,5},{13,1},{2,14},{6,10},... | collective-permute-start | bytes 147464 | tf_op jit(solution)/shard_map/ppermute | solution.py:275
  5.1 5.9 %collective-permute-start.2 = (bf16[12,2048]{1,0:T(8,128)(2,1)}, bf16[12,2048]{1,0:T(8,128)(2,1)S(1)}, u32[]{:S(2)}, u32[]{:S(2)}) collective-permute-start(bf16[12,2048]{1,0:T(8,128)(2,1)} %param.4), channel_id=1, source_target_pairs={{0,4},{4,0},{8,12},{12,8},{1,5},{5,1},{9,13},{13,9},{2,6},{6,2},{1... | collective-permute-start | bytes 147464 | tf_op jit(solution)/shard_map/ppermute | solution.py:275
  5.1 5.8 %collective-permute-start.1 = (bf16[12,2048]{1,0:T(8,128)(2,1)}, bf16[12,2048]{1,0:T(8,128)(2,1)S(1)}, u32[]{:S(2)}, u32[]{:S(2)}) collective-permute-start(bf16[12,2048]{1,0:T(8,128)(2,1)} %param.4), channel_id=1, source_target_pairs={{0,8},{4,12},{8,0},{12,4},{1,9},{5,13},{9,1},{13,5},{2,10},{6,14},... | collective-permute-start | bytes 147464 | tf_op jit(solution)/shard_map/ppermute | solution.py:275
  24.6 1.8 %collective-permute-start.3 = (bf16[48,4096]{1,0:T(8,128)(2,1)S(1)}, bf16[48,4096]{1,0:T(8,128)(2,1)S(1)}, u32[]{:S(2)}, u32[]{:S(2)}) collective-permute-start(bf16[48,4096]{1,0:T(8,128)(2,1)S(1)} %get-tuple-element.19), channel_id=1, source_target_pairs={{0,1},{1,0},{2,3},{3,2},{4,5},{5,4},{6,7},{7,6},{8,9},{9,8},{10,11... | collective-permute-start | bytes 1179656 | tf_op jit(solution)/shard_map/ppermute | solution.py:34
  26.4 13.3 %slice-start = ((s8[27262976]{0:T(1024)(128)(4,1)}), s8[4194304]{0:T(1024)(128)(4,1)S(1)}, s32[]{:S(2)}) async-start(s8[27262976]{0:T(1024)(128)(4,1)} %bitcast.4), calls=%async_computation | async-start | bytes 8388608
  26.4 13.2 %slice-start.1 = ((s8[27262976]{0:T(1024)(128)(4,1)}), s8[4194304]{0:T(1024)(128)(4,1)S(1)}, s32[]{:S(2)}) async-start(s8[27262976]{0:T(1024)(128)(4,1)} %bitcast.4), calls=%async_computation.1 | async-start | bytes 8388608
  26.5 13.2 %slice-start.2 = ((s8[27262976]{0:T(1024)(128)(4,1)}), s8[4194304]{0:T(1024)(128)(4,1)S(1)}, s32[]{:S(2)}) async-start(s8[27262976]{0:T(1024)(128)(4,1)} %bitcast.4), calls=%async_computation.2 | async-start | bytes 8388608
  26.5 13.2 %slice-start.3 = ((s8[27262976]{0:T(1024)(128)(4,1)}), s8[4194304]{0:T(1024)(128)(4,1)S(1)}, s32[]{:S(2)}) async-start(s8[27262976]{0:T(1024)(128)(4,1)} %bitcast.4), calls=%async_computation.3 | async-start | bytes 8388608
  26.5 13.3 %slice-start.4 = ((s8[27262976]{0:T(1024)(128)(4,1)}), s8[4194304]{0:T(1024)(128)(4,1)S(1)}, s32[]{:S(2)}) async-start(s8[27262976]{0:T(1024)(128)(4,1)} %bitcast.4), calls=%async_computation.4 | async-start | bytes 8388608
  26.5 14.5 %slice-start.5 = ((s8[27262976]{0:T(1024)(128)(4,1)}), s8[4194304]{0:T(1024)(128)(4,1)S(1)}, s32[]{:S(2)}) async-start(s8[27262976]{0:T(1024)(128)(4,1)} %bitcast.4), calls=%async_computation.5 | async-start | bytes 8388608
  26.5 15.1 %slice-start.6 = ((s8[27262976]{0:T(1024)(128)(4,1)}), s8[2097152]{0:T(1024)(128)(4,1)S(1)}, s32[]{:S(2)}) async-start(s8[27262976]{0:T(1024)(128)(4,1)} %bitcast.4), calls=%async_computation.6 | async-start | bytes 4194304
  26.5 11.2 %collective-permute-start.4 = (bf16[48,4096]{1,0:T(8,128)(2,1)S(1)}, bf16[48,4096]{1,0:T(8,128)(2,1)S(1)}, u32[]{:S(2)}, u32[]{:S(2)}) collective-permute-start(bf16[48,4096]{1,0:T(8,128)(2,1)S(1)} %fusion), channel_id=1, source_target_pairs={{0,2},{2,0},{1,3},{3,1},{4,6},{6,4},{5,7},{7,5},{8,10},{10,8},{9,1... | collective-permute-start | bytes 1179656 | tf_op jit(solution)/shard_map/ppermute | solution.py:34
  36.8 1.6 %collective-permute-start.5 = (bf16[48,2560]{1,0:T(8,128)(2,1)S(1)}, bf16[48,2560]{1,0:T(8,128)(2,1)S(1)}, u32[]{:S(2)}, u32[]{:S(2)}) collective-permute-start(bf16[48,2560]{1,0:T(8,128)(2,1)S(1)} %get-tuple-element.23), channel_id=1, source_target_pairs={{0,1},{1,0},{2,3},{3,2},{4,5},{5,4},{6,7},{7,6},{8,9},{9,8},{10,11... | collective-permute-start | bytes 737288 | tf_op jit(solution)/shard_map/ppermute | solution.py:34
  38.0 1.7 %collective-permute-start.7 = (bf16[48,2048]{1,0:T(8,128)(2,1)S(1)}, bf16[48,2048]{1,0:T(8,128)(2,1)S(1)}, u32[]{:S(2)}, u32[]{:S(2)}) collective-permute-start(bf16[48,2048]{1,0:T(8,128)(2,1)S(1)} %fusion.1.refs_0_), channel_id=1, source_target_pairs={{0,1},{1,0},{2,3},{3,2},{4,5},{5,4},{6,7},{7,6},{8,9},{9,8},{10,11... | collective-permute-start | bytes 589832 | tf_op jit(solution)/shard_map/ppermute | solution.py:34
  38.4 8.1 %collective-permute-start.6 = (bf16[48,2560]{1,0:T(8,128)(2,1)S(1)}, bf16[48,2560]{1,0:T(8,128)(2,1)S(1)}, u32[]{:S(2)}, u32[]{:S(2)}) collective-permute-start(bf16[48,2560]{1,0:T(8,128)(2,1)S(1)} %fusion.2), channel_id=1, source_target_pairs={{0,2},{2,0},{1,3},{3,1},{4,6},{6,4},{5,7},{7,5},{8,10},{10,8},{9,1... | collective-permute-start | bytes 737288 | tf_op jit(solution)/shard_map/ppermute | solution.py:34
  46.7 1.5 %collective-permute-start.8 = (bf16[48,1280]{1,0:T(8,128)(2,1)S(1)}, bf16[48,1280]{1,0:T(8,128)(2,1)S(1)}, u32[]{:S(2)}, u32[]{:S(2)}) collective-permute-start(bf16[48,1280]{1,0:T(8,128)(2,1)S(1)} %fusion.3.refs_0_), channel_id=1, source_target_pairs={{0,1},{1,0},{2,3},{3,2},{4,5},{5,4},{6,7},{7,6},{8,9},{9,8},{10,11... | collective-permute-start | bytes 368648 | tf_op jit(solution)/shard_map/ppermute | solution.py:34
  49.2 6.4 %collective-permute-start.9 = (bf16[24,1024]{1,0:T(8,128)(2,1)S(1)}, bf16[24,1024]{1,0:T(8,128)(2,1)S(1)}, u32[]{:S(2)}, u32[]{:S(2)}) collective-permute-start(bf16[24,1024]{1,0:T(8,128)(2,1)S(1)} %get-tuple-element.28), channel_id=1, source_target_pairs={{0,12},{4,8},{8,4},{12,0},{1,13},{5,9},{9,5},{13,1},{2,14},{6,10},... | collective-permute-start | bytes 147464 | tf_op jit(solution)/shard_map/ppermute | solution.py:275
  52.1 5.4 %collective-permute-start.10 = (bf16[24,1024]{1,0:T(8,128)(2,1)S(1)}, bf16[24,1024]{1,0:T(8,128)(2,1)S(1)}, u32[]{:S(2)}, u32[]{:S(2)}) collective-permute-start(bf16[24,1024]{1,0:T(8,128)(2,1)S(1)} %get-tuple-element.29), channel_id=1, source_target_pairs={{0,8},{4,12},{8,0},{12,4},{1,9},{5,13},{9,1},{13,5},{2,10},{6,14},... | collective-permute-start | bytes 147464 | tf_op jit(solution)/shard_map/ppermute | solution.py:275
  52.3 5.3 %collective-permute-start.11 = (bf16[24,1024]{1,0:T(8,128)(2,1)S(1)}, bf16[24,1024]{1,0:T(8,128)(2,1)S(1)}, u32[]{:S(2)}, u32[]{:S(2)}) collective-permute-start(bf16[24,1024]{1,0:T(8,128)(2,1)S(1)} %get-tuple-element.30), channel_id=1, source_target_pairs={{0,4},{4,0},{8,12},{12,8},{1,5},{5,1},{9,13},{13,9},{2,6},{6,2},{1... | collective-permute-start | bytes 147464 | tf_op jit(solution)/shard_map/ppermute | solution.py:275

commit v12 on v11

--- a/solution.py
+++ b/solution.py
@@ -49,9 +49,6 @@
     return pltpu.with_memory_space_constraint(x, pltpu.HBM)
 
 
-SLOTS = 6
-
-
 def beside_kernel(*refs):
     refs[-1][...] = jnp.zeros_like(refs[-1])
 
@@ -69,7 +66,7 @@
     )(*operands)
 
 
-def sums_kernel(first, tokens, gate, up, after, send, keep, slots, sems):
+def sums_kernel(first, tokens, gate, up, after, send, keep, held, sems):
     half = send.shape[1] // 2
     blocks = half // BLOCK
     core = lax.axis_index("sub")
@@ -80,33 +77,30 @@
         unit = first + side * half + (step - mine * blocks) * BLOCK
         return pl.ds(pl.multiple_of(unit, BLOCK), BLOCK)
 
-    def slot(step):
-        at = lax.rem(step, SLOTS)
-        return slots.at[:, pl.ds(pl.multiple_of(at * BLOCK, BLOCK), BLOCK)], sems.at[at]
+    def block_of(step):
+        return pl.ds(pl.multiple_of(step * BLOCK, BLOCK), BLOCK)
 
     def copy(step):
-        return pltpu.make_async_copy(up.at[:, columns(step)], *slot(step))
-
-    for step in range(min(SLOTS, 2 * blocks)):
+        return pltpu.make_async_copy(up.at[:, columns(step)], held.at[:, block_of(step)], sems.at[step])
+
+    for step in range(2 * blocks):
         copy(jnp.int32(step)).start()
 
     for side, out in enumerate((send, keep)):
+
+        @pl.loop(0, blocks)
+        def _(block):
+            out[:, block_of(block)] = jnp.dot(
+                tokens[...], gate[:, columns(side * blocks + block)], preferred_element_type=F32
+            ).astype(out.dtype)
 
         @pl.loop(0, blocks)
         def _(block):
             step = side * blocks + block
-            at = pl.multiple_of(block * BLOCK, BLOCK)
-            out[:, pl.ds(at, BLOCK)] = jnp.dot(
-                tokens[...], gate[:, columns(step)], preferred_element_type=F32
+            copy(step).wait()
+            out[:, block_of(blocks + block)] = jnp.dot(
+                tokens[...], held[:, block_of(step)], preferred_element_type=F32
             ).astype(out.dtype)
-            copy(step).wait()
-            out[:, pl.ds(pl.multiple_of(half + at, BLOCK), BLOCK)] = jnp.dot(
-                tokens[...], slot(step)[0][...], preferred_element_type=F32
-            ).astype(out.dtype)
-
-            @pl.when(step + SLOTS < 2 * blocks)
-            def _():
-                copy(step + SLOTS).start()
 
 
 def sums(tokens, gate, up, chunk, after):
@@ -117,8 +111,8 @@
         out_shape=(jax.ShapeDtypeStruct((rows, width), BF16), jax.ShapeDtypeStruct((rows, width), F32)),
         in_specs=[VMEM, VMEM, HBM, ANY],
         out_specs=(VMEM, VMEM),
-        scratch_shapes=[pltpu.VMEM((depth, SLOTS * BLOCK), BF16), pltpu.SemaphoreType.DMA((SLOTS,))],
-        compiler_params=pltpu.CompilerParams(vmem_limit_bytes=2 * SLOTS * depth * BLOCK + 2 * 2**20),
+        scratch_shapes=[pltpu.VMEM((depth, width), BF16), pltpu.SemaphoreType.DMA((width // BLOCK,))],
+        compiler_params=pltpu.CompilerParams(vmem_limit_bytes=2 * depth * width + 2 * 2**20),
         cost_estimate=pl.CostEstimate(
             flops=4 * rows * depth * width, bytes_accessed=4 * depth * width, transcendentals=0
         ),

time: 58.5 us -> 55 us (0.940)
  Pallas kernels: 28.1 us -> 24.5 us
    pallas_call x1, Pallas kernels: 13.6 us -> 9.99 us  [sums(): pl.pallas_call(functools.partial(sums_kernel, first), out_shape=(jax.Shap...]
  transfers between devices with their start and end apart: 12 -> 12, of which waited for: 8 -> 8; matrix products, arithmetic and copies ran while one was open for 1% -> 1% of each run, Pallas kernels for 23% -> 25%
where the time goes in v12:
time: 55 us; the launch traced here: 54.8 us
  Pallas kernels  24.5 us (45%)
  waiting for transfers between devices  13.5 us (25%)
  starting transfers between devices  13.3 us (24%)
  local copies, waits for them, and re-layouts  2.67 us (5%)
  other arithmetic  0.64 us (1%)
    ppermute x6, starting transfers between devices, across(): return lax.ppermute(x, 'wide', [(i, i ^ apart) for i in range(4)])  10.1 us
    pallas_call x1, Pallas kernels, sums(): pl.pallas_call(functools.partial(sums_kernel, first), out_shape=(jax.Shap...  9.99 us
    ppermute x6, waiting for transfers between devices, across(): return lax.ppermute(x, 'wide', [(i, i ^ apart) for i in range(4)])  9.05 us
    pallas_call x1, Pallas kernels, stream_sums(): pl.pallas_call(functools.partial(stream_kernel, first, steps), out_shape=...  8.71 us
    pallas_call x3, Pallas kernels, down(): pl.pallas_call(functools.partial(kernel, chunk[0], half, sides), out_shap...  5.77 us
    ppermute x6, waiting for transfers between devices, swap(): return lax.ppermute(x, axis, [(0, 1), (1, 0)])  4.46 us
    ppermute x6, starting transfers between devices, swap(): return lax.ppermute(x, axis, [(0, 1), (1, 0)])  3.12 us
    unnamed x20, local copies, waits for them, and re-layouts  2.6 us
  transfers between devices with their start and end apart: 12, of which 8 were waited for; matrix products, arithmetic and copies ran while one was open for 1% of the time, Pallas kernels for 25%

profile of v12, /device:TPU:0, one launch (start us, length us, event | category | flops | bytes accessed | tf_op | source)
XLA Modules:
  0.0 54.8 jit_solution(2090793253318219424)
XLA Ops:
  0.0 5.0 %collective-permute-start = (bf16[12,2048]{1,0:T(8,128)(2,1)}, bf16[12,2048]{1,0:T(8,128)(2,1)S(1)}, u32[]{:S(2)}, u32[]{:S(2)}) collective-permute-start(bf16[12,2048]{1,0:T(8,128)(2,1)} %param.4), channel_id=1, source_target_pairs={{0,12},{4,8},{8,4},{12,0},{1,13},{5,9},{9,5},{13,1},{2,14},{6,10},... | collective-permute-start | bytes 147464 | tf_op jit(solution)/shard_map/ppermute | solution.py:269
  5.1 0.6 %collective-permute-start.1 = (bf16[12,2048]{1,0:T(8,128)(2,1)}, bf16[12,2048]{1,0:T(8,128)(2,1)S(1)}, u32[]{:S(2)}, u32[]{:S(2)}) collective-permute-start(bf16[12,2048]{1,0:T(8,128)(2,1)} %param.4), channel_id=1, source_target_pairs={{0,8},{4,12},{8,0},{12,4},{1,9},{5,13},{9,1},{13,5},{2,10},{6,14},... | collective-permute-start | bytes 147464 | tf_op jit(solution)/shard_map/ppermute | solution.py:269
  5.7 2.5 %collective-permute-done = bf16[12,2048]{1,0:T(8,128)(2,1)S(1)} collective-permute-done((bf16[12,2048]{1,0:T(8,128)(2,1)}, bf16[12,2048]{1,0:T(8,128)(2,1)S(1)}, u32[]{:S(2)}, u32[]{:S(2)}) %collective-permute-start) | collective-permute-done | bytes 49184 | tf_op jit(solution)/shard_map/ppermute | solution.py:269
  8.3 2.6 %collective-permute-done.1 = bf16[12,2048]{1,0:T(8,128)(2,1)S(1)} collective-permute-done((bf16[12,2048]{1,0:T(8,128)(2,1)}, bf16[12,2048]{1,0:T(8,128)(2,1)S(1)}, u32[]{:S(2)}, u32[]{:S(2)}) %collective-permute-start.1) | collective-permute-done | bytes 49184 | tf_op jit(solution)/shard_map/ppermute | solution.py:269
  11.0 10.0 %sums.1 = (bf16[48,4096]{1,0:T(8,128)(2,1)S(1)}, f32[48,4096]{1,0:T(8,128)S(1)}) custom-call(bf16[48,2048]{1,0:T(8,128)(2,1)S(1)} %pad_maximum_fusion.tokens, bf16[2048,6656]{1,0:T(8,128)(2,1)S(1)} %copy-done, bf16[2048,6656]{1,0:T(8,128)(2,1)} %up.3, f32[8,128]{1,0:T(8,128)S(1)} %beside.1.after), custom_call_target="tpu_custom_call" | custom-call | flops 1610612736 | bytes 33554432 | tf_op jit(solution)/shard_map/sums/pallas_call | solution.py:109
  21.1 1.7 %collective-permute-done.3 = bf16[48,4096]{1,0:T(8,128)(2,1)S(1)} collective-permute-done((bf16[48,4096]{1,0:T(8,128)(2,1)S(1)}, bf16[48,4096]{1,0:T(8,128)(2,1)S(1)}, u32[]{:S(2)}, u32[]{:S(2)}) %collective-permute-start.3) | collective-permute-done | bytes 393248 | tf_op jit(solution)/shard_map/ppermute | solution.py:34
  22.9 1.6 %collective-permute-start.4 = (bf16[48,4096]{1,0:T(8,128)(2,1)S(1)}, bf16[48,4096]{1,0:T(8,128)(2,1)S(1)}, u32[]{:S(2)}, u32[]{:S(2)}) collective-permute-start(bf16[48,4096]{1,0:T(8,128)(2,1)S(1)} %fusion), channel_id=1, source_target_pairs={{0,2},{2,0},{1,3},{3,1},{4,6},{6,4},{5,7},{7,5},{8,10},{10,8},{9,1... | collective-permute-start | bytes 1179656 | tf_op jit(solution)/shard_map/ppermute | solution.py:34
  24.5 8.7 %stream_sums.1 = (bf16[48,2560]{1,0:T(8,128)(2,1)S(1)}, f32[48,2560]{1,0:T(8,128)S(1)}) custom-call(bf16[48,2048]{1,0:T(8,128)(2,1)S(1)} %pad_maximum_fusion.tokens, bf16[2048,6656]{1,0:T(8,128)(2,1)} %gate.3, bf16[2048,6656]{1,0:T(8,128)(2,1)} %up.3), custom_call_target="tpu_custom_call" | custom-call | flops 1006632960 | bytes 20971520 | tf_op jit(solution)/shard_map/stream_sums/pallas_call | solution.py:183
  33.3 0.9 %collective-permute-done.4 = bf16[48,4096]{1,0:T(8,128)(2,1)S(1)} collective-permute-done((bf16[48,4096]{1,0:T(8,128)(2,1)S(1)}, bf16[48,4096]{1,0:T(8,128)(2,1)S(1)}, u32[]{:S(2)}, u32[]{:S(2)}) %collective-permute-start.4) | collective-permute-done | bytes 393248 | tf_op jit(solution)/shard_map/ppermute | solution.py:34
  34.2 0.1 convert_add_fusion
  34.5 0.3 collective-permute-done.5
  34.8 1.3 %collective-permute-start.6 = (bf16[48,2560]{1,0:T(8,128)(2,1)S(1)}, bf16[48,2560]{1,0:T(8,128)(2,1)S(1)}, u32[]{:S(2)}, u32[]{:S(2)}) collective-permute-start(bf16[48,2560]{1,0:T(8,128)(2,1)S(1)} %fusion.2), channel_id=1, source_target_pairs={{0,2},{2,0},{1,3},{3,1},{4,6},{6,4},{5,7},{7,5},{8,10},{10,8},{9,1... | collective-permute-start | bytes 737288 | tf_op jit(solution)/shard_map/ppermute | solution.py:34
  36.2 1.2 %slice-done.5 = s8[4194304]{0:T(1024)(128)(4,1)S(1)} async-done(((s8[27262976]{0:T(1024)(128)(4,1)}), s8[4194304]{0:T(1024)(128)(4,1)S(1)}, s32[]{:S(2)}) %slice-start.5) | async-done | bytes 4194328
  37.4 0.6 %slice-done.6 = s8[2097152]{0:T(1024)(128)(4,1)S(1)} async-done(((s8[27262976]{0:T(1024)(128)(4,1)}), s8[2097152]{0:T(1024)(128)(4,1)S(1)}, s32[]{:S(2)}) %slice-start.6) | async-done | bytes 2097176
  38.0 3.4 %down.3.refs_1_ = f32[48,2048]{1,0:T(8,128)S(1)} custom-call(bf16[6656,2048]{1,0:T(8,128)(2,1)S(1)} %bitcast.5, bf16[48,2048]{1,0:T(8,128)(2,1)S(1)} %fusion.1.refs_0_, bf16[48,2048]{1,0:T(8,128)(2,1)S(1)} %collective-permute-done.7.refs_1_), custom_call_target="tpu_custom_call" | custom-call | flops 805306368 | bytes 16777216 | tf_op jit(solution)/shard_map/down/pallas_call | solution.py:248
  41.4 1.6 %collective-permute-done.6 = bf16[48,2560]{1,0:T(8,128)(2,1)S(1)} collective-permute-done((bf16[48,2560]{1,0:T(8,128)(2,1)S(1)}, bf16[48,2560]{1,0:T(8,128)(2,1)S(1)}, u32[]{:S(2)}, u32[]{:S(2)}) %collective-permute-start.6) | collective-permute-done | bytes 245792 | tf_op jit(solution)/shard_map/ppermute | solution.py:34
  43.2 1.4 %down.4.total = f32[48,2048]{1,0:T(8,128)S(1)} custom-call(bf16[6656,2048]{1,0:T(8,128)(2,1)S(1)} %bitcast.5, bf16[48,1280]{1,0:T(8,128)(2,1)S(1)} %fusion.3.refs_0_, f32[48,2048]{1,0:T(8,128)S(1)} %down.3.refs_1_), custom_call_target="tpu_custom_call" | custom-call | flops 251658240 | bytes 5242880 | tf_op jit(solution)/shard_map/down/pallas_call | solution.py:248
  44.6 1.0 %down.5 = (f32[24,1024]{1,0:T(8,128)S(1)}, bf16[24,1024]{1,0:T(8,128)(2,1)S(1)}, bf16[24,1024]{1,0:T(8,128)(2,1)S(1)}, bf16[24,1024]{1,0:T(8,128)(2,1)S(1)}) custom-call(bf16[6656,2048]{1,0:T(8,128)(2,1)S(1)} %bitcast.5, bf16[48,1280]{1,0:T(8,128)(2,1)S(1)} %collective-permute-done.8.hidden, f32[48,2048]{1,0:T(8,128)S(1)} %down.4.total), custom_call_target="tpu_custom_call" | custom-call | flops 251658240 | bytes 5242880 | tf_op jit(solution)/shard_map/down/pallas_call | solution.py:248
  45.6 2.9 %collective-permute-start.9 = (bf16[24,1024]{1,0:T(8,128)(2,1)S(1)}, bf16[24,1024]{1,0:T(8,128)(2,1)S(1)}, u32[]{:S(2)}, u32[]{:S(2)}) collective-permute-start(bf16[24,1024]{1,0:T(8,128)(2,1)S(1)} %get-tuple-element.28), channel_id=1, source_target_pairs={{0,12},{4,8},{8,4},{12,0},{1,13},{5,9},{9,5},{13,1},{2,14},{6,10},... | collective-permute-start | bytes 147464 | tf_op jit(solution)/shard_map/ppermute | solution.py:269
  48.5 0.2 collective-permute-start.10
  48.7 1.4 %collective-permute-start.11 = (bf16[24,1024]{1,0:T(8,128)(2,1)S(1)}, bf16[24,1024]{1,0:T(8,128)(2,1)S(1)}, u32[]{:S(2)}, u32[]{:S(2)}) collective-permute-start(bf16[24,1024]{1,0:T(8,128)(2,1)S(1)} %get-tuple-element.30), channel_id=1, source_target_pairs={{0,4},{4,0},{8,12},{12,8},{1,5},{5,1},{9,13},{13,9},{2,6},{6,2},{1... | collective-permute-start | bytes 147464 | tf_op jit(solution)/shard_map/ppermute | solution.py:269
  50.1 1.9 %collective-permute-done.9 = bf16[24,1024]{1,0:T(8,128)(2,1)S(1)} collective-permute-done((bf16[24,1024]{1,0:T(8,128)(2,1)S(1)}, bf16[24,1024]{1,0:T(8,128)(2,1)S(1)}, u32[]{:S(2)}, u32[]{:S(2)}) %collective-permute-start.9) | collective-permute-done | bytes 49184 | tf_op jit(solution)/shard_map/ppermute | solution.py:269
  52.0 2.0 %collective-permute-done.10 = bf16[24,1024]{1,0:T(8,128)(2,1)S(1)} collective-permute-done((bf16[24,1024]{1,0:T(8,128)(2,1)S(1)}, bf16[24,1024]{1,0:T(8,128)(2,1)S(1)}, u32[]{:S(2)}, u32[]{:S(2)}) %collective-permute-start.10) | collective-permute-done | bytes 49184 | tf_op jit(solution)/shard_map/ppermute | solution.py:269
  54.2 0.6 %copy.7 = bf16[2,8,2,1024]{3,1,2,0:T(8,128)(2,1)} copy(bf16[2,8,2,1024]{3,2,1,0:T(2,128)(2,1)S(1)} %bitcast.7) | data formatting | bytes 131072
  (41 shorter events, 1.0 us)
Async XLA Ops:
  0.0 8.2 %copy-start.1 = (bf16[12,2048]{1,0:T(8,128)(2,1)S(1)}, bf16[12,2048]{1,0:T(8,128)(2,1)}, u32[]{:S(2)}) copy-start(bf16[12,2048]{1,0:T(8,128)(2,1)} %param.4) | copy-start | bytes 147460
  0.0 11.0 %copy-start = (bf16[2048,6656]{1,0:T(8,128)(2,1)S(1)}, bf16[2048,6656]{1,0:T(8,128)(2,1)}, u32[]{:S(2)}) copy-start(bf16[2048,6656]{1,0:T(8,128)(2,1)} %gate.3) | copy-start | bytes 81788928
  0.0 8.2 %collective-permute-start = (bf16[12,2048]{1,0:T(8,128)(2,1)}, bf16[12,2048]{1,0:T(8,128)(2,1)S(1)}, u32[]{:S(2)}, u32[]{:S(2)}) collective-permute-start(bf16[12,2048]{1,0:T(8,128)(2,1)} %param.4), channel_id=1, source_target_pairs={{0,12},{4,8},{8,4},{12,0},{1,13},{5,9},{9,5},{13,1},{2,14},{6,10},... | collective-permute-start | bytes 147464 | tf_op jit(solution)/shard_map/ppermute | solution.py:269
  5.1 5.9 %collective-permute-start.2 = (bf16[12,2048]{1,0:T(8,128)(2,1)}, bf16[12,2048]{1,0:T(8,128)(2,1)S(1)}, u32[]{:S(2)}, u32[]{:S(2)}) collective-permute-start(bf16[12,2048]{1,0:T(8,128)(2,1)} %param.4), channel_id=1, source_target_pairs={{0,4},{4,0},{8,12},{12,8},{1,5},{5,1},{9,13},{13,9},{2,6},{6,2},{1... | collective-permute-start | bytes 147464 | tf_op jit(solution)/shard_map/ppermute | solution.py:269
  5.1 5.8 %collective-permute-start.1 = (bf16[12,2048]{1,0:T(8,128)(2,1)}, bf16[12,2048]{1,0:T(8,128)(2,1)S(1)}, u32[]{:S(2)}, u32[]{:S(2)}) collective-permute-start(bf16[12,2048]{1,0:T(8,128)(2,1)} %param.4), channel_id=1, source_target_pairs={{0,8},{4,12},{8,0},{12,4},{1,9},{5,13},{9,1},{13,5},{2,10},{6,14},... | collective-permute-start | bytes 147464 | tf_op jit(solution)/shard_map/ppermute | solution.py:269
  21.0 1.8 %collective-permute-start.3 = (bf16[48,4096]{1,0:T(8,128)(2,1)S(1)}, bf16[48,4096]{1,0:T(8,128)(2,1)S(1)}, u32[]{:S(2)}, u32[]{:S(2)}) collective-permute-start(bf16[48,4096]{1,0:T(8,128)(2,1)S(1)} %get-tuple-element.19), channel_id=1, source_target_pairs={{0,1},{1,0},{2,3},{3,2},{4,5},{5,4},{6,7},{7,6},{8,9},{9,8},{10,11... | collective-permute-start | bytes 1179656 | tf_op jit(solution)/shard_map/ppermute | solution.py:34
  22.8 13.4 %slice-start = ((s8[27262976]{0:T(1024)(128)(4,1)}), s8[4194304]{0:T(1024)(128)(4,1)S(1)}, s32[]{:S(2)}) async-start(s8[27262976]{0:T(1024)(128)(4,1)} %bitcast.4), calls=%async_computation | async-start | bytes 8388608
  22.9 13.3 %slice-start.1 = ((s8[27262976]{0:T(1024)(128)(4,1)}), s8[4194304]{0:T(1024)(128)(4,1)S(1)}, s32[]{:S(2)}) async-start(s8[27262976]{0:T(1024)(128)(4,1)} %bitcast.4), calls=%async_computation.1 | async-start | bytes 8388608
  22.9 13.2 %slice-start.2 = ((s8[27262976]{0:T(1024)(128)(4,1)}), s8[4194304]{0:T(1024)(128)(4,1)S(1)}, s32[]{:S(2)}) async-start(s8[27262976]{0:T(1024)(128)(4,1)} %bitcast.4), calls=%async_computation.2 | async-start | bytes 8388608
  22.9 13.2 %slice-start.3 = ((s8[27262976]{0:T(1024)(128)(4,1)}), s8[4194304]{0:T(1024)(128)(4,1)S(1)}, s32[]{:S(2)}) async-start(s8[27262976]{0:T(1024)(128)(4,1)} %bitcast.4), calls=%async_computation.3 | async-start | bytes 8388608
  22.9 13.3 %slice-start.4 = ((s8[27262976]{0:T(1024)(128)(4,1)}), s8[4194304]{0:T(1024)(128)(4,1)S(1)}, s32[]{:S(2)}) async-start(s8[27262976]{0:T(1024)(128)(4,1)} %bitcast.4), calls=%async_computation.4 | async-start | bytes 8388608
  22.9 14.5 %slice-start.5 = ((s8[27262976]{0:T(1024)(128)(4,1)}), s8[4194304]{0:T(1024)(128)(4,1)S(1)}, s32[]{:S(2)}) async-start(s8[27262976]{0:T(1024)(128)(4,1)} %bitcast.4), calls=%async_computation.5 | async-start | bytes 8388608
  22.9 15.1 %slice-start.6 = ((s8[27262976]{0:T(1024)(128)(4,1)}), s8[2097152]{0:T(1024)(128)(4,1)S(1)}, s32[]{:S(2)}) async-start(s8[27262976]{0:T(1024)(128)(4,1)} %bitcast.4), calls=%async_computation.6 | async-start | bytes 4194304
  22.9 11.2 %collective-permute-start.4 = (bf16[48,4096]{1,0:T(8,128)(2,1)S(1)}, bf16[48,4096]{1,0:T(8,128)(2,1)S(1)}, u32[]{:S(2)}, u32[]{:S(2)}) collective-permute-start(bf16[48,4096]{1,0:T(8,128)(2,1)S(1)} %fusion), channel_id=1, source_target_pairs={{0,2},{2,0},{1,3},{3,1},{4,6},{6,4},{5,7},{7,5},{8,10},{10,8},{9,1... | collective-permute-start | bytes 1179656 | tf_op jit(solution)/shard_map/ppermute | solution.py:34
  33.2 1.6 %collective-permute-start.5 = (bf16[48,2560]{1,0:T(8,128)(2,1)S(1)}, bf16[48,2560]{1,0:T(8,128)(2,1)S(1)}, u32[]{:S(2)}, u32[]{:S(2)}) collective-permute-start(bf16[48,2560]{1,0:T(8,128)(2,1)S(1)} %get-tuple-element.23), channel_id=1, source_target_pairs={{0,1},{1,0},{2,3},{3,2},{4,5},{5,4},{6,7},{7,6},{8,9},{9,8},{10,11... | collective-permute-start | bytes 737288 | tf_op jit(solution)/shard_map/ppermute | solution.py:34
  34.4 1.7 %collective-permute-start.7 = (bf16[48,2048]{1,0:T(8,128)(2,1)S(1)}, bf16[48,2048]{1,0:T(8,128)(2,1)S(1)}, u32[]{:S(2)}, u32[]{:S(2)}) collective-permute-start(bf16[48,2048]{1,0:T(8,128)(2,1)S(1)} %fusion.1.refs_0_), channel_id=1, source_target_pairs={{0,1},{1,0},{2,3},{3,2},{4,5},{5,4},{6,7},{7,6},{8,9},{9,8},{10,11... | collective-permute-start | bytes 589832 | tf_op jit(solution)/shard_map/ppermute | solution.py:34
  34.8 8.1 %collective-permute-start.6 = (bf16[48,2560]{1,0:T(8,128)(2,1)S(1)}, bf16[48,2560]{1,0:T(8,128)(2,1)S(1)}, u32[]{:S(2)}, u32[]{:S(2)}) collective-permute-start(bf16[48,2560]{1,0:T(8,128)(2,1)S(1)} %fusion.2), channel_id=1, source_target_pairs={{0,2},{2,0},{1,3},{3,1},{4,6},{6,4},{5,7},{7,5},{8,10},{10,8},{9,1... | collective-permute-start | bytes 737288 | tf_op jit(solution)/shard_map/ppermute | solution.py:34
  43.1 1.5 %collective-permute-start.8 = (bf16[48,1280]{1,0:T(8,128)(2,1)S(1)}, bf16[48,1280]{1,0:T(8,128)(2,1)S(1)}, u32[]{:S(2)}, u32[]{:S(2)}) collective-permute-start(bf16[48,1280]{1,0:T(8,128)(2,1)S(1)} %fusion.3.refs_0_), channel_id=1, source_target_pairs={{0,1},{1,0},{2,3},{3,2},{4,5},{5,4},{6,7},{7,6},{8,9},{9,8},{10,11... | collective-permute-start | bytes 368648 | tf_op jit(solution)/shard_map/ppermute | solution.py:34
  45.6 6.4 %collective-permute-start.9 = (bf16[24,1024]{1,0:T(8,128)(2,1)S(1)}, bf16[24,1024]{1,0:T(8,128)(2,1)S(1)}, u32[]{:S(2)}, u32[]{:S(2)}) collective-permute-start(bf16[24,1024]{1,0:T(8,128)(2,1)S(1)} %get-tuple-element.28), channel_id=1, source_target_pairs={{0,12},{4,8},{8,4},{12,0},{1,13},{5,9},{9,5},{13,1},{2,14},{6,10},... | collective-permute-start | bytes 147464 | tf_op jit(solution)/shard_map/ppermute | solution.py:269
  48.5 5.4 %collective-permute-start.10 = (bf16[24,1024]{1,0:T(8,128)(2,1)S(1)}, bf16[24,1024]{1,0:T(8,128)(2,1)S(1)}, u32[]{:S(2)}, u32[]{:S(2)}) collective-permute-start(bf16[24,1024]{1,0:T(8,128)(2,1)S(1)} %get-tuple-element.29), channel_id=1, source_target_pairs={{0,8},{4,12},{8,0},{12,4},{1,9},{5,13},{9,1},{13,5},{2,10},{6,14},... | collective-permute-start | bytes 147464 | tf_op jit(solution)/shard_map/ppermute | solution.py:269
  48.7 5.3 %collective-permute-start.11 = (bf16[24,1024]{1,0:T(8,128)(2,1)S(1)}, bf16[24,1024]{1,0:T(8,128)(2,1)S(1)}, u32[]{:S(2)}, u32[]{:S(2)}) collective-permute-start(bf16[24,1024]{1,0:T(8,128)(2,1)S(1)} %get-tuple-element.30), channel_id=1, source_target_pairs={{0,4},{4,0},{8,12},{12,8},{1,5},{5,1},{9,13},{13,9},{2,6},{6,2},{1... | collective-permute-start | bytes 147464 | tf_op jit(solution)/shard_map/ppermute | solution.py:269

commit v13 on v12

--- a/solution.py
+++ b/solution.py
@@ -35,6 +35,7 @@
 
 
 BLOCK = 256
+WIDE = 1024
 VMEM = pl.BlockSpec(memory_space=pltpu.VMEM)
 ANY = pl.BlockSpec(memory_space=pl.ANY)
 HBM = pl.BlockSpec(memory_space=pltpu.HBM)
@@ -68,38 +69,38 @@
 
 def sums_kernel(first, tokens, gate, up, after, send, keep, held, sems):
     half = send.shape[1] // 2
-    blocks = half // BLOCK
     core = lax.axis_index("sub")
 
-    def columns(step):
-        mine = jnp.int32(step >= blocks)
-        side = jnp.where(mine == 1, core, 1 - core)
-        unit = first + side * half + (step - mine * blocks) * BLOCK
-        return pl.ds(pl.multiple_of(unit, BLOCK), BLOCK)
-
-    def block_of(step):
-        return pl.ds(pl.multiple_of(step * BLOCK, BLOCK), BLOCK)
-
-    def copy(step):
-        return pltpu.make_async_copy(up.at[:, columns(step)], held.at[:, block_of(step)], sems.at[step])
-
-    for step in range(2 * blocks):
-        copy(jnp.int32(step)).start()
-
-    for side, out in enumerate((send, keep)):
-
-        @pl.loop(0, blocks)
-        def _(block):
-            out[:, block_of(block)] = jnp.dot(
-                tokens[...], gate[:, columns(side * blocks + block)], preferred_element_type=F32
+    def side_of(place):
+        return first + jnp.where(core == place, 1, 0) * half
+
+    copies = [
+        [
+            pltpu.make_async_copy(
+                up.at[:, pl.ds(pl.multiple_of(side_of(place) + at, BLOCK), BLOCK)],
+                held.at[:, pl.ds(place * half + at, BLOCK)],
+                sems.at[place * (half // BLOCK) + at // BLOCK],
+            )
+            for at in range(0, half, BLOCK)
+        ]
+        for place in range(2)
+    ]
+    for copy in copies[0] + copies[1]:
+        copy.start()
+
+    for place, out in enumerate((send, keep)):
+        for at in range(0, half, WIDE):
+            wide = min(WIDE, half - at)
+            columns = pl.ds(pl.multiple_of(side_of(place) + at, BLOCK), wide)
+            out[:, pl.ds(at, wide)] = jnp.dot(
+                tokens[...], gate[:, columns], preferred_element_type=F32
             ).astype(out.dtype)
-
-        @pl.loop(0, blocks)
-        def _(block):
-            step = side * blocks + block
-            copy(step).wait()
-            out[:, block_of(blocks + block)] = jnp.dot(
-                tokens[...], held[:, block_of(step)], preferred_element_type=F32
+        for at in range(0, half, WIDE):
+            wide = min(WIDE, half - at)
+            for copy in copies[place][at // BLOCK : (at + wide) // BLOCK]:
+                copy.wait()
+            out[:, pl.ds(half + at, wide)] = jnp.dot(
+                tokens[...], held[:, pl.ds(place * half + at, wide)], preferred_element_type=F32
             ).astype(out.dtype)
 
 

time: 55 us -> 53.7 us (0.976)
  Pallas kernels: 24.5 us -> 23.2 us
    pallas_call x1, Pallas kernels: 9.99 us -> 8.7 us  [sums(): pl.pallas_call(functools.partial(sums_kernel, first), out_shape=(jax.Shap...]
where the time goes in v13:
time: 53.7 us; the launch traced here: 53.5 us
  Pallas kernels  23.2 us (43%)
  waiting for transfers between devices  13.5 us (25%)
  starting transfers between devices  13.3 us (25%)
  local copies, waits for them, and re-layouts  2.67 us (5%)
  other arithmetic  0.64 us (1%)
    ppermute x6, starting transfers between devices, across(): return lax.ppermute(x, 'wide', [(i, i ^ apart) for i in range(4)])  10.1 us
    ppermute x6, waiting for transfers between devices, across(): return lax.ppermute(x, 'wide', [(i, i ^ apart) for i in range(4)])  9.05 us
    pallas_call x1, Pallas kernels, stream_sums(): pl.pallas_call(functools.partial(stream_kernel, first, steps), out_shape=...  8.71 us
    pallas_call x1, Pallas kernels, sums(): pl.pallas_call(functools.partial(sums_kernel, first), out_shape=(jax.Shap...  8.7 us
    pallas_call x3, Pallas kernels, down(): pl.pallas_call(functools.partial(kernel, chunk[0], half, sides), out_shap...  5.77 us
    ppermute x6, waiting for transfers between devices, swap(): return lax.ppermute(x, axis, [(0, 1), (1, 0)])  4.46 us
    ppermute x6, starting transfers between devices, swap(): return lax.ppermute(x, axis, [(0, 1), (1, 0)])  3.12 us
    unnamed x20, local copies, waits for them, and re-layouts  2.6 us
  transfers between devices with their start and end apart: 12, of which 8 were waited for; matrix products, arithmetic and copies ran while one was open for 1% of the time, Pallas kernels for 25%

profile of v13, /device:TPU:0, one launch (start us, length us, event | category | flops | bytes accessed | tf_op | source)
XLA Modules:
  0.0 53.5 jit_solution(12474982594739813475)
XLA Ops:
  0.0 5.0 %collective-permute-start = (bf16[12,2048]{1,0:T(8,128)(2,1)}, bf16[12,2048]{1,0:T(8,128)(2,1)S(1)}, u32[]{:S(2)}, u32[]{:S(2)}) collective-permute-start(bf16[12,2048]{1,0:T(8,128)(2,1)} %param.4), channel_id=1, source_target_pairs={{0,12},{4,8},{8,4},{12,0},{1,13},{5,9},{9,5},{13,1},{2,14},{6,10},... | collective-permute-start | bytes 147464 | tf_op jit(solution)/shard_map/ppermute | solution.py:270
  5.1 0.6 %collective-permute-start.1 = (bf16[12,2048]{1,0:T(8,128)(2,1)}, bf16[12,2048]{1,0:T(8,128)(2,1)S(1)}, u32[]{:S(2)}, u32[]{:S(2)}) collective-permute-start(bf16[12,2048]{1,0:T(8,128)(2,1)} %param.4), channel_id=1, source_target_pairs={{0,8},{4,12},{8,0},{12,4},{1,9},{5,13},{9,1},{13,5},{2,10},{6,14},... | collective-permute-start | bytes 147464 | tf_op jit(solution)/shard_map/ppermute | solution.py:270
  5.7 2.5 %collective-permute-done = bf16[12,2048]{1,0:T(8,128)(2,1)S(1)} collective-permute-done((bf16[12,2048]{1,0:T(8,128)(2,1)}, bf16[12,2048]{1,0:T(8,128)(2,1)S(1)}, u32[]{:S(2)}, u32[]{:S(2)}) %collective-permute-start) | collective-permute-done | bytes 49184 | tf_op jit(solution)/shard_map/ppermute | solution.py:270
  8.3 2.6 %collective-permute-done.1 = bf16[12,2048]{1,0:T(8,128)(2,1)S(1)} collective-permute-done((bf16[12,2048]{1,0:T(8,128)(2,1)}, bf16[12,2048]{1,0:T(8,128)(2,1)S(1)}, u32[]{:S(2)}, u32[]{:S(2)}) %collective-permute-start.1) | collective-permute-done | bytes 49184 | tf_op jit(solution)/shard_map/ppermute | solution.py:270
  11.0 8.7 %sums.1 = (bf16[48,4096]{1,0:T(8,128)(2,1)S(1)}, f32[48,4096]{1,0:T(8,128)S(1)}) custom-call(bf16[48,2048]{1,0:T(8,128)(2,1)S(1)} %pad_maximum_fusion.tokens, bf16[2048,6656]{1,0:T(8,128)(2,1)S(1)} %copy-done, bf16[2048,6656]{1,0:T(8,128)(2,1)} %up.3, f32[8,128]{1,0:T(8,128)S(1)} %beside.1.after), custom_call_target="tpu_custom_call" | custom-call | flops 1610612736 | bytes 33554432 | tf_op jit(solution)/shard_map/sums/pallas_call | solution.py:110
  19.8 1.7 %collective-permute-done.3 = bf16[48,4096]{1,0:T(8,128)(2,1)S(1)} collective-permute-done((bf16[48,4096]{1,0:T(8,128)(2,1)S(1)}, bf16[48,4096]{1,0:T(8,128)(2,1)S(1)}, u32[]{:S(2)}, u32[]{:S(2)}) %collective-permute-start.3) | collective-permute-done | bytes 393248 | tf_op jit(solution)/shard_map/ppermute | solution.py:34
  21.6 1.6 %collective-permute-start.4 = (bf16[48,4096]{1,0:T(8,128)(2,1)S(1)}, bf16[48,4096]{1,0:T(8,128)(2,1)S(1)}, u32[]{:S(2)}, u32[]{:S(2)}) collective-permute-start(bf16[48,4096]{1,0:T(8,128)(2,1)S(1)} %fusion), channel_id=1, source_target_pairs={{0,2},{2,0},{1,3},{3,1},{4,6},{6,4},{5,7},{7,5},{8,10},{10,8},{9,1... | collective-permute-start | bytes 1179656 | tf_op jit(solution)/shard_map/ppermute | solution.py:34
  23.2 8.7 %stream_sums.1 = (bf16[48,2560]{1,0:T(8,128)(2,1)S(1)}, f32[48,2560]{1,0:T(8,128)S(1)}) custom-call(bf16[48,2048]{1,0:T(8,128)(2,1)S(1)} %pad_maximum_fusion.tokens, bf16[2048,6656]{1,0:T(8,128)(2,1)} %gate.3, bf16[2048,6656]{1,0:T(8,128)(2,1)} %up.3), custom_call_target="tpu_custom_call" | custom-call | flops 1006632960 | bytes 20971520 | tf_op jit(solution)/shard_map/stream_sums/pallas_call | solution.py:184
  32.0 0.9 %collective-permute-done.4 = bf16[48,4096]{1,0:T(8,128)(2,1)S(1)} collective-permute-done((bf16[48,4096]{1,0:T(8,128)(2,1)S(1)}, bf16[48,4096]{1,0:T(8,128)(2,1)S(1)}, u32[]{:S(2)}, u32[]{:S(2)}) %collective-permute-start.4) | collective-permute-done | bytes 393248 | tf_op jit(solution)/shard_map/ppermute | solution.py:34
  32.9 0.1 convert_add_fusion
  33.2 0.3 collective-permute-done.5
  33.5 1.3 %collective-permute-start.6 = (bf16[48,2560]{1,0:T(8,128)(2,1)S(1)}, bf16[48,2560]{1,0:T(8,128)(2,1)S(1)}, u32[]{:S(2)}, u32[]{:S(2)}) collective-permute-start(bf16[48,2560]{1,0:T(8,128)(2,1)S(1)} %fusion.2), channel_id=1, source_target_pairs={{0,2},{2,0},{1,3},{3,1},{4,6},{6,4},{5,7},{7,5},{8,10},{10,8},{9,1... | collective-permute-start | bytes 737288 | tf_op jit(solution)/shard_map/ppermute | solution.py:34
  34.9 1.2 %slice-done.5 = s8[4194304]{0:T(1024)(128)(4,1)S(1)} async-done(((s8[27262976]{0:T(1024)(128)(4,1)}), s8[4194304]{0:T(1024)(128)(4,1)S(1)}, s32[]{:S(2)}) %slice-start.5) | async-done | bytes 4194328
  36.1 0.6 %slice-done.6 = s8[2097152]{0:T(1024)(128)(4,1)S(1)} async-done(((s8[27262976]{0:T(1024)(128)(4,1)}), s8[2097152]{0:T(1024)(128)(4,1)S(1)}, s32[]{:S(2)}) %slice-start.6) | async-done | bytes 2097176
  36.7 3.4 %down.3.refs_1_ = f32[48,2048]{1,0:T(8,128)S(1)} custom-call(bf16[6656,2048]{1,0:T(8,128)(2,1)S(1)} %bitcast.5, bf16[48,2048]{1,0:T(8,128)(2,1)S(1)} %fusion.1.refs_0_, bf16[48,2048]{1,0:T(8,128)(2,1)S(1)} %collective-permute-done.7.refs_1_), custom_call_target="tpu_custom_call" | custom-call | flops 805306368 | bytes 16777216 | tf_op jit(solution)/shard_map/down/pallas_call | solution.py:249
  40.1 1.6 %collective-permute-done.6 = bf16[48,2560]{1,0:T(8,128)(2,1)S(1)} collective-permute-done((bf16[48,2560]{1,0:T(8,128)(2,1)S(1)}, bf16[48,2560]{1,0:T(8,128)(2,1)S(1)}, u32[]{:S(2)}, u32[]{:S(2)}) %collective-permute-start.6) | collective-permute-done | bytes 245792 | tf_op jit(solution)/shard_map/ppermute | solution.py:34
  41.9 1.4 %down.4.total = f32[48,2048]{1,0:T(8,128)S(1)} custom-call(bf16[6656,2048]{1,0:T(8,128)(2,1)S(1)} %bitcast.5, bf16[48,1280]{1,0:T(8,128)(2,1)S(1)} %fusion.3.refs_0_, f32[48,2048]{1,0:T(8,128)S(1)} %down.3.refs_1_), custom_call_target="tpu_custom_call" | custom-call | flops 251658240 | bytes 5242880 | tf_op jit(solution)/shard_map/down/pallas_call | solution.py:249
  43.3 1.0 %down.5 = (f32[24,1024]{1,0:T(8,128)S(1)}, bf16[24,1024]{1,0:T(8,128)(2,1)S(1)}, bf16[24,1024]{1,0:T(8,128)(2,1)S(1)}, bf16[24,1024]{1,0:T(8,128)(2,1)S(1)}) custom-call(bf16[6656,2048]{1,0:T(8,128)(2,1)S(1)} %bitcast.5, bf16[48,1280]{1,0:T(8,128)(2,1)S(1)} %collective-permute-done.8.hidden, f32[48,2048]{1,0:T(8,128)S(1)} %down.4.total), custom_call_target="tpu_custom_call" | custom-call | flops 251658240 | bytes 5242880 | tf_op jit(solution)/shard_map/down/pallas_call | solution.py:249
  44.3 2.9 %collective-permute-start.9 = (bf16[24,1024]{1,0:T(8,128)(2,1)S(1)}, bf16[24,1024]{1,0:T(8,128)(2,1)S(1)}, u32[]{:S(2)}, u32[]{:S(2)}) collective-permute-start(bf16[24,1024]{1,0:T(8,128)(2,1)S(1)} %get-tuple-element.28), channel_id=1, source_target_pairs={{0,12},{4,8},{8,4},{12,0},{1,13},{5,9},{9,5},{13,1},{2,14},{6,10},... | collective-permute-start | bytes 147464 | tf_op jit(solution)/shard_map/ppermute | solution.py:270
  47.3 0.2 collective-permute-start.10
  47.4 1.4 %collective-permute-start.11 = (bf16[24,1024]{1,0:T(8,128)(2,1)S(1)}, bf16[24,1024]{1,0:T(8,128)(2,1)S(1)}, u32[]{:S(2)}, u32[]{:S(2)}) collective-permute-start(bf16[24,1024]{1,0:T(8,128)(2,1)S(1)} %get-tuple-element.30), channel_id=1, source_target_pairs={{0,4},{4,0},{8,12},{12,8},{1,5},{5,1},{9,13},{13,9},{2,6},{6,2},{1... | collective-permute-start | bytes 147464 | tf_op jit(solution)/shard_map/ppermute | solution.py:270
  48.8 1.9 %collective-permute-done.9 = bf16[24,1024]{1,0:T(8,128)(2,1)S(1)} collective-permute-done((bf16[24,1024]{1,0:T(8,128)(2,1)S(1)}, bf16[24,1024]{1,0:T(8,128)(2,1)S(1)}, u32[]{:S(2)}, u32[]{:S(2)}) %collective-permute-start.9) | collective-permute-done | bytes 49184 | tf_op jit(solution)/shard_map/ppermute | solution.py:270
  50.7 2.0 %collective-permute-done.10 = bf16[24,1024]{1,0:T(8,128)(2,1)S(1)} collective-permute-done((bf16[24,1024]{1,0:T(8,128)(2,1)S(1)}, bf16[24,1024]{1,0:T(8,128)(2,1)S(1)}, u32[]{:S(2)}, u32[]{:S(2)}) %collective-permute-start.10) | collective-permute-done | bytes 49184 | tf_op jit(solution)/shard_map/ppermute | solution.py:270
  52.9 0.6 %copy.7 = bf16[2,8,2,1024]{3,1,2,0:T(8,128)(2,1)} copy(bf16[2,8,2,1024]{3,2,1,0:T(2,128)(2,1)S(1)} %bitcast.7) | data formatting | bytes 131072
  (41 shorter events, 1.0 us)
Async XLA Ops:
  0.0 8.2 %copy-start.1 = (bf16[12,2048]{1,0:T(8,128)(2,1)S(1)}, bf16[12,2048]{1,0:T(8,128)(2,1)}, u32[]{:S(2)}) copy-start(bf16[12,2048]{1,0:T(8,128)(2,1)} %param.4) | copy-start | bytes 147460
  0.0 11.0 %copy-start = (bf16[2048,6656]{1,0:T(8,128)(2,1)S(1)}, bf16[2048,6656]{1,0:T(8,128)(2,1)}, u32[]{:S(2)}) copy-start(bf16[2048,6656]{1,0:T(8,128)(2,1)} %gate.3) | copy-start | bytes 81788928
  0.0 8.2 %collective-permute-start = (bf16[12,2048]{1,0:T(8,128)(2,1)}, bf16[12,2048]{1,0:T(8,128)(2,1)S(1)}, u32[]{:S(2)}, u32[]{:S(2)}) collective-permute-start(bf16[12,2048]{1,0:T(8,128)(2,1)} %param.4), channel_id=1, source_target_pairs={{0,12},{4,8},{8,4},{12,0},{1,13},{5,9},{9,5},{13,1},{2,14},{6,10},... | collective-permute-start | bytes 147464 | tf_op jit(solution)/shard_map/ppermute | solution.py:270
  5.1 5.9 %collective-permute-start.2 = (bf16[12,2048]{1,0:T(8,128)(2,1)}, bf16[12,2048]{1,0:T(8,128)(2,1)S(1)}, u32[]{:S(2)}, u32[]{:S(2)}) collective-permute-start(bf16[12,2048]{1,0:T(8,128)(2,1)} %param.4), channel_id=1, source_target_pairs={{0,4},{4,0},{8,12},{12,8},{1,5},{5,1},{9,13},{13,9},{2,6},{6,2},{1... | collective-permute-start | bytes 147464 | tf_op jit(solution)/shard_map/ppermute | solution.py:270
  5.1 5.8 %collective-permute-start.1 = (bf16[12,2048]{1,0:T(8,128)(2,1)}, bf16[12,2048]{1,0:T(8,128)(2,1)S(1)}, u32[]{:S(2)}, u32[]{:S(2)}) collective-permute-start(bf16[12,2048]{1,0:T(8,128)(2,1)} %param.4), channel_id=1, source_target_pairs={{0,8},{4,12},{8,0},{12,4},{1,9},{5,13},{9,1},{13,5},{2,10},{6,14},... | collective-permute-start | bytes 147464 | tf_op jit(solution)/shard_map/ppermute | solution.py:270
  19.7 1.8 %collective-permute-start.3 = (bf16[48,4096]{1,0:T(8,128)(2,1)S(1)}, bf16[48,4096]{1,0:T(8,128)(2,1)S(1)}, u32[]{:S(2)}, u32[]{:S(2)}) collective-permute-start(bf16[48,4096]{1,0:T(8,128)(2,1)S(1)} %get-tuple-element.19), channel_id=1, source_target_pairs={{0,1},{1,0},{2,3},{3,2},{4,5},{5,4},{6,7},{7,6},{8,9},{9,8},{10,11... | collective-permute-start | bytes 1179656 | tf_op jit(solution)/shard_map/ppermute | solution.py:34
  21.5 13.4 %slice-start = ((s8[27262976]{0:T(1024)(128)(4,1)}), s8[4194304]{0:T(1024)(128)(4,1)S(1)}, s32[]{:S(2)}) async-start(s8[27262976]{0:T(1024)(128)(4,1)} %bitcast.4), calls=%async_computation | async-start | bytes 8388608
  21.6 13.3 %slice-start.1 = ((s8[27262976]{0:T(1024)(128)(4,1)}), s8[4194304]{0:T(1024)(128)(4,1)S(1)}, s32[]{:S(2)}) async-start(s8[27262976]{0:T(1024)(128)(4,1)} %bitcast.4), calls=%async_computation.1 | async-start | bytes 8388608
  21.6 13.3 %slice-start.2 = ((s8[27262976]{0:T(1024)(128)(4,1)}), s8[4194304]{0:T(1024)(128)(4,1)S(1)}, s32[]{:S(2)}) async-start(s8[27262976]{0:T(1024)(128)(4,1)} %bitcast.4), calls=%async_computation.2 | async-start | bytes 8388608
  21.6 13.3 %slice-start.3 = ((s8[27262976]{0:T(1024)(128)(4,1)}), s8[4194304]{0:T(1024)(128)(4,1)S(1)}, s32[]{:S(2)}) async-start(s8[27262976]{0:T(1024)(128)(4,1)} %bitcast.4), calls=%async_computation.3 | async-start | bytes 8388608
  21.6 13.3 %slice-start.4 = ((s8[27262976]{0:T(1024)(128)(4,1)}), s8[4194304]{0:T(1024)(128)(4,1)S(1)}, s32[]{:S(2)}) async-start(s8[27262976]{0:T(1024)(128)(4,1)} %bitcast.4), calls=%async_computation.4 | async-start | bytes 8388608
  21.6 14.5 %slice-start.5 = ((s8[27262976]{0:T(1024)(128)(4,1)}), s8[4194304]{0:T(1024)(128)(4,1)S(1)}, s32[]{:S(2)}) async-start(s8[27262976]{0:T(1024)(128)(4,1)} %bitcast.4), calls=%async_computation.5 | async-start | bytes 8388608
  21.6 15.1 %slice-start.6 = ((s8[27262976]{0:T(1024)(128)(4,1)}), s8[2097152]{0:T(1024)(128)(4,1)S(1)}, s32[]{:S(2)}) async-start(s8[27262976]{0:T(1024)(128)(4,1)} %bitcast.4), calls=%async_computation.6 | async-start | bytes 4194304
  21.6 11.2 %collective-permute-start.4 = (bf16[48,4096]{1,0:T(8,128)(2,1)S(1)}, bf16[48,4096]{1,0:T(8,128)(2,1)S(1)}, u32[]{:S(2)}, u32[]{:S(2)}) collective-permute-start(bf16[48,4096]{1,0:T(8,128)(2,1)S(1)} %fusion), channel_id=1, source_target_pairs={{0,2},{2,0},{1,3},{3,1},{4,6},{6,4},{5,7},{7,5},{8,10},{10,8},{9,1... | collective-permute-start | bytes 1179656 | tf_op jit(solution)/shard_map/ppermute | solution.py:34
  31.9 1.6 %collective-permute-start.5 = (bf16[48,2560]{1,0:T(8,128)(2,1)S(1)}, bf16[48,2560]{1,0:T(8,128)(2,1)S(1)}, u32[]{:S(2)}, u32[]{:S(2)}) collective-permute-start(bf16[48,2560]{1,0:T(8,128)(2,1)S(1)} %get-tuple-element.23), channel_id=1, source_target_pairs={{0,1},{1,0},{2,3},{3,2},{4,5},{5,4},{6,7},{7,6},{8,9},{9,8},{10,11... | collective-permute-start | bytes 737288 | tf_op jit(solution)/shard_map/ppermute | solution.py:34
  33.1 1.7 %collective-permute-start.7 = (bf16[48,2048]{1,0:T(8,128)(2,1)S(1)}, bf16[48,2048]{1,0:T(8,128)(2,1)S(1)}, u32[]{:S(2)}, u32[]{:S(2)}) collective-permute-start(bf16[48,2048]{1,0:T(8,128)(2,1)S(1)} %fusion.1.refs_0_), channel_id=1, source_target_pairs={{0,1},{1,0},{2,3},{3,2},{4,5},{5,4},{6,7},{7,6},{8,9},{9,8},{10,11... | collective-permute-start | bytes 589832 | tf_op jit(solution)/shard_map/ppermute | solution.py:34
  33.5 8.1 %collective-permute-start.6 = (bf16[48,2560]{1,0:T(8,128)(2,1)S(1)}, bf16[48,2560]{1,0:T(8,128)(2,1)S(1)}, u32[]{:S(2)}, u32[]{:S(2)}) collective-permute-start(bf16[48,2560]{1,0:T(8,128)(2,1)S(1)} %fusion.2), channel_id=1, source_target_pairs={{0,2},{2,0},{1,3},{3,1},{4,6},{6,4},{5,7},{7,5},{8,10},{10,8},{9,1... | collective-permute-start | bytes 737288 | tf_op jit(solution)/shard_map/ppermute | solution.py:34
  41.8 1.5 %collective-permute-start.8 = (bf16[48,1280]{1,0:T(8,128)(2,1)S(1)}, bf16[48,1280]{1,0:T(8,128)(2,1)S(1)}, u32[]{:S(2)}, u32[]{:S(2)}) collective-permute-start(bf16[48,1280]{1,0:T(8,128)(2,1)S(1)} %fusion.3.refs_0_), channel_id=1, source_target_pairs={{0,1},{1,0},{2,3},{3,2},{4,5},{5,4},{6,7},{7,6},{8,9},{9,8},{10,11... | collective-permute-start | bytes 368648 | tf_op jit(solution)/shard_map/ppermute | solution.py:34
  44.3 6.4 %collective-permute-start.9 = (bf16[24,1024]{1,0:T(8,128)(2,1)S(1)}, bf16[24,1024]{1,0:T(8,128)(2,1)S(1)}, u32[]{:S(2)}, u32[]{:S(2)}) collective-permute-start(bf16[24,1024]{1,0:T(8,128)(2,1)S(1)} %get-tuple-element.28), channel_id=1, source_target_pairs={{0,12},{4,8},{8,4},{12,0},{1,13},{5,9},{9,5},{13,1},{2,14},{6,10},... | collective-permute-start | bytes 147464 | tf_op jit(solution)/shard_map/ppermute | solution.py:270
  47.3 5.4 %collective-permute-start.10 = (bf16[24,1024]{1,0:T(8,128)(2,1)S(1)}, bf16[24,1024]{1,0:T(8,128)(2,1)S(1)}, u32[]{:S(2)}, u32[]{:S(2)}) collective-permute-start(bf16[24,1024]{1,0:T(8,128)(2,1)S(1)} %get-tuple-element.29), channel_id=1, source_target_pairs={{0,8},{4,12},{8,0},{12,4},{1,9},{5,13},{9,1},{13,5},{2,10},{6,14},... | collective-permute-start | bytes 147464 | tf_op jit(solution)/shard_map/ppermute | solution.py:270
  47.4 5.3 %collective-permute-start.11 = (bf16[24,1024]{1,0:T(8,128)(2,1)S(1)}, bf16[24,1024]{1,0:T(8,128)(2,1)S(1)}, u32[]{:S(2)}, u32[]{:S(2)}) collective-permute-start(bf16[24,1024]{1,0:T(8,128)(2,1)S(1)} %get-tuple-element.30), channel_id=1, source_target_pairs={{0,4},{4,0},{8,12},{12,8},{1,5},{5,1},{9,13},{13,9},{2,6},{6,2},{1... | collective-permute-start | bytes 147464 | tf_op jit(solution)/shard_map/ppermute | solution.py:270

commit v14 on v13

--- a/solution.py
+++ b/solution.py
@@ -35,7 +35,7 @@
 
 
 BLOCK = 256
-WIDE = 1024
+WIDE = 512
 VMEM = pl.BlockSpec(memory_space=pltpu.VMEM)
 ANY = pl.BlockSpec(memory_space=pl.ANY)
 HBM = pl.BlockSpec(memory_space=pltpu.HBM)
@@ -210,11 +210,8 @@
 def down_kernel(first, half, sides, weight, *refs):
     hiddens, out = refs[: len(sides)], refs[-1]
     totals = refs[len(sides) : -1]
-    wide = 2 * BLOCK
-
-    @pl.loop(0, out.shape[1] // wide)
-    def _(block):
-        columns = pl.ds(pl.multiple_of(block * wide, wide), wide)
+    for at in range(0, out.shape[1], WIDE):
+        columns = pl.ds(at, WIDE)
         part = partial_sums(first, half, sides, hiddens, weight, columns)
         for total in totals:
             part += total[:, columns]
@@ -223,16 +220,14 @@
 
 def last_down_kernel(first, half, sides, weight, hidden, total, own, *sends):
     rows, columns = own.shape[0] // 2, own.shape[1]
-    wide = 2 * BLOCK
-    for block in range(columns // wide):
-        at = block * wide
+    for at in range(0, columns, WIDE):
         parts = []
         for start in (at, columns + at):
-            part = partial_sums(first, half, sides, [hidden], weight, pl.ds(start, wide))
-            parts.append(part + total[:, pl.ds(start, wide)])
+            part = partial_sums(first, half, sides, [hidden], weight, pl.ds(start, WIDE))
+            parts.append(part + total[:, pl.ds(start, WIDE)])
         for place, out in enumerate((own, *sends)):
             pieces = [part[place * rows : (place + 1) * rows] for part in parts]
-            out[:, pl.ds(at, wide)] = jnp.concatenate(pieces, axis=0).astype(out.dtype)
+            out[:, pl.ds(at, WIDE)] = jnp.concatenate(pieces, axis=0).astype(out.dtype)
 
 
 def down(weight, chunk, sides, hiddens, total=None, last=False):

time: 53.7 us -> 53.5 us (level)
  Pallas kernels: 23.2 us -> 22.4 us
  waiting for transfers between devices: 13.5 us -> 14.1 us
    pallas_call x3, Pallas kernels: 5.77 us -> 5.05 us  [down(): pl.pallas_call(functools.partial(kernel, chunk[0], half, sides), out_shap...]
    ppermute x6, waiting for transfers between devices: 4.46 us -> 5.1 us  [swap(): return lax.ppermute(x, axis, [(0, 1), (1, 0)])]
  transfers between devices with their start and end apart: 12 -> 12, of which waited for: 8 -> 9; matrix products, arithmetic and copies ran while one was open for 1% -> 1% of each run, Pallas kernels for 25% -> 24%
where the time goes in v14:
time: 53.5 us; the launch traced here: 53.3 us
  Pallas kernels  22.4 us (42%)
  waiting for transfers between devices  14.1 us (26%)
  starting transfers between devices  13.3 us (25%)
  local copies, waits for them, and re-layouts  2.67 us (5%)
  other arithmetic  0.64 us (1%)
    ppermute x6, starting transfers between devices, across(): return lax.ppermute(x, 'wide', [(i, i ^ apart) for i in range(4)])  10.1 us
    ppermute x6, waiting for transfers between devices, across(): return lax.ppermute(x, 'wide', [(i, i ^ apart) for i in range(4)])  9.01 us
    pallas_call x1, Pallas kernels, stream_sums(): pl.pallas_call(functools.partial(stream_kernel, first, steps), out_shape=...  8.71 us
    pallas_call x1, Pallas kernels, sums(): pl.pallas_call(functools.partial(sums_kernel, first), out_shape=(jax.Shap...  8.62 us
    ppermute x6, waiting for transfers between devices, swap(): return lax.ppermute(x, axis, [(0, 1), (1, 0)])  5.1 us
    pallas_call x3, Pallas kernels, down(): pl.pallas_call(functools.partial(kernel, chunk[0], half, sides), out_shap...  5.05 us
    ppermute x6, starting transfers between devices, swap(): return lax.ppermute(x, axis, [(0, 1), (1, 0)])  3.12 us
    unnamed x20, local copies, waits for them, and re-layouts  2.6 us
  transfers between devices with their start and end apart: 12, of which 9 were waited for; matrix products, arithmetic and copies ran while one was open for 1% of the time, Pallas kernels for 24%

profile of v14, /device:TPU:0, one launch (start us, length us, event | category | flops | bytes accessed | tf_op | source)
XLA Modules:
  0.0 53.3 jit_solution(3558075972473330961)
XLA Ops:
  0.0 5.0 %collective-permute-start = (bf16[12,2048]{1,0:T(8,128)(2,1)}, bf16[12,2048]{1,0:T(8,128)(2,1)S(1)}, u32[]{:S(2)}, u32[]{:S(2)}) collective-permute-start(bf16[12,2048]{1,0:T(8,128)(2,1)} %param.4), channel_id=1, source_target_pairs={{0,12},{4,8},{8,4},{12,0},{1,13},{5,9},{9,5},{13,1},{2,14},{6,10},... | collective-permute-start | bytes 147464 | tf_op jit(solution)/shard_map/ppermute | solution.py:265
  5.1 0.6 %collective-permute-start.1 = (bf16[12,2048]{1,0:T(8,128)(2,1)}, bf16[12,2048]{1,0:T(8,128)(2,1)S(1)}, u32[]{:S(2)}, u32[]{:S(2)}) collective-permute-start(bf16[12,2048]{1,0:T(8,128)(2,1)} %param.4), channel_id=1, source_target_pairs={{0,8},{4,12},{8,0},{12,4},{1,9},{5,13},{9,1},{13,5},{2,10},{6,14},... | collective-permute-start | bytes 147464 | tf_op jit(solution)/shard_map/ppermute | solution.py:265
  5.7 2.5 %collective-permute-done = bf16[12,2048]{1,0:T(8,128)(2,1)S(1)} collective-permute-done((bf16[12,2048]{1,0:T(8,128)(2,1)}, bf16[12,2048]{1,0:T(8,128)(2,1)S(1)}, u32[]{:S(2)}, u32[]{:S(2)}) %collective-permute-start) | collective-permute-done | bytes 49184 | tf_op jit(solution)/shard_map/ppermute | solution.py:265
  8.3 2.6 %collective-permute-done.1 = bf16[12,2048]{1,0:T(8,128)(2,1)S(1)} collective-permute-done((bf16[12,2048]{1,0:T(8,128)(2,1)}, bf16[12,2048]{1,0:T(8,128)(2,1)S(1)}, u32[]{:S(2)}, u32[]{:S(2)}) %collective-permute-start.1) | collective-permute-done | bytes 49184 | tf_op jit(solution)/shard_map/ppermute | solution.py:265
  11.0 8.6 %sums.1 = (bf16[48,4096]{1,0:T(8,128)(2,1)S(1)}, f32[48,4096]{1,0:T(8,128)S(1)}) custom-call(bf16[48,2048]{1,0:T(8,128)(2,1)S(1)} %pad_maximum_fusion.tokens, bf16[2048,6656]{1,0:T(8,128)(2,1)S(1)} %copy-done, bf16[2048,6656]{1,0:T(8,128)(2,1)} %up.3, f32[8,128]{1,0:T(8,128)S(1)} %beside.1.after), custom_call_target="tpu_custom_call" | custom-call | flops 1610612736 | bytes 33554432 | tf_op jit(solution)/shard_map/sums/pallas_call | solution.py:110
  19.7 1.7 %collective-permute-done.3 = bf16[48,4096]{1,0:T(8,128)(2,1)S(1)} collective-permute-done((bf16[48,4096]{1,0:T(8,128)(2,1)S(1)}, bf16[48,4096]{1,0:T(8,128)(2,1)S(1)}, u32[]{:S(2)}, u32[]{:S(2)}) %collective-permute-start.3) | collective-permute-done | bytes 393248 | tf_op jit(solution)/shard_map/ppermute | solution.py:34
  21.6 1.6 %collective-permute-start.4 = (bf16[48,4096]{1,0:T(8,128)(2,1)S(1)}, bf16[48,4096]{1,0:T(8,128)(2,1)S(1)}, u32[]{:S(2)}, u32[]{:S(2)}) collective-permute-start(bf16[48,4096]{1,0:T(8,128)(2,1)S(1)} %fusion), channel_id=1, source_target_pairs={{0,2},{2,0},{1,3},{3,1},{4,6},{6,4},{5,7},{7,5},{8,10},{10,8},{9,1... | collective-permute-start | bytes 1179656 | tf_op jit(solution)/shard_map/ppermute | solution.py:34
  23.1 8.7 %stream_sums.1 = (bf16[48,2560]{1,0:T(8,128)(2,1)S(1)}, f32[48,2560]{1,0:T(8,128)S(1)}) custom-call(bf16[48,2048]{1,0:T(8,128)(2,1)S(1)} %pad_maximum_fusion.tokens, bf16[2048,6656]{1,0:T(8,128)(2,1)} %gate.3, bf16[2048,6656]{1,0:T(8,128)(2,1)} %up.3), custom_call_target="tpu_custom_call" | custom-call | flops 1006632960 | bytes 20971520 | tf_op jit(solution)/shard_map/stream_sums/pallas_call | solution.py:184
  31.9 0.9 %collective-permute-done.4 = bf16[48,4096]{1,0:T(8,128)(2,1)S(1)} collective-permute-done((bf16[48,4096]{1,0:T(8,128)(2,1)S(1)}, bf16[48,4096]{1,0:T(8,128)(2,1)S(1)}, u32[]{:S(2)}, u32[]{:S(2)}) %collective-permute-start.4) | collective-permute-done | bytes 393248 | tf_op jit(solution)/shard_map/ppermute | solution.py:34
  33.1 0.3 collective-permute-done.5
  33.5 1.3 %collective-permute-start.6 = (bf16[48,2560]{1,0:T(8,128)(2,1)S(1)}, bf16[48,2560]{1,0:T(8,128)(2,1)S(1)}, u32[]{:S(2)}, u32[]{:S(2)}) collective-permute-start(bf16[48,2560]{1,0:T(8,128)(2,1)S(1)} %fusion.2), channel_id=1, source_target_pairs={{0,2},{2,0},{1,3},{3,1},{4,6},{6,4},{5,7},{7,5},{8,10},{10,8},{9,1... | collective-permute-start | bytes 737288 | tf_op jit(solution)/shard_map/ppermute | solution.py:34
  34.9 1.2 %slice-done.5 = s8[4194304]{0:T(1024)(128)(4,1)S(1)} async-done(((s8[27262976]{0:T(1024)(128)(4,1)}), s8[4194304]{0:T(1024)(128)(4,1)S(1)}, s32[]{:S(2)}) %slice-start.5) | async-done | bytes 4194328
  36.0 0.6 %slice-done.6 = s8[2097152]{0:T(1024)(128)(4,1)S(1)} async-done(((s8[27262976]{0:T(1024)(128)(4,1)}), s8[2097152]{0:T(1024)(128)(4,1)S(1)}, s32[]{:S(2)}) %slice-start.6) | async-done | bytes 2097176
  36.6 3.0 %down.3.refs_1_ = f32[48,2048]{1,0:T(8,128)S(1)} custom-call(bf16[6656,2048]{1,0:T(8,128)(2,1)S(1)} %bitcast.5, bf16[48,2048]{1,0:T(8,128)(2,1)S(1)} %fusion.1.refs_0_, bf16[48,2048]{1,0:T(8,128)(2,1)S(1)} %collective-permute-done.7.refs_1_), custom_call_target="tpu_custom_call" | custom-call | flops 805306368 | bytes 16777216 | tf_op jit(solution)/shard_map/down/pallas_call | solution.py:244
  39.7 1.9 %collective-permute-done.6 = bf16[48,2560]{1,0:T(8,128)(2,1)S(1)} collective-permute-done((bf16[48,2560]{1,0:T(8,128)(2,1)S(1)}, bf16[48,2560]{1,0:T(8,128)(2,1)S(1)}, u32[]{:S(2)}, u32[]{:S(2)}) %collective-permute-start.6) | collective-permute-done | bytes 245792 | tf_op jit(solution)/shard_map/ppermute | solution.py:34
  41.8 1.0 %down.4.total = f32[48,2048]{1,0:T(8,128)S(1)} custom-call(bf16[6656,2048]{1,0:T(8,128)(2,1)S(1)} %bitcast.5, bf16[48,1280]{1,0:T(8,128)(2,1)S(1)} %fusion.3.refs_0_, f32[48,2048]{1,0:T(8,128)S(1)} %down.3.refs_1_), custom_call_target="tpu_custom_call" | custom-call | flops 251658240 | bytes 5242880 | tf_op jit(solution)/shard_map/down/pallas_call | solution.py:244
  42.9 0.3 collective-permute-done.8.hidden
  43.1 1.0 %down.5 = (f32[24,1024]{1,0:T(8,128)S(1)}, bf16[24,1024]{1,0:T(8,128)(2,1)S(1)}, bf16[24,1024]{1,0:T(8,128)(2,1)S(1)}, bf16[24,1024]{1,0:T(8,128)(2,1)S(1)}) custom-call(bf16[6656,2048]{1,0:T(8,128)(2,1)S(1)} %bitcast.5, bf16[48,1280]{1,0:T(8,128)(2,1)S(1)} %collective-permute-done.8.hidden, f32[48,2048]{1,0:T(8,128)S(1)} %down.4.total), custom_call_target="tpu_custom_call" | custom-call | flops 251658240 | bytes 5242880 | tf_op jit(solution)/shard_map/down/pallas_call | solution.py:244
  44.2 2.9 %collective-permute-start.9 = (bf16[24,1024]{1,0:T(8,128)(2,1)S(1)}, bf16[24,1024]{1,0:T(8,128)(2,1)S(1)}, u32[]{:S(2)}, u32[]{:S(2)}) collective-permute-start(bf16[24,1024]{1,0:T(8,128)(2,1)S(1)} %get-tuple-element.28), channel_id=1, source_target_pairs={{0,12},{4,8},{8,4},{12,0},{1,13},{5,9},{9,5},{13,1},{2,14},{6,10},... | collective-permute-start | bytes 147464 | tf_op jit(solution)/shard_map/ppermute | solution.py:265
  47.1 0.2 collective-permute-start.10
  47.3 1.4 %collective-permute-start.11 = (bf16[24,1024]{1,0:T(8,128)(2,1)S(1)}, bf16[24,1024]{1,0:T(8,128)(2,1)S(1)}, u32[]{:S(2)}, u32[]{:S(2)}) collective-permute-start(bf16[24,1024]{1,0:T(8,128)(2,1)S(1)} %get-tuple-element.30), channel_id=1, source_target_pairs={{0,4},{4,0},{8,12},{12,8},{1,5},{5,1},{9,13},{13,9},{2,6},{6,2},{1... | collective-permute-start | bytes 147464 | tf_op jit(solution)/shard_map/ppermute | solution.py:265
  48.6 2.1 %collective-permute-done.9 = bf16[24,1024]{1,0:T(8,128)(2,1)S(1)} collective-permute-done((bf16[24,1024]{1,0:T(8,128)(2,1)S(1)}, bf16[24,1024]{1,0:T(8,128)(2,1)S(1)}, u32[]{:S(2)}, u32[]{:S(2)}) %collective-permute-start.9) | collective-permute-done | bytes 49184 | tf_op jit(solution)/shard_map/ppermute | solution.py:265
  50.7 1.8 %collective-permute-done.10 = bf16[24,1024]{1,0:T(8,128)(2,1)S(1)} collective-permute-done((bf16[24,1024]{1,0:T(8,128)(2,1)S(1)}, bf16[24,1024]{1,0:T(8,128)(2,1)S(1)}, u32[]{:S(2)}, u32[]{:S(2)}) %collective-permute-start.10) | collective-permute-done | bytes 49184 | tf_op jit(solution)/shard_map/ppermute | solution.py:265
  52.7 0.6 %copy.7 = bf16[2,8,2,1024]{3,1,2,0:T(8,128)(2,1)} copy(bf16[2,8,2,1024]{3,2,1,0:T(2,128)(2,1)S(1)} %bitcast.7) | data formatting | bytes 131072
  (41 shorter events, 1.2 us)
Async XLA Ops:
  0.0 8.2 %copy-start.1 = (bf16[12,2048]{1,0:T(8,128)(2,1)S(1)}, bf16[12,2048]{1,0:T(8,128)(2,1)}, u32[]{:S(2)}) copy-start(bf16[12,2048]{1,0:T(8,128)(2,1)} %param.4) | copy-start | bytes 147460
  0.0 11.0 %copy-start = (bf16[2048,6656]{1,0:T(8,128)(2,1)S(1)}, bf16[2048,6656]{1,0:T(8,128)(2,1)}, u32[]{:S(2)}) copy-start(bf16[2048,6656]{1,0:T(8,128)(2,1)} %gate.3) | copy-start | bytes 81788928
  0.0 8.2 %collective-permute-start = (bf16[12,2048]{1,0:T(8,128)(2,1)}, bf16[12,2048]{1,0:T(8,128)(2,1)S(1)}, u32[]{:S(2)}, u32[]{:S(2)}) collective-permute-start(bf16[12,2048]{1,0:T(8,128)(2,1)} %param.4), channel_id=1, source_target_pairs={{0,12},{4,8},{8,4},{12,0},{1,13},{5,9},{9,5},{13,1},{2,14},{6,10},... | collective-permute-start | bytes 147464 | tf_op jit(solution)/shard_map/ppermute | solution.py:265
  5.1 5.9 %collective-permute-start.2 = (bf16[12,2048]{1,0:T(8,128)(2,1)}, bf16[12,2048]{1,0:T(8,128)(2,1)S(1)}, u32[]{:S(2)}, u32[]{:S(2)}) collective-permute-start(bf16[12,2048]{1,0:T(8,128)(2,1)} %param.4), channel_id=1, source_target_pairs={{0,4},{4,0},{8,12},{12,8},{1,5},{5,1},{9,13},{13,9},{2,6},{6,2},{1... | collective-permute-start | bytes 147464 | tf_op jit(solution)/shard_map/ppermute | solution.py:265
  5.1 5.8 %collective-permute-start.1 = (bf16[12,2048]{1,0:T(8,128)(2,1)}, bf16[12,2048]{1,0:T(8,128)(2,1)S(1)}, u32[]{:S(2)}, u32[]{:S(2)}) collective-permute-start(bf16[12,2048]{1,0:T(8,128)(2,1)} %param.4), channel_id=1, source_target_pairs={{0,8},{4,12},{8,0},{12,4},{1,9},{5,13},{9,1},{13,5},{2,10},{6,14},... | collective-permute-start | bytes 147464 | tf_op jit(solution)/shard_map/ppermute | solution.py:265
  19.6 1.8 %collective-permute-start.3 = (bf16[48,4096]{1,0:T(8,128)(2,1)S(1)}, bf16[48,4096]{1,0:T(8,128)(2,1)S(1)}, u32[]{:S(2)}, u32[]{:S(2)}) collective-permute-start(bf16[48,4096]{1,0:T(8,128)(2,1)S(1)} %get-tuple-element.19), channel_id=1, source_target_pairs={{0,1},{1,0},{2,3},{3,2},{4,5},{5,4},{6,7},{7,6},{8,9},{9,8},{10,11... | collective-permute-start | bytes 1179656 | tf_op jit(solution)/shard_map/ppermute | solution.py:34
  21.4 13.4 %slice-start = ((s8[27262976]{0:T(1024)(128)(4,1)}), s8[4194304]{0:T(1024)(128)(4,1)S(1)}, s32[]{:S(2)}) async-start(s8[27262976]{0:T(1024)(128)(4,1)} %bitcast.4), calls=%async_computation | async-start | bytes 8388608
  21.5 13.3 %slice-start.1 = ((s8[27262976]{0:T(1024)(128)(4,1)}), s8[4194304]{0:T(1024)(128)(4,1)S(1)}, s32[]{:S(2)}) async-start(s8[27262976]{0:T(1024)(128)(4,1)} %bitcast.4), calls=%async_computation.1 | async-start | bytes 8388608
  21.5 13.2 %slice-start.2 = ((s8[27262976]{0:T(1024)(128)(4,1)}), s8[4194304]{0:T(1024)(128)(4,1)S(1)}, s32[]{:S(2)}) async-start(s8[27262976]{0:T(1024)(128)(4,1)} %bitcast.4), calls=%async_computation.2 | async-start | bytes 8388608
  21.5 13.2 %slice-start.3 = ((s8[27262976]{0:T(1024)(128)(4,1)}), s8[4194304]{0:T(1024)(128)(4,1)S(1)}, s32[]{:S(2)}) async-start(s8[27262976]{0:T(1024)(128)(4,1)} %bitcast.4), calls=%async_computation.3 | async-start | bytes 8388608
  21.5 13.3 %slice-start.4 = ((s8[27262976]{0:T(1024)(128)(4,1)}), s8[4194304]{0:T(1024)(128)(4,1)S(1)}, s32[]{:S(2)}) async-start(s8[27262976]{0:T(1024)(128)(4,1)} %bitcast.4), calls=%async_computation.4 | async-start | bytes 8388608
  21.5 14.5 %slice-start.5 = ((s8[27262976]{0:T(1024)(128)(4,1)}), s8[4194304]{0:T(1024)(128)(4,1)S(1)}, s32[]{:S(2)}) async-start(s8[27262976]{0:T(1024)(128)(4,1)} %bitcast.4), calls=%async_computation.5 | async-start | bytes 8388608
  21.5 15.1 %slice-start.6 = ((s8[27262976]{0:T(1024)(128)(4,1)}), s8[2097152]{0:T(1024)(128)(4,1)S(1)}, s32[]{:S(2)}) async-start(s8[27262976]{0:T(1024)(128)(4,1)} %bitcast.4), calls=%async_computation.6 | async-start | bytes 4194304
  21.6 11.2 %collective-permute-start.4 = (bf16[48,4096]{1,0:T(8,128)(2,1)S(1)}, bf16[48,4096]{1,0:T(8,128)(2,1)S(1)}, u32[]{:S(2)}, u32[]{:S(2)}) collective-permute-start(bf16[48,4096]{1,0:T(8,128)(2,1)S(1)} %fusion), channel_id=1, source_target_pairs={{0,2},{2,0},{1,3},{3,1},{4,6},{6,4},{5,7},{7,5},{8,10},{10,8},{9,1... | collective-permute-start | bytes 1179656 | tf_op jit(solution)/shard_map/ppermute | solution.py:34
  31.8 1.6 %collective-permute-start.5 = (bf16[48,2560]{1,0:T(8,128)(2,1)S(1)}, bf16[48,2560]{1,0:T(8,128)(2,1)S(1)}, u32[]{:S(2)}, u32[]{:S(2)}) collective-permute-start(bf16[48,2560]{1,0:T(8,128)(2,1)S(1)} %get-tuple-element.23), channel_id=1, source_target_pairs={{0,1},{1,0},{2,3},{3,2},{4,5},{5,4},{6,7},{7,6},{8,9},{9,8},{10,11... | collective-permute-start | bytes 737288 | tf_op jit(solution)/shard_map/ppermute | solution.py:34
  33.0 1.7 %collective-permute-start.7 = (bf16[48,2048]{1,0:T(8,128)(2,1)S(1)}, bf16[48,2048]{1,0:T(8,128)(2,1)S(1)}, u32[]{:S(2)}, u32[]{:S(2)}) collective-permute-start(bf16[48,2048]{1,0:T(8,128)(2,1)S(1)} %fusion.1.refs_0_), channel_id=1, source_target_pairs={{0,1},{1,0},{2,3},{3,2},{4,5},{5,4},{6,7},{7,6},{8,9},{9,8},{10,11... | collective-permute-start | bytes 589832 | tf_op jit(solution)/shard_map/ppermute | solution.py:34
  33.5 8.1 %collective-permute-start.6 = (bf16[48,2560]{1,0:T(8,128)(2,1)S(1)}, bf16[48,2560]{1,0:T(8,128)(2,1)S(1)}, u32[]{:S(2)}, u32[]{:S(2)}) collective-permute-start(bf16[48,2560]{1,0:T(8,128)(2,1)S(1)} %fusion.2), channel_id=1, source_target_pairs={{0,2},{2,0},{1,3},{3,1},{4,6},{6,4},{5,7},{7,5},{8,10},{10,8},{9,1... | collective-permute-start | bytes 737288 | tf_op jit(solution)/shard_map/ppermute | solution.py:34
  41.7 1.4 %collective-permute-start.8 = (bf16[48,1280]{1,0:T(8,128)(2,1)S(1)}, bf16[48,1280]{1,0:T(8,128)(2,1)S(1)}, u32[]{:S(2)}, u32[]{:S(2)}) collective-permute-start(bf16[48,1280]{1,0:T(8,128)(2,1)S(1)} %fusion.3.refs_0_), channel_id=1, source_target_pairs={{0,1},{1,0},{2,3},{3,2},{4,5},{5,4},{6,7},{7,6},{8,9},{9,8},{10,11... | collective-permute-start | bytes 368648 | tf_op jit(solution)/shard_map/ppermute | solution.py:34
  44.2 6.5 %collective-permute-start.9 = (bf16[24,1024]{1,0:T(8,128)(2,1)S(1)}, bf16[24,1024]{1,0:T(8,128)(2,1)S(1)}, u32[]{:S(2)}, u32[]{:S(2)}) collective-permute-start(bf16[24,1024]{1,0:T(8,128)(2,1)S(1)} %get-tuple-element.28), channel_id=1, source_target_pairs={{0,12},{4,8},{8,4},{12,0},{1,13},{5,9},{9,5},{13,1},{2,14},{6,10},... | collective-permute-start | bytes 147464 | tf_op jit(solution)/shard_map/ppermute | solution.py:265
  47.1 5.4 %collective-permute-start.10 = (bf16[24,1024]{1,0:T(8,128)(2,1)S(1)}, bf16[24,1024]{1,0:T(8,128)(2,1)S(1)}, u32[]{:S(2)}, u32[]{:S(2)}) collective-permute-start(bf16[24,1024]{1,0:T(8,128)(2,1)S(1)} %get-tuple-element.29), channel_id=1, source_target_pairs={{0,8},{4,12},{8,0},{12,4},{1,9},{5,13},{9,1},{13,5},{2,10},{6,14},... | collective-permute-start | bytes 147464 | tf_op jit(solution)/shard_map/ppermute | solution.py:265
  47.3 5.2 %collective-permute-start.11 = (bf16[24,1024]{1,0:T(8,128)(2,1)S(1)}, bf16[24,1024]{1,0:T(8,128)(2,1)S(1)}, u32[]{:S(2)}, u32[]{:S(2)}) collective-permute-start(bf16[24,1024]{1,0:T(8,128)(2,1)S(1)} %get-tuple-element.30), channel_id=1, source_target_pairs={{0,4},{4,0},{8,12},{12,8},{1,5},{5,1},{9,13},{13,9},{2,6},{6,2},{1... | collective-permute-start | bytes 147464 | tf_op jit(solution)/shard_map/ppermute | solution.py:265

commit v15 on v14

--- a/solution.py
+++ b/solution.py
@@ -88,20 +88,22 @@
     for copy in copies[0] + copies[1]:
         copy.start()
 
-    for place, out in enumerate((send, keep)):
-        for at in range(0, half, WIDE):
-            wide = min(WIDE, half - at)
-            columns = pl.ds(pl.multiple_of(side_of(place) + at, BLOCK), wide)
-            out[:, pl.ds(at, wide)] = jnp.dot(
-                tokens[...], gate[:, columns], preferred_element_type=F32
-            ).astype(out.dtype)
-        for at in range(0, half, WIDE):
-            wide = min(WIDE, half - at)
-            for copy in copies[place][at // BLOCK : (at + wide) // BLOCK]:
-                copy.wait()
-            out[:, pl.ds(half + at, wide)] = jnp.dot(
-                tokens[...], held[:, pl.ds(place * half + at, wide)], preferred_element_type=F32
-            ).astype(out.dtype)
+    pieces = [
+        (place, out, at, min(WIDE, half - at))
+        for place, out in enumerate((send, keep))
+        for at in range(0, half, WIDE)
+    ]
+    for place, out, at, wide in pieces:
+        columns = pl.ds(pl.multiple_of(side_of(place) + at, BLOCK), wide)
+        out[:, pl.ds(at, wide)] = jnp.dot(tokens[...], gate[:, columns], preferred_element_type=F32).astype(
+            out.dtype
+        )
+    for place, out, at, wide in pieces:
+        for copy in copies[place][at // BLOCK : (at + wide) // BLOCK]:
+            copy.wait()
+        out[:, pl.ds(half + at, wide)] = jnp.dot(
+            tokens[...], held[:, pl.ds(place * half + at, wide)], preferred_element_type=F32
+        ).astype(out.dtype)
 
 
 def sums(tokens, gate, up, chunk, after):

time: 53.5 us -> 53.7 us (level)
  no operation moved by 1% of the time
where the time goes in v15:
time: 53.7 us; the launch traced here: 53.6 us
  Pallas kernels  22.7 us (42%)
  waiting for transfers between devices  14.1 us (26%)
  starting transfers between devices  13.3 us (25%)
  local copies, waits for them, and re-layouts  2.67 us (5%)
  other arithmetic  0.64 us (1%)
    ppermute x6, starting transfers between devices, across(): return lax.ppermute(x, 'wide', [(i, i ^ apart) for i in range(4)])  10.1 us
    ppermute x6, waiting for transfers between devices, across(): return lax.ppermute(x, 'wide', [(i, i ^ apart) for i in range(4)])  9.01 us
    pallas_call x1, Pallas kernels, sums(): pl.pallas_call(functools.partial(sums_kernel, first), out_shape=(jax.Shap...  8.89 us
    pallas_call x1, Pallas kernels, stream_sums(): pl.pallas_call(functools.partial(stream_kernel, first, steps), out_shape=...  8.71 us
    ppermute x6, waiting for transfers between devices, swap(): return lax.ppermute(x, axis, [(0, 1), (1, 0)])  5.1 us
    pallas_call x3, Pallas kernels, down(): pl.pallas_call(functools.partial(kernel, chunk[0], half, sides), out_shap...  5.05 us
    ppermute x6, starting transfers between devices, swap(): return lax.ppermute(x, axis, [(0, 1), (1, 0)])  3.12 us
    unnamed x20, local copies, waits for them, and re-layouts  2.6 us
  transfers between devices with their start and end apart: 12, of which 9 were waited for; matrix products, arithmetic and copies ran while one was open for 1% of the time, Pallas kernels for 24%

profile of v15, /device:TPU:0, one launch (start us, length us, event | category | flops | bytes accessed | tf_op | source)
XLA Modules:
  0.0 53.6 jit_solution(16351747044595183609)
XLA Ops:
  0.0 5.0 %collective-permute-start = (bf16[12,2048]{1,0:T(8,128)(2,1)}, bf16[12,2048]{1,0:T(8,128)(2,1)S(1)}, u32[]{:S(2)}, u32[]{:S(2)}) collective-permute-start(bf16[12,2048]{1,0:T(8,128)(2,1)} %param.4), channel_id=1, source_target_pairs={{0,12},{4,8},{8,4},{12,0},{1,13},{5,9},{9,5},{13,1},{2,14},{6,10},... | collective-permute-start | bytes 147464 | tf_op jit(solution)/shard_map/ppermute | solution.py:267
  5.1 0.6 %collective-permute-start.1 = (bf16[12,2048]{1,0:T(8,128)(2,1)}, bf16[12,2048]{1,0:T(8,128)(2,1)S(1)}, u32[]{:S(2)}, u32[]{:S(2)}) collective-permute-start(bf16[12,2048]{1,0:T(8,128)(2,1)} %param.4), channel_id=1, source_target_pairs={{0,8},{4,12},{8,0},{12,4},{1,9},{5,13},{9,1},{13,5},{2,10},{6,14},... | collective-permute-start | bytes 147464 | tf_op jit(solution)/shard_map/ppermute | solution.py:267
  5.7 2.5 %collective-permute-done = bf16[12,2048]{1,0:T(8,128)(2,1)S(1)} collective-permute-done((bf16[12,2048]{1,0:T(8,128)(2,1)}, bf16[12,2048]{1,0:T(8,128)(2,1)S(1)}, u32[]{:S(2)}, u32[]{:S(2)}) %collective-permute-start) | collective-permute-done | bytes 49184 | tf_op jit(solution)/shard_map/ppermute | solution.py:267
  8.3 2.6 %collective-permute-done.1 = bf16[12,2048]{1,0:T(8,128)(2,1)S(1)} collective-permute-done((bf16[12,2048]{1,0:T(8,128)(2,1)}, bf16[12,2048]{1,0:T(8,128)(2,1)S(1)}, u32[]{:S(2)}, u32[]{:S(2)}) %collective-permute-start.1) | collective-permute-done | bytes 49184 | tf_op jit(solution)/shard_map/ppermute | solution.py:267
  11.0 8.9 %sums.1 = (bf16[48,4096]{1,0:T(8,128)(2,1)S(1)}, f32[48,4096]{1,0:T(8,128)S(1)}) custom-call(bf16[48,2048]{1,0:T(8,128)(2,1)S(1)} %pad_maximum_fusion.tokens, bf16[2048,6656]{1,0:T(8,128)(2,1)S(1)} %copy-done, bf16[2048,6656]{1,0:T(8,128)(2,1)} %up.3, f32[8,128]{1,0:T(8,128)S(1)} %beside.1.after), custom_call_target="tpu_custom_call" | custom-call | flops 1610612736 | bytes 33554432 | tf_op jit(solution)/shard_map/sums/pallas_call | solution.py:112
  19.9 1.7 %collective-permute-done.3 = bf16[48,4096]{1,0:T(8,128)(2,1)S(1)} collective-permute-done((bf16[48,4096]{1,0:T(8,128)(2,1)S(1)}, bf16[48,4096]{1,0:T(8,128)(2,1)S(1)}, u32[]{:S(2)}, u32[]{:S(2)}) %collective-permute-start.3) | collective-permute-done | bytes 393248 | tf_op jit(solution)/shard_map/ppermute | solution.py:34
  21.8 1.6 %collective-permute-start.4 = (bf16[48,4096]{1,0:T(8,128)(2,1)S(1)}, bf16[48,4096]{1,0:T(8,128)(2,1)S(1)}, u32[]{:S(2)}, u32[]{:S(2)}) collective-permute-start(bf16[48,4096]{1,0:T(8,128)(2,1)S(1)} %fusion), channel_id=1, source_target_pairs={{0,2},{2,0},{1,3},{3,1},{4,6},{6,4},{5,7},{7,5},{8,10},{10,8},{9,1... | collective-permute-start | bytes 1179656 | tf_op jit(solution)/shard_map/ppermute | solution.py:34
  23.4 8.7 %stream_sums.1 = (bf16[48,2560]{1,0:T(8,128)(2,1)S(1)}, f32[48,2560]{1,0:T(8,128)S(1)}) custom-call(bf16[48,2048]{1,0:T(8,128)(2,1)S(1)} %pad_maximum_fusion.tokens, bf16[2048,6656]{1,0:T(8,128)(2,1)} %gate.3, bf16[2048,6656]{1,0:T(8,128)(2,1)} %up.3), custom_call_target="tpu_custom_call" | custom-call | flops 1006632960 | bytes 20971520 | tf_op jit(solution)/shard_map/stream_sums/pallas_call | solution.py:186
  32.2 0.9 %collective-permute-done.4 = bf16[48,4096]{1,0:T(8,128)(2,1)S(1)} collective-permute-done((bf16[48,4096]{1,0:T(8,128)(2,1)S(1)}, bf16[48,4096]{1,0:T(8,128)(2,1)S(1)}, u32[]{:S(2)}, u32[]{:S(2)}) %collective-permute-start.4) | collective-permute-done | bytes 393248 | tf_op jit(solution)/shard_map/ppermute | solution.py:34
  33.4 0.3 collective-permute-done.5
  33.7 1.3 %collective-permute-start.6 = (bf16[48,2560]{1,0:T(8,128)(2,1)S(1)}, bf16[48,2560]{1,0:T(8,128)(2,1)S(1)}, u32[]{:S(2)}, u32[]{:S(2)}) collective-permute-start(bf16[48,2560]{1,0:T(8,128)(2,1)S(1)} %fusion.2), channel_id=1, source_target_pairs={{0,2},{2,0},{1,3},{3,1},{4,6},{6,4},{5,7},{7,5},{8,10},{10,8},{9,1... | collective-permute-start | bytes 737288 | tf_op jit(solution)/shard_map/ppermute | solution.py:34
  35.1 1.2 %slice-done.5 = s8[4194304]{0:T(1024)(128)(4,1)S(1)} async-done(((s8[27262976]{0:T(1024)(128)(4,1)}), s8[4194304]{0:T(1024)(128)(4,1)S(1)}, s32[]{:S(2)}) %slice-start.5) | async-done | bytes 4194328
  36.3 0.6 %slice-done.6 = s8[2097152]{0:T(1024)(128)(4,1)S(1)} async-done(((s8[27262976]{0:T(1024)(128)(4,1)}), s8[2097152]{0:T(1024)(128)(4,1)S(1)}, s32[]{:S(2)}) %slice-start.6) | async-done | bytes 2097176
  36.9 3.0 %down.3.refs_1_ = f32[48,2048]{1,0:T(8,128)S(1)} custom-call(bf16[6656,2048]{1,0:T(8,128)(2,1)S(1)} %bitcast.5, bf16[48,2048]{1,0:T(8,128)(2,1)S(1)} %fusion.1.refs_0_, bf16[48,2048]{1,0:T(8,128)(2,1)S(1)} %collective-permute-done.7.refs_1_), custom_call_target="tpu_custom_call" | custom-call | flops 805306368 | bytes 16777216 | tf_op jit(solution)/shard_map/down/pallas_call | solution.py:246
  39.9 1.9 %collective-permute-done.6 = bf16[48,2560]{1,0:T(8,128)(2,1)S(1)} collective-permute-done((bf16[48,2560]{1,0:T(8,128)(2,1)S(1)}, bf16[48,2560]{1,0:T(8,128)(2,1)S(1)}, u32[]{:S(2)}, u32[]{:S(2)}) %collective-permute-start.6) | collective-permute-done | bytes 245792 | tf_op jit(solution)/shard_map/ppermute | solution.py:34
  42.1 1.0 %down.4.total = f32[48,2048]{1,0:T(8,128)S(1)} custom-call(bf16[6656,2048]{1,0:T(8,128)(2,1)S(1)} %bitcast.5, bf16[48,1280]{1,0:T(8,128)(2,1)S(1)} %fusion.3.refs_0_, f32[48,2048]{1,0:T(8,128)S(1)} %down.3.refs_1_), custom_call_target="tpu_custom_call" | custom-call | flops 251658240 | bytes 5242880 | tf_op jit(solution)/shard_map/down/pallas_call | solution.py:246
  43.1 0.3 collective-permute-done.8.hidden
  43.4 1.0 %down.5 = (f32[24,1024]{1,0:T(8,128)S(1)}, bf16[24,1024]{1,0:T(8,128)(2,1)S(1)}, bf16[24,1024]{1,0:T(8,128)(2,1)S(1)}, bf16[24,1024]{1,0:T(8,128)(2,1)S(1)}) custom-call(bf16[6656,2048]{1,0:T(8,128)(2,1)S(1)} %bitcast.5, bf16[48,1280]{1,0:T(8,128)(2,1)S(1)} %collective-permute-done.8.hidden, f32[48,2048]{1,0:T(8,128)S(1)} %down.4.total), custom_call_target="tpu_custom_call" | custom-call | flops 251658240 | bytes 5242880 | tf_op jit(solution)/shard_map/down/pallas_call | solution.py:246
  44.5 2.9 %collective-permute-start.9 = (bf16[24,1024]{1,0:T(8,128)(2,1)S(1)}, bf16[24,1024]{1,0:T(8,128)(2,1)S(1)}, u32[]{:S(2)}, u32[]{:S(2)}) collective-permute-start(bf16[24,1024]{1,0:T(8,128)(2,1)S(1)} %get-tuple-element.28), channel_id=1, source_target_pairs={{0,12},{4,8},{8,4},{12,0},{1,13},{5,9},{9,5},{13,1},{2,14},{6,10},... | collective-permute-start | bytes 147464 | tf_op jit(solution)/shard_map/ppermute | solution.py:267
  47.4 0.2 collective-permute-start.10
  47.5 1.4 %collective-permute-start.11 = (bf16[24,1024]{1,0:T(8,128)(2,1)S(1)}, bf16[24,1024]{1,0:T(8,128)(2,1)S(1)}, u32[]{:S(2)}, u32[]{:S(2)}) collective-permute-start(bf16[24,1024]{1,0:T(8,128)(2,1)S(1)} %get-tuple-element.30), channel_id=1, source_target_pairs={{0,4},{4,0},{8,12},{12,8},{1,5},{5,1},{9,13},{13,9},{2,6},{6,2},{1... | collective-permute-start | bytes 147464 | tf_op jit(solution)/shard_map/ppermute | solution.py:267
  48.9 2.1 %collective-permute-done.9 = bf16[24,1024]{1,0:T(8,128)(2,1)S(1)} collective-permute-done((bf16[24,1024]{1,0:T(8,128)(2,1)S(1)}, bf16[24,1024]{1,0:T(8,128)(2,1)S(1)}, u32[]{:S(2)}, u32[]{:S(2)}) %collective-permute-start.9) | collective-permute-done | bytes 49184 | tf_op jit(solution)/shard_map/ppermute | solution.py:267
  51.0 1.8 %collective-permute-done.10 = bf16[24,1024]{1,0:T(8,128)(2,1)S(1)} collective-permute-done((bf16[24,1024]{1,0:T(8,128)(2,1)S(1)}, bf16[24,1024]{1,0:T(8,128)(2,1)S(1)}, u32[]{:S(2)}, u32[]{:S(2)}) %collective-permute-start.10) | collective-permute-done | bytes 49184 | tf_op jit(solution)/shard_map/ppermute | solution.py:267
  52.9 0.6 %copy.7 = bf16[2,8,2,1024]{3,1,2,0:T(8,128)(2,1)} copy(bf16[2,8,2,1024]{3,2,1,0:T(2,128)(2,1)S(1)} %bitcast.7) | data formatting | bytes 131072
  (41 shorter events, 1.2 us)
Async XLA Ops:
  0.0 8.2 %copy-start.1 = (bf16[12,2048]{1,0:T(8,128)(2,1)S(1)}, bf16[12,2048]{1,0:T(8,128)(2,1)}, u32[]{:S(2)}) copy-start(bf16[12,2048]{1,0:T(8,128)(2,1)} %param.4) | copy-start | bytes 147460
  0.0 11.0 %copy-start = (bf16[2048,6656]{1,0:T(8,128)(2,1)S(1)}, bf16[2048,6656]{1,0:T(8,128)(2,1)}, u32[]{:S(2)}) copy-start(bf16[2048,6656]{1,0:T(8,128)(2,1)} %gate.3) | copy-start | bytes 81788928
  0.0 8.2 %collective-permute-start = (bf16[12,2048]{1,0:T(8,128)(2,1)}, bf16[12,2048]{1,0:T(8,128)(2,1)S(1)}, u32[]{:S(2)}, u32[]{:S(2)}) collective-permute-start(bf16[12,2048]{1,0:T(8,128)(2,1)} %param.4), channel_id=1, source_target_pairs={{0,12},{4,8},{8,4},{12,0},{1,13},{5,9},{9,5},{13,1},{2,14},{6,10},... | collective-permute-start | bytes 147464 | tf_op jit(solution)/shard_map/ppermute | solution.py:267
  5.1 5.9 %collective-permute-start.2 = (bf16[12,2048]{1,0:T(8,128)(2,1)}, bf16[12,2048]{1,0:T(8,128)(2,1)S(1)}, u32[]{:S(2)}, u32[]{:S(2)}) collective-permute-start(bf16[12,2048]{1,0:T(8,128)(2,1)} %param.4), channel_id=1, source_target_pairs={{0,4},{4,0},{8,12},{12,8},{1,5},{5,1},{9,13},{13,9},{2,6},{6,2},{1... | collective-permute-start | bytes 147464 | tf_op jit(solution)/shard_map/ppermute | solution.py:267
  5.1 5.8 %collective-permute-start.1 = (bf16[12,2048]{1,0:T(8,128)(2,1)}, bf16[12,2048]{1,0:T(8,128)(2,1)S(1)}, u32[]{:S(2)}, u32[]{:S(2)}) collective-permute-start(bf16[12,2048]{1,0:T(8,128)(2,1)} %param.4), channel_id=1, source_target_pairs={{0,8},{4,12},{8,0},{12,4},{1,9},{5,13},{9,1},{13,5},{2,10},{6,14},... | collective-permute-start | bytes 147464 | tf_op jit(solution)/shard_map/ppermute | solution.py:267
  19.9 1.8 %collective-permute-start.3 = (bf16[48,4096]{1,0:T(8,128)(2,1)S(1)}, bf16[48,4096]{1,0:T(8,128)(2,1)S(1)}, u32[]{:S(2)}, u32[]{:S(2)}) collective-permute-start(bf16[48,4096]{1,0:T(8,128)(2,1)S(1)} %get-tuple-element.19), channel_id=1, source_target_pairs={{0,1},{1,0},{2,3},{3,2},{4,5},{5,4},{6,7},{7,6},{8,9},{9,8},{10,11... | collective-permute-start | bytes 1179656 | tf_op jit(solution)/shard_map/ppermute | solution.py:34
  21.7 13.4 %slice-start = ((s8[27262976]{0:T(1024)(128)(4,1)}), s8[4194304]{0:T(1024)(128)(4,1)S(1)}, s32[]{:S(2)}) async-start(s8[27262976]{0:T(1024)(128)(4,1)} %bitcast.4), calls=%async_computation | async-start | bytes 8388608
  21.8 13.3 %slice-start.1 = ((s8[27262976]{0:T(1024)(128)(4,1)}), s8[4194304]{0:T(1024)(128)(4,1)S(1)}, s32[]{:S(2)}) async-start(s8[27262976]{0:T(1024)(128)(4,1)} %bitcast.4), calls=%async_computation.1 | async-start | bytes 8388608
  21.8 13.2 %slice-start.2 = ((s8[27262976]{0:T(1024)(128)(4,1)}), s8[4194304]{0:T(1024)(128)(4,1)S(1)}, s32[]{:S(2)}) async-start(s8[27262976]{0:T(1024)(128)(4,1)} %bitcast.4), calls=%async_computation.2 | async-start | bytes 8388608
  21.8 13.2 %slice-start.3 = ((s8[27262976]{0:T(1024)(128)(4,1)}), s8[4194304]{0:T(1024)(128)(4,1)S(1)}, s32[]{:S(2)}) async-start(s8[27262976]{0:T(1024)(128)(4,1)} %bitcast.4), calls=%async_computation.3 | async-start | bytes 8388608
  21.8 13.3 %slice-start.4 = ((s8[27262976]{0:T(1024)(128)(4,1)}), s8[4194304]{0:T(1024)(128)(4,1)S(1)}, s32[]{:S(2)}) async-start(s8[27262976]{0:T(1024)(128)(4,1)} %bitcast.4), calls=%async_computation.4 | async-start | bytes 8388608
  21.8 14.5 %slice-start.5 = ((s8[27262976]{0:T(1024)(128)(4,1)}), s8[4194304]{0:T(1024)(128)(4,1)S(1)}, s32[]{:S(2)}) async-start(s8[27262976]{0:T(1024)(128)(4,1)} %bitcast.4), calls=%async_computation.5 | async-start | bytes 8388608
  21.8 15.1 %slice-start.6 = ((s8[27262976]{0:T(1024)(128)(4,1)}), s8[2097152]{0:T(1024)(128)(4,1)S(1)}, s32[]{:S(2)}) async-start(s8[27262976]{0:T(1024)(128)(4,1)} %bitcast.4), calls=%async_computation.6 | async-start | bytes 4194304
  21.8 11.2 %collective-permute-start.4 = (bf16[48,4096]{1,0:T(8,128)(2,1)S(1)}, bf16[48,4096]{1,0:T(8,128)(2,1)S(1)}, u32[]{:S(2)}, u32[]{:S(2)}) collective-permute-start(bf16[48,4096]{1,0:T(8,128)(2,1)S(1)} %fusion), channel_id=1, source_target_pairs={{0,2},{2,0},{1,3},{3,1},{4,6},{6,4},{5,7},{7,5},{8,10},{10,8},{9,1... | collective-permute-start | bytes 1179656 | tf_op jit(solution)/shard_map/ppermute | solution.py:34
  32.1 1.6 %collective-permute-start.5 = (bf16[48,2560]{1,0:T(8,128)(2,1)S(1)}, bf16[48,2560]{1,0:T(8,128)(2,1)S(1)}, u32[]{:S(2)}, u32[]{:S(2)}) collective-permute-start(bf16[48,2560]{1,0:T(8,128)(2,1)S(1)} %get-tuple-element.23), channel_id=1, source_target_pairs={{0,1},{1,0},{2,3},{3,2},{4,5},{5,4},{6,7},{7,6},{8,9},{9,8},{10,11... | collective-permute-start | bytes 737288 | tf_op jit(solution)/shard_map/ppermute | solution.py:34
  33.3 1.7 %collective-permute-start.7 = (bf16[48,2048]{1,0:T(8,128)(2,1)S(1)}, bf16[48,2048]{1,0:T(8,128)(2,1)S(1)}, u32[]{:S(2)}, u32[]{:S(2)}) collective-permute-start(bf16[48,2048]{1,0:T(8,128)(2,1)S(1)} %fusion.1.refs_0_), channel_id=1, source_target_pairs={{0,1},{1,0},{2,3},{3,2},{4,5},{5,4},{6,7},{7,6},{8,9},{9,8},{10,11... | collective-permute-start | bytes 589832 | tf_op jit(solution)/shard_map/ppermute | solution.py:34
  33.7 8.1 %collective-permute-start.6 = (bf16[48,2560]{1,0:T(8,128)(2,1)S(1)}, bf16[48,2560]{1,0:T(8,128)(2,1)S(1)}, u32[]{:S(2)}, u32[]{:S(2)}) collective-permute-start(bf16[48,2560]{1,0:T(8,128)(2,1)S(1)} %fusion.2), channel_id=1, source_target_pairs={{0,2},{2,0},{1,3},{3,1},{4,6},{6,4},{5,7},{7,5},{8,10},{10,8},{9,1... | collective-permute-start | bytes 737288 | tf_op jit(solution)/shard_map/ppermute | solution.py:34
  42.0 1.4 %collective-permute-start.8 = (bf16[48,1280]{1,0:T(8,128)(2,1)S(1)}, bf16[48,1280]{1,0:T(8,128)(2,1)S(1)}, u32[]{:S(2)}, u32[]{:S(2)}) collective-permute-start(bf16[48,1280]{1,0:T(8,128)(2,1)S(1)} %fusion.3.refs_0_), channel_id=1, source_target_pairs={{0,1},{1,0},{2,3},{3,2},{4,5},{5,4},{6,7},{7,6},{8,9},{9,8},{10,11... | collective-permute-start | bytes 368648 | tf_op jit(solution)/shard_map/ppermute | solution.py:34
  44.5 6.5 %collective-permute-start.9 = (bf16[24,1024]{1,0:T(8,128)(2,1)S(1)}, bf16[24,1024]{1,0:T(8,128)(2,1)S(1)}, u32[]{:S(2)}, u32[]{:S(2)}) collective-permute-start(bf16[24,1024]{1,0:T(8,128)(2,1)S(1)} %get-tuple-element.28), channel_id=1, source_target_pairs={{0,12},{4,8},{8,4},{12,0},{1,13},{5,9},{9,5},{13,1},{2,14},{6,10},... | collective-permute-start | bytes 147464 | tf_op jit(solution)/shard_map/ppermute | solution.py:267
  47.4 5.4 %collective-permute-start.10 = (bf16[24,1024]{1,0:T(8,128)(2,1)S(1)}, bf16[24,1024]{1,0:T(8,128)(2,1)S(1)}, u32[]{:S(2)}, u32[]{:S(2)}) collective-permute-start(bf16[24,1024]{1,0:T(8,128)(2,1)S(1)} %get-tuple-element.29), channel_id=1, source_target_pairs={{0,8},{4,12},{8,0},{12,4},{1,9},{5,13},{9,1},{13,5},{2,10},{6,14},... | collective-permute-start | bytes 147464 | tf_op jit(solution)/shard_map/ppermute | solution.py:267
  47.5 5.2 %collective-permute-start.11 = (bf16[24,1024]{1,0:T(8,128)(2,1)S(1)}, bf16[24,1024]{1,0:T(8,128)(2,1)S(1)}, u32[]{:S(2)}, u32[]{:S(2)}) collective-permute-start(bf16[24,1024]{1,0:T(8,128)(2,1)S(1)} %get-tuple-element.30), channel_id=1, source_target_pairs={{0,4},{4,0},{8,12},{12,8},{1,5},{5,1},{9,13},{13,9},{2,6},{6,2},{1... | collective-permute-start | bytes 147464 | tf_op jit(solution)/shard_map/ppermute | solution.py:267

commit v16 on v10

--- a/solution.py
+++ b/solution.py
@@ -35,6 +35,8 @@
 
 
 BLOCK = 256
+WIDE = 512
+HELD = 8
 VMEM = pl.BlockSpec(memory_space=pltpu.VMEM)
 ANY = pl.BlockSpec(memory_space=pl.ANY)
 HBM = pl.BlockSpec(memory_space=pltpu.HBM)
@@ -51,25 +53,20 @@
 
 def block_copies(first, half, step, gate, up, dst, sem):
     core = lax.axis_index("sub")
-    mine = jnp.int32(step >= half // BLOCK)
-    side = jnp.where(mine == 1, core, 1 - core)
-    unit = first + side * half + (step - mine * (half // BLOCK)) * BLOCK
+    mine, block = divmod(step, half // BLOCK)
+    side = core if mine else 1 - core
+    unit = first + side * half + block * BLOCK
     columns = pl.ds(pl.multiple_of(unit, BLOCK), BLOCK)
     return [
-        pltpu.make_async_copy(weight.at[:, columns], dst.at[:, pl.ds(i * BLOCK, BLOCK)], sem.at[i])
-        for i, weight in enumerate((gate, up))
+        pltpu.make_async_copy(weight.at[:, columns], dst.at[i], sem.at[i]) for i, weight in enumerate((gate, up))
     ]
-
-
-def pair(ref, at):
-    return ref.at[:, pl.ds(pl.multiple_of(at * 2 * BLOCK, 2 * BLOCK), 2 * BLOCK)]
 
 
 def load_kernel(first, half, gate, up, held, sems):
     copies = [
         copy
-        for step in range(sems.shape[0])
-        for copy in block_copies(first, half, step, gate, up, pair(held, step), sems.at[step])
+        for step in range(held.shape[0])
+        for copy in block_copies(first, half, step, gate, up, held.at[step], sems.at[step])
     ]
     for copy in copies:
         copy.start()
@@ -81,7 +78,7 @@
     depth = gate.shape[0]
     return pl.pallas_call(
         functools.partial(load_kernel, chunk[0], chunk[1] // 2),
-        out_shape=pltpu.VMEM((depth, steps * 2 * BLOCK), BF16),
+        out_shape=pltpu.VMEM((steps, 2, depth, BLOCK), BF16),
         in_specs=[HBM, HBM],
         out_specs=VMEM,
         scratch_shapes=[pltpu.SemaphoreType.DMA((steps, 2))],
@@ -101,52 +98,36 @@
 
     def copies(step):
         at = step - steps
-        return block_copies(first, half, step, gate, up, pair(streamed, at), sems.at[at])
+        return block_copies(first, half, step, gate, up, streamed.at[at], sems.at[at])
 
     for step in range(steps, 2 * blocks):
         for copy in copies(step):
             copy.start()
 
-    def add(out, start, source, block):
-        both = jnp.dot(tokens[...], source[...], preferred_element_type=F32).astype(out.dtype)
+    for step in range(2 * blocks):
+        out, block = (send, step) if step < blocks else (keep, step - blocks)
+        source = held.at[step] if step < steps else streamed.at[step - steps]
+        if step >= steps:
+            for copy in copies(step):
+                copy.wait()
         for i in range(2):
-            column = pl.multiple_of((i * blocks + block - start) * BLOCK, BLOCK)
-            out[:, pl.ds(column, BLOCK)] = both[:, i * BLOCK : (i + 1) * BLOCK]
-
-    for side, out in enumerate((send, keep)):
-        start, end = side * blocks, (side + 1) * blocks
-
-        middle = min(max(steps, start), end)
-        if start < middle:
-
-            @pl.loop(start, middle)
-            def _(step):
-                add(out, start, pair(held, step), step)
-
-        if middle < end:
-
-            @pl.loop(middle, end)
-            def _(step):
-                for copy in copies(step):
-                    copy.wait()
-                add(out, start, pair(streamed, step - steps), step)
+            out[:, pl.ds((i * blocks + block) * BLOCK, BLOCK)] = jnp.dot(
+                tokens[...], source[i], preferred_element_type=F32
+            ).astype(out.dtype)
 
 
 def sums(tokens, gate, up, chunk, held=None):
     rows, depth = tokens.shape
     first, width = chunk
-    steps = 0 if held is None else held.shape[1] // (2 * BLOCK)
-    streamed = width // BLOCK - steps
+    steps = 0 if held is None else held.shape[0]
+    shape = (width // BLOCK - steps, 2, depth, BLOCK)
     return pl.pallas_call(
         functools.partial(sums_kernel, first, steps),
         out_shape=(jax.ShapeDtypeStruct((rows, width), BF16), jax.ShapeDtypeStruct((rows, width), F32)),
         in_specs=[VMEM, HBM, HBM] + [VMEM] * (steps > 0),
         out_specs=(VMEM, VMEM),
-        scratch_shapes=[
-            pltpu.VMEM((depth, streamed * 2 * BLOCK), BF16),
-            pltpu.SemaphoreType.DMA((streamed, 2)),
-        ],
-        compiler_params=pltpu.CompilerParams(vmem_limit_bytes=4 * streamed * depth * BLOCK + 4 * 2**20),
+        scratch_shapes=[pltpu.VMEM(shape, BF16), pltpu.SemaphoreType.DMA(shape[:2])],
+        compiler_params=pltpu.CompilerParams(vmem_limit_bytes=4 * shape[0] * depth * BLOCK + 4 * 2**20),
         cost_estimate=pl.CostEstimate(
             flops=4 * rows * depth * width, bytes_accessed=4 * depth * width, transcendentals=0
         ),
@@ -166,11 +147,8 @@
 def down_kernel(first, half, sides, weight, *refs):
     hiddens, out = refs[: len(sides)], refs[-1]
     totals = refs[len(sides) : -1]
-    wide = 2 * BLOCK
-
-    @pl.loop(0, out.shape[1] // wide)
-    def _(block):
-        columns = pl.ds(pl.multiple_of(block * wide, wide), wide)
+    for at in range(0, out.shape[1], WIDE):
+        columns = pl.ds(at, WIDE)
         part = partial_sums(first, half, sides, hiddens, weight, columns)
         for total in totals:
             part += total[:, columns]
@@ -179,16 +157,14 @@
 
 def last_down_kernel(first, half, sides, weight, hidden, total, own, *sends):
     rows, columns = own.shape[0] // 2, own.shape[1]
-    wide = 2 * BLOCK
-    for block in range(columns // wide):
-        at = block * wide
+    for at in range(0, columns, WIDE):
         parts = []
         for start in (at, columns + at):
-            part = partial_sums(first, half, sides, [hidden], weight, pl.ds(start, wide))
-            parts.append(part + total[:, pl.ds(start, wide)])
+            part = partial_sums(first, half, sides, [hidden], weight, pl.ds(start, WIDE))
+            parts.append(part + total[:, pl.ds(start, WIDE)])
         for place, out in enumerate((own, *sends)):
             pieces = [part[place * rows : (place + 1) * rows] for part in parts]
-            out[:, pl.ds(at, wide)] = jnp.concatenate(pieces, axis=0).astype(out.dtype)
+            out[:, pl.ds(at, WIDE)] = jnp.concatenate(pieces, axis=0).astype(out.dtype)
 
 
 def down(weight, chunk, sides, hiddens, total=None, last=False):
@@ -232,7 +208,7 @@
     section = tokens
     for apart in (3, 2, 1):
         section = lax.optimization_barrier(jnp.concatenate([section, across(tokens, apart)], axis=0))
-    held = load(gate_weight, up_weight, chunks[0], 7)
+    held = load(gate_weight, up_weight, chunks[0], HELD)
 
     def core_sums(send, keep):
         total = keep + swap(send, "sub").astype(F32)

time: 53.7 us -> 55.4 us (1.032)
  Pallas kernels: 27.8 us -> 28.9 us
  waiting for transfers between devices: 8.96 us -> 9.56 us
    pallas_call x2, Pallas kernels: 16.5 us -> 17.7 us  [sums(): pl.pallas_call(functools.partial(sums_kernel, first, steps), out_shape=(j...]
    pallas_call x3, Pallas kernels: 5.77 us -> 5.05 us  [down(): pl.pallas_call(functools.partial(kernel, chunk[0], half, sides), out_shap...]
    pallas_call x1, Pallas kernels: 5.53 us -> 6.18 us  [load(): pl.pallas_call(functools.partial(load_kernel, chunk[0], chunk[1] // 2), o...]
    ppermute x6, waiting for transfers between devices: 4.55 us -> 5.19 us  [swap(): return lax.ppermute(x, axis, [(0, 1), (1, 0)])]
  transfers between devices with their start and end apart: 12 -> 12, of which waited for: 7 -> 7; matrix products, arithmetic and copies ran while one was open for 1% -> 1% of each run, Pallas kernels for 35% -> 34%
where the time goes in v16:
time: 55.4 us; the launch traced here: 55.3 us
  Pallas kernels  28.9 us (52%)
  starting transfers between devices  13.4 us (24%)
  waiting for transfers between devices  9.56 us (17%)
  local copies, waits for them, and re-layouts  2.49 us (4%)
  other arithmetic  0.64 us (1%)
    pallas_call x2, Pallas kernels, sums(): pl.pallas_call(functools.partial(sums_kernel, first, steps), out_shape=(j...  17.7 us
    ppermute x6, starting transfers between devices, across(): return lax.ppermute(x, 'wide', [(i, i ^ apart) for i in range(4)])  10.1 us
    pallas_call x1, Pallas kernels, load(): pl.pallas_call(functools.partial(load_kernel, chunk[0], chunk[1] // 2), o...  6.18 us
    ppermute x6, waiting for transfers between devices, swap(): return lax.ppermute(x, axis, [(0, 1), (1, 0)])  5.19 us
    pallas_call x3, Pallas kernels, down(): pl.pallas_call(functools.partial(kernel, chunk[0], half, sides), out_shap...  5.05 us
    ppermute x6, waiting for transfers between devices, across(): return lax.ppermute(x, 'wide', [(i, i ^ apart) for i in range(4)])  4.37 us
    ppermute x6, starting transfers between devices, swap(): return lax.ppermute(x, axis, [(0, 1), (1, 0)])  3.28 us
    unnamed x18, local copies, waits for them, and re-layouts  2.42 us
  transfers between devices with their start and end apart: 12, of which 7 were waited for; matrix products, arithmetic and copies ran while one was open for 1% of the time, Pallas kernels for 34%

profile of v16, /device:TPU:0, one launch (start us, length us, event | category | flops | bytes accessed | tf_op | source)
XLA Modules:
  0.0 55.3 jit_solution(5404249723893592295)
XLA Ops:
  0.0 5.0 %collective-permute-start = (bf16[12,2048]{1,0:T(8,128)(2,1)}, bf16[12,2048]{1,0:T(8,128)(2,1)S(1)}, u32[]{:S(2)}, u32[]{:S(2)}) collective-permute-start(bf16[12,2048]{1,0:T(8,128)(2,1)} %param.4), channel_id=1, source_target_pairs={{0,12},{4,8},{8,4},{12,0},{1,13},{5,9},{9,5},{13,1},{2,14},{6,10},... | collective-permute-start | bytes 147464 | tf_op jit(solution)/shard_map/ppermute | solution.py:202
  5.1 0.6 %collective-permute-start.1 = (bf16[12,2048]{1,0:T(8,128)(2,1)}, bf16[12,2048]{1,0:T(8,128)(2,1)S(1)}, u32[]{:S(2)}, u32[]{:S(2)}) collective-permute-start(bf16[12,2048]{1,0:T(8,128)(2,1)} %param.4), channel_id=1, source_target_pairs={{0,8},{4,12},{8,0},{12,4},{1,9},{5,13},{9,1},{13,5},{2,10},{6,14},... | collective-permute-start | bytes 147464 | tf_op jit(solution)/shard_map/ppermute | solution.py:202
  5.7 6.2 %load.1.refs_0_ = bf16[8,2,2048,256]{3,2,1,0:T(8,128)(2,1)S(1)} custom-call(bf16[2048,6656]{1,0:T(8,128)(2,1)} %gate.5, bf16[2048,6656]{1,0:T(8,128)(2,1)} %up.5), custom_call_target="tpu_custom_call" | custom-call | bytes 16777216 | tf_op jit(solution)/shard_map/load/pallas_call | solution.py:79
  12.0 9.0 %sums.2 = (bf16[48,4096]{1,0:T(8,128)(2,1)S(1)}, f32[48,4096]{1,0:T(8,128)S(1)}) custom-call(bf16[48,2048]{1,0:T(8,128)(2,1)S(1)} %pad_maximum_fusion.tokens, bf16[2048,6656]{1,0:T(8,128)(2,1)} %gate.5, bf16[2048,6656]{1,0:T(8,128)(2,1)} %up.5, bf16[8,2,2048,256]{3,2,1,0:T(8,128)(2,1)S(1)} %load.1.refs_0_), custom_call_target="tpu_custom_call" | custom-call | flops 1610612736 | bytes 33554432 | tf_op jit(solution)/shard_map/sums/pallas_call | solution.py:124
  21.0 1.7 %collective-permute-done.3 = bf16[48,4096]{1,0:T(8,128)(2,1)S(1)} collective-permute-done((bf16[48,4096]{1,0:T(8,128)(2,1)S(1)}, bf16[48,4096]{1,0:T(8,128)(2,1)S(1)}, u32[]{:S(2)}, u32[]{:S(2)}) %collective-permute-start.3) | collective-permute-done | bytes 393248 | tf_op jit(solution)/shard_map/ppermute | solution.py:34
  22.9 1.7 %collective-permute-start.4 = (bf16[48,4096]{1,0:T(8,128)(2,1)S(1)}, bf16[48,4096]{1,0:T(8,128)(2,1)S(1)}, u32[]{:S(2)}, u32[]{:S(2)}) collective-permute-start(bf16[48,4096]{1,0:T(8,128)(2,1)S(1)} %fusion), channel_id=1, source_target_pairs={{0,2},{2,0},{1,3},{3,1},{4,6},{6,4},{5,7},{7,5},{8,10},{10,8},{9,1... | collective-permute-start | bytes 1179656 | tf_op jit(solution)/shard_map/ppermute | solution.py:34
  24.6 8.7 %sums.3 = (bf16[48,2560]{1,0:T(8,128)(2,1)S(1)}, f32[48,2560]{1,0:T(8,128)S(1)}) custom-call(bf16[48,2048]{1,0:T(8,128)(2,1)S(1)} %pad_maximum_fusion.tokens, bf16[2048,6656]{1,0:T(8,128)(2,1)} %gate.5, bf16[2048,6656]{1,0:T(8,128)(2,1)} %up.5), custom_call_target="tpu_custom_call" | custom-call | flops 1006632960 | bytes 20971520 | tf_op jit(solution)/shard_map/sums/pallas_call | solution.py:124
  33.5 0.7 %collective-permute-done.4 = bf16[48,4096]{1,0:T(8,128)(2,1)S(1)} collective-permute-done((bf16[48,4096]{1,0:T(8,128)(2,1)S(1)}, bf16[48,4096]{1,0:T(8,128)(2,1)S(1)}, u32[]{:S(2)}, u32[]{:S(2)}) %collective-permute-start.4) | collective-permute-done | bytes 393248 | tf_op jit(solution)/shard_map/ppermute | solution.py:34
  34.1 0.1 convert_add_fusion
  34.3 0.1 fusion.1.refs_0_
  34.5 0.5 collective-permute-done.5
  35.0 1.3 %collective-permute-start.6 = (bf16[48,2560]{1,0:T(8,128)(2,1)S(1)}, bf16[48,2560]{1,0:T(8,128)(2,1)S(1)}, u32[]{:S(2)}, u32[]{:S(2)}) collective-permute-start(bf16[48,2560]{1,0:T(8,128)(2,1)S(1)} %fusion.2), channel_id=1, source_target_pairs={{0,2},{2,0},{1,3},{3,1},{4,6},{6,4},{5,7},{7,5},{8,10},{10,8},{9,1... | collective-permute-start | bytes 737288 | tf_op jit(solution)/shard_map/ppermute | solution.py:34
  36.3 1.1 %slice-done.5 = s8[4194304]{0:T(1024)(128)(4,1)S(1)} async-done(((s8[27262976]{0:T(1024)(128)(4,1)}), s8[4194304]{0:T(1024)(128)(4,1)S(1)}, s32[]{:S(2)}) %slice-start.5) | async-done | bytes 4194328
  37.4 0.6 %slice-done.6 = s8[2097152]{0:T(1024)(128)(4,1)S(1)} async-done(((s8[27262976]{0:T(1024)(128)(4,1)}), s8[2097152]{0:T(1024)(128)(4,1)S(1)}, s32[]{:S(2)}) %slice-start.6) | async-done | bytes 2097176
  38.0 3.0 %down.3.refs_1_ = f32[48,2048]{1,0:T(8,128)S(1)} custom-call(bf16[6656,2048]{1,0:T(8,128)(2,1)S(1)} %bitcast.5, bf16[48,2048]{1,0:T(8,128)(2,1)S(1)} %fusion.1.refs_0_, bf16[48,2048]{1,0:T(8,128)(2,1)S(1)} %collective-permute-done.7.refs_1_), custom_call_target="tpu_custom_call" | custom-call | flops 805306368 | bytes 16777216 | tf_op jit(solution)/shard_map/down/pallas_call | solution.py:181
  41.0 2.0 %collective-permute-done.6 = bf16[48,2560]{1,0:T(8,128)(2,1)S(1)} collective-permute-done((bf16[48,2560]{1,0:T(8,128)(2,1)S(1)}, bf16[48,2560]{1,0:T(8,128)(2,1)S(1)}, u32[]{:S(2)}, u32[]{:S(2)}) %collective-permute-start.6) | collective-permute-done | bytes 245792 | tf_op jit(solution)/shard_map/ppermute | solution.py:34
  43.3 1.0 %down.4.total = f32[48,2048]{1,0:T(8,128)S(1)} custom-call(bf16[6656,2048]{1,0:T(8,128)(2,1)S(1)} %bitcast.5, bf16[48,1280]{1,0:T(8,128)(2,1)S(1)} %fusion.3.refs_0_, f32[48,2048]{1,0:T(8,128)S(1)} %down.3.refs_1_), custom_call_target="tpu_custom_call" | custom-call | flops 251658240 | bytes 5242880 | tf_op jit(solution)/shard_map/down/pallas_call | solution.py:181
  44.3 0.3 collective-permute-done.8.hidden
  44.6 1.0 %down.5 = (f32[24,1024]{1,0:T(8,128)S(1)}, bf16[24,1024]{1,0:T(8,128)(2,1)S(1)}, bf16[24,1024]{1,0:T(8,128)(2,1)S(1)}, bf16[24,1024]{1,0:T(8,128)(2,1)S(1)}) custom-call(bf16[6656,2048]{1,0:T(8,128)(2,1)S(1)} %bitcast.5, bf16[48,1280]{1,0:T(8,128)(2,1)S(1)} %collective-permute-done.8.hidden, f32[48,2048]{1,0:T(8,128)S(1)} %down.4.total), custom_call_target="tpu_custom_call" | custom-call | flops 251658240 | bytes 5242880 | tf_op jit(solution)/shard_map/down/pallas_call | solution.py:181
  45.6 3.7 %collective-permute-start.9 = (bf16[24,1024]{1,0:T(8,128)(2,1)S(1)}, bf16[24,1024]{1,0:T(8,128)(2,1)S(1)}, u32[]{:S(2)}, u32[]{:S(2)}) collective-permute-start(bf16[24,1024]{1,0:T(8,128)(2,1)S(1)} %get-tuple-element.28), channel_id=1, source_target_pairs={{0,12},{4,8},{8,4},{12,0},{1,13},{5,9},{9,5},{13,1},{2,14},{6,10},... | collective-permute-start | bytes 147464 | tf_op jit(solution)/shard_map/ppermute | solution.py:202
  49.4 0.7 %collective-permute-start.11 = (bf16[24,1024]{1,0:T(8,128)(2,1)S(1)}, bf16[24,1024]{1,0:T(8,128)(2,1)S(1)}, u32[]{:S(2)}, u32[]{:S(2)}) collective-permute-start(bf16[24,1024]{1,0:T(8,128)(2,1)S(1)} %get-tuple-element.30), channel_id=1, source_target_pairs={{0,4},{4,0},{8,12},{12,8},{1,5},{5,1},{9,13},{13,9},{2,6},{6,2},{1... | collective-permute-start | bytes 147464 | tf_op jit(solution)/shard_map/ppermute | solution.py:202
  50.1 1.8 %collective-permute-done.9 = bf16[24,1024]{1,0:T(8,128)(2,1)S(1)} collective-permute-done((bf16[24,1024]{1,0:T(8,128)(2,1)S(1)}, bf16[24,1024]{1,0:T(8,128)(2,1)S(1)}, u32[]{:S(2)}, u32[]{:S(2)}) %collective-permute-start.9) | collective-permute-done | bytes 49184 | tf_op jit(solution)/shard_map/ppermute | solution.py:202
  51.9 2.6 %collective-permute-done.10 = bf16[24,1024]{1,0:T(8,128)(2,1)S(1)} collective-permute-done((bf16[24,1024]{1,0:T(8,128)(2,1)S(1)}, bf16[24,1024]{1,0:T(8,128)(2,1)S(1)}, u32[]{:S(2)}, u32[]{:S(2)}) %collective-permute-start.10) | collective-permute-done | bytes 49184 | tf_op jit(solution)/shard_map/ppermute | solution.py:202
  54.6 0.6 %copy.7 = bf16[2,8,2,1024]{3,1,2,0:T(8,128)(2,1)} copy(bf16[2,8,2,1024]{3,2,1,0:T(2,128)(2,1)S(1)} %bitcast.7) | data formatting | bytes 131072
  (39 shorter events, 0.9 us)
Async XLA Ops:
  0.0 11.9 %copy-start = (bf16[12,2048]{1,0:T(8,128)(2,1)S(1)}, bf16[12,2048]{1,0:T(8,128)(2,1)}, u32[]{:S(2)}) copy-start(bf16[12,2048]{1,0:T(8,128)(2,1)} %param.4) | copy-start | bytes 147460
  0.0 11.9 %collective-permute-start = (bf16[12,2048]{1,0:T(8,128)(2,1)}, bf16[12,2048]{1,0:T(8,128)(2,1)S(1)}, u32[]{:S(2)}, u32[]{:S(2)}) collective-permute-start(bf16[12,2048]{1,0:T(8,128)(2,1)} %param.4), channel_id=1, source_target_pairs={{0,12},{4,8},{8,4},{12,0},{1,13},{5,9},{9,5},{13,1},{2,14},{6,10},... | collective-permute-start | bytes 147464 | tf_op jit(solution)/shard_map/ppermute | solution.py:202
  5.1 6.9 %collective-permute-start.2 = (bf16[12,2048]{1,0:T(8,128)(2,1)}, bf16[12,2048]{1,0:T(8,128)(2,1)S(1)}, u32[]{:S(2)}, u32[]{:S(2)}) collective-permute-start(bf16[12,2048]{1,0:T(8,128)(2,1)} %param.4), channel_id=1, source_target_pairs={{0,4},{4,0},{8,12},{12,8},{1,5},{5,1},{9,13},{13,9},{2,6},{6,2},{1... | collective-permute-start | bytes 147464 | tf_op jit(solution)/shard_map/ppermute | solution.py:202
  5.1 6.9 %collective-permute-start.1 = (bf16[12,2048]{1,0:T(8,128)(2,1)}, bf16[12,2048]{1,0:T(8,128)(2,1)S(1)}, u32[]{:S(2)}, u32[]{:S(2)}) collective-permute-start(bf16[12,2048]{1,0:T(8,128)(2,1)} %param.4), channel_id=1, source_target_pairs={{0,8},{4,12},{8,0},{12,4},{1,9},{5,13},{9,1},{13,5},{2,10},{6,14},... | collective-permute-start | bytes 147464 | tf_op jit(solution)/shard_map/ppermute | solution.py:202
  21.0 1.8 %collective-permute-start.3 = (bf16[48,4096]{1,0:T(8,128)(2,1)S(1)}, bf16[48,4096]{1,0:T(8,128)(2,1)S(1)}, u32[]{:S(2)}, u32[]{:S(2)}) collective-permute-start(bf16[48,4096]{1,0:T(8,128)(2,1)S(1)} %get-tuple-element.19), channel_id=1, source_target_pairs={{0,1},{1,0},{2,3},{3,2},{4,5},{5,4},{6,7},{7,6},{8,9},{9,8},{10,11... | collective-permute-start | bytes 1179656 | tf_op jit(solution)/shard_map/ppermute | solution.py:34
  22.8 13.5 %slice-start = ((s8[27262976]{0:T(1024)(128)(4,1)}), s8[4194304]{0:T(1024)(128)(4,1)S(1)}, s32[]{:S(2)}) async-start(s8[27262976]{0:T(1024)(128)(4,1)} %bitcast.4), calls=%async_computation | async-start | bytes 8388608
  22.9 13.4 %slice-start.1 = ((s8[27262976]{0:T(1024)(128)(4,1)}), s8[4194304]{0:T(1024)(128)(4,1)S(1)}, s32[]{:S(2)}) async-start(s8[27262976]{0:T(1024)(128)(4,1)} %bitcast.4), calls=%async_computation.1 | async-start | bytes 8388608
  22.9 13.4 %slice-start.2 = ((s8[27262976]{0:T(1024)(128)(4,1)}), s8[4194304]{0:T(1024)(128)(4,1)S(1)}, s32[]{:S(2)}) async-start(s8[27262976]{0:T(1024)(128)(4,1)} %bitcast.4), calls=%async_computation.2 | async-start | bytes 8388608
  22.9 13.4 %slice-start.3 = ((s8[27262976]{0:T(1024)(128)(4,1)}), s8[4194304]{0:T(1024)(128)(4,1)S(1)}, s32[]{:S(2)}) async-start(s8[27262976]{0:T(1024)(128)(4,1)} %bitcast.4), calls=%async_computation.3 | async-start | bytes 8388608
  22.9 13.4 %slice-start.4 = ((s8[27262976]{0:T(1024)(128)(4,1)}), s8[4194304]{0:T(1024)(128)(4,1)S(1)}, s32[]{:S(2)}) async-start(s8[27262976]{0:T(1024)(128)(4,1)} %bitcast.4), calls=%async_computation.4 | async-start | bytes 8388608
  22.9 14.5 %slice-start.5 = ((s8[27262976]{0:T(1024)(128)(4,1)}), s8[4194304]{0:T(1024)(128)(4,1)S(1)}, s32[]{:S(2)}) async-start(s8[27262976]{0:T(1024)(128)(4,1)} %bitcast.4), calls=%async_computation.5 | async-start | bytes 8388608
  22.9 15.1 %slice-start.6 = ((s8[27262976]{0:T(1024)(128)(4,1)}), s8[2097152]{0:T(1024)(128)(4,1)S(1)}, s32[]{:S(2)}) async-start(s8[27262976]{0:T(1024)(128)(4,1)} %bitcast.4), calls=%async_computation.6 | async-start | bytes 4194304
  22.9 11.2 %collective-permute-start.4 = (bf16[48,4096]{1,0:T(8,128)(2,1)S(1)}, bf16[48,4096]{1,0:T(8,128)(2,1)S(1)}, u32[]{:S(2)}, u32[]{:S(2)}) collective-permute-start(bf16[48,4096]{1,0:T(8,128)(2,1)S(1)} %fusion), channel_id=1, source_target_pairs={{0,2},{2,0},{1,3},{3,1},{4,6},{6,4},{5,7},{7,5},{8,10},{10,8},{9,1... | collective-permute-start | bytes 1179656 | tf_op jit(solution)/shard_map/ppermute | solution.py:34
  33.4 1.6 %collective-permute-start.5 = (bf16[48,2560]{1,0:T(8,128)(2,1)S(1)}, bf16[48,2560]{1,0:T(8,128)(2,1)S(1)}, u32[]{:S(2)}, u32[]{:S(2)}) collective-permute-start(bf16[48,2560]{1,0:T(8,128)(2,1)S(1)} %get-tuple-element.23), channel_id=1, source_target_pairs={{0,1},{1,0},{2,3},{3,2},{4,5},{5,4},{6,7},{7,6},{8,9},{9,8},{10,11... | collective-permute-start | bytes 737288 | tf_op jit(solution)/shard_map/ppermute | solution.py:34
  34.4 1.9 %collective-permute-start.7 = (bf16[48,2048]{1,0:T(8,128)(2,1)S(1)}, bf16[48,2048]{1,0:T(8,128)(2,1)S(1)}, u32[]{:S(2)}, u32[]{:S(2)}) collective-permute-start(bf16[48,2048]{1,0:T(8,128)(2,1)S(1)} %fusion.1.refs_0_), channel_id=1, source_target_pairs={{0,1},{1,0},{2,3},{3,2},{4,5},{5,4},{6,7},{7,6},{8,9},{9,8},{10,11... | collective-permute-start | bytes 589832 | tf_op jit(solution)/shard_map/ppermute | solution.py:34
  35.0 8.1 %collective-permute-start.6 = (bf16[48,2560]{1,0:T(8,128)(2,1)S(1)}, bf16[48,2560]{1,0:T(8,128)(2,1)S(1)}, u32[]{:S(2)}, u32[]{:S(2)}) collective-permute-start(bf16[48,2560]{1,0:T(8,128)(2,1)S(1)} %fusion.2), channel_id=1, source_target_pairs={{0,2},{2,0},{1,3},{3,1},{4,6},{6,4},{5,7},{7,5},{8,10},{10,8},{9,1... | collective-permute-start | bytes 737288 | tf_op jit(solution)/shard_map/ppermute | solution.py:34
  43.2 1.4 %collective-permute-start.8 = (bf16[48,1280]{1,0:T(8,128)(2,1)S(1)}, bf16[48,1280]{1,0:T(8,128)(2,1)S(1)}, u32[]{:S(2)}, u32[]{:S(2)}) collective-permute-start(bf16[48,1280]{1,0:T(8,128)(2,1)S(1)} %fusion.3.refs_0_), channel_id=1, source_target_pairs={{0,1},{1,0},{2,3},{3,2},{4,5},{5,4},{6,7},{7,6},{8,9},{9,8},{10,11... | collective-permute-start | bytes 368648 | tf_op jit(solution)/shard_map/ppermute | solution.py:34
  45.6 6.2 %collective-permute-start.9 = (bf16[24,1024]{1,0:T(8,128)(2,1)S(1)}, bf16[24,1024]{1,0:T(8,128)(2,1)S(1)}, u32[]{:S(2)}, u32[]{:S(2)}) collective-permute-start(bf16[24,1024]{1,0:T(8,128)(2,1)S(1)} %get-tuple-element.28), channel_id=1, source_target_pairs={{0,12},{4,8},{8,4},{12,0},{1,13},{5,9},{9,5},{13,1},{2,14},{6,10},... | collective-permute-start | bytes 147464 | tf_op jit(solution)/shard_map/ppermute | solution.py:202
  49.4 5.0 %collective-permute-start.10 = (bf16[24,1024]{1,0:T(8,128)(2,1)S(1)}, bf16[24,1024]{1,0:T(8,128)(2,1)S(1)}, u32[]{:S(2)}, u32[]{:S(2)}) collective-permute-start(bf16[24,1024]{1,0:T(8,128)(2,1)S(1)} %get-tuple-element.29), channel_id=1, source_target_pairs={{0,8},{4,12},{8,0},{12,4},{1,9},{5,13},{9,1},{13,5},{2,10},{6,14},... | collective-permute-start | bytes 147464 | tf_op jit(solution)/shard_map/ppermute | solution.py:202
  49.4 5.1 %collective-permute-start.11 = (bf16[24,1024]{1,0:T(8,128)(2,1)S(1)}, bf16[24,1024]{1,0:T(8,128)(2,1)S(1)}, u32[]{:S(2)}, u32[]{:S(2)}) collective-permute-start(bf16[24,1024]{1,0:T(8,128)(2,1)S(1)} %get-tuple-element.30), channel_id=1, source_target_pairs={{0,4},{4,0},{8,12},{12,8},{1,5},{5,1},{9,13},{13,9},{2,6},{6,2},{1... | collective-permute-start | bytes 147464 | tf_op jit(solution)/shard_map/ppermute | solution.py:202

commit v17 on v14

--- a/solution.py
+++ b/solution.py
@@ -74,34 +74,40 @@
     def side_of(place):
         return first + jnp.where(core == place, 1, 0) * half
 
-    copies = [
-        [
-            pltpu.make_async_copy(
-                up.at[:, pl.ds(pl.multiple_of(side_of(place) + at, BLOCK), BLOCK)],
-                held.at[:, pl.ds(place * half + at, BLOCK)],
-                sems.at[place * (half // BLOCK) + at // BLOCK],
-            )
-            for at in range(0, half, BLOCK)
-        ]
-        for place in range(2)
-    ]
-    for copy in copies[0] + copies[1]:
-        copy.start()
+    def copy(place, block):
+        at = pl.multiple_of(block * BLOCK, BLOCK)
+        return pltpu.make_async_copy(
+            up.at[:, pl.ds(pl.multiple_of(side_of(place) + at, BLOCK), BLOCK)],
+            held.at[:, pl.ds(pl.multiple_of(place * half + at, BLOCK), BLOCK)],
+            sems.at[place * (half // BLOCK) + block],
+        )
+
+    for place in range(2):
+        for block in range(half // BLOCK):
+            copy(place, block).start()
 
     for place, out in enumerate((send, keep)):
-        for at in range(0, half, WIDE):
-            wide = min(WIDE, half - at)
+
+        def steps(body):
+            pl.loop(0, half // WIDE)(lambda step: body(pl.multiple_of(step * WIDE, WIDE), WIDE))
+            if half % WIDE:
+                body(half - half % WIDE, half % WIDE)
+
+        def gate_sums(at, wide):
             columns = pl.ds(pl.multiple_of(side_of(place) + at, BLOCK), wide)
             out[:, pl.ds(at, wide)] = jnp.dot(
                 tokens[...], gate[:, columns], preferred_element_type=F32
             ).astype(out.dtype)
-        for at in range(0, half, WIDE):
-            wide = min(WIDE, half - at)
-            for copy in copies[place][at // BLOCK : (at + wide) // BLOCK]:
-                copy.wait()
+
+        def up_sums(at, wide):
+            for block in range(wide // BLOCK):
+                copy(place, at // BLOCK + block).wait()
             out[:, pl.ds(half + at, wide)] = jnp.dot(
                 tokens[...], held[:, pl.ds(place * half + at, wide)], preferred_element_type=F32
             ).astype(out.dtype)
+
+        steps(gate_sums)
+        steps(up_sums)
 
 
 def sums(tokens, gate, up, chunk, after):

time: 53.5 us -> 52.8 us (0.987)
  Pallas kernels: 22.4 us -> 21.7 us
    pallas_call x1, Pallas kernels: 8.62 us -> 7.97 us  [sums(): pl.pallas_call(functools.partial(sums_kernel, first), out_shape=(jax.Shap...]
where the time goes in v17:
time: 52.8 us; the launch traced here: 52.7 us
  Pallas kernels  21.7 us (41%)
  waiting for transfers between devices  14.1 us (27%)
  starting transfers between devices  13.3 us (25%)
  local copies, waits for them, and re-layouts  2.67 us (5%)
  other arithmetic  0.64 us (1%)
    ppermute x6, starting transfers between devices, across(): return lax.ppermute(x, 'wide', [(i, i ^ apart) for i in range(4)])  10.1 us
    ppermute x6, waiting for transfers between devices, across(): return lax.ppermute(x, 'wide', [(i, i ^ apart) for i in range(4)])  9.01 us
    pallas_call x1, Pallas kernels, stream_sums(): pl.pallas_call(functools.partial(stream_kernel, first, steps), out_shape=...  8.71 us
    pallas_call x1, Pallas kernels, sums(): pl.pallas_call(functools.partial(sums_kernel, first), out_shape=(jax.Shap...  7.97 us
    ppermute x6, waiting for transfers between devices, swap(): return lax.ppermute(x, axis, [(0, 1), (1, 0)])  5.1 us
    pallas_call x3, Pallas kernels, down(): pl.pallas_call(functools.partial(kernel, chunk[0], half, sides), out_shap...  5.06 us
    ppermute x6, starting transfers between devices, swap(): return lax.ppermute(x, axis, [(0, 1), (1, 0)])  3.12 us
    unnamed x20, local copies, waits for them, and re-layouts  2.6 us
  transfers between devices with their start and end apart: 12, of which 9 were waited for; matrix products, arithmetic and copies ran while one was open for 1% of the time, Pallas kernels for 24%

profile of v17, /device:TPU:0, one launch (start us, length us, event | category | flops | bytes accessed | tf_op | source)
XLA Modules:
  0.0 52.7 jit_solution(14416670933023105324)
XLA Ops:
  0.0 5.0 %collective-permute-start = (bf16[12,2048]{1,0:T(8,128)(2,1)}, bf16[12,2048]{1,0:T(8,128)(2,1)S(1)}, u32[]{:S(2)}, u32[]{:S(2)}) collective-permute-start(bf16[12,2048]{1,0:T(8,128)(2,1)} %param.4), channel_id=1, source_target_pairs={{0,12},{4,8},{8,4},{12,0},{1,13},{5,9},{9,5},{13,1},{2,14},{6,10},... | collective-permute-start | bytes 147464 | tf_op jit(solution)/shard_map/ppermute | solution.py:271
  5.1 0.6 %collective-permute-start.1 = (bf16[12,2048]{1,0:T(8,128)(2,1)}, bf16[12,2048]{1,0:T(8,128)(2,1)S(1)}, u32[]{:S(2)}, u32[]{:S(2)}) collective-permute-start(bf16[12,2048]{1,0:T(8,128)(2,1)} %param.4), channel_id=1, source_target_pairs={{0,8},{4,12},{8,0},{12,4},{1,9},{5,13},{9,1},{13,5},{2,10},{6,14},... | collective-permute-start | bytes 147464 | tf_op jit(solution)/shard_map/ppermute | solution.py:271
  5.7 2.5 %collective-permute-done = bf16[12,2048]{1,0:T(8,128)(2,1)S(1)} collective-permute-done((bf16[12,2048]{1,0:T(8,128)(2,1)}, bf16[12,2048]{1,0:T(8,128)(2,1)S(1)}, u32[]{:S(2)}, u32[]{:S(2)}) %collective-permute-start) | collective-permute-done | bytes 49184 | tf_op jit(solution)/shard_map/ppermute | solution.py:271
  8.3 2.6 %collective-permute-done.1 = bf16[12,2048]{1,0:T(8,128)(2,1)S(1)} collective-permute-done((bf16[12,2048]{1,0:T(8,128)(2,1)}, bf16[12,2048]{1,0:T(8,128)(2,1)S(1)}, u32[]{:S(2)}, u32[]{:S(2)}) %collective-permute-start.1) | collective-permute-done | bytes 49184 | tf_op jit(solution)/shard_map/ppermute | solution.py:271
  11.0 8.0 %sums.1 = (bf16[48,4096]{1,0:T(8,128)(2,1)S(1)}, f32[48,4096]{1,0:T(8,128)S(1)}) custom-call(bf16[48,2048]{1,0:T(8,128)(2,1)S(1)} %pad_maximum_fusion.tokens, bf16[2048,6656]{1,0:T(8,128)(2,1)S(1)} %copy-done, bf16[2048,6656]{1,0:T(8,128)(2,1)} %up.3, f32[8,128]{1,0:T(8,128)S(1)} %beside.1.after), custom_call_target="tpu_custom_call" | custom-call | flops 1610612736 | bytes 33554432 | tf_op jit(solution)/shard_map/sums/pallas_call | solution.py:116
  19.0 1.7 %collective-permute-done.3 = bf16[48,4096]{1,0:T(8,128)(2,1)S(1)} collective-permute-done((bf16[48,4096]{1,0:T(8,128)(2,1)S(1)}, bf16[48,4096]{1,0:T(8,128)(2,1)S(1)}, u32[]{:S(2)}, u32[]{:S(2)}) %collective-permute-start.3) | collective-permute-done | bytes 393248 | tf_op jit(solution)/shard_map/ppermute | solution.py:34
  20.9 1.6 %collective-permute-start.4 = (bf16[48,4096]{1,0:T(8,128)(2,1)S(1)}, bf16[48,4096]{1,0:T(8,128)(2,1)S(1)}, u32[]{:S(2)}, u32[]{:S(2)}) collective-permute-start(bf16[48,4096]{1,0:T(8,128)(2,1)S(1)} %fusion), channel_id=1, source_target_pairs={{0,2},{2,0},{1,3},{3,1},{4,6},{6,4},{5,7},{7,5},{8,10},{10,8},{9,1... | collective-permute-start | bytes 1179656 | tf_op jit(solution)/shard_map/ppermute | solution.py:34
  22.5 8.7 %stream_sums.1 = (bf16[48,2560]{1,0:T(8,128)(2,1)S(1)}, f32[48,2560]{1,0:T(8,128)S(1)}) custom-call(bf16[48,2048]{1,0:T(8,128)(2,1)S(1)} %pad_maximum_fusion.tokens, bf16[2048,6656]{1,0:T(8,128)(2,1)} %gate.3, bf16[2048,6656]{1,0:T(8,128)(2,1)} %up.3), custom_call_target="tpu_custom_call" | custom-call | flops 1006632960 | bytes 20971520 | tf_op jit(solution)/shard_map/stream_sums/pallas_call | solution.py:190
  31.3 0.9 %collective-permute-done.4 = bf16[48,4096]{1,0:T(8,128)(2,1)S(1)} collective-permute-done((bf16[48,4096]{1,0:T(8,128)(2,1)S(1)}, bf16[48,4096]{1,0:T(8,128)(2,1)S(1)}, u32[]{:S(2)}, u32[]{:S(2)}) %collective-permute-start.4) | collective-permute-done | bytes 393248 | tf_op jit(solution)/shard_map/ppermute | solution.py:34
  32.5 0.3 collective-permute-done.5
  32.8 1.3 %collective-permute-start.6 = (bf16[48,2560]{1,0:T(8,128)(2,1)S(1)}, bf16[48,2560]{1,0:T(8,128)(2,1)S(1)}, u32[]{:S(2)}, u32[]{:S(2)}) collective-permute-start(bf16[48,2560]{1,0:T(8,128)(2,1)S(1)} %fusion.2), channel_id=1, source_target_pairs={{0,2},{2,0},{1,3},{3,1},{4,6},{6,4},{5,7},{7,5},{8,10},{10,8},{9,1... | collective-permute-start | bytes 737288 | tf_op jit(solution)/shard_map/ppermute | solution.py:34
  34.2 1.2 %slice-done.5 = s8[4194304]{0:T(1024)(128)(4,1)S(1)} async-done(((s8[27262976]{0:T(1024)(128)(4,1)}), s8[4194304]{0:T(1024)(128)(4,1)S(1)}, s32[]{:S(2)}) %slice-start.5) | async-done | bytes 4194328
  35.4 0.6 %slice-done.6 = s8[2097152]{0:T(1024)(128)(4,1)S(1)} async-done(((s8[27262976]{0:T(1024)(128)(4,1)}), s8[2097152]{0:T(1024)(128)(4,1)S(1)}, s32[]{:S(2)}) %slice-start.6) | async-done | bytes 2097176
  36.0 3.0 %down.3.refs_1_ = f32[48,2048]{1,0:T(8,128)S(1)} custom-call(bf16[6656,2048]{1,0:T(8,128)(2,1)S(1)} %bitcast.5, bf16[48,2048]{1,0:T(8,128)(2,1)S(1)} %fusion.1.refs_0_, bf16[48,2048]{1,0:T(8,128)(2,1)S(1)} %collective-permute-done.7.refs_1_), custom_call_target="tpu_custom_call" | custom-call | flops 805306368 | bytes 16777216 | tf_op jit(solution)/shard_map/down/pallas_call | solution.py:250
  39.0 1.9 %collective-permute-done.6 = bf16[48,2560]{1,0:T(8,128)(2,1)S(1)} collective-permute-done((bf16[48,2560]{1,0:T(8,128)(2,1)S(1)}, bf16[48,2560]{1,0:T(8,128)(2,1)S(1)}, u32[]{:S(2)}, u32[]{:S(2)}) %collective-permute-start.6) | collective-permute-done | bytes 245792 | tf_op jit(solution)/shard_map/ppermute | solution.py:34
  41.2 1.0 %down.4.total = f32[48,2048]{1,0:T(8,128)S(1)} custom-call(bf16[6656,2048]{1,0:T(8,128)(2,1)S(1)} %bitcast.5, bf16[48,1280]{1,0:T(8,128)(2,1)S(1)} %fusion.3.refs_0_, f32[48,2048]{1,0:T(8,128)S(1)} %down.3.refs_1_), custom_call_target="tpu_custom_call" | custom-call | flops 251658240 | bytes 5242880 | tf_op jit(solution)/shard_map/down/pallas_call | solution.py:250
  42.2 0.3 collective-permute-done.8.hidden
  42.5 1.0 %down.5 = (f32[24,1024]{1,0:T(8,128)S(1)}, bf16[24,1024]{1,0:T(8,128)(2,1)S(1)}, bf16[24,1024]{1,0:T(8,128)(2,1)S(1)}, bf16[24,1024]{1,0:T(8,128)(2,1)S(1)}) custom-call(bf16[6656,2048]{1,0:T(8,128)(2,1)S(1)} %bitcast.5, bf16[48,1280]{1,0:T(8,128)(2,1)S(1)} %collective-permute-done.8.hidden, f32[48,2048]{1,0:T(8,128)S(1)} %down.4.total), custom_call_target="tpu_custom_call" | custom-call | flops 251658240 | bytes 5242880 | tf_op jit(solution)/shard_map/down/pallas_call | solution.py:250
  43.5 2.9 %collective-permute-start.9 = (bf16[24,1024]{1,0:T(8,128)(2,1)S(1)}, bf16[24,1024]{1,0:T(8,128)(2,1)S(1)}, u32[]{:S(2)}, u32[]{:S(2)}) collective-permute-start(bf16[24,1024]{1,0:T(8,128)(2,1)S(1)} %get-tuple-element.28), channel_id=1, source_target_pairs={{0,12},{4,8},{8,4},{12,0},{1,13},{5,9},{9,5},{13,1},{2,14},{6,10},... | collective-permute-start | bytes 147464 | tf_op jit(solution)/shard_map/ppermute | solution.py:271
  46.4 0.2 collective-permute-start.10
  46.6 1.4 %collective-permute-start.11 = (bf16[24,1024]{1,0:T(8,128)(2,1)S(1)}, bf16[24,1024]{1,0:T(8,128)(2,1)S(1)}, u32[]{:S(2)}, u32[]{:S(2)}) collective-permute-start(bf16[24,1024]{1,0:T(8,128)(2,1)S(1)} %get-tuple-element.30), channel_id=1, source_target_pairs={{0,4},{4,0},{8,12},{12,8},{1,5},{5,1},{9,13},{13,9},{2,6},{6,2},{1... | collective-permute-start | bytes 147464 | tf_op jit(solution)/shard_map/ppermute | solution.py:271
  48.0 2.1 %collective-permute-done.9 = bf16[24,1024]{1,0:T(8,128)(2,1)S(1)} collective-permute-done((bf16[24,1024]{1,0:T(8,128)(2,1)S(1)}, bf16[24,1024]{1,0:T(8,128)(2,1)S(1)}, u32[]{:S(2)}, u32[]{:S(2)}) %collective-permute-start.9) | collective-permute-done | bytes 49184 | tf_op jit(solution)/shard_map/ppermute | solution.py:271
  50.1 1.8 %collective-permute-done.10 = bf16[24,1024]{1,0:T(8,128)(2,1)S(1)} collective-permute-done((bf16[24,1024]{1,0:T(8,128)(2,1)S(1)}, bf16[24,1024]{1,0:T(8,128)(2,1)S(1)}, u32[]{:S(2)}, u32[]{:S(2)}) %collective-permute-start.10) | collective-permute-done | bytes 49184 | tf_op jit(solution)/shard_map/ppermute | solution.py:271
  52.0 0.6 %copy.7 = bf16[2,8,2,1024]{3,1,2,0:T(8,128)(2,1)} copy(bf16[2,8,2,1024]{3,2,1,0:T(2,128)(2,1)S(1)} %bitcast.7) | data formatting | bytes 131072
  (41 shorter events, 1.2 us)
Async XLA Ops:
  0.0 8.2 %copy-start.1 = (bf16[12,2048]{1,0:T(8,128)(2,1)S(1)}, bf16[12,2048]{1,0:T(8,128)(2,1)}, u32[]{:S(2)}) copy-start(bf16[12,2048]{1,0:T(8,128)(2,1)} %param.4) | copy-start | bytes 147460
  0.0 11.0 %copy-start = (bf16[2048,6656]{1,0:T(8,128)(2,1)S(1)}, bf16[2048,6656]{1,0:T(8,128)(2,1)}, u32[]{:S(2)}) copy-start(bf16[2048,6656]{1,0:T(8,128)(2,1)} %gate.3) | copy-start | bytes 81788928
  0.0 8.2 %collective-permute-start = (bf16[12,2048]{1,0:T(8,128)(2,1)}, bf16[12,2048]{1,0:T(8,128)(2,1)S(1)}, u32[]{:S(2)}, u32[]{:S(2)}) collective-permute-start(bf16[12,2048]{1,0:T(8,128)(2,1)} %param.4), channel_id=1, source_target_pairs={{0,12},{4,8},{8,4},{12,0},{1,13},{5,9},{9,5},{13,1},{2,14},{6,10},... | collective-permute-start | bytes 147464 | tf_op jit(solution)/shard_map/ppermute | solution.py:271
  5.1 5.9 %collective-permute-start.2 = (bf16[12,2048]{1,0:T(8,128)(2,1)}, bf16[12,2048]{1,0:T(8,128)(2,1)S(1)}, u32[]{:S(2)}, u32[]{:S(2)}) collective-permute-start(bf16[12,2048]{1,0:T(8,128)(2,1)} %param.4), channel_id=1, source_target_pairs={{0,4},{4,0},{8,12},{12,8},{1,5},{5,1},{9,13},{13,9},{2,6},{6,2},{1... | collective-permute-start | bytes 147464 | tf_op jit(solution)/shard_map/ppermute | solution.py:271
  5.1 5.8 %collective-permute-start.1 = (bf16[12,2048]{1,0:T(8,128)(2,1)}, bf16[12,2048]{1,0:T(8,128)(2,1)S(1)}, u32[]{:S(2)}, u32[]{:S(2)}) collective-permute-start(bf16[12,2048]{1,0:T(8,128)(2,1)} %param.4), channel_id=1, source_target_pairs={{0,8},{4,12},{8,0},{12,4},{1,9},{5,13},{9,1},{13,5},{2,10},{6,14},... | collective-permute-start | bytes 147464 | tf_op jit(solution)/shard_map/ppermute | solution.py:271
  18.9 1.8 %collective-permute-start.3 = (bf16[48,4096]{1,0:T(8,128)(2,1)S(1)}, bf16[48,4096]{1,0:T(8,128)(2,1)S(1)}, u32[]{:S(2)}, u32[]{:S(2)}) collective-permute-start(bf16[48,4096]{1,0:T(8,128)(2,1)S(1)} %get-tuple-element.19), channel_id=1, source_target_pairs={{0,1},{1,0},{2,3},{3,2},{4,5},{5,4},{6,7},{7,6},{8,9},{9,8},{10,11... | collective-permute-start | bytes 1179656 | tf_op jit(solution)/shard_map/ppermute | solution.py:34
  20.7 13.4 %slice-start = ((s8[27262976]{0:T(1024)(128)(4,1)}), s8[4194304]{0:T(1024)(128)(4,1)S(1)}, s32[]{:S(2)}) async-start(s8[27262976]{0:T(1024)(128)(4,1)} %bitcast.4), calls=%async_computation | async-start | bytes 8388608
  20.8 13.3 %slice-start.1 = ((s8[27262976]{0:T(1024)(128)(4,1)}), s8[4194304]{0:T(1024)(128)(4,1)S(1)}, s32[]{:S(2)}) async-start(s8[27262976]{0:T(1024)(128)(4,1)} %bitcast.4), calls=%async_computation.1 | async-start | bytes 8388608
  20.9 13.2 %slice-start.2 = ((s8[27262976]{0:T(1024)(128)(4,1)}), s8[4194304]{0:T(1024)(128)(4,1)S(1)}, s32[]{:S(2)}) async-start(s8[27262976]{0:T(1024)(128)(4,1)} %bitcast.4), calls=%async_computation.2 | async-start | bytes 8388608
  20.9 13.2 %slice-start.3 = ((s8[27262976]{0:T(1024)(128)(4,1)}), s8[4194304]{0:T(1024)(128)(4,1)S(1)}, s32[]{:S(2)}) async-start(s8[27262976]{0:T(1024)(128)(4,1)} %bitcast.4), calls=%async_computation.3 | async-start | bytes 8388608
  20.9 13.3 %slice-start.4 = ((s8[27262976]{0:T(1024)(128)(4,1)}), s8[4194304]{0:T(1024)(128)(4,1)S(1)}, s32[]{:S(2)}) async-start(s8[27262976]{0:T(1024)(128)(4,1)} %bitcast.4), calls=%async_computation.4 | async-start | bytes 8388608
  20.9 14.5 %slice-start.5 = ((s8[27262976]{0:T(1024)(128)(4,1)}), s8[4194304]{0:T(1024)(128)(4,1)S(1)}, s32[]{:S(2)}) async-start(s8[27262976]{0:T(1024)(128)(4,1)} %bitcast.4), calls=%async_computation.5 | async-start | bytes 8388608
  20.9 15.1 %slice-start.6 = ((s8[27262976]{0:T(1024)(128)(4,1)}), s8[2097152]{0:T(1024)(128)(4,1)S(1)}, s32[]{:S(2)}) async-start(s8[27262976]{0:T(1024)(128)(4,1)} %bitcast.4), calls=%async_computation.6 | async-start | bytes 4194304
  20.9 11.2 %collective-permute-start.4 = (bf16[48,4096]{1,0:T(8,128)(2,1)S(1)}, bf16[48,4096]{1,0:T(8,128)(2,1)S(1)}, u32[]{:S(2)}, u32[]{:S(2)}) collective-permute-start(bf16[48,4096]{1,0:T(8,128)(2,1)S(1)} %fusion), channel_id=1, source_target_pairs={{0,2},{2,0},{1,3},{3,1},{4,6},{6,4},{5,7},{7,5},{8,10},{10,8},{9,1... | collective-permute-start | bytes 1179656 | tf_op jit(solution)/shard_map/ppermute | solution.py:34
  31.2 1.6 %collective-permute-start.5 = (bf16[48,2560]{1,0:T(8,128)(2,1)S(1)}, bf16[48,2560]{1,0:T(8,128)(2,1)S(1)}, u32[]{:S(2)}, u32[]{:S(2)}) collective-permute-start(bf16[48,2560]{1,0:T(8,128)(2,1)S(1)} %get-tuple-element.23), channel_id=1, source_target_pairs={{0,1},{1,0},{2,3},{3,2},{4,5},{5,4},{6,7},{7,6},{8,9},{9,8},{10,11... | collective-permute-start | bytes 737288 | tf_op jit(solution)/shard_map/ppermute | solution.py:34
  32.4 1.7 %collective-permute-start.7 = (bf16[48,2048]{1,0:T(8,128)(2,1)S(1)}, bf16[48,2048]{1,0:T(8,128)(2,1)S(1)}, u32[]{:S(2)}, u32[]{:S(2)}) collective-permute-start(bf16[48,2048]{1,0:T(8,128)(2,1)S(1)} %fusion.1.refs_0_), channel_id=1, source_target_pairs={{0,1},{1,0},{2,3},{3,2},{4,5},{5,4},{6,7},{7,6},{8,9},{9,8},{10,11... | collective-permute-start | bytes 589832 | tf_op jit(solution)/shard_map/ppermute | solution.py:34
  32.8 8.1 %collective-permute-start.6 = (bf16[48,2560]{1,0:T(8,128)(2,1)S(1)}, bf16[48,2560]{1,0:T(8,128)(2,1)S(1)}, u32[]{:S(2)}, u32[]{:S(2)}) collective-permute-start(bf16[48,2560]{1,0:T(8,128)(2,1)S(1)} %fusion.2), channel_id=1, source_target_pairs={{0,2},{2,0},{1,3},{3,1},{4,6},{6,4},{5,7},{7,5},{8,10},{10,8},{9,1... | collective-permute-start | bytes 737288 | tf_op jit(solution)/shard_map/ppermute | solution.py:34
  41.1 1.4 %collective-permute-start.8 = (bf16[48,1280]{1,0:T(8,128)(2,1)S(1)}, bf16[48,1280]{1,0:T(8,128)(2,1)S(1)}, u32[]{:S(2)}, u32[]{:S(2)}) collective-permute-start(bf16[48,1280]{1,0:T(8,128)(2,1)S(1)} %fusion.3.refs_0_), channel_id=1, source_target_pairs={{0,1},{1,0},{2,3},{3,2},{4,5},{5,4},{6,7},{7,6},{8,9},{9,8},{10,11... | collective-permute-start | bytes 368648 | tf_op jit(solution)/shard_map/ppermute | solution.py:34
  43.5 6.5 %collective-permute-start.9 = (bf16[24,1024]{1,0:T(8,128)(2,1)S(1)}, bf16[24,1024]{1,0:T(8,128)(2,1)S(1)}, u32[]{:S(2)}, u32[]{:S(2)}) collective-permute-start(bf16[24,1024]{1,0:T(8,128)(2,1)S(1)} %get-tuple-element.28), channel_id=1, source_target_pairs={{0,12},{4,8},{8,4},{12,0},{1,13},{5,9},{9,5},{13,1},{2,14},{6,10},... | collective-permute-start | bytes 147464 | tf_op jit(solution)/shard_map/ppermute | solution.py:271
  46.4 5.4 %collective-permute-start.10 = (bf16[24,1024]{1,0:T(8,128)(2,1)S(1)}, bf16[24,1024]{1,0:T(8,128)(2,1)S(1)}, u32[]{:S(2)}, u32[]{:S(2)}) collective-permute-start(bf16[24,1024]{1,0:T(8,128)(2,1)S(1)} %get-tuple-element.29), channel_id=1, source_target_pairs={{0,8},{4,12},{8,0},{12,4},{1,9},{5,13},{9,1},{13,5},{2,10},{6,14},... | collective-permute-start | bytes 147464 | tf_op jit(solution)/shard_map/ppermute | solution.py:271
  46.6 5.2 %collective-permute-start.11 = (bf16[24,1024]{1,0:T(8,128)(2,1)S(1)}, bf16[24,1024]{1,0:T(8,128)(2,1)S(1)}, u32[]{:S(2)}, u32[]{:S(2)}) collective-permute-start(bf16[24,1024]{1,0:T(8,128)(2,1)S(1)} %get-tuple-element.30), channel_id=1, source_target_pairs={{0,4},{4,0},{8,12},{12,8},{1,5},{5,1},{9,13},{13,9},{2,6},{6,2},{1... | collective-permute-start | bytes 147464 | tf_op jit(solution)/shard_map/ppermute | solution.py:271

commit v18 on v15

--- a/solution.py
+++ b/solution.py
@@ -67,59 +67,56 @@
     )(*operands)
 
 
-def sums_kernel(first, tokens, gate, up, after, send, keep, held, sems):
-    half = send.shape[1] // 2
+def half_sums_kernel(first, half, mine, tokens, gate, up, after, out, held, sems):
     core = lax.axis_index("sub")
-
-    def side_of(place):
-        return first + jnp.where(core == place, 1, 0) * half
-
-    copies = [
-        [
-            pltpu.make_async_copy(
-                up.at[:, pl.ds(pl.multiple_of(side_of(place) + at, BLOCK), BLOCK)],
-                held.at[:, pl.ds(place * half + at, BLOCK)],
-                sems.at[place * (half // BLOCK) + at // BLOCK],
-            )
-            for at in range(0, half, BLOCK)
-        ]
-        for place in range(2)
-    ]
-    for copy in copies[0] + copies[1]:
-        copy.start()
-
-    pieces = [
-        (place, out, at, min(WIDE, half - at))
-        for place, out in enumerate((send, keep))
-        for at in range(0, half, WIDE)
-    ]
-    for place, out, at, wide in pieces:
-        columns = pl.ds(pl.multiple_of(side_of(place) + at, BLOCK), wide)
+    start = first + jnp.where(core == mine, 1, 0) * half
+
+    def copy(block):
+        at = pl.multiple_of(block * BLOCK, BLOCK)
+        return pltpu.make_async_copy(
+            up.at[:, pl.ds(pl.multiple_of(start + at, BLOCK), BLOCK)], held.at[:, pl.ds(at, BLOCK)], sems.at[block]
+        )
+
+    for block in range(half // BLOCK):
+        copy(block).start()
+
+    def steps(body):
+        pl.loop(0, half // WIDE)(lambda step: body(pl.multiple_of(step * WIDE, WIDE), WIDE))
+        if half % WIDE:
+            body(half - half % WIDE, half % WIDE)
+
+    def gate_sums(at, wide):
+        columns = pl.ds(pl.multiple_of(start + at, BLOCK), wide)
         out[:, pl.ds(at, wide)] = jnp.dot(tokens[...], gate[:, columns], preferred_element_type=F32).astype(
             out.dtype
         )
-    for place, out, at, wide in pieces:
-        for copy in copies[place][at // BLOCK : (at + wide) // BLOCK]:
-            copy.wait()
+
+    def up_sums(at, wide):
+        for block in range(wide // BLOCK):
+            copy(at // BLOCK + block).wait()
         out[:, pl.ds(half + at, wide)] = jnp.dot(
-            tokens[...], held[:, pl.ds(place * half + at, wide)], preferred_element_type=F32
+            tokens[...], held[:, pl.ds(at, wide)], preferred_element_type=F32
         ).astype(out.dtype)
 
-
-def sums(tokens, gate, up, chunk, after):
+    steps(gate_sums)
+    steps(up_sums)
+
+
+def half_sums(tokens, gate, up, chunk, mine, after):
     rows, depth = tokens.shape
     first, width = chunk
+    half = width // 2
     return pl.pallas_call(
-        functools.partial(sums_kernel, first),
-        out_shape=(jax.ShapeDtypeStruct((rows, width), BF16), jax.ShapeDtypeStruct((rows, width), F32)),
+        functools.partial(half_sums_kernel, first, half, mine),
+        out_shape=jax.ShapeDtypeStruct((rows, width), F32 if mine else BF16),
         in_specs=[VMEM, VMEM, HBM, ANY],
-        out_specs=(VMEM, VMEM),
-        scratch_shapes=[pltpu.VMEM((depth, width), BF16), pltpu.SemaphoreType.DMA((width // BLOCK,))],
-        compiler_params=pltpu.CompilerParams(vmem_limit_bytes=2 * depth * width + 2 * 2**20),
+        out_specs=VMEM,
+        scratch_shapes=[pltpu.VMEM((depth, half), BF16), pltpu.SemaphoreType.DMA((half // BLOCK,))],
+        compiler_params=pltpu.CompilerParams(vmem_limit_bytes=2 * depth * half + 2 * 2**20),
         cost_estimate=pl.CostEstimate(
-            flops=4 * rows * depth * width, bytes_accessed=4 * depth * width, transcendentals=0
+            flops=2 * rows * depth * width, bytes_accessed=2 * depth * width, transcendentals=0
         ),
-        name="sums",
+        name="half_sums",
     )(tokens, held_in(gate), left_in_hbm(up), after)
 
 
@@ -281,7 +278,8 @@
         return activate(*jnp.split(total + received.astype(F32), 2, axis=1))
 
     ready = beside(gate_weight)
-    send, keep = sums(section, gate_weight, up_weight, chunks[0], ready)
+    send = half_sums(section, gate_weight, up_weight, chunks[0], 0, ready)
+    keep = half_sums(section, gate_weight, up_weight, chunks[0], 1, send)
     total, sent = core_sums(send, keep)
     later, _ = lax.optimization_barrier((section, sent))
     send, keep = stream_sums(later, gate_weight, up_weight, chunks[1])

time: 53.7 us -> 51.6 us (0.961)
  waiting for transfers between devices: 14.1 us -> 12.7 us
  Pallas kernels: 22.7 us -> 21.9 us
    ppermute x6, waiting for transfers between devices: 5.1 us -> 3.68 us  [swap(): return lax.ppermute(x, axis, [(0, 1), (1, 0)])]
    pallas_call x1 -> x2, Pallas kernels: 8.89 us -> 8.16 us  [half_sums(): pl.pallas_call(functools.partial(half_sums_kernel, first, half, mine), ou...]
  transfers between devices with their start and end apart: 12 -> 12, of which waited for: 9 -> 7; matrix products, arithmetic and copies ran while one was open for 1% -> 1% of each run, Pallas kernels for 24% -> 33%
where the time goes in v18:
time: 51.6 us; the launch traced here: 51.5 us
  Pallas kernels  21.9 us (42%)
  starting transfers between devices  13.6 us (26%)
  waiting for transfers between devices  12.7 us (25%)
  local copies, waits for them, and re-layouts  2.36 us (5%)
  other arithmetic  0.59 us (1%)
    ppermute x6, starting transfers between devices, across(): return lax.ppermute(x, 'wide', [(i, i ^ apart) for i in range(4)])  10.1 us
    ppermute x6, waiting for transfers between devices, across(): return lax.ppermute(x, 'wide', [(i, i ^ apart) for i in range(4)])  9.01 us
    pallas_call x1, Pallas kernels, stream_sums(): pl.pallas_call(functools.partial(stream_kernel, first, steps), out_shape=...  8.71 us
    pallas_call x2, Pallas kernels, half_sums(): pl.pallas_call(functools.partial(half_sums_kernel, first, half, mine), ou...  8.16 us
    pallas_call x3, Pallas kernels, down(): pl.pallas_call(functools.partial(kernel, chunk[0], half, sides), out_shap...  5.06 us
    ppermute x6, waiting for transfers between devices, swap(): return lax.ppermute(x, axis, [(0, 1), (1, 0)])  3.68 us
    ppermute x6, starting transfers between devices, swap(): return lax.ppermute(x, axis, [(0, 1), (1, 0)])  3.48 us
    unnamed x20, local copies, waits for them, and re-layouts  2.29 us
  transfers between devices with their start and end apart: 12, of which 7 were waited for; matrix products, arithmetic and copies ran while one was open for 1% of the time, Pallas kernels for 33%

profile of v18, /device:TPU:0, one launch (start us, length us, event | category | flops | bytes accessed | tf_op | source)
XLA Modules:
  0.0 51.5 jit_solution(14435339147865335886)
XLA Ops:
  0.0 5.0 %collective-permute-start = (bf16[12,2048]{1,0:T(8,128)(2,1)}, bf16[12,2048]{1,0:T(8,128)(2,1)S(1)}, u32[]{:S(2)}, u32[]{:S(2)}) collective-permute-start(bf16[12,2048]{1,0:T(8,128)(2,1)} %param.4), channel_id=1, source_target_pairs={{0,12},{4,8},{8,4},{12,0},{1,13},{5,9},{9,5},{13,1},{2,14},{6,10},... | collective-permute-start | bytes 147464 | tf_op jit(solution)/shard_map/ppermute | solution.py:264
  5.1 0.6 %collective-permute-start.1 = (bf16[12,2048]{1,0:T(8,128)(2,1)}, bf16[12,2048]{1,0:T(8,128)(2,1)S(1)}, u32[]{:S(2)}, u32[]{:S(2)}) collective-permute-start(bf16[12,2048]{1,0:T(8,128)(2,1)} %param.4), channel_id=1, source_target_pairs={{0,8},{4,12},{8,0},{12,4},{1,9},{5,13},{9,1},{13,5},{2,10},{6,14},... | collective-permute-start | bytes 147464 | tf_op jit(solution)/shard_map/ppermute | solution.py:264
  5.7 2.5 %collective-permute-done = bf16[12,2048]{1,0:T(8,128)(2,1)S(1)} collective-permute-done((bf16[12,2048]{1,0:T(8,128)(2,1)}, bf16[12,2048]{1,0:T(8,128)(2,1)S(1)}, u32[]{:S(2)}, u32[]{:S(2)}) %collective-permute-start) | collective-permute-done | bytes 49184 | tf_op jit(solution)/shard_map/ppermute | solution.py:264
  8.3 2.6 %collective-permute-done.1 = bf16[12,2048]{1,0:T(8,128)(2,1)S(1)} collective-permute-done((bf16[12,2048]{1,0:T(8,128)(2,1)}, bf16[12,2048]{1,0:T(8,128)(2,1)S(1)}, u32[]{:S(2)}, u32[]{:S(2)}) %collective-permute-start.1) | collective-permute-done | bytes 49184 | tf_op jit(solution)/shard_map/ppermute | solution.py:264
  11.0 4.1 %half_sums.2.after = bf16[48,4096]{1,0:T(8,128)(2,1)S(1)} custom-call(bf16[48,2048]{1,0:T(8,128)(2,1)S(1)} %pad_maximum_fusion.tokens, bf16[2048,6656]{1,0:T(8,128)(2,1)S(1)} %copy-done, bf16[2048,6656]{1,0:T(8,128)(2,1)} %up.5, f32[8,128]{1,0:T(8,128)S(1)} %beside.1.after), custom_call_target="tpu_custom_call" | custom-call | flops 805306368 | bytes 16777216 | tf_op jit(solution)/shard_map/half_sums/pallas_call | solution.py:109
  15.1 4.1 %half_sums.3 = f32[48,4096]{1,0:T(8,128)S(1)} custom-call(bf16[48,2048]{1,0:T(8,128)(2,1)S(1)} %pad_maximum_fusion.tokens, bf16[2048,6656]{1,0:T(8,128)(2,1)S(1)} %copy-done, bf16[2048,6656]{1,0:T(8,128)(2,1)} %up.5, bf16[48,4096]{1,0:T(8,128)(2,1)S(1)} %half_sums.2.after), custom_call_target="tpu_custom_call" | custom-call | flops 805306368 | bytes 16777216 | tf_op jit(solution)/shard_map/half_sums/pallas_call | solution.py:109
  19.4 1.6 %collective-permute-start.4 = (bf16[48,4096]{1,0:T(8,128)(2,1)S(1)}, bf16[48,4096]{1,0:T(8,128)(2,1)S(1)}, u32[]{:S(2)}, u32[]{:S(2)}) collective-permute-start(bf16[48,4096]{1,0:T(8,128)(2,1)S(1)} %fusion), channel_id=1, source_target_pairs={{0,2},{2,0},{1,3},{3,1},{4,6},{6,4},{5,7},{7,5},{8,10},{10,8},{9,1... | collective-permute-start | bytes 1179656 | tf_op jit(solution)/shard_map/ppermute | solution.py:34
  20.9 8.7 %stream_sums.1 = (bf16[48,2560]{1,0:T(8,128)(2,1)S(1)}, f32[48,2560]{1,0:T(8,128)S(1)}) custom-call(bf16[48,2048]{1,0:T(8,128)(2,1)S(1)} %pad_maximum_fusion.tokens, bf16[2048,6656]{1,0:T(8,128)(2,1)} %gate.5, bf16[2048,6656]{1,0:T(8,128)(2,1)} %up.5), custom_call_target="tpu_custom_call" | custom-call | flops 1006632960 | bytes 20971520 | tf_op jit(solution)/shard_map/stream_sums/pallas_call | solution.py:183
  29.7 0.2 collective-permute-start.5
  29.8 1.1 %collective-permute-done.4 = bf16[48,4096]{1,0:T(8,128)(2,1)S(1)} collective-permute-done((bf16[48,4096]{1,0:T(8,128)(2,1)S(1)}, bf16[48,4096]{1,0:T(8,128)(2,1)S(1)}, u32[]{:S(2)}, u32[]{:S(2)}) %collective-permute-start.4) | collective-permute-done | bytes 393248 | tf_op jit(solution)/shard_map/ppermute | solution.py:34
  31.3 1.6 %collective-permute-start.6 = (bf16[48,2560]{1,0:T(8,128)(2,1)S(1)}, bf16[48,2560]{1,0:T(8,128)(2,1)S(1)}, u32[]{:S(2)}, u32[]{:S(2)}) collective-permute-start(bf16[48,2560]{1,0:T(8,128)(2,1)S(1)} %fusion.2), channel_id=1, source_target_pairs={{0,2},{2,0},{1,3},{3,1},{4,6},{6,4},{5,7},{7,5},{8,10},{10,8},{9,1... | collective-permute-start | bytes 737288 | tf_op jit(solution)/shard_map/ppermute | solution.py:34
  32.9 1.0 %slice-done.5 = s8[4194304]{0:T(1024)(128)(4,1)S(1)} async-done(((s8[27262976]{0:T(1024)(128)(4,1)}), s8[4194304]{0:T(1024)(128)(4,1)S(1)}, s32[]{:S(2)}) %slice-start.5) | async-done | bytes 4194328
  33.9 0.6 %slice-done.6 = s8[2097152]{0:T(1024)(128)(4,1)S(1)} async-done(((s8[27262976]{0:T(1024)(128)(4,1)}), s8[2097152]{0:T(1024)(128)(4,1)S(1)}, s32[]{:S(2)}) %slice-start.6) | async-done | bytes 2097176
  34.5 3.0 %down.3.refs_1_ = f32[48,2048]{1,0:T(8,128)S(1)} custom-call(bf16[6656,2048]{1,0:T(8,128)(2,1)S(1)} %bitcast.5, bf16[48,2048]{1,0:T(8,128)(2,1)S(1)} %fusion.1.refs_0_, bf16[48,2048]{1,0:T(8,128)(2,1)S(1)} %collective-permute-done.7.refs_1_), custom_call_target="tpu_custom_call" | custom-call | flops 805306368 | bytes 16777216 | tf_op jit(solution)/shard_map/down/pallas_call | solution.py:243
  37.5 2.2 %collective-permute-done.6 = bf16[48,2560]{1,0:T(8,128)(2,1)S(1)} collective-permute-done((bf16[48,2560]{1,0:T(8,128)(2,1)S(1)}, bf16[48,2560]{1,0:T(8,128)(2,1)S(1)}, u32[]{:S(2)}, u32[]{:S(2)}) %collective-permute-start.6) | collective-permute-done | bytes 245792 | tf_op jit(solution)/shard_map/ppermute | solution.py:34
  40.0 1.0 %down.4.total = f32[48,2048]{1,0:T(8,128)S(1)} custom-call(bf16[6656,2048]{1,0:T(8,128)(2,1)S(1)} %bitcast.5, bf16[48,1280]{1,0:T(8,128)(2,1)S(1)} %fusion.3.refs_0_, f32[48,2048]{1,0:T(8,128)S(1)} %down.3.refs_1_), custom_call_target="tpu_custom_call" | custom-call | flops 251658240 | bytes 5242880 | tf_op jit(solution)/shard_map/down/pallas_call | solution.py:243
  41.0 0.3 collective-permute-done.8.hidden
  41.3 1.0 %down.5 = (f32[24,1024]{1,0:T(8,128)S(1)}, bf16[24,1024]{1,0:T(8,128)(2,1)S(1)}, bf16[24,1024]{1,0:T(8,128)(2,1)S(1)}, bf16[24,1024]{1,0:T(8,128)(2,1)S(1)}) custom-call(bf16[6656,2048]{1,0:T(8,128)(2,1)S(1)} %bitcast.5, bf16[48,1280]{1,0:T(8,128)(2,1)S(1)} %collective-permute-done.8.hidden, f32[48,2048]{1,0:T(8,128)S(1)} %down.4.total), custom_call_target="tpu_custom_call" | custom-call | flops 251658240 | bytes 5242880 | tf_op jit(solution)/shard_map/down/pallas_call | solution.py:243
  42.3 2.9 %collective-permute-start.9 = (bf16[24,1024]{1,0:T(8,128)(2,1)S(1)}, bf16[24,1024]{1,0:T(8,128)(2,1)S(1)}, u32[]{:S(2)}, u32[]{:S(2)}) collective-permute-start(bf16[24,1024]{1,0:T(8,128)(2,1)S(1)} %get-tuple-element.24), channel_id=1, source_target_pairs={{0,12},{4,8},{8,4},{12,0},{1,13},{5,9},{9,5},{13,1},{2,14},{6,10},... | collective-permute-start | bytes 147464 | tf_op jit(solution)/shard_map/ppermute | solution.py:264
  45.3 0.2 collective-permute-start.10
  45.4 1.4 %collective-permute-start.11 = (bf16[24,1024]{1,0:T(8,128)(2,1)S(1)}, bf16[24,1024]{1,0:T(8,128)(2,1)S(1)}, u32[]{:S(2)}, u32[]{:S(2)}) collective-permute-start(bf16[24,1024]{1,0:T(8,128)(2,1)S(1)} %get-tuple-element.26), channel_id=1, source_target_pairs={{0,4},{4,0},{8,12},{12,8},{1,5},{5,1},{9,13},{13,9},{2,6},{6,2},{1... | collective-permute-start | bytes 147464 | tf_op jit(solution)/shard_map/ppermute | solution.py:264
  46.8 2.1 %collective-permute-done.9 = bf16[24,1024]{1,0:T(8,128)(2,1)S(1)} collective-permute-done((bf16[24,1024]{1,0:T(8,128)(2,1)S(1)}, bf16[24,1024]{1,0:T(8,128)(2,1)S(1)}, u32[]{:S(2)}, u32[]{:S(2)}) %collective-permute-start.9) | collective-permute-done | bytes 49184 | tf_op jit(solution)/shard_map/ppermute | solution.py:264
  48.9 1.8 %collective-permute-done.10 = bf16[24,1024]{1,0:T(8,128)(2,1)S(1)} collective-permute-done((bf16[24,1024]{1,0:T(8,128)(2,1)S(1)}, bf16[24,1024]{1,0:T(8,128)(2,1)S(1)}, u32[]{:S(2)}, u32[]{:S(2)}) %collective-permute-start.10) | collective-permute-done | bytes 49184 | tf_op jit(solution)/shard_map/ppermute | solution.py:264
  50.8 0.6 %copy.7 = bf16[2,8,2,1024]{3,1,2,0:T(8,128)(2,1)} copy(bf16[2,8,2,1024]{3,2,1,0:T(2,128)(2,1)S(1)} %bitcast.7) | data formatting | bytes 131072
  (42 shorter events, 1.0 us)
Async XLA Ops:
  0.0 8.2 %copy-start.1 = (bf16[12,2048]{1,0:T(8,128)(2,1)S(1)}, bf16[12,2048]{1,0:T(8,128)(2,1)}, u32[]{:S(2)}) copy-start(bf16[12,2048]{1,0:T(8,128)(2,1)} %param.4) | copy-start | bytes 147460
  0.0 11.0 %copy-start = (bf16[2048,6656]{1,0:T(8,128)(2,1)S(1)}, bf16[2048,6656]{1,0:T(8,128)(2,1)}, u32[]{:S(2)}) copy-start(bf16[2048,6656]{1,0:T(8,128)(2,1)} %gate.5) | copy-start | bytes 81788928
  0.0 8.2 %collective-permute-start = (bf16[12,2048]{1,0:T(8,128)(2,1)}, bf16[12,2048]{1,0:T(8,128)(2,1)S(1)}, u32[]{:S(2)}, u32[]{:S(2)}) collective-permute-start(bf16[12,2048]{1,0:T(8,128)(2,1)} %param.4), channel_id=1, source_target_pairs={{0,12},{4,8},{8,4},{12,0},{1,13},{5,9},{9,5},{13,1},{2,14},{6,10},... | collective-permute-start | bytes 147464 | tf_op jit(solution)/shard_map/ppermute | solution.py:264
  5.1 5.9 %collective-permute-start.2 = (bf16[12,2048]{1,0:T(8,128)(2,1)}, bf16[12,2048]{1,0:T(8,128)(2,1)S(1)}, u32[]{:S(2)}, u32[]{:S(2)}) collective-permute-start(bf16[12,2048]{1,0:T(8,128)(2,1)} %param.4), channel_id=1, source_target_pairs={{0,4},{4,0},{8,12},{12,8},{1,5},{5,1},{9,13},{13,9},{2,6},{6,2},{1... | collective-permute-start | bytes 147464 | tf_op jit(solution)/shard_map/ppermute | solution.py:264
  5.1 5.8 %collective-permute-start.1 = (bf16[12,2048]{1,0:T(8,128)(2,1)}, bf16[12,2048]{1,0:T(8,128)(2,1)S(1)}, u32[]{:S(2)}, u32[]{:S(2)}) collective-permute-start(bf16[12,2048]{1,0:T(8,128)(2,1)} %param.4), channel_id=1, source_target_pairs={{0,8},{4,12},{8,0},{12,4},{1,9},{5,13},{9,1},{13,5},{2,10},{6,14},... | collective-permute-start | bytes 147464 | tf_op jit(solution)/shard_map/ppermute | solution.py:264
  15.1 4.2 %collective-permute-start.3 = (bf16[48,4096]{1,0:T(8,128)(2,1)S(1)}, bf16[48,4096]{1,0:T(8,128)(2,1)S(1)}, u32[]{:S(2)}, u32[]{:S(2)}) collective-permute-start(bf16[48,4096]{1,0:T(8,128)(2,1)S(1)} %half_sums.2.after), channel_id=1, source_target_pairs={{0,1},{1,0},{2,3},{3,2},{4,5},{5,4},{6,7},{7,6},{8,9},{9,8},{10,11... | collective-permute-start | bytes 1179656 | tf_op jit(solution)/shard_map/ppermute | solution.py:34
  19.2 13.7 %slice-start = ((s8[27262976]{0:T(1024)(128)(4,1)}), s8[4194304]{0:T(1024)(128)(4,1)S(1)}, s32[]{:S(2)}) async-start(s8[27262976]{0:T(1024)(128)(4,1)} %bitcast.4), calls=%async_computation | async-start | bytes 8388608
  19.3 13.6 %slice-start.1 = ((s8[27262976]{0:T(1024)(128)(4,1)}), s8[4194304]{0:T(1024)(128)(4,1)S(1)}, s32[]{:S(2)}) async-start(s8[27262976]{0:T(1024)(128)(4,1)} %bitcast.4), calls=%async_computation.1 | async-start | bytes 8388608
  19.3 13.6 %slice-start.2 = ((s8[27262976]{0:T(1024)(128)(4,1)}), s8[4194304]{0:T(1024)(128)(4,1)S(1)}, s32[]{:S(2)}) async-start(s8[27262976]{0:T(1024)(128)(4,1)} %bitcast.4), calls=%async_computation.2 | async-start | bytes 8388608
  19.4 13.6 %slice-start.3 = ((s8[27262976]{0:T(1024)(128)(4,1)}), s8[4194304]{0:T(1024)(128)(4,1)S(1)}, s32[]{:S(2)}) async-start(s8[27262976]{0:T(1024)(128)(4,1)} %bitcast.4), calls=%async_computation.3 | async-start | bytes 8388608
  19.4 13.6 %slice-start.4 = ((s8[27262976]{0:T(1024)(128)(4,1)}), s8[4194304]{0:T(1024)(128)(4,1)S(1)}, s32[]{:S(2)}) async-start(s8[27262976]{0:T(1024)(128)(4,1)} %bitcast.4), calls=%async_computation.4 | async-start | bytes 8388608
  19.4 14.5 %slice-start.5 = ((s8[27262976]{0:T(1024)(128)(4,1)}), s8[4194304]{0:T(1024)(128)(4,1)S(1)}, s32[]{:S(2)}) async-start(s8[27262976]{0:T(1024)(128)(4,1)} %bitcast.4), calls=%async_computation.5 | async-start | bytes 8388608
  19.4 15.1 %slice-start.6 = ((s8[27262976]{0:T(1024)(128)(4,1)}), s8[2097152]{0:T(1024)(128)(4,1)S(1)}, s32[]{:S(2)}) async-start(s8[27262976]{0:T(1024)(128)(4,1)} %bitcast.4), calls=%async_computation.6 | async-start | bytes 4194304
  19.4 11.6 %collective-permute-start.4 = (bf16[48,4096]{1,0:T(8,128)(2,1)S(1)}, bf16[48,4096]{1,0:T(8,128)(2,1)S(1)}, u32[]{:S(2)}, u32[]{:S(2)}) collective-permute-start(bf16[48,4096]{1,0:T(8,128)(2,1)S(1)} %fusion), channel_id=1, source_target_pairs={{0,2},{2,0},{1,3},{3,1},{4,6},{6,4},{5,7},{7,5},{8,10},{10,8},{9,1... | collective-permute-start | bytes 1179656 | tf_op jit(solution)/shard_map/ppermute | solution.py:34
  29.7 1.6 %collective-permute-start.5 = (bf16[48,2560]{1,0:T(8,128)(2,1)S(1)}, bf16[48,2560]{1,0:T(8,128)(2,1)S(1)}, u32[]{:S(2)}, u32[]{:S(2)}) collective-permute-start(bf16[48,2560]{1,0:T(8,128)(2,1)S(1)} %get-tuple-element.19), channel_id=1, source_target_pairs={{0,1},{1,0},{2,3},{3,2},{4,5},{5,4},{6,7},{7,6},{8,9},{9,8},{10,11... | collective-permute-start | bytes 737288 | tf_op jit(solution)/shard_map/ppermute | solution.py:34
  31.2 1.7 %collective-permute-start.7 = (bf16[48,2048]{1,0:T(8,128)(2,1)S(1)}, bf16[48,2048]{1,0:T(8,128)(2,1)S(1)}, u32[]{:S(2)}, u32[]{:S(2)}) collective-permute-start(bf16[48,2048]{1,0:T(8,128)(2,1)S(1)} %fusion.1.refs_0_), channel_id=1, source_target_pairs={{0,1},{1,0},{2,3},{3,2},{4,5},{5,4},{6,7},{7,6},{8,9},{9,8},{10,11... | collective-permute-start | bytes 589832 | tf_op jit(solution)/shard_map/ppermute | solution.py:34
  31.3 8.4 %collective-permute-start.6 = (bf16[48,2560]{1,0:T(8,128)(2,1)S(1)}, bf16[48,2560]{1,0:T(8,128)(2,1)S(1)}, u32[]{:S(2)}, u32[]{:S(2)}) collective-permute-start(bf16[48,2560]{1,0:T(8,128)(2,1)S(1)} %fusion.2), channel_id=1, source_target_pairs={{0,2},{2,0},{1,3},{3,1},{4,6},{6,4},{5,7},{7,5},{8,10},{10,8},{9,1... | collective-permute-start | bytes 737288 | tf_op jit(solution)/shard_map/ppermute | solution.py:34
  39.9 1.4 %collective-permute-start.8 = (bf16[48,1280]{1,0:T(8,128)(2,1)S(1)}, bf16[48,1280]{1,0:T(8,128)(2,1)S(1)}, u32[]{:S(2)}, u32[]{:S(2)}) collective-permute-start(bf16[48,1280]{1,0:T(8,128)(2,1)S(1)} %fusion.3.refs_0_), channel_id=1, source_target_pairs={{0,1},{1,0},{2,3},{3,2},{4,5},{5,4},{6,7},{7,6},{8,9},{9,8},{10,11... | collective-permute-start | bytes 368648 | tf_op jit(solution)/shard_map/ppermute | solution.py:34
  42.3 6.5 %collective-permute-start.9 = (bf16[24,1024]{1,0:T(8,128)(2,1)S(1)}, bf16[24,1024]{1,0:T(8,128)(2,1)S(1)}, u32[]{:S(2)}, u32[]{:S(2)}) collective-permute-start(bf16[24,1024]{1,0:T(8,128)(2,1)S(1)} %get-tuple-element.24), channel_id=1, source_target_pairs={{0,12},{4,8},{8,4},{12,0},{1,13},{5,9},{9,5},{13,1},{2,14},{6,10},... | collective-permute-start | bytes 147464 | tf_op jit(solution)/shard_map/ppermute | solution.py:264
  45.3 5.4 %collective-permute-start.10 = (bf16[24,1024]{1,0:T(8,128)(2,1)S(1)}, bf16[24,1024]{1,0:T(8,128)(2,1)S(1)}, u32[]{:S(2)}, u32[]{:S(2)}) collective-permute-start(bf16[24,1024]{1,0:T(8,128)(2,1)S(1)} %get-tuple-element.25), channel_id=1, source_target_pairs={{0,8},{4,12},{8,0},{12,4},{1,9},{5,13},{9,1},{13,5},{2,10},{6,14},... | collective-permute-start | bytes 147464 | tf_op jit(solution)/shard_map/ppermute | solution.py:264
  45.4 5.2 %collective-permute-start.11 = (bf16[24,1024]{1,0:T(8,128)(2,1)S(1)}, bf16[24,1024]{1,0:T(8,128)(2,1)S(1)}, u32[]{:S(2)}, u32[]{:S(2)}) collective-permute-start(bf16[24,1024]{1,0:T(8,128)(2,1)S(1)} %get-tuple-element.26), channel_id=1, source_target_pairs={{0,4},{4,0},{8,12},{12,8},{1,5},{5,1},{9,13},{13,9},{2,6},{6,2},{1... | collective-permute-start | bytes 147464 | tf_op jit(solution)/shard_map/ppermute | solution.py:264

commit v19 on v18

--- a/solution.py
+++ b/solution.py
@@ -81,7 +81,7 @@
         copy(block).start()
 
     def steps(body):
-        pl.loop(0, half // WIDE)(lambda step: body(pl.multiple_of(step * WIDE, WIDE), WIDE))
+        pl.loop(0, half // WIDE, unroll=2)(lambda step: body(pl.multiple_of(step * WIDE, WIDE), WIDE))
         if half % WIDE:
             body(half - half % WIDE, half % WIDE)
 

time: 51.6 us -> 51.6 us (level)
  no operation moved by 1% of the time
where the time goes in v19:
time: 51.6 us; the launch traced here: 51.5 us
  Pallas kernels  21.9 us (42%)
  starting transfers between devices  13.6 us (26%)
  waiting for transfers between devices  12.7 us (25%)
  local copies, waits for them, and re-layouts  2.36 us (5%)
  other arithmetic  0.59 us (1%)
    ppermute x6, starting transfers between devices, across(): return lax.ppermute(x, 'wide', [(i, i ^ apart) for i in range(4)])  10.1 us
    ppermute x6, waiting for transfers between devices, across(): return lax.ppermute(x, 'wide', [(i, i ^ apart) for i in range(4)])  9.01 us
    pallas_call x1, Pallas kernels, stream_sums(): pl.pallas_call(functools.partial(stream_kernel, first, steps), out_shape=...  8.71 us
    pallas_call x2, Pallas kernels, half_sums(): pl.pallas_call(functools.partial(half_sums_kernel, first, half, mine), ou...  8.16 us
    pallas_call x3, Pallas kernels, down(): pl.pallas_call(functools.partial(kernel, chunk[0], half, sides), out_shap...  5.06 us
    ppermute x6, waiting for transfers between devices, swap(): return lax.ppermute(x, axis, [(0, 1), (1, 0)])  3.68 us
    ppermute x6, starting transfers between devices, swap(): return lax.ppermute(x, axis, [(0, 1), (1, 0)])  3.48 us
    unnamed x20, local copies, waits for them, and re-layouts  2.29 us
  transfers between devices with their start and end apart: 12, of which 7 were waited for; matrix products, arithmetic and copies ran while one was open for 1% of the time, Pallas kernels for 33%

profile of v19, /device:TPU:0, one launch (start us, length us, event | category | flops | bytes accessed | tf_op | source)
XLA Modules:
  0.0 51.5 jit_solution(5644415845599075725)
XLA Ops:
  0.0 5.0 %collective-permute-start = (bf16[12,2048]{1,0:T(8,128)(2,1)}, bf16[12,2048]{1,0:T(8,128)(2,1)S(1)}, u32[]{:S(2)}, u32[]{:S(2)}) collective-permute-start(bf16[12,2048]{1,0:T(8,128)(2,1)} %param.4), channel_id=1, source_target_pairs={{0,12},{4,8},{8,4},{12,0},{1,13},{5,9},{9,5},{13,1},{2,14},{6,10},... | collective-permute-start | bytes 147464 | tf_op jit(solution)/shard_map/ppermute | solution.py:264
  5.1 0.6 %collective-permute-start.1 = (bf16[12,2048]{1,0:T(8,128)(2,1)}, bf16[12,2048]{1,0:T(8,128)(2,1)S(1)}, u32[]{:S(2)}, u32[]{:S(2)}) collective-permute-start(bf16[12,2048]{1,0:T(8,128)(2,1)} %param.4), channel_id=1, source_target_pairs={{0,8},{4,12},{8,0},{12,4},{1,9},{5,13},{9,1},{13,5},{2,10},{6,14},... | collective-permute-start | bytes 147464 | tf_op jit(solution)/shard_map/ppermute | solution.py:264
  5.7 2.5 %collective-permute-done = bf16[12,2048]{1,0:T(8,128)(2,1)S(1)} collective-permute-done((bf16[12,2048]{1,0:T(8,128)(2,1)}, bf16[12,2048]{1,0:T(8,128)(2,1)S(1)}, u32[]{:S(2)}, u32[]{:S(2)}) %collective-permute-start) | collective-permute-done | bytes 49184 | tf_op jit(solution)/shard_map/ppermute | solution.py:264
  8.3 2.6 %collective-permute-done.1 = bf16[12,2048]{1,0:T(8,128)(2,1)S(1)} collective-permute-done((bf16[12,2048]{1,0:T(8,128)(2,1)}, bf16[12,2048]{1,0:T(8,128)(2,1)S(1)}, u32[]{:S(2)}, u32[]{:S(2)}) %collective-permute-start.1) | collective-permute-done | bytes 49184 | tf_op jit(solution)/shard_map/ppermute | solution.py:264
  11.0 4.1 %half_sums.2.after = bf16[48,4096]{1,0:T(8,128)(2,1)S(1)} custom-call(bf16[48,2048]{1,0:T(8,128)(2,1)S(1)} %pad_maximum_fusion.tokens, bf16[2048,6656]{1,0:T(8,128)(2,1)S(1)} %copy-done, bf16[2048,6656]{1,0:T(8,128)(2,1)} %up.5, f32[8,128]{1,0:T(8,128)S(1)} %beside.1.after), custom_call_target="tpu_custom_call" | custom-call | flops 805306368 | bytes 16777216 | tf_op jit(solution)/shard_map/half_sums/pallas_call | solution.py:109
  15.1 4.1 %half_sums.3 = f32[48,4096]{1,0:T(8,128)S(1)} custom-call(bf16[48,2048]{1,0:T(8,128)(2,1)S(1)} %pad_maximum_fusion.tokens, bf16[2048,6656]{1,0:T(8,128)(2,1)S(1)} %copy-done, bf16[2048,6656]{1,0:T(8,128)(2,1)} %up.5, bf16[48,4096]{1,0:T(8,128)(2,1)S(1)} %half_sums.2.after), custom_call_target="tpu_custom_call" | custom-call | flops 805306368 | bytes 16777216 | tf_op jit(solution)/shard_map/half_sums/pallas_call | solution.py:109
  19.4 1.6 %collective-permute-start.4 = (bf16[48,4096]{1,0:T(8,128)(2,1)S(1)}, bf16[48,4096]{1,0:T(8,128)(2,1)S(1)}, u32[]{:S(2)}, u32[]{:S(2)}) collective-permute-start(bf16[48,4096]{1,0:T(8,128)(2,1)S(1)} %fusion), channel_id=1, source_target_pairs={{0,2},{2,0},{1,3},{3,1},{4,6},{6,4},{5,7},{7,5},{8,10},{10,8},{9,1... | collective-permute-start | bytes 1179656 | tf_op jit(solution)/shard_map/ppermute | solution.py:34
  20.9 8.7 %stream_sums.1 = (bf16[48,2560]{1,0:T(8,128)(2,1)S(1)}, f32[48,2560]{1,0:T(8,128)S(1)}) custom-call(bf16[48,2048]{1,0:T(8,128)(2,1)S(1)} %pad_maximum_fusion.tokens, bf16[2048,6656]{1,0:T(8,128)(2,1)} %gate.5, bf16[2048,6656]{1,0:T(8,128)(2,1)} %up.5), custom_call_target="tpu_custom_call" | custom-call | flops 1006632960 | bytes 20971520 | tf_op jit(solution)/shard_map/stream_sums/pallas_call | solution.py:183
  29.7 0.2 collective-permute-start.5
  29.8 1.1 %collective-permute-done.4 = bf16[48,4096]{1,0:T(8,128)(2,1)S(1)} collective-permute-done((bf16[48,4096]{1,0:T(8,128)(2,1)S(1)}, bf16[48,4096]{1,0:T(8,128)(2,1)S(1)}, u32[]{:S(2)}, u32[]{:S(2)}) %collective-permute-start.4) | collective-permute-done | bytes 393248 | tf_op jit(solution)/shard_map/ppermute | solution.py:34
  31.3 1.6 %collective-permute-start.6 = (bf16[48,2560]{1,0:T(8,128)(2,1)S(1)}, bf16[48,2560]{1,0:T(8,128)(2,1)S(1)}, u32[]{:S(2)}, u32[]{:S(2)}) collective-permute-start(bf16[48,2560]{1,0:T(8,128)(2,1)S(1)} %fusion.2), channel_id=1, source_target_pairs={{0,2},{2,0},{1,3},{3,1},{4,6},{6,4},{5,7},{7,5},{8,10},{10,8},{9,1... | collective-permute-start | bytes 737288 | tf_op jit(solution)/shard_map/ppermute | solution.py:34
  32.9 1.0 %slice-done.5 = s8[4194304]{0:T(1024)(128)(4,1)S(1)} async-done(((s8[27262976]{0:T(1024)(128)(4,1)}), s8[4194304]{0:T(1024)(128)(4,1)S(1)}, s32[]{:S(2)}) %slice-start.5) | async-done | bytes 4194328
  33.9 0.6 %slice-done.6 = s8[2097152]{0:T(1024)(128)(4,1)S(1)} async-done(((s8[27262976]{0:T(1024)(128)(4,1)}), s8[2097152]{0:T(1024)(128)(4,1)S(1)}, s32[]{:S(2)}) %slice-start.6) | async-done | bytes 2097176
  34.5 3.0 %down.3.refs_1_ = f32[48,2048]{1,0:T(8,128)S(1)} custom-call(bf16[6656,2048]{1,0:T(8,128)(2,1)S(1)} %bitcast.5, bf16[48,2048]{1,0:T(8,128)(2,1)S(1)} %fusion.1.refs_0_, bf16[48,2048]{1,0:T(8,128)(2,1)S(1)} %collective-permute-done.7.refs_1_), custom_call_target="tpu_custom_call" | custom-call | flops 805306368 | bytes 16777216 | tf_op jit(solution)/shard_map/down/pallas_call | solution.py:243
  37.5 2.2 %collective-permute-done.6 = bf16[48,2560]{1,0:T(8,128)(2,1)S(1)} collective-permute-done((bf16[48,2560]{1,0:T(8,128)(2,1)S(1)}, bf16[48,2560]{1,0:T(8,128)(2,1)S(1)}, u32[]{:S(2)}, u32[]{:S(2)}) %collective-permute-start.6) | collective-permute-done | bytes 245792 | tf_op jit(solution)/shard_map/ppermute | solution.py:34
  40.0 1.0 %down.4.total = f32[48,2048]{1,0:T(8,128)S(1)} custom-call(bf16[6656,2048]{1,0:T(8,128)(2,1)S(1)} %bitcast.5, bf16[48,1280]{1,0:T(8,128)(2,1)S(1)} %fusion.3.refs_0_, f32[48,2048]{1,0:T(8,128)S(1)} %down.3.refs_1_), custom_call_target="tpu_custom_call" | custom-call | flops 251658240 | bytes 5242880 | tf_op jit(solution)/shard_map/down/pallas_call | solution.py:243
  41.0 0.3 collective-permute-done.8.hidden
  41.3 1.0 %down.5 = (f32[24,1024]{1,0:T(8,128)S(1)}, bf16[24,1024]{1,0:T(8,128)(2,1)S(1)}, bf16[24,1024]{1,0:T(8,128)(2,1)S(1)}, bf16[24,1024]{1,0:T(8,128)(2,1)S(1)}) custom-call(bf16[6656,2048]{1,0:T(8,128)(2,1)S(1)} %bitcast.5, bf16[48,1280]{1,0:T(8,128)(2,1)S(1)} %collective-permute-done.8.hidden, f32[48,2048]{1,0:T(8,128)S(1)} %down.4.total), custom_call_target="tpu_custom_call" | custom-call | flops 251658240 | bytes 5242880 | tf_op jit(solution)/shard_map/down/pallas_call | solution.py:243
  42.3 2.9 %collective-permute-start.9 = (bf16[24,1024]{1,0:T(8,128)(2,1)S(1)}, bf16[24,1024]{1,0:T(8,128)(2,1)S(1)}, u32[]{:S(2)}, u32[]{:S(2)}) collective-permute-start(bf16[24,1024]{1,0:T(8,128)(2,1)S(1)} %get-tuple-element.24), channel_id=1, source_target_pairs={{0,12},{4,8},{8,4},{12,0},{1,13},{5,9},{9,5},{13,1},{2,14},{6,10},... | collective-permute-start | bytes 147464 | tf_op jit(solution)/shard_map/ppermute | solution.py:264
  45.3 0.2 collective-permute-start.10
  45.4 1.4 %collective-permute-start.11 = (bf16[24,1024]{1,0:T(8,128)(2,1)S(1)}, bf16[24,1024]{1,0:T(8,128)(2,1)S(1)}, u32[]{:S(2)}, u32[]{:S(2)}) collective-permute-start(bf16[24,1024]{1,0:T(8,128)(2,1)S(1)} %get-tuple-element.26), channel_id=1, source_target_pairs={{0,4},{4,0},{8,12},{12,8},{1,5},{5,1},{9,13},{13,9},{2,6},{6,2},{1... | collective-permute-start | bytes 147464 | tf_op jit(solution)/shard_map/ppermute | solution.py:264
  46.8 2.1 %collective-permute-done.9 = bf16[24,1024]{1,0:T(8,128)(2,1)S(1)} collective-permute-done((bf16[24,1024]{1,0:T(8,128)(2,1)S(1)}, bf16[24,1024]{1,0:T(8,128)(2,1)S(1)}, u32[]{:S(2)}, u32[]{:S(2)}) %collective-permute-start.9) | collective-permute-done | bytes 49184 | tf_op jit(solution)/shard_map/ppermute | solution.py:264
  48.9 1.8 %collective-permute-done.10 = bf16[24,1024]{1,0:T(8,128)(2,1)S(1)} collective-permute-done((bf16[24,1024]{1,0:T(8,128)(2,1)S(1)}, bf16[24,1024]{1,0:T(8,128)(2,1)S(1)}, u32[]{:S(2)}, u32[]{:S(2)}) %collective-permute-start.10) | collective-permute-done | bytes 49184 | tf_op jit(solution)/shard_map/ppermute | solution.py:264
  50.8 0.6 %copy.7 = bf16[2,8,2,1024]{3,1,2,0:T(8,128)(2,1)} copy(bf16[2,8,2,1024]{3,2,1,0:T(2,128)(2,1)S(1)} %bitcast.7) | data formatting | bytes 131072
  (42 shorter events, 1.0 us)
Async XLA Ops:
  0.0 8.2 %copy-start.1 = (bf16[12,2048]{1,0:T(8,128)(2,1)S(1)}, bf16[12,2048]{1,0:T(8,128)(2,1)}, u32[]{:S(2)}) copy-start(bf16[12,2048]{1,0:T(8,128)(2,1)} %param.4) | copy-start | bytes 147460
  0.0 11.0 %copy-start = (bf16[2048,6656]{1,0:T(8,128)(2,1)S(1)}, bf16[2048,6656]{1,0:T(8,128)(2,1)}, u32[]{:S(2)}) copy-start(bf16[2048,6656]{1,0:T(8,128)(2,1)} %gate.5) | copy-start | bytes 81788928
  0.0 8.2 %collective-permute-start = (bf16[12,2048]{1,0:T(8,128)(2,1)}, bf16[12,2048]{1,0:T(8,128)(2,1)S(1)}, u32[]{:S(2)}, u32[]{:S(2)}) collective-permute-start(bf16[12,2048]{1,0:T(8,128)(2,1)} %param.4), channel_id=1, source_target_pairs={{0,12},{4,8},{8,4},{12,0},{1,13},{5,9},{9,5},{13,1},{2,14},{6,10},... | collective-permute-start | bytes 147464 | tf_op jit(solution)/shard_map/ppermute | solution.py:264
  5.1 5.9 %collective-permute-start.2 = (bf16[12,2048]{1,0:T(8,128)(2,1)}, bf16[12,2048]{1,0:T(8,128)(2,1)S(1)}, u32[]{:S(2)}, u32[]{:S(2)}) collective-permute-start(bf16[12,2048]{1,0:T(8,128)(2,1)} %param.4), channel_id=1, source_target_pairs={{0,4},{4,0},{8,12},{12,8},{1,5},{5,1},{9,13},{13,9},{2,6},{6,2},{1... | collective-permute-start | bytes 147464 | tf_op jit(solution)/shard_map/ppermute | solution.py:264
  5.1 5.8 %collective-permute-start.1 = (bf16[12,2048]{1,0:T(8,128)(2,1)}, bf16[12,2048]{1,0:T(8,128)(2,1)S(1)}, u32[]{:S(2)}, u32[]{:S(2)}) collective-permute-start(bf16[12,2048]{1,0:T(8,128)(2,1)} %param.4), channel_id=1, source_target_pairs={{0,8},{4,12},{8,0},{12,4},{1,9},{5,13},{9,1},{13,5},{2,10},{6,14},... | collective-permute-start | bytes 147464 | tf_op jit(solution)/shard_map/ppermute | solution.py:264
  15.1 4.2 %collective-permute-start.3 = (bf16[48,4096]{1,0:T(8,128)(2,1)S(1)}, bf16[48,4096]{1,0:T(8,128)(2,1)S(1)}, u32[]{:S(2)}, u32[]{:S(2)}) collective-permute-start(bf16[48,4096]{1,0:T(8,128)(2,1)S(1)} %half_sums.2.after), channel_id=1, source_target_pairs={{0,1},{1,0},{2,3},{3,2},{4,5},{5,4},{6,7},{7,6},{8,9},{9,8},{10,11... | collective-permute-start | bytes 1179656 | tf_op jit(solution)/shard_map/ppermute | solution.py:34
  19.2 13.7 %slice-start = ((s8[27262976]{0:T(1024)(128)(4,1)}), s8[4194304]{0:T(1024)(128)(4,1)S(1)}, s32[]{:S(2)}) async-start(s8[27262976]{0:T(1024)(128)(4,1)} %bitcast.4), calls=%async_computation | async-start | bytes 8388608
  19.3 13.6 %slice-start.1 = ((s8[27262976]{0:T(1024)(128)(4,1)}), s8[4194304]{0:T(1024)(128)(4,1)S(1)}, s32[]{:S(2)}) async-start(s8[27262976]{0:T(1024)(128)(4,1)} %bitcast.4), calls=%async_computation.1 | async-start | bytes 8388608
  19.3 13.6 %slice-start.2 = ((s8[27262976]{0:T(1024)(128)(4,1)}), s8[4194304]{0:T(1024)(128)(4,1)S(1)}, s32[]{:S(2)}) async-start(s8[27262976]{0:T(1024)(128)(4,1)} %bitcast.4), calls=%async_computation.2 | async-start | bytes 8388608
  19.4 13.6 %slice-start.3 = ((s8[27262976]{0:T(1024)(128)(4,1)}), s8[4194304]{0:T(1024)(128)(4,1)S(1)}, s32[]{:S(2)}) async-start(s8[27262976]{0:T(1024)(128)(4,1)} %bitcast.4), calls=%async_computation.3 | async-start | bytes 8388608
  19.4 13.6 %slice-start.4 = ((s8[27262976]{0:T(1024)(128)(4,1)}), s8[4194304]{0:T(1024)(128)(4,1)S(1)}, s32[]{:S(2)}) async-start(s8[27262976]{0:T(1024)(128)(4,1)} %bitcast.4), calls=%async_computation.4 | async-start | bytes 8388608
  19.4 14.5 %slice-start.5 = ((s8[27262976]{0:T(1024)(128)(4,1)}), s8[4194304]{0:T(1024)(128)(4,1)S(1)}, s32[]{:S(2)}) async-start(s8[27262976]{0:T(1024)(128)(4,1)} %bitcast.4), calls=%async_computation.5 | async-start | bytes 8388608
  19.4 15.1 %slice-start.6 = ((s8[27262976]{0:T(1024)(128)(4,1)}), s8[2097152]{0:T(1024)(128)(4,1)S(1)}, s32[]{:S(2)}) async-start(s8[27262976]{0:T(1024)(128)(4,1)} %bitcast.4), calls=%async_computation.6 | async-start | bytes 4194304
  19.4 11.6 %collective-permute-start.4 = (bf16[48,4096]{1,0:T(8,128)(2,1)S(1)}, bf16[48,4096]{1,0:T(8,128)(2,1)S(1)}, u32[]{:S(2)}, u32[]{:S(2)}) collective-permute-start(bf16[48,4096]{1,0:T(8,128)(2,1)S(1)} %fusion), channel_id=1, source_target_pairs={{0,2},{2,0},{1,3},{3,1},{4,6},{6,4},{5,7},{7,5},{8,10},{10,8},{9,1... | collective-permute-start | bytes 1179656 | tf_op jit(solution)/shard_map/ppermute | solution.py:34
  29.7 1.6 %collective-permute-start.5 = (bf16[48,2560]{1,0:T(8,128)(2,1)S(1)}, bf16[48,2560]{1,0:T(8,128)(2,1)S(1)}, u32[]{:S(2)}, u32[]{:S(2)}) collective-permute-start(bf16[48,2560]{1,0:T(8,128)(2,1)S(1)} %get-tuple-element.19), channel_id=1, source_target_pairs={{0,1},{1,0},{2,3},{3,2},{4,5},{5,4},{6,7},{7,6},{8,9},{9,8},{10,11... | collective-permute-start | bytes 737288 | tf_op jit(solution)/shard_map/ppermute | solution.py:34
  31.2 1.7 %collective-permute-start.7 = (bf16[48,2048]{1,0:T(8,128)(2,1)S(1)}, bf16[48,2048]{1,0:T(8,128)(2,1)S(1)}, u32[]{:S(2)}, u32[]{:S(2)}) collective-permute-start(bf16[48,2048]{1,0:T(8,128)(2,1)S(1)} %fusion.1.refs_0_), channel_id=1, source_target_pairs={{0,1},{1,0},{2,3},{3,2},{4,5},{5,4},{6,7},{7,6},{8,9},{9,8},{10,11... | collective-permute-start | bytes 589832 | tf_op jit(solution)/shard_map/ppermute | solution.py:34
  31.3 8.4 %collective-permute-start.6 = (bf16[48,2560]{1,0:T(8,128)(2,1)S(1)}, bf16[48,2560]{1,0:T(8,128)(2,1)S(1)}, u32[]{:S(2)}, u32[]{:S(2)}) collective-permute-start(bf16[48,2560]{1,0:T(8,128)(2,1)S(1)} %fusion.2), channel_id=1, source_target_pairs={{0,2},{2,0},{1,3},{3,1},{4,6},{6,4},{5,7},{7,5},{8,10},{10,8},{9,1... | collective-permute-start | bytes 737288 | tf_op jit(solution)/shard_map/ppermute | solution.py:34
  39.9 1.4 %collective-permute-start.8 = (bf16[48,1280]{1,0:T(8,128)(2,1)S(1)}, bf16[48,1280]{1,0:T(8,128)(2,1)S(1)}, u32[]{:S(2)}, u32[]{:S(2)}) collective-permute-start(bf16[48,1280]{1,0:T(8,128)(2,1)S(1)} %fusion.3.refs_0_), channel_id=1, source_target_pairs={{0,1},{1,0},{2,3},{3,2},{4,5},{5,4},{6,7},{7,6},{8,9},{9,8},{10,11... | collective-permute-start | bytes 368648 | tf_op jit(solution)/shard_map/ppermute | solution.py:34
  42.3 6.5 %collective-permute-start.9 = (bf16[24,1024]{1,0:T(8,128)(2,1)S(1)}, bf16[24,1024]{1,0:T(8,128)(2,1)S(1)}, u32[]{:S(2)}, u32[]{:S(2)}) collective-permute-start(bf16[24,1024]{1,0:T(8,128)(2,1)S(1)} %get-tuple-element.24), channel_id=1, source_target_pairs={{0,12},{4,8},{8,4},{12,0},{1,13},{5,9},{9,5},{13,1},{2,14},{6,10},... | collective-permute-start | bytes 147464 | tf_op jit(solution)/shard_map/ppermute | solution.py:264
  45.3 5.4 %collective-permute-start.10 = (bf16[24,1024]{1,0:T(8,128)(2,1)S(1)}, bf16[24,1024]{1,0:T(8,128)(2,1)S(1)}, u32[]{:S(2)}, u32[]{:S(2)}) collective-permute-start(bf16[24,1024]{1,0:T(8,128)(2,1)S(1)} %get-tuple-element.25), channel_id=1, source_target_pairs={{0,8},{4,12},{8,0},{12,4},{1,9},{5,13},{9,1},{13,5},{2,10},{6,14},... | collective-permute-start | bytes 147464 | tf_op jit(solution)/shard_map/ppermute | solution.py:264
  45.4 5.2 %collective-permute-start.11 = (bf16[24,1024]{1,0:T(8,128)(2,1)S(1)}, bf16[24,1024]{1,0:T(8,128)(2,1)S(1)}, u32[]{:S(2)}, u32[]{:S(2)}) collective-permute-start(bf16[24,1024]{1,0:T(8,128)(2,1)S(1)} %get-tuple-element.26), channel_id=1, source_target_pairs={{0,4},{4,0},{8,12},{12,8},{1,5},{5,1},{9,13},{13,9},{2,6},{6,2},{1... | collective-permute-start | bytes 147464 | tf_op jit(solution)/shard_map/ppermute | solution.py:264

commit v20 on v18

--- a/solution.py
+++ b/solution.py
@@ -267,9 +267,11 @@
 def chunked(tokens, gate_weight, up_weight, down_weight):
     rows = tokens.shape[0]
     chunks = split(gate_weight.shape[1])
+    apart_by = (3, 1, 2)
     section = tokens
-    for apart in (3, 2, 1):
+    for apart in apart_by:
         section = lax.optimization_barrier(jnp.concatenate([section, across(tokens, apart)], axis=0))
+
     def core_sums(send, keep):
         total = keep + swap(send, "sub").astype(F32)
         return total, total.astype(BF16)
@@ -291,7 +293,8 @@
     mine = hidden_half(total, received)
     mixed = down(down_weight, chunks[1], (0,), (mine,), mixed)
     out, *blocks = down(down_weight, chunks[1], (1,), (swap(mine, "sub"),), mixed, last=True)
-    for block, apart in zip(blocks, (3, 2, 1)):
+    for apart in (3, 2, 1):
+        block = blocks[apart_by.index(apart)]
         out = lax.optimization_barrier(out + across(block, apart).astype(F32))
     return out.astype(BF16).reshape(2, rows, -1).swapaxes(0, 1).reshape(rows, -1)
 

time: 51.6 us -> 51.3 us (level)
  transfers between devices with their start and end apart: 12 -> 12, of which waited for: 7 -> 8; matrix products, arithmetic and copies ran while one was open for 1% -> 1% of each run, Pallas kernels for 33% -> 33%
where the time goes in v20:
time: 51.3 us; the launch traced here: 51.2 us
  Pallas kernels  21.9 us (43%)
  starting transfers between devices  13.6 us (27%)
  waiting for transfers between devices  12.5 us (24%)
  local copies, waits for them, and re-layouts  2.36 us (5%)
  other arithmetic  0.59 us (1%)
    ppermute x6, starting transfers between devices, across(): return lax.ppermute(x, 'wide', [(i, i ^ apart) for i in range(4)])  10.1 us
    ppermute x6, waiting for transfers between devices, across(): return lax.ppermute(x, 'wide', [(i, i ^ apart) for i in range(4)])  8.77 us
    pallas_call x1, Pallas kernels, stream_sums(): pl.pallas_call(functools.partial(stream_kernel, first, steps), out_shape=...  8.71 us
    pallas_call x2, Pallas kernels, half_sums(): pl.pallas_call(functools.partial(half_sums_kernel, first, half, mine), ou...  8.16 us
    pallas_call x3, Pallas kernels, down(): pl.pallas_call(functools.partial(kernel, chunk[0], half, sides), out_shap...  5.06 us
    ppermute x6, waiting for transfers between devices, swap(): return lax.ppermute(x, axis, [(0, 1), (1, 0)])  3.68 us
    ppermute x6, starting transfers between devices, swap(): return lax.ppermute(x, axis, [(0, 1), (1, 0)])  3.48 us
    unnamed x20, local copies, waits for them, and re-layouts  2.29 us
  transfers between devices with their start and end apart: 12, of which 8 were waited for; matrix products, arithmetic and copies ran while one was open for 1% of the time, Pallas kernels for 33%

profile of v20, /device:TPU:0, one launch (start us, length us, event | category | flops | bytes accessed | tf_op | source)
XLA Modules:
  0.0 51.2 jit_solution(1050904005147628906)
XLA Ops:
  0.0 5.0 %collective-permute-start = (bf16[12,2048]{1,0:T(8,128)(2,1)}, bf16[12,2048]{1,0:T(8,128)(2,1)S(1)}, u32[]{:S(2)}, u32[]{:S(2)}) collective-permute-start(bf16[12,2048]{1,0:T(8,128)(2,1)} %param.4), channel_id=1, source_target_pairs={{0,12},{4,8},{8,4},{12,0},{1,13},{5,9},{9,5},{13,1},{2,14},{6,10},... | collective-permute-start | bytes 147464 | tf_op jit(solution)/shard_map/ppermute | solution.py:264
  5.1 0.6 %collective-permute-start.1 = (bf16[12,2048]{1,0:T(8,128)(2,1)}, bf16[12,2048]{1,0:T(8,128)(2,1)S(1)}, u32[]{:S(2)}, u32[]{:S(2)}) collective-permute-start(bf16[12,2048]{1,0:T(8,128)(2,1)} %param.4), channel_id=1, source_target_pairs={{0,4},{4,0},{8,12},{12,8},{1,5},{5,1},{9,13},{13,9},{2,6},{6,2},{1... | collective-permute-start | bytes 147464 | tf_op jit(solution)/shard_map/ppermute | solution.py:264
  5.7 2.3 %collective-permute-done = bf16[12,2048]{1,0:T(8,128)(2,1)S(1)} collective-permute-done((bf16[12,2048]{1,0:T(8,128)(2,1)}, bf16[12,2048]{1,0:T(8,128)(2,1)S(1)}, u32[]{:S(2)}, u32[]{:S(2)}) %collective-permute-start) | collective-permute-done | bytes 49184 | tf_op jit(solution)/shard_map/ppermute | solution.py:264
  8.0 1.6 %collective-permute-done.1 = bf16[12,2048]{1,0:T(8,128)(2,1)S(1)} collective-permute-done((bf16[12,2048]{1,0:T(8,128)(2,1)}, bf16[12,2048]{1,0:T(8,128)(2,1)S(1)}, u32[]{:S(2)}, u32[]{:S(2)}) %collective-permute-start.1) | collective-permute-done | bytes 49184 | tf_op jit(solution)/shard_map/ppermute | solution.py:264
  9.7 1.3 %collective-permute-done.2 = bf16[12,2048]{1,0:T(8,128)(2,1)S(1)} collective-permute-done((bf16[12,2048]{1,0:T(8,128)(2,1)}, bf16[12,2048]{1,0:T(8,128)(2,1)S(1)}, u32[]{:S(2)}, u32[]{:S(2)}) %collective-permute-start.2) | collective-permute-done | bytes 49184 | tf_op jit(solution)/shard_map/ppermute | solution.py:264
  11.0 4.1 %half_sums.2.after = bf16[48,4096]{1,0:T(8,128)(2,1)S(1)} custom-call(bf16[48,2048]{1,0:T(8,128)(2,1)S(1)} %pad_maximum_fusion.tokens, bf16[2048,6656]{1,0:T(8,128)(2,1)S(1)} %copy-done, bf16[2048,6656]{1,0:T(8,128)(2,1)} %up.5, f32[8,128]{1,0:T(8,128)S(1)} %beside.1.after), custom_call_target="tpu_custom_call" | custom-call | flops 805306368 | bytes 16777216 | tf_op jit(solution)/shard_map/half_sums/pallas_call | solution.py:109
  15.1 4.1 %half_sums.3 = f32[48,4096]{1,0:T(8,128)S(1)} custom-call(bf16[48,2048]{1,0:T(8,128)(2,1)S(1)} %pad_maximum_fusion.tokens, bf16[2048,6656]{1,0:T(8,128)(2,1)S(1)} %copy-done, bf16[2048,6656]{1,0:T(8,128)(2,1)} %up.5, bf16[48,4096]{1,0:T(8,128)(2,1)S(1)} %half_sums.2.after), custom_call_target="tpu_custom_call" | custom-call | flops 805306368 | bytes 16777216 | tf_op jit(solution)/shard_map/half_sums/pallas_call | solution.py:109
  19.4 1.6 %collective-permute-start.4 = (bf16[48,4096]{1,0:T(8,128)(2,1)S(1)}, bf16[48,4096]{1,0:T(8,128)(2,1)S(1)}, u32[]{:S(2)}, u32[]{:S(2)}) collective-permute-start(bf16[48,4096]{1,0:T(8,128)(2,1)S(1)} %fusion), channel_id=1, source_target_pairs={{0,2},{2,0},{1,3},{3,1},{4,6},{6,4},{5,7},{7,5},{8,10},{10,8},{9,1... | collective-permute-start | bytes 1179656 | tf_op jit(solution)/shard_map/ppermute | solution.py:34
  21.0 8.7 %stream_sums.1 = (bf16[48,2560]{1,0:T(8,128)(2,1)S(1)}, f32[48,2560]{1,0:T(8,128)S(1)}) custom-call(bf16[48,2048]{1,0:T(8,128)(2,1)S(1)} %pad_maximum_fusion.tokens, bf16[2048,6656]{1,0:T(8,128)(2,1)} %gate.5, bf16[2048,6656]{1,0:T(8,128)(2,1)} %up.5), custom_call_target="tpu_custom_call" | custom-call | flops 1006632960 | bytes 20971520 | tf_op jit(solution)/shard_map/stream_sums/pallas_call | solution.py:183
  29.7 0.2 collective-permute-start.5
  29.8 1.1 %collective-permute-done.4 = bf16[48,4096]{1,0:T(8,128)(2,1)S(1)} collective-permute-done((bf16[48,4096]{1,0:T(8,128)(2,1)S(1)}, bf16[48,4096]{1,0:T(8,128)(2,1)S(1)}, u32[]{:S(2)}, u32[]{:S(2)}) %collective-permute-start.4) | collective-permute-done | bytes 393248 | tf_op jit(solution)/shard_map/ppermute | solution.py:34
  31.3 1.6 %collective-permute-start.6 = (bf16[48,2560]{1,0:T(8,128)(2,1)S(1)}, bf16[48,2560]{1,0:T(8,128)(2,1)S(1)}, u32[]{:S(2)}, u32[]{:S(2)}) collective-permute-start(bf16[48,2560]{1,0:T(8,128)(2,1)S(1)} %fusion.2), channel_id=1, source_target_pairs={{0,2},{2,0},{1,3},{3,1},{4,6},{6,4},{5,7},{7,5},{8,10},{10,8},{9,1... | collective-permute-start | bytes 737288 | tf_op jit(solution)/shard_map/ppermute | solution.py:34
  32.9 1.0 %slice-done.5 = s8[4194304]{0:T(1024)(128)(4,1)S(1)} async-done(((s8[27262976]{0:T(1024)(128)(4,1)}), s8[4194304]{0:T(1024)(128)(4,1)S(1)}, s32[]{:S(2)}) %slice-start.5) | async-done | bytes 4194328
  33.9 0.6 %slice-done.6 = s8[2097152]{0:T(1024)(128)(4,1)S(1)} async-done(((s8[27262976]{0:T(1024)(128)(4,1)}), s8[2097152]{0:T(1024)(128)(4,1)S(1)}, s32[]{:S(2)}) %slice-start.6) | async-done | bytes 2097176
  34.5 3.0 %down.3.refs_1_ = f32[48,2048]{1,0:T(8,128)S(1)} custom-call(bf16[6656,2048]{1,0:T(8,128)(2,1)S(1)} %bitcast.5, bf16[48,2048]{1,0:T(8,128)(2,1)S(1)} %fusion.1.refs_0_, bf16[48,2048]{1,0:T(8,128)(2,1)S(1)} %collective-permute-done.7.refs_1_), custom_call_target="tpu_custom_call" | custom-call | flops 805306368 | bytes 16777216 | tf_op jit(solution)/shard_map/down/pallas_call | solution.py:243
  37.5 2.2 %collective-permute-done.6 = bf16[48,2560]{1,0:T(8,128)(2,1)S(1)} collective-permute-done((bf16[48,2560]{1,0:T(8,128)(2,1)S(1)}, bf16[48,2560]{1,0:T(8,128)(2,1)S(1)}, u32[]{:S(2)}, u32[]{:S(2)}) %collective-permute-start.6) | collective-permute-done | bytes 245792 | tf_op jit(solution)/shard_map/ppermute | solution.py:34
  40.0 1.0 %down.4.total = f32[48,2048]{1,0:T(8,128)S(1)} custom-call(bf16[6656,2048]{1,0:T(8,128)(2,1)S(1)} %bitcast.5, bf16[48,1280]{1,0:T(8,128)(2,1)S(1)} %fusion.3.refs_0_, f32[48,2048]{1,0:T(8,128)S(1)} %down.3.refs_1_), custom_call_target="tpu_custom_call" | custom-call | flops 251658240 | bytes 5242880 | tf_op jit(solution)/shard_map/down/pallas_call | solution.py:243
  41.0 0.3 collective-permute-done.8.hidden
  41.3 1.0 %down.5 = (f32[24,1024]{1,0:T(8,128)S(1)}, bf16[24,1024]{1,0:T(8,128)(2,1)S(1)}, bf16[24,1024]{1,0:T(8,128)(2,1)S(1)}, bf16[24,1024]{1,0:T(8,128)(2,1)S(1)}) custom-call(bf16[6656,2048]{1,0:T(8,128)(2,1)S(1)} %bitcast.5, bf16[48,1280]{1,0:T(8,128)(2,1)S(1)} %collective-permute-done.8.hidden, f32[48,2048]{1,0:T(8,128)S(1)} %down.4.total), custom_call_target="tpu_custom_call" | custom-call | flops 251658240 | bytes 5242880 | tf_op jit(solution)/shard_map/down/pallas_call | solution.py:243
  42.3 2.9 %collective-permute-start.9 = (bf16[24,1024]{1,0:T(8,128)(2,1)S(1)}, bf16[24,1024]{1,0:T(8,128)(2,1)S(1)}, u32[]{:S(2)}, u32[]{:S(2)}) collective-permute-start(bf16[24,1024]{1,0:T(8,128)(2,1)S(1)} %get-tuple-element.24), channel_id=1, source_target_pairs={{0,12},{4,8},{8,4},{12,0},{1,13},{5,9},{9,5},{13,1},{2,14},{6,10},... | collective-permute-start | bytes 147464 | tf_op jit(solution)/shard_map/ppermute | solution.py:264
  45.3 1.5 %collective-permute-start.11 = (bf16[24,1024]{1,0:T(8,128)(2,1)S(1)}, bf16[24,1024]{1,0:T(8,128)(2,1)S(1)}, u32[]{:S(2)}, u32[]{:S(2)}) collective-permute-start(bf16[24,1024]{1,0:T(8,128)(2,1)S(1)} %get-tuple-element.26), channel_id=1, source_target_pairs={{0,4},{4,0},{8,12},{12,8},{1,5},{5,1},{9,13},{13,9},{2,6},{6,2},{1... | collective-permute-start | bytes 147464 | tf_op jit(solution)/shard_map/ppermute | solution.py:264
  46.8 2.0 %collective-permute-done.9 = bf16[24,1024]{1,0:T(8,128)(2,1)S(1)} collective-permute-done((bf16[24,1024]{1,0:T(8,128)(2,1)S(1)}, bf16[24,1024]{1,0:T(8,128)(2,1)S(1)}, u32[]{:S(2)}, u32[]{:S(2)}) %collective-permute-start.9) | collective-permute-done | bytes 49184 | tf_op jit(solution)/shard_map/ppermute | solution.py:264
  48.8 1.5 %collective-permute-done.10 = bf16[24,1024]{1,0:T(8,128)(2,1)S(1)} collective-permute-done((bf16[24,1024]{1,0:T(8,128)(2,1)S(1)}, bf16[24,1024]{1,0:T(8,128)(2,1)S(1)}, u32[]{:S(2)}, u32[]{:S(2)}) %collective-permute-start.10) | collective-permute-done | bytes 49184 | tf_op jit(solution)/shard_map/ppermute | solution.py:264
  50.6 0.6 %copy.7 = bf16[2,8,2,1024]{3,1,2,0:T(8,128)(2,1)} copy(bf16[2,8,2,1024]{3,2,1,0:T(2,128)(2,1)S(1)} %bitcast.7) | data formatting | bytes 131072
  (42 shorter events, 1.0 us)
Async XLA Ops:
  0.0 8.0 %copy-start.1 = (bf16[12,2048]{1,0:T(8,128)(2,1)S(1)}, bf16[12,2048]{1,0:T(8,128)(2,1)}, u32[]{:S(2)}) copy-start(bf16[12,2048]{1,0:T(8,128)(2,1)} %param.4) | copy-start | bytes 147460
  0.0 11.0 %copy-start = (bf16[2048,6656]{1,0:T(8,128)(2,1)S(1)}, bf16[2048,6656]{1,0:T(8,128)(2,1)}, u32[]{:S(2)}) copy-start(bf16[2048,6656]{1,0:T(8,128)(2,1)} %gate.5) | copy-start | bytes 81788928
  0.0 8.0 %collective-permute-start = (bf16[12,2048]{1,0:T(8,128)(2,1)}, bf16[12,2048]{1,0:T(8,128)(2,1)S(1)}, u32[]{:S(2)}, u32[]{:S(2)}) collective-permute-start(bf16[12,2048]{1,0:T(8,128)(2,1)} %param.4), channel_id=1, source_target_pairs={{0,12},{4,8},{8,4},{12,0},{1,13},{5,9},{9,5},{13,1},{2,14},{6,10},... | collective-permute-start | bytes 147464 | tf_op jit(solution)/shard_map/ppermute | solution.py:264
  5.1 5.9 %collective-permute-start.2 = (bf16[12,2048]{1,0:T(8,128)(2,1)}, bf16[12,2048]{1,0:T(8,128)(2,1)S(1)}, u32[]{:S(2)}, u32[]{:S(2)}) collective-permute-start(bf16[12,2048]{1,0:T(8,128)(2,1)} %param.4), channel_id=1, source_target_pairs={{0,8},{4,12},{8,0},{12,4},{1,9},{5,13},{9,1},{13,5},{2,10},{6,14},... | collective-permute-start | bytes 147464 | tf_op jit(solution)/shard_map/ppermute | solution.py:264
  5.1 4.6 %collective-permute-start.1 = (bf16[12,2048]{1,0:T(8,128)(2,1)}, bf16[12,2048]{1,0:T(8,128)(2,1)S(1)}, u32[]{:S(2)}, u32[]{:S(2)}) collective-permute-start(bf16[12,2048]{1,0:T(8,128)(2,1)} %param.4), channel_id=1, source_target_pairs={{0,4},{4,0},{8,12},{12,8},{1,5},{5,1},{9,13},{13,9},{2,6},{6,2},{1... | collective-permute-start | bytes 147464 | tf_op jit(solution)/shard_map/ppermute | solution.py:264
  15.1 4.2 %collective-permute-start.3 = (bf16[48,4096]{1,0:T(8,128)(2,1)S(1)}, bf16[48,4096]{1,0:T(8,128)(2,1)S(1)}, u32[]{:S(2)}, u32[]{:S(2)}) collective-permute-start(bf16[48,4096]{1,0:T(8,128)(2,1)S(1)} %half_sums.2.after), channel_id=1, source_target_pairs={{0,1},{1,0},{2,3},{3,2},{4,5},{5,4},{6,7},{7,6},{8,9},{9,8},{10,11... | collective-permute-start | bytes 1179656 | tf_op jit(solution)/shard_map/ppermute | solution.py:34
  19.2 13.7 %slice-start = ((s8[27262976]{0:T(1024)(128)(4,1)}), s8[4194304]{0:T(1024)(128)(4,1)S(1)}, s32[]{:S(2)}) async-start(s8[27262976]{0:T(1024)(128)(4,1)} %bitcast.4), calls=%async_computation | async-start | bytes 8388608
  19.3 13.6 %slice-start.1 = ((s8[27262976]{0:T(1024)(128)(4,1)}), s8[4194304]{0:T(1024)(128)(4,1)S(1)}, s32[]{:S(2)}) async-start(s8[27262976]{0:T(1024)(128)(4,1)} %bitcast.4), calls=%async_computation.1 | async-start | bytes 8388608
  19.3 13.6 %slice-start.2 = ((s8[27262976]{0:T(1024)(128)(4,1)}), s8[4194304]{0:T(1024)(128)(4,1)S(1)}, s32[]{:S(2)}) async-start(s8[27262976]{0:T(1024)(128)(4,1)} %bitcast.4), calls=%async_computation.2 | async-start | bytes 8388608
  19.4 13.6 %slice-start.3 = ((s8[27262976]{0:T(1024)(128)(4,1)}), s8[4194304]{0:T(1024)(128)(4,1)S(1)}, s32[]{:S(2)}) async-start(s8[27262976]{0:T(1024)(128)(4,1)} %bitcast.4), calls=%async_computation.3 | async-start | bytes 8388608
  19.4 13.6 %slice-start.4 = ((s8[27262976]{0:T(1024)(128)(4,1)}), s8[4194304]{0:T(1024)(128)(4,1)S(1)}, s32[]{:S(2)}) async-start(s8[27262976]{0:T(1024)(128)(4,1)} %bitcast.4), calls=%async_computation.4 | async-start | bytes 8388608
  19.4 14.5 %slice-start.5 = ((s8[27262976]{0:T(1024)(128)(4,1)}), s8[4194304]{0:T(1024)(128)(4,1)S(1)}, s32[]{:S(2)}) async-start(s8[27262976]{0:T(1024)(128)(4,1)} %bitcast.4), calls=%async_computation.5 | async-start | bytes 8388608
  19.4 15.1 %slice-start.6 = ((s8[27262976]{0:T(1024)(128)(4,1)}), s8[2097152]{0:T(1024)(128)(4,1)S(1)}, s32[]{:S(2)}) async-start(s8[27262976]{0:T(1024)(128)(4,1)} %bitcast.4), calls=%async_computation.6 | async-start | bytes 4194304
  19.4 11.6 %collective-permute-start.4 = (bf16[48,4096]{1,0:T(8,128)(2,1)S(1)}, bf16[48,4096]{1,0:T(8,128)(2,1)S(1)}, u32[]{:S(2)}, u32[]{:S(2)}) collective-permute-start(bf16[48,4096]{1,0:T(8,128)(2,1)S(1)} %fusion), channel_id=1, source_target_pairs={{0,2},{2,0},{1,3},{3,1},{4,6},{6,4},{5,7},{7,5},{8,10},{10,8},{9,1... | collective-permute-start | bytes 1179656 | tf_op jit(solution)/shard_map/ppermute | solution.py:34
  29.7 1.6 %collective-permute-start.5 = (bf16[48,2560]{1,0:T(8,128)(2,1)S(1)}, bf16[48,2560]{1,0:T(8,128)(2,1)S(1)}, u32[]{:S(2)}, u32[]{:S(2)}) collective-permute-start(bf16[48,2560]{1,0:T(8,128)(2,1)S(1)} %get-tuple-element.19), channel_id=1, source_target_pairs={{0,1},{1,0},{2,3},{3,2},{4,5},{5,4},{6,7},{7,6},{8,9},{9,8},{10,11... | collective-permute-start | bytes 737288 | tf_op jit(solution)/shard_map/ppermute | solution.py:34
  31.2 1.7 %collective-permute-start.7 = (bf16[48,2048]{1,0:T(8,128)(2,1)S(1)}, bf16[48,2048]{1,0:T(8,128)(2,1)S(1)}, u32[]{:S(2)}, u32[]{:S(2)}) collective-permute-start(bf16[48,2048]{1,0:T(8,128)(2,1)S(1)} %fusion.1.refs_0_), channel_id=1, source_target_pairs={{0,1},{1,0},{2,3},{3,2},{4,5},{5,4},{6,7},{7,6},{8,9},{9,8},{10,11... | collective-permute-start | bytes 589832 | tf_op jit(solution)/shard_map/ppermute | solution.py:34
  31.3 8.4 %collective-permute-start.6 = (bf16[48,2560]{1,0:T(8,128)(2,1)S(1)}, bf16[48,2560]{1,0:T(8,128)(2,1)S(1)}, u32[]{:S(2)}, u32[]{:S(2)}) collective-permute-start(bf16[48,2560]{1,0:T(8,128)(2,1)S(1)} %fusion.2), channel_id=1, source_target_pairs={{0,2},{2,0},{1,3},{3,1},{4,6},{6,4},{5,7},{7,5},{8,10},{10,8},{9,1... | collective-permute-start | bytes 737288 | tf_op jit(solution)/shard_map/ppermute | solution.py:34
  39.9 1.4 %collective-permute-start.8 = (bf16[48,1280]{1,0:T(8,128)(2,1)S(1)}, bf16[48,1280]{1,0:T(8,128)(2,1)S(1)}, u32[]{:S(2)}, u32[]{:S(2)}) collective-permute-start(bf16[48,1280]{1,0:T(8,128)(2,1)S(1)} %fusion.3.refs_0_), channel_id=1, source_target_pairs={{0,1},{1,0},{2,3},{3,2},{4,5},{5,4},{6,7},{7,6},{8,9},{9,8},{10,11... | collective-permute-start | bytes 368648 | tf_op jit(solution)/shard_map/ppermute | solution.py:34
  42.3 6.5 %collective-permute-start.9 = (bf16[24,1024]{1,0:T(8,128)(2,1)S(1)}, bf16[24,1024]{1,0:T(8,128)(2,1)S(1)}, u32[]{:S(2)}, u32[]{:S(2)}) collective-permute-start(bf16[24,1024]{1,0:T(8,128)(2,1)S(1)} %get-tuple-element.24), channel_id=1, source_target_pairs={{0,12},{4,8},{8,4},{12,0},{1,13},{5,9},{9,5},{13,1},{2,14},{6,10},... | collective-permute-start | bytes 147464 | tf_op jit(solution)/shard_map/ppermute | solution.py:264
  45.3 5.1 %collective-permute-start.10 = (bf16[24,1024]{1,0:T(8,128)(2,1)S(1)}, bf16[24,1024]{1,0:T(8,128)(2,1)S(1)}, u32[]{:S(2)}, u32[]{:S(2)}) collective-permute-start(bf16[24,1024]{1,0:T(8,128)(2,1)S(1)} %get-tuple-element.25), channel_id=1, source_target_pairs={{0,8},{4,12},{8,0},{12,4},{1,9},{5,13},{9,1},{13,5},{2,10},{6,14},... | collective-permute-start | bytes 147464 | tf_op jit(solution)/shard_map/ppermute | solution.py:264
  45.3 5.1 %collective-permute-start.11 = (bf16[24,1024]{1,0:T(8,128)(2,1)S(1)}, bf16[24,1024]{1,0:T(8,128)(2,1)S(1)}, u32[]{:S(2)}, u32[]{:S(2)}) collective-permute-start(bf16[24,1024]{1,0:T(8,128)(2,1)S(1)} %get-tuple-element.26), channel_id=1, source_target_pairs={{0,4},{4,0},{8,12},{12,8},{1,5},{5,1},{9,13},{13,9},{2,6},{6,2},{1... | collective-permute-start | bytes 147464 | tf_op jit(solution)/shard_map/ppermute | solution.py:264

commit v21 on v20

--- a/solution.py
+++ b/solution.py
@@ -108,7 +108,7 @@
     half = width // 2
     return pl.pallas_call(
         functools.partial(half_sums_kernel, first, half, mine),
-        out_shape=jax.ShapeDtypeStruct((rows, width), F32 if mine else BF16),
+        out_shape=jax.ShapeDtypeStruct((rows, width), F32),
         in_specs=[VMEM, VMEM, HBM, ANY],
         out_specs=VMEM,
         scratch_shapes=[pltpu.VMEM((depth, half), BF16), pltpu.SemaphoreType.DMA((half // BLOCK,))],

time: 51.3 us -> 51.3 us (level)
  no operation moved by 1% of the time
where the time goes in v21:
time: 51.3 us; the launch traced here: 51.2 us
  Pallas kernels  21.9 us (43%)
  starting transfers between devices  13.6 us (27%)
  waiting for transfers between devices  12.4 us (24%)
  local copies, waits for them, and re-layouts  2.45 us (5%)
  other arithmetic  0.57 us (1%)
    ppermute x6, starting transfers between devices, across(): return lax.ppermute(x, 'wide', [(i, i ^ apart) for i in range(4)])  10.1 us
    ppermute x6, waiting for transfers between devices, across(): return lax.ppermute(x, 'wide', [(i, i ^ apart) for i in range(4)])  8.77 us
    pallas_call x1, Pallas kernels, stream_sums(): pl.pallas_call(functools.partial(stream_kernel, first, steps), out_shape=...  8.68 us
    pallas_call x2, Pallas kernels, half_sums(): pl.pallas_call(functools.partial(half_sums_kernel, first, half, mine), ou...  8.16 us
    pallas_call x3, Pallas kernels, down(): pl.pallas_call(functools.partial(kernel, chunk[0], half, sides), out_shap...  5.06 us
    ppermute x6, waiting for transfers between devices, swap(): return lax.ppermute(x, axis, [(0, 1), (1, 0)])  3.61 us
    ppermute x6, starting transfers between devices, swap(): return lax.ppermute(x, axis, [(0, 1), (1, 0)])  3.48 us
    unnamed x20, local copies, waits for them, and re-layouts  2.38 us
  transfers between devices with their start and end apart: 12, of which 8 were waited for; matrix products, arithmetic and copies ran while one was open for 1% of the time, Pallas kernels for 33%

profile of v21, /device:TPU:0, one launch (start us, length us, event | category | flops | bytes accessed | tf_op | source)
XLA Modules:
  0.0 51.2 jit_solution(12782447764256570475)
XLA Ops:
  0.0 5.0 %collective-permute-start = (bf16[12,2048]{1,0:T(8,128)(2,1)}, bf16[12,2048]{1,0:T(8,128)(2,1)S(1)}, u32[]{:S(2)}, u32[]{:S(2)}) collective-permute-start(bf16[12,2048]{1,0:T(8,128)(2,1)} %param.4), channel_id=1, source_target_pairs={{0,12},{4,8},{8,4},{12,0},{1,13},{5,9},{9,5},{13,1},{2,14},{6,10},... | collective-permute-start | bytes 147464 | tf_op jit(solution)/shard_map/ppermute | solution.py:264
  5.1 0.6 %collective-permute-start.1 = (bf16[12,2048]{1,0:T(8,128)(2,1)}, bf16[12,2048]{1,0:T(8,128)(2,1)S(1)}, u32[]{:S(2)}, u32[]{:S(2)}) collective-permute-start(bf16[12,2048]{1,0:T(8,128)(2,1)} %param.4), channel_id=1, source_target_pairs={{0,4},{4,0},{8,12},{12,8},{1,5},{5,1},{9,13},{13,9},{2,6},{6,2},{1... | collective-permute-start | bytes 147464 | tf_op jit(solution)/shard_map/ppermute | solution.py:264
  5.7 2.3 %collective-permute-done = bf16[12,2048]{1,0:T(8,128)(2,1)S(1)} collective-permute-done((bf16[12,2048]{1,0:T(8,128)(2,1)}, bf16[12,2048]{1,0:T(8,128)(2,1)S(1)}, u32[]{:S(2)}, u32[]{:S(2)}) %collective-permute-start) | collective-permute-done | bytes 49184 | tf_op jit(solution)/shard_map/ppermute | solution.py:264
  8.0 1.6 %collective-permute-done.1 = bf16[12,2048]{1,0:T(8,128)(2,1)S(1)} collective-permute-done((bf16[12,2048]{1,0:T(8,128)(2,1)}, bf16[12,2048]{1,0:T(8,128)(2,1)S(1)}, u32[]{:S(2)}, u32[]{:S(2)}) %collective-permute-start.1) | collective-permute-done | bytes 49184 | tf_op jit(solution)/shard_map/ppermute | solution.py:264
  9.7 1.3 %collective-permute-done.2 = bf16[12,2048]{1,0:T(8,128)(2,1)S(1)} collective-permute-done((bf16[12,2048]{1,0:T(8,128)(2,1)}, bf16[12,2048]{1,0:T(8,128)(2,1)S(1)}, u32[]{:S(2)}, u32[]{:S(2)}) %collective-permute-start.2) | collective-permute-done | bytes 49184 | tf_op jit(solution)/shard_map/ppermute | solution.py:264
  11.0 4.1 %half_sums.2.after = f32[48,4096]{1,0:T(8,128)S(1)} custom-call(bf16[48,2048]{1,0:T(8,128)(2,1)S(1)} %pad_maximum_fusion.tokens, bf16[2048,6656]{1,0:T(8,128)(2,1)S(1)} %copy-done, bf16[2048,6656]{1,0:T(8,128)(2,1)} %up.5, f32[8,128]{1,0:T(8,128)S(1)} %beside.1.after), custom_call_target="tpu_custom_call" | custom-call | flops 805306368 | bytes 16777216 | tf_op jit(solution)/shard_map/half_sums/pallas_call | solution.py:109
  15.1 4.1 %half_sums.3 = f32[48,4096]{1,0:T(8,128)S(1)} custom-call(bf16[48,2048]{1,0:T(8,128)(2,1)S(1)} %pad_maximum_fusion.tokens, bf16[2048,6656]{1,0:T(8,128)(2,1)S(1)} %copy-done, bf16[2048,6656]{1,0:T(8,128)(2,1)} %up.5, f32[48,4096]{1,0:T(8,128)S(1)} %half_sums.2.after), custom_call_target="tpu_custom_call" | custom-call | flops 805306368 | bytes 16777216 | tf_op jit(solution)/shard_map/half_sums/pallas_call | solution.py:109
  19.4 1.6 %collective-permute-start.4 = (bf16[48,4096]{1,0:T(8,128)(2,1)S(1)}, bf16[48,4096]{1,0:T(8,128)(2,1)S(1)}, u32[]{:S(2)}, u32[]{:S(2)}) collective-permute-start(bf16[48,4096]{1,0:T(8,128)(2,1)S(1)} %get-tuple-element.27), channel_id=1, source_target_pairs={{0,2},{2,0},{1,3},{3,1},{4,6},{6,4},{5,7},{7,5},{8,10},{10,8},{9,1... | collective-permute-start | bytes 1179656 | tf_op jit(solution)/shard_map/ppermute | solution.py:34
  21.0 8.7 %stream_sums.1 = (bf16[48,2560]{1,0:T(8,128)(2,1)S(1)}, f32[48,2560]{1,0:T(8,128)S(1)}) custom-call(bf16[48,2048]{1,0:T(8,128)(2,1)S(1)} %pad_maximum_fusion.tokens, bf16[2048,6656]{1,0:T(8,128)(2,1)} %gate.5, bf16[2048,6656]{1,0:T(8,128)(2,1)} %up.5), custom_call_target="tpu_custom_call" | custom-call | flops 1006632960 | bytes 20971520 | tf_op jit(solution)/shard_map/stream_sums/pallas_call | solution.py:183
  29.7 0.2 collective-permute-start.5
  29.8 1.2 %collective-permute-done.4 = bf16[48,4096]{1,0:T(8,128)(2,1)S(1)} collective-permute-done((bf16[48,4096]{1,0:T(8,128)(2,1)S(1)}, bf16[48,4096]{1,0:T(8,128)(2,1)S(1)}, u32[]{:S(2)}, u32[]{:S(2)}) %collective-permute-start.4) | collective-permute-done | bytes 393248 | tf_op jit(solution)/shard_map/ppermute | solution.py:34
  31.3 1.6 %collective-permute-start.6 = (bf16[48,2560]{1,0:T(8,128)(2,1)S(1)}, bf16[48,2560]{1,0:T(8,128)(2,1)S(1)}, u32[]{:S(2)}, u32[]{:S(2)}) collective-permute-start(bf16[48,2560]{1,0:T(8,128)(2,1)S(1)} %fusion.1), channel_id=1, source_target_pairs={{0,2},{2,0},{1,3},{3,1},{4,6},{6,4},{5,7},{7,5},{8,10},{10,8},{9,1... | collective-permute-start | bytes 737288 | tf_op jit(solution)/shard_map/ppermute | solution.py:34
  32.9 1.1 %slice-done.5 = s8[4194304]{0:T(1024)(128)(4,1)S(1)} async-done(((s8[27262976]{0:T(1024)(128)(4,1)}), s8[4194304]{0:T(1024)(128)(4,1)S(1)}, s32[]{:S(2)}) %slice-start.5) | async-done | bytes 4194328
  34.0 0.6 %slice-done.6 = s8[2097152]{0:T(1024)(128)(4,1)S(1)} async-done(((s8[27262976]{0:T(1024)(128)(4,1)}), s8[2097152]{0:T(1024)(128)(4,1)S(1)}, s32[]{:S(2)}) %slice-start.6) | async-done | bytes 2097176
  34.6 3.0 %down.3.refs_1_ = f32[48,2048]{1,0:T(8,128)S(1)} custom-call(bf16[6656,2048]{1,0:T(8,128)(2,1)S(1)} %bitcast.5, bf16[48,2048]{1,0:T(8,128)(2,1)S(1)} %fusion.refs_0_, bf16[48,2048]{1,0:T(8,128)(2,1)S(1)} %collective-permute-done.7.refs_1_), custom_call_target="tpu_custom_call" | custom-call | flops 805306368 | bytes 16777216 | tf_op jit(solution)/shard_map/down/pallas_call | solution.py:243
  37.6 2.1 %collective-permute-done.6 = bf16[48,2560]{1,0:T(8,128)(2,1)S(1)} collective-permute-done((bf16[48,2560]{1,0:T(8,128)(2,1)S(1)}, bf16[48,2560]{1,0:T(8,128)(2,1)S(1)}, u32[]{:S(2)}, u32[]{:S(2)}) %collective-permute-start.6) | collective-permute-done | bytes 245792 | tf_op jit(solution)/shard_map/ppermute | solution.py:34
  40.0 1.0 %down.4.total = f32[48,2048]{1,0:T(8,128)S(1)} custom-call(bf16[6656,2048]{1,0:T(8,128)(2,1)S(1)} %bitcast.5, bf16[48,1280]{1,0:T(8,128)(2,1)S(1)} %fusion.2.refs_0_, f32[48,2048]{1,0:T(8,128)S(1)} %down.3.refs_1_), custom_call_target="tpu_custom_call" | custom-call | flops 251658240 | bytes 5242880 | tf_op jit(solution)/shard_map/down/pallas_call | solution.py:243
  41.0 0.3 collective-permute-done.8.hidden
  41.3 1.0 %down.5 = (f32[24,1024]{1,0:T(8,128)S(1)}, bf16[24,1024]{1,0:T(8,128)(2,1)S(1)}, bf16[24,1024]{1,0:T(8,128)(2,1)S(1)}, bf16[24,1024]{1,0:T(8,128)(2,1)S(1)}) custom-call(bf16[6656,2048]{1,0:T(8,128)(2,1)S(1)} %bitcast.5, bf16[48,1280]{1,0:T(8,128)(2,1)S(1)} %collective-permute-done.8.hidden, f32[48,2048]{1,0:T(8,128)S(1)} %down.4.total), custom_call_target="tpu_custom_call" | custom-call | flops 251658240 | bytes 5242880 | tf_op jit(solution)/shard_map/down/pallas_call | solution.py:243
  42.3 2.9 %collective-permute-start.9 = (bf16[24,1024]{1,0:T(8,128)(2,1)S(1)}, bf16[24,1024]{1,0:T(8,128)(2,1)S(1)}, u32[]{:S(2)}, u32[]{:S(2)}) collective-permute-start(bf16[24,1024]{1,0:T(8,128)(2,1)S(1)} %get-tuple-element.24), channel_id=1, source_target_pairs={{0,12},{4,8},{8,4},{12,0},{1,13},{5,9},{9,5},{13,1},{2,14},{6,10},... | collective-permute-start | bytes 147464 | tf_op jit(solution)/shard_map/ppermute | solution.py:264
  45.2 1.5 %collective-permute-start.11 = (bf16[24,1024]{1,0:T(8,128)(2,1)S(1)}, bf16[24,1024]{1,0:T(8,128)(2,1)S(1)}, u32[]{:S(2)}, u32[]{:S(2)}) collective-permute-start(bf16[24,1024]{1,0:T(8,128)(2,1)S(1)} %get-tuple-element.26), channel_id=1, source_target_pairs={{0,4},{4,0},{8,12},{12,8},{1,5},{5,1},{9,13},{13,9},{2,6},{6,2},{1... | collective-permute-start | bytes 147464 | tf_op jit(solution)/shard_map/ppermute | solution.py:264
  46.8 2.0 %collective-permute-done.9 = bf16[24,1024]{1,0:T(8,128)(2,1)S(1)} collective-permute-done((bf16[24,1024]{1,0:T(8,128)(2,1)S(1)}, bf16[24,1024]{1,0:T(8,128)(2,1)S(1)}, u32[]{:S(2)}, u32[]{:S(2)}) %collective-permute-start.9) | collective-permute-done | bytes 49184 | tf_op jit(solution)/shard_map/ppermute | solution.py:264
  48.8 1.5 %collective-permute-done.10 = bf16[24,1024]{1,0:T(8,128)(2,1)S(1)} collective-permute-done((bf16[24,1024]{1,0:T(8,128)(2,1)S(1)}, bf16[24,1024]{1,0:T(8,128)(2,1)S(1)}, u32[]{:S(2)}, u32[]{:S(2)}) %collective-permute-start.10) | collective-permute-done | bytes 49184 | tf_op jit(solution)/shard_map/ppermute | solution.py:264
  50.5 0.6 %copy.7 = bf16[2,8,2,1024]{3,1,2,0:T(8,128)(2,1)} copy(bf16[2,8,2,1024]{3,2,1,0:T(2,128)(2,1)S(1)} %bitcast.7) | data formatting | bytes 131072
  (42 shorter events, 1.0 us)
Async XLA Ops:
  0.0 8.0 %copy-start.1 = (bf16[12,2048]{1,0:T(8,128)(2,1)S(1)}, bf16[12,2048]{1,0:T(8,128)(2,1)}, u32[]{:S(2)}) copy-start(bf16[12,2048]{1,0:T(8,128)(2,1)} %param.4) | copy-start | bytes 147460
  0.0 11.0 %copy-start = (bf16[2048,6656]{1,0:T(8,128)(2,1)S(1)}, bf16[2048,6656]{1,0:T(8,128)(2,1)}, u32[]{:S(2)}) copy-start(bf16[2048,6656]{1,0:T(8,128)(2,1)} %gate.5) | copy-start | bytes 81788928
  0.0 8.0 %collective-permute-start = (bf16[12,2048]{1,0:T(8,128)(2,1)}, bf16[12,2048]{1,0:T(8,128)(2,1)S(1)}, u32[]{:S(2)}, u32[]{:S(2)}) collective-permute-start(bf16[12,2048]{1,0:T(8,128)(2,1)} %param.4), channel_id=1, source_target_pairs={{0,12},{4,8},{8,4},{12,0},{1,13},{5,9},{9,5},{13,1},{2,14},{6,10},... | collective-permute-start | bytes 147464 | tf_op jit(solution)/shard_map/ppermute | solution.py:264
  5.1 5.9 %collective-permute-start.2 = (bf16[12,2048]{1,0:T(8,128)(2,1)}, bf16[12,2048]{1,0:T(8,128)(2,1)S(1)}, u32[]{:S(2)}, u32[]{:S(2)}) collective-permute-start(bf16[12,2048]{1,0:T(8,128)(2,1)} %param.4), channel_id=1, source_target_pairs={{0,8},{4,12},{8,0},{12,4},{1,9},{5,13},{9,1},{13,5},{2,10},{6,14},... | collective-permute-start | bytes 147464 | tf_op jit(solution)/shard_map/ppermute | solution.py:264
  5.1 4.6 %collective-permute-start.1 = (bf16[12,2048]{1,0:T(8,128)(2,1)}, bf16[12,2048]{1,0:T(8,128)(2,1)S(1)}, u32[]{:S(2)}, u32[]{:S(2)}) collective-permute-start(bf16[12,2048]{1,0:T(8,128)(2,1)} %param.4), channel_id=1, source_target_pairs={{0,4},{4,0},{8,12},{12,8},{1,5},{5,1},{9,13},{13,9},{2,6},{6,2},{1... | collective-permute-start | bytes 147464 | tf_op jit(solution)/shard_map/ppermute | solution.py:264
  15.1 4.2 %collective-permute-start.3 = (f32[48,4096]{1,0:T(8,128)S(1)}, f32[48,4096]{1,0:T(8,128)S(1)}, u32[]{:S(2)}, u32[]{:S(2)}) collective-permute-start(f32[48,4096]{1,0:T(8,128)S(1)} %half_sums.2.after), channel_id=1, source_target_pairs={{0,1},{1,0},{2,3},{3,2},{4,5},{5,4},{6,7},{7,6},{8,9},{9,8},{10,11... | collective-permute-start | bytes 2359304 | tf_op jit(solution)/shard_map/ppermute | solution.py:34
  19.3 13.5 %slice-start = ((s8[27262976]{0:T(1024)(128)(4,1)}), s8[4194304]{0:T(1024)(128)(4,1)S(1)}, s32[]{:S(2)}) async-start(s8[27262976]{0:T(1024)(128)(4,1)} %bitcast.4), calls=%async_computation | async-start | bytes 8388608
  19.4 13.5 %slice-start.1 = ((s8[27262976]{0:T(1024)(128)(4,1)}), s8[4194304]{0:T(1024)(128)(4,1)S(1)}, s32[]{:S(2)}) async-start(s8[27262976]{0:T(1024)(128)(4,1)} %bitcast.4), calls=%async_computation.1 | async-start | bytes 8388608
  19.4 13.5 %slice-start.2 = ((s8[27262976]{0:T(1024)(128)(4,1)}), s8[4194304]{0:T(1024)(128)(4,1)S(1)}, s32[]{:S(2)}) async-start(s8[27262976]{0:T(1024)(128)(4,1)} %bitcast.4), calls=%async_computation.2 | async-start | bytes 8388608
  19.4 13.5 %slice-start.3 = ((s8[27262976]{0:T(1024)(128)(4,1)}), s8[4194304]{0:T(1024)(128)(4,1)S(1)}, s32[]{:S(2)}) async-start(s8[27262976]{0:T(1024)(128)(4,1)} %bitcast.4), calls=%async_computation.3 | async-start | bytes 8388608
  19.4 13.5 %slice-start.4 = ((s8[27262976]{0:T(1024)(128)(4,1)}), s8[4194304]{0:T(1024)(128)(4,1)S(1)}, s32[]{:S(2)}) async-start(s8[27262976]{0:T(1024)(128)(4,1)} %bitcast.4), calls=%async_computation.4 | async-start | bytes 8388608
  19.4 14.6 %slice-start.5 = ((s8[27262976]{0:T(1024)(128)(4,1)}), s8[4194304]{0:T(1024)(128)(4,1)S(1)}, s32[]{:S(2)}) async-start(s8[27262976]{0:T(1024)(128)(4,1)} %bitcast.4), calls=%async_computation.5 | async-start | bytes 8388608
  19.4 15.2 %slice-start.6 = ((s8[27262976]{0:T(1024)(128)(4,1)}), s8[2097152]{0:T(1024)(128)(4,1)S(1)}, s32[]{:S(2)}) async-start(s8[27262976]{0:T(1024)(128)(4,1)} %bitcast.4), calls=%async_computation.6 | async-start | bytes 4194304
  19.4 11.6 %collective-permute-start.4 = (bf16[48,4096]{1,0:T(8,128)(2,1)S(1)}, bf16[48,4096]{1,0:T(8,128)(2,1)S(1)}, u32[]{:S(2)}, u32[]{:S(2)}) collective-permute-start(bf16[48,4096]{1,0:T(8,128)(2,1)S(1)} %get-tuple-element.27), channel_id=1, source_target_pairs={{0,2},{2,0},{1,3},{3,1},{4,6},{6,4},{5,7},{7,5},{8,10},{10,8},{9,1... | collective-permute-start | bytes 1179656 | tf_op jit(solution)/shard_map/ppermute | solution.py:34
  29.7 1.6 %collective-permute-start.5 = (bf16[48,2560]{1,0:T(8,128)(2,1)S(1)}, bf16[48,2560]{1,0:T(8,128)(2,1)S(1)}, u32[]{:S(2)}, u32[]{:S(2)}) collective-permute-start(bf16[48,2560]{1,0:T(8,128)(2,1)S(1)} %get-tuple-element.19), channel_id=1, source_target_pairs={{0,1},{1,0},{2,3},{3,2},{4,5},{5,4},{6,7},{7,6},{8,9},{9,8},{10,11... | collective-permute-start | bytes 737288 | tf_op jit(solution)/shard_map/ppermute | solution.py:34
  31.2 1.7 %collective-permute-start.7 = (bf16[48,2048]{1,0:T(8,128)(2,1)S(1)}, bf16[48,2048]{1,0:T(8,128)(2,1)S(1)}, u32[]{:S(2)}, u32[]{:S(2)}) collective-permute-start(bf16[48,2048]{1,0:T(8,128)(2,1)S(1)} %fusion.refs_0_), channel_id=1, source_target_pairs={{0,1},{1,0},{2,3},{3,2},{4,5},{5,4},{6,7},{7,6},{8,9},{9,8},{10,11... | collective-permute-start | bytes 589832 | tf_op jit(solution)/shard_map/ppermute | solution.py:34
  31.3 8.4 %collective-permute-start.6 = (bf16[48,2560]{1,0:T(8,128)(2,1)S(1)}, bf16[48,2560]{1,0:T(8,128)(2,1)S(1)}, u32[]{:S(2)}, u32[]{:S(2)}) collective-permute-start(bf16[48,2560]{1,0:T(8,128)(2,1)S(1)} %fusion.1), channel_id=1, source_target_pairs={{0,2},{2,0},{1,3},{3,1},{4,6},{6,4},{5,7},{7,5},{8,10},{10,8},{9,1... | collective-permute-start | bytes 737288 | tf_op jit(solution)/shard_map/ppermute | solution.py:34
  39.9 1.4 %collective-permute-start.8 = (bf16[48,1280]{1,0:T(8,128)(2,1)S(1)}, bf16[48,1280]{1,0:T(8,128)(2,1)S(1)}, u32[]{:S(2)}, u32[]{:S(2)}) collective-permute-start(bf16[48,1280]{1,0:T(8,128)(2,1)S(1)} %fusion.2.refs_0_), channel_id=1, source_target_pairs={{0,1},{1,0},{2,3},{3,2},{4,5},{5,4},{6,7},{7,6},{8,9},{9,8},{10,11... | collective-permute-start | bytes 368648 | tf_op jit(solution)/shard_map/ppermute | solution.py:34
  42.3 6.5 %collective-permute-start.9 = (bf16[24,1024]{1,0:T(8,128)(2,1)S(1)}, bf16[24,1024]{1,0:T(8,128)(2,1)S(1)}, u32[]{:S(2)}, u32[]{:S(2)}) collective-permute-start(bf16[24,1024]{1,0:T(8,128)(2,1)S(1)} %get-tuple-element.24), channel_id=1, source_target_pairs={{0,12},{4,8},{8,4},{12,0},{1,13},{5,9},{9,5},{13,1},{2,14},{6,10},... | collective-permute-start | bytes 147464 | tf_op jit(solution)/shard_map/ppermute | solution.py:264
  45.2 5.1 %collective-permute-start.10 = (bf16[24,1024]{1,0:T(8,128)(2,1)S(1)}, bf16[24,1024]{1,0:T(8,128)(2,1)S(1)}, u32[]{:S(2)}, u32[]{:S(2)}) collective-permute-start(bf16[24,1024]{1,0:T(8,128)(2,1)S(1)} %get-tuple-element.25), channel_id=1, source_target_pairs={{0,8},{4,12},{8,0},{12,4},{1,9},{5,13},{9,1},{13,5},{2,10},{6,14},... | collective-permute-start | bytes 147464 | tf_op jit(solution)/shard_map/ppermute | solution.py:264
  45.2 5.1 %collective-permute-start.11 = (bf16[24,1024]{1,0:T(8,128)(2,1)S(1)}, bf16[24,1024]{1,0:T(8,128)(2,1)S(1)}, u32[]{:S(2)}, u32[]{:S(2)}) collective-permute-start(bf16[24,1024]{1,0:T(8,128)(2,1)S(1)} %get-tuple-element.26), channel_id=1, source_target_pairs={{0,4},{4,0},{8,12},{12,8},{1,5},{5,1},{9,13},{13,9},{2,6},{6,2},{1... | collective-permute-start | bytes 147464 | tf_op jit(solution)/shard_map/ppermute | solution.py:264

commit v22 on v21

--- a/solution.py
+++ b/solution.py
@@ -202,7 +202,7 @@
     part = 0.0
     for side, hidden in zip(sides, hiddens):
         start = pl.multiple_of(first + jnp.where(core == side, 0, half), BLOCK)
-        part += jnp.dot(hidden[...], weight[pl.ds(start, half), columns], preferred_element_type=F32)
+        part += jnp.dot(hidden[...], weight[pl.ds(start, hidden.shape[1]), columns], preferred_element_type=F32)
     return part
 
 
@@ -229,8 +229,9 @@
             out[:, pl.ds(at, WIDE)] = jnp.concatenate(pieces, axis=0).astype(out.dtype)
 
 
-def down(weight, chunk, sides, hiddens, total=None, last=False):
-    rows, half = hiddens[0].shape
+def down(weight, chunk, sides, hiddens, total=None, last=False, offset=0):
+    rows, units = hiddens[0].shape
+    half = chunk[1] // 2
     features = weight.shape[1]
     if last:
         packed = (rows // 2, features // 2)
@@ -241,14 +242,14 @@
         kernel = down_kernel
     operands = [held_in(weight), *hiddens] + ([] if total is None else [total])
     return pl.pallas_call(
-        functools.partial(kernel, chunk[0], half, sides),
+        functools.partial(kernel, chunk[0] + offset, half, sides),
         out_shape=out_shape,
         in_specs=[VMEM] * len(operands),
         out_specs=(VMEM,) * 4 if last else VMEM,
         compiler_params=GRANT,
         cost_estimate=pl.CostEstimate(
-            flops=2 * rows * features * half * len(sides),
-            bytes_accessed=2 * features * half * len(sides),
+            flops=2 * rows * features * units * len(sides),
+            bytes_accessed=2 * features * units * len(sides),
             transcendentals=0,
         ),
         name="down",
@@ -289,10 +290,22 @@
     mine = hidden_half(total, received)
     total, sent = core_sums(send, keep)
     mixed = down(down_weight, chunks[0], (0, 1), (mine, swap(mine, "sub")))
-    received, mixed = lax.optimization_barrier((swap(sent, "narrow"), mixed))
-    mine = hidden_half(total, received)
-    mixed = down(down_weight, chunks[1], (0,), (mine,), mixed)
-    out, *blocks = down(down_weight, chunks[1], (1,), (swap(mine, "sub"),), mixed, last=True)
+    half = chunks[1][1] // 2
+    cut = half // BLOCK // 2 * BLOCK
+
+    def part(x, start, end):
+        return jnp.concatenate([x[:, start:end], x[:, half + start : half + end]], axis=1)
+
+    received = [swap(part(sent, *ends), "narrow") for ends in ((0, cut), (cut, half))]
+    received[0], mixed = lax.optimization_barrier((received[0], mixed))
+    mine = hidden_half(part(total, 0, cut), received[0])
+    mixed = down(down_weight, chunks[1], (0, 1), (mine, swap(mine, "sub")), mixed)
+    received[1], mixed = lax.optimization_barrier((received[1], mixed))
+    mine = hidden_half(part(total, cut, half), received[1])
+    mixed = down(down_weight, chunks[1], (0,), (mine,), mixed, offset=cut)
+    out, *blocks = down(
+        down_weight, chunks[1], (1,), (swap(mine, "sub"),), mixed, last=True, offset=cut
+    )
     for apart in (3, 2, 1):
         block = blocks[apart_by.index(apart)]
         out = lax.optimization_barrier(out + across(block, apart).astype(F32))

time: 51.3 us -> 51.2 us (level)
  starting transfers between devices: 13.6 us -> 15.2 us
  local copies, waits for them, and re-layouts: 2.45 us -> 1.42 us
  waiting for transfers between devices: 12.4 us -> 11.5 us
    ppermute x6 -> x8, starting transfers between devices: 3.48 us -> 5.04 us  [swap(): return lax.ppermute(x, axis, [(0, 1), (1, 0)])]
    unnamed x20, local copies, waits for them, and re-layouts: 2.38 us -> 1.29 us
    ppermute x6 -> x8, waiting for transfers between devices: 3.61 us -> 2.7 us  [swap(): return lax.ppermute(x, axis, [(0, 1), (1, 0)])]
    pallas_call x3 -> x4, Pallas kernels: 5.06 us -> 5.16 us  [down(): pl.pallas_call(functools.partial(kernel, chunk[0] + offset, half, sides),...]
  transfers between devices with their start and end apart: 12 -> 14, of which waited for: 8 -> 10; matrix products, arithmetic and copies ran while one was open for 1% -> 0% of each run, Pallas kernels for 33% -> 34%
where the time goes in v22:
time: 51.2 us; the launch traced here: 51 us
  Pallas kernels  22 us (43%)
  starting transfers between devices  15.2 us (30%)
  waiting for transfers between devices  11.5 us (22%)
  local copies, waits for them, and re-layouts  1.42 us (3%)
  other arithmetic  0.59 us (1%)
    ppermute x6, starting transfers between devices, across(): return lax.ppermute(x, 'wide', [(i, i ^ apart) for i in range(4)])  10.1 us
    ppermute x6, waiting for transfers between devices, across(): return lax.ppermute(x, 'wide', [(i, i ^ apart) for i in range(4)])  8.81 us
    pallas_call x1, Pallas kernels, stream_sums(): pl.pallas_call(functools.partial(stream_kernel, first, steps), out_shape=...  8.68 us
    pallas_call x2, Pallas kernels, half_sums(): pl.pallas_call(functools.partial(half_sums_kernel, first, half, mine), ou...  8.16 us
    pallas_call x4, Pallas kernels, down(): pl.pallas_call(functools.partial(kernel, chunk[0] + offset, half, sides),...  5.16 us
    ppermute x8, starting transfers between devices, swap(): return lax.ppermute(x, axis, [(0, 1), (1, 0)])  5.04 us
    ppermute x8, waiting for transfers between devices, swap(): return lax.ppermute(x, axis, [(0, 1), (1, 0)])  2.7 us
    unnamed x20, local copies, waits for them, and re-layouts  1.29 us
  transfers between devices with their start and end apart: 14, of which 10 were waited for; matrix products, arithmetic and copies ran while one was open for 0% of the time, Pallas kernels for 34%

profile of v22, /device:TPU:0, one launch (start us, length us, event | category | flops | bytes accessed | tf_op | source)
XLA Modules:
  0.0 51.0 jit_solution(14810973413325752894)
XLA Ops:
  0.0 5.0 %collective-permute-start = (bf16[12,2048]{1,0:T(8,128)(2,1)}, bf16[12,2048]{1,0:T(8,128)(2,1)S(1)}, u32[]{:S(2)}, u32[]{:S(2)}) collective-permute-start(bf16[12,2048]{1,0:T(8,128)(2,1)} %param.4), channel_id=1, source_target_pairs={{0,12},{4,8},{8,4},{12,0},{1,13},{5,9},{9,5},{13,1},{2,14},{6,10},... | collective-permute-start | bytes 147464 | tf_op jit(solution)/shard_map/ppermute | solution.py:265
  5.1 0.6 %collective-permute-start.1 = (bf16[12,2048]{1,0:T(8,128)(2,1)}, bf16[12,2048]{1,0:T(8,128)(2,1)S(1)}, u32[]{:S(2)}, u32[]{:S(2)}) collective-permute-start(bf16[12,2048]{1,0:T(8,128)(2,1)} %param.4), channel_id=1, source_target_pairs={{0,4},{4,0},{8,12},{12,8},{1,5},{5,1},{9,13},{13,9},{2,6},{6,2},{1... | collective-permute-start | bytes 147464 | tf_op jit(solution)/shard_map/ppermute | solution.py:265
  5.7 2.3 %collective-permute-done = bf16[12,2048]{1,0:T(8,128)(2,1)S(1)} collective-permute-done((bf16[12,2048]{1,0:T(8,128)(2,1)}, bf16[12,2048]{1,0:T(8,128)(2,1)S(1)}, u32[]{:S(2)}, u32[]{:S(2)}) %collective-permute-start) | collective-permute-done | bytes 49184 | tf_op jit(solution)/shard_map/ppermute | solution.py:265
  8.0 1.6 %collective-permute-done.1 = bf16[12,2048]{1,0:T(8,128)(2,1)S(1)} collective-permute-done((bf16[12,2048]{1,0:T(8,128)(2,1)}, bf16[12,2048]{1,0:T(8,128)(2,1)S(1)}, u32[]{:S(2)}, u32[]{:S(2)}) %collective-permute-start.1) | collective-permute-done | bytes 49184 | tf_op jit(solution)/shard_map/ppermute | solution.py:265
  9.7 1.3 %collective-permute-done.2 = bf16[12,2048]{1,0:T(8,128)(2,1)S(1)} collective-permute-done((bf16[12,2048]{1,0:T(8,128)(2,1)}, bf16[12,2048]{1,0:T(8,128)(2,1)S(1)}, u32[]{:S(2)}, u32[]{:S(2)}) %collective-permute-start.2) | collective-permute-done | bytes 49184 | tf_op jit(solution)/shard_map/ppermute | solution.py:265
  11.0 4.1 %half_sums.2.after = f32[48,4096]{1,0:T(8,128)S(1)} custom-call(bf16[48,2048]{1,0:T(8,128)(2,1)S(1)} %pad_maximum_fusion.tokens, bf16[2048,6656]{1,0:T(8,128)(2,1)S(1)} %copy-done, bf16[2048,6656]{1,0:T(8,128)(2,1)} %up.5, f32[8,128]{1,0:T(8,128)S(1)} %beside.1.after), custom_call_target="tpu_custom_call" | custom-call | flops 805306368 | bytes 16777216 | tf_op jit(solution)/shard_map/half_sums/pallas_call | solution.py:109
  15.1 4.1 %half_sums.3 = f32[48,4096]{1,0:T(8,128)S(1)} custom-call(bf16[48,2048]{1,0:T(8,128)(2,1)S(1)} %pad_maximum_fusion.tokens, bf16[2048,6656]{1,0:T(8,128)(2,1)S(1)} %copy-done, bf16[2048,6656]{1,0:T(8,128)(2,1)} %up.5, f32[48,4096]{1,0:T(8,128)S(1)} %half_sums.2.after), custom_call_target="tpu_custom_call" | custom-call | flops 805306368 | bytes 16777216 | tf_op jit(solution)/shard_map/half_sums/pallas_call | solution.py:109
  19.4 1.6 %collective-permute-start.4 = (bf16[48,4096]{1,0:T(8,128)(2,1)S(1)}, bf16[48,4096]{1,0:T(8,128)(2,1)S(1)}, u32[]{:S(2)}, u32[]{:S(2)}) collective-permute-start(bf16[48,4096]{1,0:T(8,128)(2,1)S(1)} %get-tuple-element.33), channel_id=1, source_target_pairs={{0,2},{2,0},{1,3},{3,1},{4,6},{6,4},{5,7},{7,5},{8,10},{10,8},{9,1... | collective-permute-start | bytes 1179656 | tf_op jit(solution)/shard_map/ppermute | solution.py:34
  21.0 8.7 %stream_sums.1 = (bf16[48,2560]{1,0:T(8,128)(2,1)S(1)}, f32[48,2560]{1,0:T(8,128)S(1)}) custom-call(bf16[48,2048]{1,0:T(8,128)(2,1)S(1)} %pad_maximum_fusion.tokens, bf16[2048,6656]{1,0:T(8,128)(2,1)} %gate.5, bf16[2048,6656]{1,0:T(8,128)(2,1)} %up.5), custom_call_target="tpu_custom_call" | custom-call | flops 1006632960 | bytes 20971520 | tf_op jit(solution)/shard_map/stream_sums/pallas_call | solution.py:183
  29.8 1.2 %collective-permute-done.4 = bf16[48,4096]{1,0:T(8,128)(2,1)S(1)} collective-permute-done((bf16[48,4096]{1,0:T(8,128)(2,1)S(1)}, bf16[48,4096]{1,0:T(8,128)(2,1)S(1)}, u32[]{:S(2)}, u32[]{:S(2)}) %collective-permute-start.4) | collective-permute-done | bytes 393248 | tf_op jit(solution)/shard_map/ppermute | solution.py:34
  31.7 1.2 %collective-permute-start.7 = (bf16[48,1024]{1,0:T(8,128)(2,1)S(1)}, bf16[48,1024]{1,0:T(8,128)(2,1)S(1)}, u32[]{:S(2)}, u32[]{:S(2)}) collective-permute-start(bf16[48,1024]{1,0:T(8,128)(2,1)S(1)} %pad_maximum_fusion.4), channel_id=1, source_target_pairs={{0,2},{2,0},{1,3},{3,1},{4,6},{6,4},{5,7},{7,5},{8,10},{10,8},{9,1... | collective-permute-start | bytes 294920 | tf_op jit(solution)/shard_map/ppermute | solution.py:34
  33.0 1.0 %collective-permute-start.6 = (bf16[48,1536]{1,0:T(8,128)(2,1)S(1)}, bf16[48,1536]{1,0:T(8,128)(2,1)S(1)}, u32[]{:S(2)}, u32[]{:S(2)}) collective-permute-start(bf16[48,1536]{1,0:T(8,128)(2,1)S(1)} %pad_maximum_fusion.2), channel_id=1, source_target_pairs={{0,2},{2,0},{1,3},{3,1},{4,6},{6,4},{5,7},{7,5},{8,10},{10,8},{9,1... | collective-permute-start | bytes 442376 | tf_op jit(solution)/shard_map/ppermute | solution.py:34
  34.0 0.6 %slice-done.6 = s8[2097152]{0:T(1024)(128)(4,1)S(1)} async-done(((s8[27262976]{0:T(1024)(128)(4,1)}), s8[2097152]{0:T(1024)(128)(4,1)S(1)}, s32[]{:S(2)}) %slice-start.6) | async-done | bytes 2097176
  34.6 3.0 %down.4.refs_2_ = f32[48,2048]{1,0:T(8,128)S(1)} custom-call(bf16[6656,2048]{1,0:T(8,128)(2,1)S(1)} %bitcast.5, bf16[48,2048]{1,0:T(8,128)(2,1)S(1)} %fusion.refs_0_, bf16[48,2048]{1,0:T(8,128)(2,1)S(1)} %collective-permute-done.8.refs_1_), custom_call_target="tpu_custom_call" | custom-call | flops 805306368 | bytes 16777216 | tf_op jit(solution)/shard_map/down/pallas_call | solution.py:244
  37.7 0.5 %collective-permute-start.9 = (bf16[48,512]{1,0:T(8,128)(2,1)S(1)}, bf16[48,512]{1,0:T(8,128)(2,1)S(1)}, u32[]{:S(2)}, u32[]{:S(2)}) collective-permute-start(bf16[48,512]{1,0:T(8,128)(2,1)S(1)} %fusion.2.refs_0_), channel_id=1, source_target_pairs={{0,1},{1,0},{2,3},{3,2},{4,5},{5,4},{6,7},{7,6},{8,9},{9,8},{10,11... | collective-permute-start | bytes 147464 | tf_op jit(solution)/shard_map/ppermute | solution.py:34
  38.3 0.9 %collective-permute-done.9.refs_1_ = bf16[48,512]{1,0:T(8,128)(2,1)S(1)} collective-permute-done((bf16[48,512]{1,0:T(8,128)(2,1)S(1)}, bf16[48,512]{1,0:T(8,128)(2,1)S(1)}, u32[]{:S(2)}, u32[]{:S(2)}) %collective-permute-start.9) | collective-permute-done | bytes 49184 | tf_op jit(solution)/shard_map/ppermute | solution.py:34
  39.1 0.8 %down.5.refs_1_ = f32[48,2048]{1,0:T(8,128)S(1)} custom-call(bf16[6656,2048]{1,0:T(8,128)(2,1)S(1)} %bitcast.5, bf16[48,512]{1,0:T(8,128)(2,1)S(1)} %fusion.2.refs_0_, bf16[48,512]{1,0:T(8,128)(2,1)S(1)} %collective-permute-done.9.refs_1_, f32[48,2048]{1,0:T(8,128)S(1)} %down.4.refs_2_), custom_call_target="tpu_custom_call" | custom-call | flops 201326592 | bytes 4194304 | tf_op jit(solution)/shard_map/down/pallas_call | solution.py:244
  40.5 0.7 %down.6.total = f32[48,2048]{1,0:T(8,128)S(1)} custom-call(bf16[6656,2048]{1,0:T(8,128)(2,1)S(1)} %bitcast.5, bf16[48,768]{1,0:T(8,128)(2,1)S(1)} %fusion.1.refs_0_, f32[48,2048]{1,0:T(8,128)S(1)} %down.5.refs_1_), custom_call_target="tpu_custom_call" | custom-call | flops 150994944 | bytes 3145728 | tf_op jit(solution)/shard_map/down/pallas_call | solution.py:244
  41.5 0.7 %down.7 = (f32[24,1024]{1,0:T(8,128)S(1)}, bf16[24,1024]{1,0:T(8,128)(2,1)S(1)}, bf16[24,1024]{1,0:T(8,128)(2,1)S(1)}, bf16[24,1024]{1,0:T(8,128)(2,1)S(1)}) custom-call(bf16[6656,2048]{1,0:T(8,128)(2,1)S(1)} %bitcast.5, bf16[48,768]{1,0:T(8,128)(2,1)S(1)} %collective-permute-done.10.hidden, f32[48,2048]{1,0:T(8,128)S(1)} %down.6.total), custom_call_target="tpu_custom_call" | custom-call | flops 150994944 | bytes 3145728 | tf_op jit(solution)/shard_map/down/pallas_call | solution.py:244
  42.1 2.9 %collective-permute-start.11 = (bf16[24,1024]{1,0:T(8,128)(2,1)S(1)}, bf16[24,1024]{1,0:T(8,128)(2,1)S(1)}, u32[]{:S(2)}, u32[]{:S(2)}) collective-permute-start(bf16[24,1024]{1,0:T(8,128)(2,1)S(1)} %get-tuple-element.28), channel_id=1, source_target_pairs={{0,12},{4,8},{8,4},{12,0},{1,13},{5,9},{9,5},{13,1},{2,14},{6,10},... | collective-permute-start | bytes 147464 | tf_op jit(solution)/shard_map/ppermute | solution.py:265
  45.1 1.5 %collective-permute-start.13 = (bf16[24,1024]{1,0:T(8,128)(2,1)S(1)}, bf16[24,1024]{1,0:T(8,128)(2,1)S(1)}, u32[]{:S(2)}, u32[]{:S(2)}) collective-permute-start(bf16[24,1024]{1,0:T(8,128)(2,1)S(1)} %get-tuple-element.30), channel_id=1, source_target_pairs={{0,4},{4,0},{8,12},{12,8},{1,5},{5,1},{9,13},{13,9},{2,6},{6,2},{1... | collective-permute-start | bytes 147464 | tf_op jit(solution)/shard_map/ppermute | solution.py:265
  46.6 2.1 %collective-permute-done.11 = bf16[24,1024]{1,0:T(8,128)(2,1)S(1)} collective-permute-done((bf16[24,1024]{1,0:T(8,128)(2,1)S(1)}, bf16[24,1024]{1,0:T(8,128)(2,1)S(1)}, u32[]{:S(2)}, u32[]{:S(2)}) %collective-permute-start.11) | collective-permute-done | bytes 49184 | tf_op jit(solution)/shard_map/ppermute | solution.py:265
  48.7 1.5 %collective-permute-done.12 = bf16[24,1024]{1,0:T(8,128)(2,1)S(1)} collective-permute-done((bf16[24,1024]{1,0:T(8,128)(2,1)S(1)}, bf16[24,1024]{1,0:T(8,128)(2,1)S(1)}, u32[]{:S(2)}, u32[]{:S(2)}) %collective-permute-start.12) | collective-permute-done | bytes 49184 | tf_op jit(solution)/shard_map/ppermute | solution.py:265
  50.4 0.6 %copy.7 = bf16[2,8,2,1024]{3,1,2,0:T(8,128)(2,1)} copy(bf16[2,8,2,1024]{3,2,1,0:T(2,128)(2,1)S(1)} %bitcast.7) | data formatting | bytes 131072
  (55 shorter events, 2.3 us)
Async XLA Ops:
  0.0 8.0 %copy-start.1 = (bf16[12,2048]{1,0:T(8,128)(2,1)S(1)}, bf16[12,2048]{1,0:T(8,128)(2,1)}, u32[]{:S(2)}) copy-start(bf16[12,2048]{1,0:T(8,128)(2,1)} %param.4) | copy-start | bytes 147460
  0.0 11.0 %copy-start = (bf16[2048,6656]{1,0:T(8,128)(2,1)S(1)}, bf16[2048,6656]{1,0:T(8,128)(2,1)}, u32[]{:S(2)}) copy-start(bf16[2048,6656]{1,0:T(8,128)(2,1)} %gate.5) | copy-start | bytes 81788928
  0.0 8.0 %collective-permute-start = (bf16[12,2048]{1,0:T(8,128)(2,1)}, bf16[12,2048]{1,0:T(8,128)(2,1)S(1)}, u32[]{:S(2)}, u32[]{:S(2)}) collective-permute-start(bf16[12,2048]{1,0:T(8,128)(2,1)} %param.4), channel_id=1, source_target_pairs={{0,12},{4,8},{8,4},{12,0},{1,13},{5,9},{9,5},{13,1},{2,14},{6,10},... | collective-permute-start | bytes 147464 | tf_op jit(solution)/shard_map/ppermute | solution.py:265
  5.1 5.9 %collective-permute-start.2 = (bf16[12,2048]{1,0:T(8,128)(2,1)}, bf16[12,2048]{1,0:T(8,128)(2,1)S(1)}, u32[]{:S(2)}, u32[]{:S(2)}) collective-permute-start(bf16[12,2048]{1,0:T(8,128)(2,1)} %param.4), channel_id=1, source_target_pairs={{0,8},{4,12},{8,0},{12,4},{1,9},{5,13},{9,1},{13,5},{2,10},{6,14},... | collective-permute-start | bytes 147464 | tf_op jit(solution)/shard_map/ppermute | solution.py:265
  5.1 4.6 %collective-permute-start.1 = (bf16[12,2048]{1,0:T(8,128)(2,1)}, bf16[12,2048]{1,0:T(8,128)(2,1)S(1)}, u32[]{:S(2)}, u32[]{:S(2)}) collective-permute-start(bf16[12,2048]{1,0:T(8,128)(2,1)} %param.4), channel_id=1, source_target_pairs={{0,4},{4,0},{8,12},{12,8},{1,5},{5,1},{9,13},{13,9},{2,6},{6,2},{1... | collective-permute-start | bytes 147464 | tf_op jit(solution)/shard_map/ppermute | solution.py:265
  15.1 4.2 %collective-permute-start.3 = (f32[48,4096]{1,0:T(8,128)S(1)}, f32[48,4096]{1,0:T(8,128)S(1)}, u32[]{:S(2)}, u32[]{:S(2)}) collective-permute-start(f32[48,4096]{1,0:T(8,128)S(1)} %half_sums.2.after), channel_id=1, source_target_pairs={{0,1},{1,0},{2,3},{3,2},{4,5},{5,4},{6,7},{7,6},{8,9},{9,8},{10,11... | collective-permute-start | bytes 2359304 | tf_op jit(solution)/shard_map/ppermute | solution.py:34
  19.3 14.6 %slice-start = ((s8[27262976]{0:T(1024)(128)(4,1)}), s8[4194304]{0:T(1024)(128)(4,1)S(1)}, s32[]{:S(2)}) async-start(s8[27262976]{0:T(1024)(128)(4,1)} %bitcast.4), calls=%async_computation | async-start | bytes 8388608
  19.4 14.6 %slice-start.1 = ((s8[27262976]{0:T(1024)(128)(4,1)}), s8[4194304]{0:T(1024)(128)(4,1)S(1)}, s32[]{:S(2)}) async-start(s8[27262976]{0:T(1024)(128)(4,1)} %bitcast.4), calls=%async_computation.1 | async-start | bytes 8388608
  19.4 14.6 %slice-start.2 = ((s8[27262976]{0:T(1024)(128)(4,1)}), s8[4194304]{0:T(1024)(128)(4,1)S(1)}, s32[]{:S(2)}) async-start(s8[27262976]{0:T(1024)(128)(4,1)} %bitcast.4), calls=%async_computation.2 | async-start | bytes 8388608
  19.4 14.6 %slice-start.3 = ((s8[27262976]{0:T(1024)(128)(4,1)}), s8[4194304]{0:T(1024)(128)(4,1)S(1)}, s32[]{:S(2)}) async-start(s8[27262976]{0:T(1024)(128)(4,1)} %bitcast.4), calls=%async_computation.3 | async-start | bytes 8388608
  19.4 14.6 %slice-start.4 = ((s8[27262976]{0:T(1024)(128)(4,1)}), s8[4194304]{0:T(1024)(128)(4,1)S(1)}, s32[]{:S(2)}) async-start(s8[27262976]{0:T(1024)(128)(4,1)} %bitcast.4), calls=%async_computation.4 | async-start | bytes 8388608
  19.4 14.6 %slice-start.5 = ((s8[27262976]{0:T(1024)(128)(4,1)}), s8[4194304]{0:T(1024)(128)(4,1)S(1)}, s32[]{:S(2)}) async-start(s8[27262976]{0:T(1024)(128)(4,1)} %bitcast.4), calls=%async_computation.5 | async-start | bytes 8388608
  19.4 15.2 %slice-start.6 = ((s8[27262976]{0:T(1024)(128)(4,1)}), s8[2097152]{0:T(1024)(128)(4,1)S(1)}, s32[]{:S(2)}) async-start(s8[27262976]{0:T(1024)(128)(4,1)} %bitcast.4), calls=%async_computation.6 | async-start | bytes 4194304
  19.4 11.6 %collective-permute-start.4 = (bf16[48,4096]{1,0:T(8,128)(2,1)S(1)}, bf16[48,4096]{1,0:T(8,128)(2,1)S(1)}, u32[]{:S(2)}, u32[]{:S(2)}) collective-permute-start(bf16[48,4096]{1,0:T(8,128)(2,1)S(1)} %get-tuple-element.33), channel_id=1, source_target_pairs={{0,2},{2,0},{1,3},{3,1},{4,6},{6,4},{5,7},{7,5},{8,10},{10,8},{9,1... | collective-permute-start | bytes 1179656 | tf_op jit(solution)/shard_map/ppermute | solution.py:34
  29.7 1.6 %collective-permute-start.5 = (bf16[48,2560]{1,0:T(8,128)(2,1)S(1)}, bf16[48,2560]{1,0:T(8,128)(2,1)S(1)}, u32[]{:S(2)}, u32[]{:S(2)}) collective-permute-start(bf16[48,2560]{1,0:T(8,128)(2,1)S(1)} %get-tuple-element.21), channel_id=1, source_target_pairs={{0,1},{1,0},{2,3},{3,2},{4,5},{5,4},{6,7},{7,6},{8,9},{9,8},{10,11... | collective-permute-start | bytes 737288 | tf_op jit(solution)/shard_map/ppermute | solution.py:34
  31.5 2.4 %collective-permute-start.8 = (bf16[48,2048]{1,0:T(8,128)(2,1)S(1)}, bf16[48,2048]{1,0:T(8,128)(2,1)S(1)}, u32[]{:S(2)}, u32[]{:S(2)}) collective-permute-start(bf16[48,2048]{1,0:T(8,128)(2,1)S(1)} %fusion.refs_0_), channel_id=1, source_target_pairs={{0,1},{1,0},{2,3},{3,2},{4,5},{5,4},{6,7},{7,6},{8,9},{9,8},{10,11... | collective-permute-start | bytes 589832 | tf_op jit(solution)/shard_map/ppermute | solution.py:34
  31.7 5.9 %collective-permute-start.7 = (bf16[48,1024]{1,0:T(8,128)(2,1)S(1)}, bf16[48,1024]{1,0:T(8,128)(2,1)S(1)}, u32[]{:S(2)}, u32[]{:S(2)}) collective-permute-start(bf16[48,1024]{1,0:T(8,128)(2,1)S(1)} %pad_maximum_fusion.4), channel_id=1, source_target_pairs={{0,2},{2,0},{1,3},{3,1},{4,6},{6,4},{5,7},{7,5},{8,10},{10,8},{9,1... | collective-permute-start | bytes 294920 | tf_op jit(solution)/shard_map/ppermute | solution.py:34
  33.0 7.1 %collective-permute-start.6 = (bf16[48,1536]{1,0:T(8,128)(2,1)S(1)}, bf16[48,1536]{1,0:T(8,128)(2,1)S(1)}, u32[]{:S(2)}, u32[]{:S(2)}) collective-permute-start(bf16[48,1536]{1,0:T(8,128)(2,1)S(1)} %pad_maximum_fusion.2), channel_id=1, source_target_pairs={{0,2},{2,0},{1,3},{3,1},{4,6},{6,4},{5,7},{7,5},{8,10},{10,8},{9,1... | collective-permute-start | bytes 442376 | tf_op jit(solution)/shard_map/ppermute | solution.py:34
  37.7 1.4 %collective-permute-start.9 = (bf16[48,512]{1,0:T(8,128)(2,1)S(1)}, bf16[48,512]{1,0:T(8,128)(2,1)S(1)}, u32[]{:S(2)}, u32[]{:S(2)}) collective-permute-start(bf16[48,512]{1,0:T(8,128)(2,1)S(1)} %fusion.2.refs_0_), channel_id=1, source_target_pairs={{0,1},{1,0},{2,3},{3,2},{4,5},{5,4},{6,7},{7,6},{8,9},{9,8},{10,11... | collective-permute-start | bytes 147464 | tf_op jit(solution)/shard_map/ppermute | solution.py:34
  40.1 1.3 %collective-permute-start.10 = (bf16[48,768]{1,0:T(8,128)(2,1)S(1)}, bf16[48,768]{1,0:T(8,128)(2,1)S(1)}, u32[]{:S(2)}, u32[]{:S(2)}) collective-permute-start(bf16[48,768]{1,0:T(8,128)(2,1)S(1)} %fusion.1.refs_0_), channel_id=1, source_target_pairs={{0,1},{1,0},{2,3},{3,2},{4,5},{5,4},{6,7},{7,6},{8,9},{9,8},{10,11... | collective-permute-start | bytes 221192 | tf_op jit(solution)/shard_map/ppermute | solution.py:34
  42.1 6.5 %collective-permute-start.11 = (bf16[24,1024]{1,0:T(8,128)(2,1)S(1)}, bf16[24,1024]{1,0:T(8,128)(2,1)S(1)}, u32[]{:S(2)}, u32[]{:S(2)}) collective-permute-start(bf16[24,1024]{1,0:T(8,128)(2,1)S(1)} %get-tuple-element.28), channel_id=1, source_target_pairs={{0,12},{4,8},{8,4},{12,0},{1,13},{5,9},{9,5},{13,1},{2,14},{6,10},... | collective-permute-start | bytes 147464 | tf_op jit(solution)/shard_map/ppermute | solution.py:265
  45.1 5.2 %collective-permute-start.12 = (bf16[24,1024]{1,0:T(8,128)(2,1)S(1)}, bf16[24,1024]{1,0:T(8,128)(2,1)S(1)}, u32[]{:S(2)}, u32[]{:S(2)}) collective-permute-start(bf16[24,1024]{1,0:T(8,128)(2,1)S(1)} %get-tuple-element.29), channel_id=1, source_target_pairs={{0,8},{4,12},{8,0},{12,4},{1,9},{5,13},{9,1},{13,5},{2,10},{6,14},... | collective-permute-start | bytes 147464 | tf_op jit(solution)/shard_map/ppermute | solution.py:265
  45.1 5.2 %collective-permute-start.13 = (bf16[24,1024]{1,0:T(8,128)(2,1)S(1)}, bf16[24,1024]{1,0:T(8,128)(2,1)S(1)}, u32[]{:S(2)}, u32[]{:S(2)}) collective-permute-start(bf16[24,1024]{1,0:T(8,128)(2,1)S(1)} %get-tuple-element.30), channel_id=1, source_target_pairs={{0,4},{4,0},{8,12},{12,8},{1,5},{5,1},{9,13},{13,9},{2,6},{6,2},{1... | collective-permute-start | bytes 147464 | tf_op jit(solution)/shard_map/ppermute | solution.py:265

commit v23 on v22

--- a/solution.py
+++ b/solution.py
@@ -289,7 +289,8 @@
     received, keep = lax.optimization_barrier((swap(sent, "narrow"), keep))
     mine = hidden_half(total, received)
     total, sent = core_sums(send, keep)
-    mixed = down(down_weight, chunks[0], (0, 1), (mine, swap(mine, "sub")))
+    other = swap(mine, "sub")
+    mixed = down(down_weight, chunks[0], (0,), (mine,))
     half = chunks[1][1] // 2
     cut = half // BLOCK // 2 * BLOCK
 
@@ -299,6 +300,7 @@
     received = [swap(part(sent, *ends), "narrow") for ends in ((0, cut), (cut, half))]
     received[0], mixed = lax.optimization_barrier((received[0], mixed))
     mine = hidden_half(part(total, 0, cut), received[0])
+    mixed = down(down_weight, chunks[0], (1,), (other,), mixed)
     mixed = down(down_weight, chunks[1], (0, 1), (mine, swap(mine, "sub")), mixed)
     received[1], mixed = lax.optimization_barrier((received[1], mixed))
     mine = hidden_half(part(total, cut, half), received[1])

time: 51.2 us -> 51.4 us (level)
    pallas_call x4 -> x5, Pallas kernels: 5.16 us -> 5.29 us  [down(): pl.pallas_call(functools.partial(kernel, chunk[0] + offset, half, sides),...]
  transfers between devices with their start and end apart: 14 -> 14, of which waited for: 10 -> 9; matrix products, arithmetic and copies ran while one was open for 0% -> 0% of each run, Pallas kernels for 34% -> 34%
where the time goes in v23:
time: 51.4 us; the launch traced here: 51.3 us
  Pallas kernels  22.1 us (43%)
  starting transfers between devices  14.9 us (29%)
  waiting for transfers between devices  11.8 us (23%)
  local copies, waits for them, and re-layouts  1.43 us (3%)
  other arithmetic  0.59 us (1%)
    ppermute x6, starting transfers between devices, across(): return lax.ppermute(x, 'wide', [(i, i ^ apart) for i in range(4)])  10.1 us
    ppermute x6, waiting for transfers between devices, across(): return lax.ppermute(x, 'wide', [(i, i ^ apart) for i in range(4)])  8.84 us
    pallas_call x1, Pallas kernels, stream_sums(): pl.pallas_call(functools.partial(stream_kernel, first, steps), out_shape=...  8.68 us
    pallas_call x2, Pallas kernels, half_sums(): pl.pallas_call(functools.partial(half_sums_kernel, first, half, mine), ou...  8.16 us
    pallas_call x5, Pallas kernels, down(): pl.pallas_call(functools.partial(kernel, chunk[0] + offset, half, sides),...  5.29 us
    ppermute x8, starting transfers between devices, swap(): return lax.ppermute(x, axis, [(0, 1), (1, 0)])  4.78 us
    ppermute x8, waiting for transfers between devices, swap(): return lax.ppermute(x, axis, [(0, 1), (1, 0)])  2.98 us
    unnamed x20, local copies, waits for them, and re-layouts  1.31 us
  transfers between devices with their start and end apart: 14, of which 9 were waited for; matrix products, arithmetic and copies ran while one was open for 0% of the time, Pallas kernels for 34%

profile of v23, /device:TPU:0, one launch (start us, length us, event | category | flops | bytes accessed | tf_op | source)
XLA Modules:
  0.0 51.3 jit_solution(12280924671270973620)
XLA Ops:
  0.0 5.0 %collective-permute-start = (bf16[12,2048]{1,0:T(8,128)(2,1)}, bf16[12,2048]{1,0:T(8,128)(2,1)S(1)}, u32[]{:S(2)}, u32[]{:S(2)}) collective-permute-start(bf16[12,2048]{1,0:T(8,128)(2,1)} %param.4), channel_id=1, source_target_pairs={{0,12},{4,8},{8,4},{12,0},{1,13},{5,9},{9,5},{13,1},{2,14},{6,10},... | collective-permute-start | bytes 147464 | tf_op jit(solution)/shard_map/ppermute | solution.py:265
  5.1 0.6 %collective-permute-start.1 = (bf16[12,2048]{1,0:T(8,128)(2,1)}, bf16[12,2048]{1,0:T(8,128)(2,1)S(1)}, u32[]{:S(2)}, u32[]{:S(2)}) collective-permute-start(bf16[12,2048]{1,0:T(8,128)(2,1)} %param.4), channel_id=1, source_target_pairs={{0,4},{4,0},{8,12},{12,8},{1,5},{5,1},{9,13},{13,9},{2,6},{6,2},{1... | collective-permute-start | bytes 147464 | tf_op jit(solution)/shard_map/ppermute | solution.py:265
  5.7 2.3 %collective-permute-done = bf16[12,2048]{1,0:T(8,128)(2,1)S(1)} collective-permute-done((bf16[12,2048]{1,0:T(8,128)(2,1)}, bf16[12,2048]{1,0:T(8,128)(2,1)S(1)}, u32[]{:S(2)}, u32[]{:S(2)}) %collective-permute-start) | collective-permute-done | bytes 49184 | tf_op jit(solution)/shard_map/ppermute | solution.py:265
  8.0 1.6 %collective-permute-done.1 = bf16[12,2048]{1,0:T(8,128)(2,1)S(1)} collective-permute-done((bf16[12,2048]{1,0:T(8,128)(2,1)}, bf16[12,2048]{1,0:T(8,128)(2,1)S(1)}, u32[]{:S(2)}, u32[]{:S(2)}) %collective-permute-start.1) | collective-permute-done | bytes 49184 | tf_op jit(solution)/shard_map/ppermute | solution.py:265
  9.7 1.3 %collective-permute-done.2 = bf16[12,2048]{1,0:T(8,128)(2,1)S(1)} collective-permute-done((bf16[12,2048]{1,0:T(8,128)(2,1)}, bf16[12,2048]{1,0:T(8,128)(2,1)S(1)}, u32[]{:S(2)}, u32[]{:S(2)}) %collective-permute-start.2) | collective-permute-done | bytes 49184 | tf_op jit(solution)/shard_map/ppermute | solution.py:265
  11.0 4.1 %half_sums.2.after = f32[48,4096]{1,0:T(8,128)S(1)} custom-call(bf16[48,2048]{1,0:T(8,128)(2,1)S(1)} %pad_maximum_fusion.tokens, bf16[2048,6656]{1,0:T(8,128)(2,1)S(1)} %copy-done, bf16[2048,6656]{1,0:T(8,128)(2,1)} %up.5, f32[8,128]{1,0:T(8,128)S(1)} %beside.1.after), custom_call_target="tpu_custom_call" | custom-call | flops 805306368 | bytes 16777216 | tf_op jit(solution)/shard_map/half_sums/pallas_call | solution.py:109
  15.1 4.1 %half_sums.3 = f32[48,4096]{1,0:T(8,128)S(1)} custom-call(bf16[48,2048]{1,0:T(8,128)(2,1)S(1)} %pad_maximum_fusion.tokens, bf16[2048,6656]{1,0:T(8,128)(2,1)S(1)} %copy-done, bf16[2048,6656]{1,0:T(8,128)(2,1)} %up.5, f32[48,4096]{1,0:T(8,128)S(1)} %half_sums.2.after), custom_call_target="tpu_custom_call" | custom-call | flops 805306368 | bytes 16777216 | tf_op jit(solution)/shard_map/half_sums/pallas_call | solution.py:109
  19.4 1.6 %collective-permute-start.4 = (bf16[48,4096]{1,0:T(8,128)(2,1)S(1)}, bf16[48,4096]{1,0:T(8,128)(2,1)S(1)}, u32[]{:S(2)}, u32[]{:S(2)}) collective-permute-start(bf16[48,4096]{1,0:T(8,128)(2,1)S(1)} %get-tuple-element.33), channel_id=1, source_target_pairs={{0,2},{2,0},{1,3},{3,1},{4,6},{6,4},{5,7},{7,5},{8,10},{10,8},{9,1... | collective-permute-start | bytes 1179656 | tf_op jit(solution)/shard_map/ppermute | solution.py:34
  21.0 8.7 %stream_sums.1 = (bf16[48,2560]{1,0:T(8,128)(2,1)S(1)}, f32[48,2560]{1,0:T(8,128)S(1)}) custom-call(bf16[48,2048]{1,0:T(8,128)(2,1)S(1)} %pad_maximum_fusion.tokens, bf16[2048,6656]{1,0:T(8,128)(2,1)} %gate.5, bf16[2048,6656]{1,0:T(8,128)(2,1)} %up.5), custom_call_target="tpu_custom_call" | custom-call | flops 1006632960 | bytes 20971520 | tf_op jit(solution)/shard_map/stream_sums/pallas_call | solution.py:183
  29.8 1.2 %collective-permute-done.4 = bf16[48,4096]{1,0:T(8,128)(2,1)S(1)} collective-permute-done((bf16[48,4096]{1,0:T(8,128)(2,1)S(1)}, bf16[48,4096]{1,0:T(8,128)(2,1)S(1)}, u32[]{:S(2)}, u32[]{:S(2)}) %collective-permute-start.4) | collective-permute-done | bytes 393248 | tf_op jit(solution)/shard_map/ppermute | solution.py:34
  31.7 1.2 %collective-permute-start.7 = (bf16[48,1024]{1,0:T(8,128)(2,1)S(1)}, bf16[48,1024]{1,0:T(8,128)(2,1)S(1)}, u32[]{:S(2)}, u32[]{:S(2)}) collective-permute-start(bf16[48,1024]{1,0:T(8,128)(2,1)S(1)} %pad_maximum_fusion.4), channel_id=1, source_target_pairs={{0,2},{2,0},{1,3},{3,1},{4,6},{6,4},{5,7},{7,5},{8,10},{10,8},{9,1... | collective-permute-start | bytes 294920 | tf_op jit(solution)/shard_map/ppermute | solution.py:34
  33.0 1.0 %collective-permute-start.6 = (bf16[48,1536]{1,0:T(8,128)(2,1)S(1)}, bf16[48,1536]{1,0:T(8,128)(2,1)S(1)}, u32[]{:S(2)}, u32[]{:S(2)}) collective-permute-start(bf16[48,1536]{1,0:T(8,128)(2,1)S(1)} %pad_maximum_fusion.2), channel_id=1, source_target_pairs={{0,2},{2,0},{1,3},{3,1},{4,6},{6,4},{5,7},{7,5},{8,10},{10,8},{9,1... | collective-permute-start | bytes 442376 | tf_op jit(solution)/shard_map/ppermute | solution.py:34
  34.0 0.6 %slice-done.6 = s8[2097152]{0:T(1024)(128)(4,1)S(1)} async-done(((s8[27262976]{0:T(1024)(128)(4,1)}), s8[2097152]{0:T(1024)(128)(4,1)S(1)}, s32[]{:S(2)}) %slice-start.6) | async-done | bytes 2097176
  34.6 1.6 %down.5.refs_1_ = f32[48,2048]{1,0:T(8,128)S(1)} custom-call(bf16[6656,2048]{1,0:T(8,128)(2,1)S(1)} %bitcast.5, bf16[48,2048]{1,0:T(8,128)(2,1)S(1)} %fusion.refs_0_), custom_call_target="tpu_custom_call" | custom-call | flops 402653184 | bytes 8388608 | tf_op jit(solution)/shard_map/down/pallas_call | solution.py:244
  36.1 1.3 %collective-permute-done.7 = bf16[48,1024]{1,0:T(8,128)(2,1)S(1)} collective-permute-done((bf16[48,1024]{1,0:T(8,128)(2,1)S(1)}, bf16[48,1024]{1,0:T(8,128)(2,1)S(1)}, u32[]{:S(2)}, u32[]{:S(2)}) %collective-permute-start.7) | collective-permute-done | bytes 98336 | tf_op jit(solution)/shard_map/ppermute | solution.py:34
  37.6 1.6 %down.6.refs_2_ = f32[48,2048]{1,0:T(8,128)S(1)} custom-call(bf16[6656,2048]{1,0:T(8,128)(2,1)S(1)} %bitcast.5, bf16[48,2048]{1,0:T(8,128)(2,1)S(1)} %collective-permute-done.9.refs_0_, f32[48,2048]{1,0:T(8,128)S(1)} %down.5.refs_1_), custom_call_target="tpu_custom_call" | custom-call | flops 402653184 | bytes 8388608 | tf_op jit(solution)/shard_map/down/pallas_call | solution.py:244
  39.2 0.8 %down.7.refs_1_ = f32[48,2048]{1,0:T(8,128)S(1)} custom-call(bf16[6656,2048]{1,0:T(8,128)(2,1)S(1)} %bitcast.5, bf16[48,512]{1,0:T(8,128)(2,1)S(1)} %fusion.2.refs_0_, bf16[48,512]{1,0:T(8,128)(2,1)S(1)} %collective-permute-done.8.refs_1_, f32[48,2048]{1,0:T(8,128)S(1)} %down.6.refs_2_), custom_call_target="tpu_custom_call" | custom-call | flops 201326592 | bytes 4194304 | tf_op jit(solution)/shard_map/down/pallas_call | solution.py:244
  40.7 0.7 %down.8.total = f32[48,2048]{1,0:T(8,128)S(1)} custom-call(bf16[6656,2048]{1,0:T(8,128)(2,1)S(1)} %bitcast.5, bf16[48,768]{1,0:T(8,128)(2,1)S(1)} %fusion.1.refs_0_, f32[48,2048]{1,0:T(8,128)S(1)} %down.7.refs_1_), custom_call_target="tpu_custom_call" | custom-call | flops 150994944 | bytes 3145728 | tf_op jit(solution)/shard_map/down/pallas_call | solution.py:244
  41.6 0.7 %down.9 = (f32[24,1024]{1,0:T(8,128)S(1)}, bf16[24,1024]{1,0:T(8,128)(2,1)S(1)}, bf16[24,1024]{1,0:T(8,128)(2,1)S(1)}, bf16[24,1024]{1,0:T(8,128)(2,1)S(1)}) custom-call(bf16[6656,2048]{1,0:T(8,128)(2,1)S(1)} %bitcast.5, bf16[48,768]{1,0:T(8,128)(2,1)S(1)} %collective-permute-done.10.hidden, f32[48,2048]{1,0:T(8,128)S(1)} %down.8.total), custom_call_target="tpu_custom_call" | custom-call | flops 150994944 | bytes 3145728 | tf_op jit(solution)/shard_map/down/pallas_call | solution.py:244
  42.3 2.9 %collective-permute-start.11 = (bf16[24,1024]{1,0:T(8,128)(2,1)S(1)}, bf16[24,1024]{1,0:T(8,128)(2,1)S(1)}, u32[]{:S(2)}, u32[]{:S(2)}) collective-permute-start(bf16[24,1024]{1,0:T(8,128)(2,1)S(1)} %get-tuple-element.28), channel_id=1, source_target_pairs={{0,12},{4,8},{8,4},{12,0},{1,13},{5,9},{9,5},{13,1},{2,14},{6,10},... | collective-permute-start | bytes 147464 | tf_op jit(solution)/shard_map/ppermute | solution.py:265
  45.2 1.5 %collective-permute-start.13 = (bf16[24,1024]{1,0:T(8,128)(2,1)S(1)}, bf16[24,1024]{1,0:T(8,128)(2,1)S(1)}, u32[]{:S(2)}, u32[]{:S(2)}) collective-permute-start(bf16[24,1024]{1,0:T(8,128)(2,1)S(1)} %get-tuple-element.30), channel_id=1, source_target_pairs={{0,4},{4,0},{8,12},{12,8},{1,5},{5,1},{9,13},{13,9},{2,6},{6,2},{1... | collective-permute-start | bytes 147464 | tf_op jit(solution)/shard_map/ppermute | solution.py:265
  46.8 2.0 %collective-permute-done.11 = bf16[24,1024]{1,0:T(8,128)(2,1)S(1)} collective-permute-done((bf16[24,1024]{1,0:T(8,128)(2,1)S(1)}, bf16[24,1024]{1,0:T(8,128)(2,1)S(1)}, u32[]{:S(2)}, u32[]{:S(2)}) %collective-permute-start.11) | collective-permute-done | bytes 49184 | tf_op jit(solution)/shard_map/ppermute | solution.py:265
  48.8 1.7 %collective-permute-done.12 = bf16[24,1024]{1,0:T(8,128)(2,1)S(1)} collective-permute-done((bf16[24,1024]{1,0:T(8,128)(2,1)S(1)}, bf16[24,1024]{1,0:T(8,128)(2,1)S(1)}, u32[]{:S(2)}, u32[]{:S(2)}) %collective-permute-start.12) | collective-permute-done | bytes 49184 | tf_op jit(solution)/shard_map/ppermute | solution.py:265
  50.6 0.6 %copy.7 = bf16[2,8,2,1024]{3,1,2,0:T(8,128)(2,1)} copy(bf16[2,8,2,1024]{3,2,1,0:T(2,128)(2,1)S(1)} %bitcast.7) | data formatting | bytes 131072
  (56 shorter events, 2.4 us)
Async XLA Ops:
  0.0 8.0 %copy-start.1 = (bf16[12,2048]{1,0:T(8,128)(2,1)S(1)}, bf16[12,2048]{1,0:T(8,128)(2,1)}, u32[]{:S(2)}) copy-start(bf16[12,2048]{1,0:T(8,128)(2,1)} %param.4) | copy-start | bytes 147460
  0.0 11.0 %copy-start = (bf16[2048,6656]{1,0:T(8,128)(2,1)S(1)}, bf16[2048,6656]{1,0:T(8,128)(2,1)}, u32[]{:S(2)}) copy-start(bf16[2048,6656]{1,0:T(8,128)(2,1)} %gate.5) | copy-start | bytes 81788928
  0.0 8.0 %collective-permute-start = (bf16[12,2048]{1,0:T(8,128)(2,1)}, bf16[12,2048]{1,0:T(8,128)(2,1)S(1)}, u32[]{:S(2)}, u32[]{:S(2)}) collective-permute-start(bf16[12,2048]{1,0:T(8,128)(2,1)} %param.4), channel_id=1, source_target_pairs={{0,12},{4,8},{8,4},{12,0},{1,13},{5,9},{9,5},{13,1},{2,14},{6,10},... | collective-permute-start | bytes 147464 | tf_op jit(solution)/shard_map/ppermute | solution.py:265
  5.1 5.9 %collective-permute-start.2 = (bf16[12,2048]{1,0:T(8,128)(2,1)}, bf16[12,2048]{1,0:T(8,128)(2,1)S(1)}, u32[]{:S(2)}, u32[]{:S(2)}) collective-permute-start(bf16[12,2048]{1,0:T(8,128)(2,1)} %param.4), channel_id=1, source_target_pairs={{0,8},{4,12},{8,0},{12,4},{1,9},{5,13},{9,1},{13,5},{2,10},{6,14},... | collective-permute-start | bytes 147464 | tf_op jit(solution)/shard_map/ppermute | solution.py:265
  5.1 4.6 %collective-permute-start.1 = (bf16[12,2048]{1,0:T(8,128)(2,1)}, bf16[12,2048]{1,0:T(8,128)(2,1)S(1)}, u32[]{:S(2)}, u32[]{:S(2)}) collective-permute-start(bf16[12,2048]{1,0:T(8,128)(2,1)} %param.4), channel_id=1, source_target_pairs={{0,4},{4,0},{8,12},{12,8},{1,5},{5,1},{9,13},{13,9},{2,6},{6,2},{1... | collective-permute-start | bytes 147464 | tf_op jit(solution)/shard_map/ppermute | solution.py:265
  15.1 4.2 %collective-permute-start.3 = (f32[48,4096]{1,0:T(8,128)S(1)}, f32[48,4096]{1,0:T(8,128)S(1)}, u32[]{:S(2)}, u32[]{:S(2)}) collective-permute-start(f32[48,4096]{1,0:T(8,128)S(1)} %half_sums.2.after), channel_id=1, source_target_pairs={{0,1},{1,0},{2,3},{3,2},{4,5},{5,4},{6,7},{7,6},{8,9},{9,8},{10,11... | collective-permute-start | bytes 2359304 | tf_op jit(solution)/shard_map/ppermute | solution.py:34
  19.3 14.6 %slice-start = ((s8[27262976]{0:T(1024)(128)(4,1)}), s8[4194304]{0:T(1024)(128)(4,1)S(1)}, s32[]{:S(2)}) async-start(s8[27262976]{0:T(1024)(128)(4,1)} %bitcast.4), calls=%async_computation | async-start | bytes 8388608
  19.4 14.6 %slice-start.1 = ((s8[27262976]{0:T(1024)(128)(4,1)}), s8[4194304]{0:T(1024)(128)(4,1)S(1)}, s32[]{:S(2)}) async-start(s8[27262976]{0:T(1024)(128)(4,1)} %bitcast.4), calls=%async_computation.1 | async-start | bytes 8388608
  19.4 14.6 %slice-start.2 = ((s8[27262976]{0:T(1024)(128)(4,1)}), s8[4194304]{0:T(1024)(128)(4,1)S(1)}, s32[]{:S(2)}) async-start(s8[27262976]{0:T(1024)(128)(4,1)} %bitcast.4), calls=%async_computation.2 | async-start | bytes 8388608
  19.4 14.6 %slice-start.3 = ((s8[27262976]{0:T(1024)(128)(4,1)}), s8[4194304]{0:T(1024)(128)(4,1)S(1)}, s32[]{:S(2)}) async-start(s8[27262976]{0:T(1024)(128)(4,1)} %bitcast.4), calls=%async_computation.3 | async-start | bytes 8388608
  19.4 14.6 %slice-start.4 = ((s8[27262976]{0:T(1024)(128)(4,1)}), s8[4194304]{0:T(1024)(128)(4,1)S(1)}, s32[]{:S(2)}) async-start(s8[27262976]{0:T(1024)(128)(4,1)} %bitcast.4), calls=%async_computation.4 | async-start | bytes 8388608
  19.4 14.6 %slice-start.5 = ((s8[27262976]{0:T(1024)(128)(4,1)}), s8[4194304]{0:T(1024)(128)(4,1)S(1)}, s32[]{:S(2)}) async-start(s8[27262976]{0:T(1024)(128)(4,1)} %bitcast.4), calls=%async_computation.5 | async-start | bytes 8388608
  19.4 15.2 %slice-start.6 = ((s8[27262976]{0:T(1024)(128)(4,1)}), s8[2097152]{0:T(1024)(128)(4,1)S(1)}, s32[]{:S(2)}) async-start(s8[27262976]{0:T(1024)(128)(4,1)} %bitcast.4), calls=%async_computation.6 | async-start | bytes 4194304
  19.4 11.6 %collective-permute-start.4 = (bf16[48,4096]{1,0:T(8,128)(2,1)S(1)}, bf16[48,4096]{1,0:T(8,128)(2,1)S(1)}, u32[]{:S(2)}, u32[]{:S(2)}) collective-permute-start(bf16[48,4096]{1,0:T(8,128)(2,1)S(1)} %get-tuple-element.33), channel_id=1, source_target_pairs={{0,2},{2,0},{1,3},{3,1},{4,6},{6,4},{5,7},{7,5},{8,10},{10,8},{9,1... | collective-permute-start | bytes 1179656 | tf_op jit(solution)/shard_map/ppermute | solution.py:34
  29.7 1.6 %collective-permute-start.5 = (bf16[48,2560]{1,0:T(8,128)(2,1)S(1)}, bf16[48,2560]{1,0:T(8,128)(2,1)S(1)}, u32[]{:S(2)}, u32[]{:S(2)}) collective-permute-start(bf16[48,2560]{1,0:T(8,128)(2,1)S(1)} %get-tuple-element.21), channel_id=1, source_target_pairs={{0,1},{1,0},{2,3},{3,2},{4,5},{5,4},{6,7},{7,6},{8,9},{9,8},{10,11... | collective-permute-start | bytes 737288 | tf_op jit(solution)/shard_map/ppermute | solution.py:34
  31.5 6.1 %collective-permute-start.9 = (bf16[48,2048]{1,0:T(8,128)(2,1)S(1)}, bf16[48,2048]{1,0:T(8,128)(2,1)S(1)}, u32[]{:S(2)}, u32[]{:S(2)}) collective-permute-start(bf16[48,2048]{1,0:T(8,128)(2,1)S(1)} %fusion.refs_0_), channel_id=1, source_target_pairs={{0,1},{1,0},{2,3},{3,2},{4,5},{5,4},{6,7},{7,6},{8,9},{9,8},{10,11... | collective-permute-start | bytes 589832 | tf_op jit(solution)/shard_map/ppermute | solution.py:34
  31.7 5.7 %collective-permute-start.7 = (bf16[48,1024]{1,0:T(8,128)(2,1)S(1)}, bf16[48,1024]{1,0:T(8,128)(2,1)S(1)}, u32[]{:S(2)}, u32[]{:S(2)}) collective-permute-start(bf16[48,1024]{1,0:T(8,128)(2,1)S(1)} %pad_maximum_fusion.4), channel_id=1, source_target_pairs={{0,2},{2,0},{1,3},{3,1},{4,6},{6,4},{5,7},{7,5},{8,10},{10,8},{9,1... | collective-permute-start | bytes 294920 | tf_op jit(solution)/shard_map/ppermute | solution.py:34
  33.0 7.1 %collective-permute-start.6 = (bf16[48,1536]{1,0:T(8,128)(2,1)S(1)}, bf16[48,1536]{1,0:T(8,128)(2,1)S(1)}, u32[]{:S(2)}, u32[]{:S(2)}) collective-permute-start(bf16[48,1536]{1,0:T(8,128)(2,1)S(1)} %pad_maximum_fusion.2), channel_id=1, source_target_pairs={{0,2},{2,0},{1,3},{3,1},{4,6},{6,4},{5,7},{7,5},{8,10},{10,8},{9,1... | collective-permute-start | bytes 442376 | tf_op jit(solution)/shard_map/ppermute | solution.py:34
  37.5 1.7 %collective-permute-start.8 = (bf16[48,512]{1,0:T(8,128)(2,1)S(1)}, bf16[48,512]{1,0:T(8,128)(2,1)S(1)}, u32[]{:S(2)}, u32[]{:S(2)}) collective-permute-start(bf16[48,512]{1,0:T(8,128)(2,1)S(1)} %fusion.2.refs_0_), channel_id=1, source_target_pairs={{0,1},{1,0},{2,3},{3,2},{4,5},{5,4},{6,7},{7,6},{8,9},{9,8},{10,11... | collective-permute-start | bytes 147464 | tf_op jit(solution)/shard_map/ppermute | solution.py:34
  40.2 1.5 %collective-permute-start.10 = (bf16[48,768]{1,0:T(8,128)(2,1)S(1)}, bf16[48,768]{1,0:T(8,128)(2,1)S(1)}, u32[]{:S(2)}, u32[]{:S(2)}) collective-permute-start(bf16[48,768]{1,0:T(8,128)(2,1)S(1)} %fusion.1.refs_0_), channel_id=1, source_target_pairs={{0,1},{1,0},{2,3},{3,2},{4,5},{5,4},{6,7},{7,6},{8,9},{9,8},{10,11... | collective-permute-start | bytes 221192 | tf_op jit(solution)/shard_map/ppermute | solution.py:34
  42.3 6.4 %collective-permute-start.11 = (bf16[24,1024]{1,0:T(8,128)(2,1)S(1)}, bf16[24,1024]{1,0:T(8,128)(2,1)S(1)}, u32[]{:S(2)}, u32[]{:S(2)}) collective-permute-start(bf16[24,1024]{1,0:T(8,128)(2,1)S(1)} %get-tuple-element.28), channel_id=1, source_target_pairs={{0,12},{4,8},{8,4},{12,0},{1,13},{5,9},{9,5},{13,1},{2,14},{6,10},... | collective-permute-start | bytes 147464 | tf_op jit(solution)/shard_map/ppermute | solution.py:265
  45.2 5.2 %collective-permute-start.12 = (bf16[24,1024]{1,0:T(8,128)(2,1)S(1)}, bf16[24,1024]{1,0:T(8,128)(2,1)S(1)}, u32[]{:S(2)}, u32[]{:S(2)}) collective-permute-start(bf16[24,1024]{1,0:T(8,128)(2,1)S(1)} %get-tuple-element.29), channel_id=1, source_target_pairs={{0,8},{4,12},{8,0},{12,4},{1,9},{5,13},{9,1},{13,5},{2,10},{6,14},... | collective-permute-start | bytes 147464 | tf_op jit(solution)/shard_map/ppermute | solution.py:265
  45.2 5.2 %collective-permute-start.13 = (bf16[24,1024]{1,0:T(8,128)(2,1)S(1)}, bf16[24,1024]{1,0:T(8,128)(2,1)S(1)}, u32[]{:S(2)}, u32[]{:S(2)}) collective-permute-start(bf16[24,1024]{1,0:T(8,128)(2,1)S(1)} %get-tuple-element.30), channel_id=1, source_target_pairs={{0,4},{4,0},{8,12},{12,8},{1,5},{5,1},{9,13},{13,9},{2,6},{6,2},{1... | collective-permute-start | bytes 147464 | tf_op jit(solution)/shard_map/ppermute | solution.py:265
